TPU v7x, 32 devices: a whole 2x2x4 slice. The times are simulated.
32 devices in a mesh: sys: 4 (over y, x), edge: 8 (over z, core).
Axes of the slice: x: 2, y: 2, z: 4, core: 2. Of those that a mesh axis runs over, the one named last changes fastest.
Arguments:
- atoms: bfloat16 [4, 512, 896], P('sys', 'edge'), may hold values from -6 to 6
- cotangent: bfloat16 [4, 512, 896], P('sys', 'edge'), may hold values from -6 to 6
- experts: bfloat16 [16, 1792, 896], P('sys', 'edge'), may hold values from -0.125 to 0.125
- radial: bfloat16 [4, 16384, 896], P('sys', 'edge'), may hold values from -6 to 6
- coef: float32 [4, 16], replicated, may hold values from 0.02 to 0.5
- source: int32 [4, 16384], P('sys', 'edge'), may hold values from 0 to 511
- target: int32 [4, 16384], P('sys', 'edge'), may hold values from 0 to 511
Outputs:
- node_out: bfloat16 [4, 512, 896], P('sys', 'edge')
- atom_grad: float32 [4, 512, 896], P('sys', 'edge')
- expert_grad: float32 [16, 1792, 896], P('sys', 'edge')
All inputs are finite; a program needn't handle non-finite values.
Results may differ from a plain program's by a relative error of at most 0.018.
Values may be sent and summed in bfloat16 or wider, within the bound.
No kernel may reach another device: no remote copies, remote signals or barrier semaphores. Data moves between devices by JAX's collectives and lax.ppermute only.
A program may use at most 128 MiB of HBM per device.

v0:
```python
import jax
import jax.numpy as jnp
from jax import lax
from jax.sharding import PartitionSpec as P


def shards(atoms, cotangent, experts, radial, coef, source, target):
    sys_index = lax.axis_index("sys")
    exp_dev = experts.shape[0]
    width = experts.shape[2]
    highest = lax.Precision.HIGHEST
    all_atoms, all_cot = (
        lax.all_gather(atoms[0], "edge", axis=0, tiled=True),
        lax.all_gather(cotangent[0], "edge", axis=0, tiled=True),
    )
    atom_total = all_atoms.shape[0]
    own_coef = lax.dynamic_slice_in_dim(coef, sys_index * exp_dev, exp_dev, 1)
    own_experts = experts.astype(jnp.float32)
    chosen = own_coef
    merged_part = lax.psum_scatter(
        jnp.einsum("se,erd->srd", chosen, own_experts, precision=highest),
        "sys",
        scatter_dimension=0,
        tiled=True,
    )[0]
    merged_rows = merged_part.astype(jnp.bfloat16)
    src_idx = source[0]
    tgt_idx = target[0]
    edge_in = jnp.concatenate(
        [jnp.take(all_atoms, src_idx, axis=0), jnp.take(all_atoms, tgt_idx, axis=0)], axis=1
    )
    full_weight = lax.all_gather(merged_rows, "edge", axis=0, tiled=True)
    pre = jnp.dot(edge_in, full_weight, preferred_element_type=jnp.float32)
    radial_f = radial[0].astype(jnp.float32)
    message = (jax.nn.silu(pre) * radial_f).astype(jnp.bfloat16)
    node_part = jax.ops.segment_sum(message.astype(jnp.float32), tgt_idx, num_segments=atom_total)
    edge_cot = jnp.take(all_cot, tgt_idx, axis=0).astype(jnp.float32)
    sigma = jax.nn.sigmoid(pre)
    slope = sigma * (1.0 + pre * (1.0 - sigma))
    pre_grad = (edge_cot * radial_f * slope).astype(jnp.bfloat16)
    input_grad = lax.dot_general(
        pre_grad, full_weight, (((1,), (1,)), ((), ())), preferred_element_type=jnp.float32
    )
    input_grad = input_grad.astype(jnp.bfloat16)
    grad_part = jax.ops.segment_sum(
        input_grad[:, :width].astype(jnp.float32), src_idx, num_segments=atom_total
    )
    grad_part = grad_part + jax.ops.segment_sum(
        input_grad[:, width:].astype(jnp.float32), tgt_idx, num_segments=atom_total
    )
    node_sum = lax.psum_scatter(node_part, "edge", scatter_dimension=0, tiled=True)
    grad_sum = lax.psum_scatter(
        grad_part.astype(jnp.bfloat16), "edge", scatter_dimension=0, tiled=True
    ).astype(jnp.float32)
    merged_grad = lax.psum_scatter(
        lax.dot_general(
            edge_in, pre_grad, (((0,), (0,)), ((), ())), preferred_element_type=jnp.float32
        ),
        "edge",
        scatter_dimension=0,
        tiled=True,
    )
    piece = lax.all_gather(merged_grad[None], "sys", axis=0, tiled=True)
    chosen = lax.dynamic_slice(coef, (0, sys_index * exp_dev), (piece.shape[0], exp_dev))
    expert_grad = jnp.einsum("se,srd->erd", chosen, piece, precision=highest)
    return (node_sum.astype(jnp.bfloat16)[None], grad_sum[None], expert_grad)


def solution(mesh):
    return jax.shard_map(
        shards,
        mesh=mesh,
        in_specs=(
            P("sys", "edge", None),
            P("sys", "edge", None),
            P("sys", "edge", None),
            P("sys", "edge", None),
            P(),
            P("sys", "edge"),
            P("sys", "edge"),
        ),
        out_specs=(P("sys", "edge", None), P("sys", "edge", None), P("sys", "edge", None)),
        check_vma=False,
    )
```

profile of v0, /device:TPU:0, one launch (start us, length us, event | category | flops | bytes accessed | tf_op | source)
XLA Modules:
  0.0 366.9 jit_solution(780004315283068892)
XLA Ops:
  7.2 0.0 copy-start
  7.2 0.0 reduce-scatter.13.cloned.1.call-start
  7.2 1.4 copy-done
  8.6 4.0 %fusion.18 = f32[4,224,896]{2,0,1:T(4,128)S(1)} fusion(bf16[4,224,896]{2,1,0:T(8,128)(2,1)S(1)} %copy-done, f32[4,16]{1,0:T(4,128)} %param.13, s32[]{:T(128)S(6)} %select_n.11), kind=kOutput, calls=%fused_computation.31 | convolution fusion | flops 38535168 | bytes 4817156 | tf_op jit(solution)/shard_map/se,erd->srd/dot_general | solution.py:21
  12.6 1.9 copy.19
  14.5 0.0 copy-start.7
  14.5 0.0 copy-start.4
  14.5 0.0 reduce-scatter.13.cloned.1.call-update
  14.5 0.0 all-gather.7.cloned.1.call-start
  14.5 47.3 %reduce-scatter.13.cloned.1.call-done = f32[1,224,896]{2,1,0:T(8,128)} async-done(((f32[4,224,896]{2,1,0:T(8,128)}), f32[1,224,896]{2,1,0:T(8,128)}) %reduce-scatter.13.cloned.1.call-update) | async-done | bytes 802832
  61.9 1.9 convert_element_type.41
  63.8 0.0 all-gather.7.cloned.1.call-update
  63.8 0.0 reduce-scatter.11.cloned.1.call-start
  63.9 0.0 copy-done.7
  63.9 0.0 copy-done.4
  63.9 19.0 %all-gather.2 = bf16[1,512,896]{2,1,0:T(8,128)(2,1)S(1)} all-gather(bf16[1,64,896]{2,1,0:T(8,128)(2,1)S(1)} %copy-done.4), channel_id=4, replica_groups=mesh['sys'=4,'edge'=8] {'edge'}, dimensions={1}, use_global_device_ids=true | all-gather | bytes 1032192 | tf_op jit(solution)/shard_map/all_gather | solution.py:14
  82.9 0.0 copy-start.5
  82.9 9.5 %gather_fusion.2 = bf16[2048,896]{1,0:T(8,128)(2,1)} fusion(bf16[512,896]{1,0:T(8,128)(2,1)S(1)} %bitcast.35, s32[2048]{0:T(1024)S(1)} %fusion.24), kind=kCustom, calls=%fused_computation.2.clone | custom fusion | bytes 7348224 | tf_op jit(solution)/shard_map/jit(_take)/gather | solution.py:37
  92.5 0.0 copy-done.5
  92.5 20.9 %all-gather = bf16[1,512,896]{2,1,0:T(8,128)(2,1)S(1)} all-gather(bf16[1,64,896]{2,1,0:T(8,128)(2,1)S(1)} %copy-done.5), channel_id=2, replica_groups=mesh['sys'=4,'edge'=8] {'edge'}, dimensions={1}, use_global_device_ids=true | all-gather | bytes 1032192 | tf_op jit(solution)/shard_map/all_gather | solution.py:13
  113.4 0.0 copy-start.6
  113.4 9.5 %gather_fusion.1 = bf16[2048,896]{1,0:T(8,128)(2,1)} fusion(bf16[512,896]{1,0:T(8,128)(2,1)S(1)} %bitcast.33, s32[2048]{0:T(1024)S(1)} %fusion.24), kind=kCustom, calls=%fused_computation.1.clone | custom fusion | bytes 7348224 | tf_op jit(solution)/shard_map/jit(_take)/gather | solution.py:30
  122.9 0.0 copy-done.6
  122.9 9.5 %gather_fusion = bf16[2048,896]{1,0:T(8,128)(2,1)} fusion(bf16[512,896]{1,0:T(8,128)(2,1)S(1)} %bitcast.34, s32[2048]{0:T(1024)S(1)} %fusion.23), kind=kCustom, calls=%fused_computation.clone | custom fusion | bytes 7348224 | tf_op jit(solution)/shard_map/jit(_take)/gather | solution.py:30
  132.4 5.6 %broadcast_select_fusion = (bf16[2048,896]{1,0:T(8,128)(2,1)}, bf16[2048,896]{1,0:T(8,128)(2,1)}) fusion(bf16[2048,896]{1,0:T(8,128)(2,1)} %gather_fusion.1, pred[2048]{0:T(1024)(128)(4,1)S(1)} %compare_and_fusion, bf16[2048,896]{1,0:T(8,128)(2,1)} %gather_fusion, pred[2048]{0:T(1024)(128)(4,1)S(1)} %compare_and_fusion.1), kind=kLoop, calls=%fused_computation.24 | loop fusion | flops 3670016 | bytes 14684160 | tf_op jit(solution)/shard_map/jit(_take)/select_n | solution.py:30
  138.0 0.0 all-gather.7.cloned.1.call-done
  138.0 0.0 copy-start.2
  138.0 0.0 copy-start.3
  138.0 15.8 %fusion.2 = (bf16[2048,896]{1,0:T(8,128)(2,1)S(1)}, f32[2048,896]{1,0:T(8,128)}) fusion(bf16[1,2048,896]{2,1,0:T(8,128)(2,1)} %param.12, bf16[2048,896]{1,0:T(8,128)(2,1)} %gather_fusion.2, pred[2048]{0:T(1024)(128)(4,1)S(1)} %compare_and_fusion, bf16[1,1792,896]{2,1,0:T(8,128)(2,1)} %all-gather.7.cloned.1.call-done, ...), kind=kOutput, calls=%fused_computation.11 | convolution fusion | flops 6615203840 | bytes 28903424 | tf_op jit(solution)/shard_map/dot_general | solution.py:33
  153.8 0.0 copy-start.9
  153.8 1.8 copy-done.9
  155.6 0.0 copy-done.2
  155.6 0.0 copy-done.3
  155.6 10.0 %fusion.9 = f32[1792,896]{1,0:T(8,128)} fusion(bf16[2048,896]{1,0:T(8,128)(2,1)S(1)} %get-tuple-element.13, bf16[2048,896]{1,0:T(8,128)(2,1)S(1)} %copy-done.2, bf16[2048,896]{1,0:T(8,128)(2,1)S(1)} %copy-done.3), kind=kOutput, calls=%fused_computation.20 | convolution fusion | flops 6591348736 | bytes 17432576 | tf_op jit(solution)/shard_map/dot_general | solution.py:56
  165.6 0.0 reduce-scatter.11.cloned.1.call-update
  165.6 0.3 reduce-scatter.9.cloned.1.call-start
  165.9 12.4 %convolution_convert_fusion = bf16[2048,1792]{1,0:T(8,128)(2,1)} fusion(bf16[2048,896]{1,0:T(8,128)(2,1)} %copy-done.9, bf16[1,1792,896]{2,1,0:T(8,128)(2,1)} %all-gather.7.cloned.1.call-done), kind=kOutput, calls=%fused_computation.8 | convolution fusion | flops 6580338688 | bytes 14221312 | tf_op jit(solution)/shard_map/dot_general | solution.py:41
  178.2 18.4 %scatter_custom_fusion.1 = f32[512,896]{1,0:T(8,128)S(1)} fusion(s32[2048]{0:T(1024)S(1)} %bitcast.39, bf16[2048,1792]{1,0:T(8,128)(2,1)} %convolution_convert_fusion, f32[]{:T(128)} %constant.3.clone.1), kind=kCustom, calls=%fused_computation.15 | custom fusion | flops 3670016 | bytes 5505536 | tf_op jit(solution)/shard_map/scatter-add | solution.py:45
  196.7 19.3 %scatter_custom_fusion.2 = f32[512,896]{1,0:T(8,128)} fusion(s32[2048]{0:T(1024)S(1)} %bitcast.42, bf16[2048,1792]{1,0:T(8,128)(2,1)} %convolution_convert_fusion, f32[]{:T(128)} %constant.3.clone.1), kind=kCustom, calls=%fused_computation.13 | custom fusion | flops 3670016 | bytes 5505536 | tf_op jit(solution)/shard_map/scatter-add | solution.py:48
  215.9 2.6 add_convert_fusion
  218.5 0.0 reduce-scatter.9.cloned.1.call-update
  218.6 0.3 reduce-scatter.7.cloned.1.call-start
  218.9 0.0 copy-start.8
  218.9 21.4 %scatter_custom_fusion = f32[512,896]{1,0:T(8,128)} fusion(s32[2048]{0:T(1024)S(1)} %bitcast.43, f32[2048,896]{1,0:T(8,128)} %get-tuple-element.14, bf16[1,2048,896]{2,1,0:T(8,128)(2,1)} %param.12, f32[]{:T(128)} %constant.19.clone.1, f32[]{:T(128)} %constant.3.clone.1), kind=kCustom, calls=%fused_computation.17 | custom fusion | flops 16515072 | bytes 12845064 | tf_op jit(solution)/shard_map/scatter-add | solution.py:36
  240.3 0.0 reduce-scatter.7.cloned.1.call-update
  240.3 0.0 all-gather.9.cloned.1.call-start
  240.4 0.0 reduce-scatter.11.cloned.1.call-done
  240.4 0.5 all-gather.9.cloned.1.call-update
  240.9 26.6 %reduce-scatter.9.cloned.1.call-done = bf16[64,896]{1,0:T(8,128)(2,1)} async-done(((bf16[512,896]{1,0:T(8,128)(2,1)}), bf16[64,896]{1,0:T(8,128)(2,1)}) %reduce-scatter.9.cloned.1.call-update) | async-done | bytes 114704 | tf_op jit(solution)/shard_map/reduce_scatter | solution.py:52
  267.5 1.6 bitcast_convert_fusion
  269.1 34.3 %reduce-scatter.7.cloned.1.call-done = f32[64,896]{1,0:T(8,128)} async-done(((f32[512,896]{1,0:T(8,128)}), f32[64,896]{1,0:T(8,128)}) %reduce-scatter.7.cloned.1.call-update) | async-done | bytes 229392 | tf_op jit(solution)/shard_map/reduce_scatter | solution.py:51
  303.4 1.6 convert_bitcast_fusion
  305.0 42.8 %all-gather.9.cloned.1.call-done = f32[896,896]{1,0:T(8,128)} async-done(((f32[224,896]{1,0:T(8,128)}), f32[896,896]{1,0:T(8,128)}) %all-gather.9.cloned.1.call-update) | async-done | bytes 3211280 | tf_op jit(solution)/shard_map/all_gather | solution.py:63
  347.8 0.0 copy-done.8
  347.8 0.0 copy-start.1
  347.8 10.3 %fusion.16 = f32[4,224,896]{2,0,1:T(4,128)S(1)} fusion(f32[4,224,896]{2,1,0:T(8,128)} %bitcast.36, f32[4,16]{1,0:T(4,128)S(1)} %copy-done.8, s32[]{:T(128)S(6)} %select_n.11), kind=kOutput, calls=%fused_computation.28 | convolution fusion | flops 38535168 | bytes 6422788 | tf_op jit(solution)/shard_map/se,srd->erd/dot_general | solution.py:65
  358.2 1.9 copy.22
  360.1 0.0 copy-done.1
  (4 shorter events, 0.0 us)
Async XLA Ops:
  7.2 1.4 copy-start
  7.2 54.7 %reduce-scatter.13.cloned.1.call-start = ((), (), s32[]{:S(2)}) async-start(), calls=%async_computation.9 | async-start | bytes 4014080
  14.5 49.4 %copy-start.7 = (s32[1,2048]{1,0:T(1,128)S(1)}, s32[1,2048]{1,0:T(1,128)}, u32[]{:S(2)}) copy-start(s32[1,2048]{1,0:T(1,128)} %param.15) | copy-start | bytes 24580
  14.5 49.4 %copy-start.4 = (bf16[1,64,896]{2,1,0:T(8,128)(2,1)S(1)}, bf16[1,64,896]{2,1,0:T(8,128)(2,1)}, u32[]{:S(2)}) copy-start(bf16[1,64,896]{2,1,0:T(8,128)(2,1)} %param.10) | copy-start | bytes 344068
  14.5 123.5 %all-gather.7.cloned.1.call-start = ((), (), s32[]{:S(2)}) async-start(), calls=%async_computation.7 | async-start | bytes 3612672 | tf_op jit(solution)/shard_map/all_gather | solution.py:32
  63.8 176.5 %reduce-scatter.11.cloned.1.call-start = ((), (), s32[]{:S(2)}) async-start(), calls=%async_computation.6 | async-start | bytes 7225344 | tf_op jit(solution)/shard_map/reduce_scatter | solution.py:55
  82.9 9.5 %copy-start.5 = (bf16[1,64,896]{2,1,0:T(8,128)(2,1)S(1)}, bf16[1,64,896]{2,1,0:T(8,128)(2,1)}, u32[]{:S(2)}) copy-start(bf16[1,64,896]{2,1,0:T(8,128)(2,1)} %param.9) | copy-start | bytes 344068
  113.4 9.5 %copy-start.6 = (s32[1,2048]{1,0:T(1,128)S(1)}, s32[1,2048]{1,0:T(1,128)}, u32[]{:S(2)}) copy-start(s32[1,2048]{1,0:T(1,128)} %param.14) | copy-start | bytes 24580
  138.0 17.6 %copy-start.2 = (bf16[2048,896]{1,0:T(8,128)(2,1)S(1)}, bf16[2048,896]{1,0:T(8,128)(2,1)}, u32[]{:S(2)}) copy-start(bf16[2048,896]{1,0:T(8,128)(2,1)} %get-tuple-element.15) | copy-start | bytes 11010052
  138.0 17.6 %copy-start.3 = (bf16[2048,896]{1,0:T(8,128)(2,1)S(1)}, bf16[2048,896]{1,0:T(8,128)(2,1)}, u32[]{:S(2)}) copy-start(bf16[2048,896]{1,0:T(8,128)(2,1)} %get-tuple-element.16) | copy-start | bytes 11010052
  153.8 1.8 copy-start.9
  165.6 101.9 %reduce-scatter.9.cloned.1.call-start = ((), (), s32[]{:S(2)}) async-start(), calls=%async_computation.5 | async-start | bytes 1032192 | tf_op jit(solution)/shard_map/reduce_scatter | solution.py:52
  218.6 84.9 %reduce-scatter.7.cloned.1.call-start = ((), (), s32[]{:S(2)}) async-start(), calls=%async_computation.4 | async-start | bytes 2064384 | tf_op jit(solution)/shard_map/reduce_scatter | solution.py:51
  218.9 128.9 %copy-start.8 = (f32[4,16]{1,0:T(4,128)S(1)}, f32[4,16]{1,0:T(4,128)}, u32[]{:S(2)}) copy-start(f32[4,16]{1,0:T(4,128)} %param.13) | copy-start | bytes 772
  240.3 107.5 %all-gather.9.cloned.1.call-start = ((), (), s32[]{:S(2)}) async-start(), calls=%async_computation.8 | async-start | bytes 4014080 | tf_op jit(solution)/shard_map/all_gather | solution.py:63
  347.8 12.3 %copy-start.1 = (bf16[4,224,896]{2,1,0:T(8,128)(2,1)S(1)}, bf16[4,224,896]{2,1,0:T(8,128)(2,1)}, u32[]{:S(2)}) copy-start(bf16[4,224,896]{2,1,0:T(8,128)(2,1)} %param.11) | copy-start | bytes 4816900
Sparse Core Ops, SparseCore 0:
  14.6 47.2 reduce-scatter.12
  64.1 47.5 all-gather.6
  165.7 69.0 reduce-scatter.10
  237.1 30.3 reduce-scatter.8
  270.2 33.1 reduce-scatter.6
  305.1 42.6 all-gather.8
where the time goes:
time: 367 us
  waiting for transfers between devices  152 us (41%)
  other arithmetic  72.5 us (20%)
  matrix products  52.4 us (14%)
  blocking collectives  40 us (11%)
  local copies, waits for them, and re-layouts  35.5 us (10%)
  between operations  14.2 us (4%)
    unnamed x7, waiting for transfers between devices  47.9 us
    all_gather x1, waiting for transfers between devices, shards(): piece = lax.all_gather(merged_grad[None], 'sys', axis=0, tiled=True)  42.8 us
    reduce_scatter x1, waiting for transfers between devices, shards(): lax.psum_scatter(node_part, 'edge', scatter_dimension=0, tiled=True)  34.3 us
    reduce_scatter x1, waiting for transfers between devices, shards(): lax.psum_scatter(grad_part.astype(jnp.bfloat16), 'edge', scatter_dimensio...  26.6 us
    scatter-add x1, other arithmetic, shards(): jax.ops.segment_sum(message.astype(jnp.float32), tgt_idx, num_segments=at...  21.4 us
    all_gather x1, blocking collectives, shards(): lax.all_gather(atoms[0], 'edge', axis=0, tiled=True)  20.9 us
    scatter-add x1, other arithmetic, shards(): jax.ops.segment_sum(input_grad[:, width:].astype(jnp.float32), tgt_idx, n...  19.3 us
    all_gather x1, blocking collectives, shards(): lax.all_gather(cotangent[0], 'edge', axis=0, tiled=True)  19 us
  transfers between devices with their start and end apart: 6, of which 4 were waited for; matrix products, arithmetic and copies ran while one was open for 30% of the time, Pallas kernels for 0%

commit v1 on v0

v1 whole, which is shorter than its diff:
```python
import functools

import jax
import jax.numpy as jnp
from jax import lax
from jax.experimental import pallas as pl
from jax.experimental.pallas import tpu as pltpu
from jax.sharding import PartitionSpec as P

F32 = jnp.float32
BF16 = jnp.bfloat16
VMEM_LIMIT = 48 << 20
LANES = 128


def whole_vmem():
    return pl.BlockSpec(memory_space=pltpu.VMEM)


def whole_smem():
    return pl.BlockSpec(memory_space=pltpu.SMEM)


def params():
    return pltpu.CompilerParams(vmem_limit_bytes=VMEM_LIMIT)


def merge_kernel(place_ref, coef_ref, experts_ref, *part_refs):
    me = place_ref[0]
    count, rows, _ = experts_ref.shape
    step = 16
    for k, part_ref in enumerate(part_refs):
        scales = [coef_ref[me ^ k, me * count + e] for e in range(count)]

        @pl.loop(0, rows // step)
        def _(i):
            at = pl.ds(pl.multiple_of(i * step, step), step)
            total = scales[0] * experts_ref[0, at, :].astype(F32)
            for e in range(1, count):
                total = total + scales[e] * experts_ref[e, at, :].astype(F32)
            part_ref[at, :] = total.astype(part_ref.dtype)


def merge_parts(place, coef, experts, systems):
    _, rows, width = experts.shape
    return pl.pallas_call(
        merge_kernel,
        out_shape=[
            jax.ShapeDtypeStruct((rows, width), BF16 if k else F32) for k in range(systems)
        ],
        in_specs=[whole_smem(), whole_smem(), whole_vmem()],
        out_specs=[whole_vmem()] * systems,
        compiler_params=params(),
        name="merge_parts",
    )(place, coef, experts)


def expert_kernel(place_ref, coef_ref, *refs):
    me = place_ref[0]
    grad_refs, out_ref = refs[:-1], refs[-1]
    count, rows, _ = out_ref.shape
    step = 16
    scales = [
        [coef_ref[me ^ k, me * count + e] for e in range(count)] for k in range(len(grad_refs))
    ]

    @pl.loop(0, rows // step)
    def _(i):
        at = pl.ds(pl.multiple_of(i * step, step), step)
        grads = [ref[at, :].astype(F32) for ref in grad_refs]
        for e in range(count):
            total = scales[0][e] * grads[0]
            for k in range(1, len(grads)):
                total = total + scales[k][e] * grads[k]
            out_ref[e, at, :] = total


def expert_grads(place, coef, grads, count):
    rows, width = grads[0].shape
    return pl.pallas_call(
        expert_kernel,
        out_shape=jax.ShapeDtypeStruct((count, rows, width), F32),
        in_specs=[whole_smem(), whole_smem()] + [whole_vmem()] * len(grads),
        out_specs=whole_vmem(),
        compiler_params=params(),
        name="expert_grads",
    )(place, coef, *grads)


def edge_kernel(chips, place_ref, cols_ref, rows_ref, radial_ref, atoms_ref, cot_ref, *refs):
    block_refs = refs[: 2 * chips]
    kept_ref, sent_ref, weight_ref, proj_ref, acc_ref = refs[2 * chips :]
    step = pl.program_id(0)
    atoms, width_in = atoms_ref.shape
    tile = radial_ref.shape[0]

    @pl.when(step == 0)
    def _():
        chip, core = place_ref[1], place_ref[2]
        depth = block_refs[0].shape[0]
        for k in range(chips):
            source = lax.rem(chip - k + chips, chips)
            for other in range(2):
                device = 2 * source + (core if other == 0 else 1 - core)
                at = pl.ds(pl.multiple_of(device * depth, depth), depth)
                weight_ref[at, :] = block_refs[2 * k + other][...]
        for half in range(2):
            proj_ref[half * atoms : (half + 1) * atoms, :] = jnp.dot(
                atoms_ref[...],
                weight_ref[half * width_in : (half + 1) * width_in, :],
                preferred_element_type=F32,
            ).astype(BF16)
        acc_ref[...] = jnp.zeros_like(acc_ref)

    def hot(index, shape, axis):
        return jnp.where(index == lax.broadcasted_iota(jnp.int32, shape, axis), 1.0, 0.0).astype(BF16)

    hot_src = hot(cols_ref[:, 0:1], (tile, atoms), 1)
    hot_tgt = hot(cols_ref[:, 1:2], (tile, atoms), 1)
    pre = jnp.dot(hot_src, proj_ref[:atoms, :], preferred_element_type=F32)
    pre = pre + jnp.dot(hot_tgt, proj_ref[atoms:, :], preferred_element_type=F32)
    cot = jnp.dot(hot_tgt, cot_ref[...], preferred_element_type=F32)
    radial = radial_ref[...].astype(F32)
    sigma = 0.5 + 0.5 * jnp.tanh(0.5 * pre)
    silu = pre * sigma
    message = (silu * radial).astype(BF16)
    pre_grad = (cot * radial * (sigma + silu * (1.0 - sigma))).astype(BF16)
    sum_src = hot(rows_ref[0:1, :], (atoms, tile), 0)
    sum_tgt = hot(rows_ref[1:2, :], (atoms, tile), 0)
    acc_ref[0] += jnp.dot(sum_src, pre_grad, preferred_element_type=F32)
    acc_ref[1] += jnp.dot(sum_tgt, pre_grad, preferred_element_type=F32)
    acc_ref[2] += jnp.dot(sum_tgt, message, preferred_element_type=F32)

    @pl.when(step == pl.num_programs(0) - 1)
    def _():
        half = atoms // 2
        kept_ref[...] = acc_ref[:, :half, :]
        sent_ref[...] = acc_ref[:, half:, :].astype(BF16)


def edge_sums(chips, place, cols, rows, radial, atoms, cot, blocks, tile):
    edges = radial.shape[0]
    count, width_in = atoms.shape
    width = blocks[0].shape[1]
    flops = 2 * count * width * (2 * width_in + 6 * edges)
    fixed = lambda *shape: pl.BlockSpec(shape, lambda i: (0,) * len(shape))
    return pl.pallas_call(
        functools.partial(edge_kernel, chips),
        grid=(edges // tile,),
        out_shape=[
            jax.ShapeDtypeStruct((3, count // 2, width), F32),
            jax.ShapeDtypeStruct((3, count // 2, width), BF16),
            jax.ShapeDtypeStruct((2 * width_in, width), BF16),
        ],
        in_specs=[
            whole_smem(),
            pl.BlockSpec((tile, 2), lambda i: (i, 0)),
            pl.BlockSpec((2, tile), lambda i: (0, i)),
            pl.BlockSpec((tile, width), lambda i: (i, 0)),
            fixed(count, width_in),
            fixed(count, width),
        ]
        + [whole_vmem()] * len(blocks),
        out_specs=[
            fixed(3, count // 2, width),
            fixed(3, count // 2, width),
            fixed(2 * width_in, width),
        ],
        scratch_shapes=[
            pltpu.VMEM((2 * count, width), BF16),
            pltpu.VMEM((3, count, width), F32),
        ],
        compiler_params=params(),
        cost_estimate=pl.CostEstimate(
            flops=flops, bytes_accessed=4 * edges * width, transcendentals=edges * width
        ),
        name="edge_sums",
    )(place, cols, rows, radial, atoms, cot, *blocks)


def shards(systems, ways, atoms, cotangent, experts, radial, coef, source, target):
    chips = ways // 2
    me_sys = lax.axis_index("sys")
    me_edge = lax.axis_index("edge")
    chip, core = me_edge // 2, me_edge % 2
    place = jnp.stack([me_sys, chip, core]).astype(jnp.int32)
    count = experts.shape[0]
    width = experts.shape[2]
    own_atoms = atoms.shape[1]

    def across(x, k):
        return lax.ppermute(x, "sys", [(s, s ^ k) for s in range(systems)])

    def swap(x):
        return lax.ppermute(x, "edge", [(e, e ^ 1) for e in range(ways)])

    def shift(x, k):
        return lax.ppermute(x, "edge", [(e, (e + 2 * k) % ways) for e in range(ways)])

    def gather(x):
        got = [x]
        for _ in range(chips - 1):
            got.append(shift(got[-1], 1))
        return got

    parts = merge_parts(place, coef, experts, systems)
    got = [across(parts[k], k) for k in range(1, systems)]

    features = gather(jnp.concatenate([atoms, cotangent], axis=0))
    features = jnp.concatenate(features, axis=1)
    features = jnp.concatenate([features, swap(features)], axis=1)
    all_atoms, all_cot = features[0], features[1]

    def slot(index):
        owner, offset = index // own_atoms, index % own_atoms
        back = (chip - owner // 2 + chips) % chips
        return ((owner % 2) ^ core) * (chips * own_atoms) + back * own_atoms + offset

    ends = jnp.stack([slot(source[0]), slot(target[0])])
    ends_t = ends.T

    total = parts[0]
    for part in got:
        total = total + part.astype(F32)
    blocks = []
    for block in gather(total.astype(BF16)):
        blocks += [block, swap(block)]

    edges = radial.shape[1]
    kept, sent, weight = edge_sums(
        chips, place, ends_t, ends, radial[0], all_atoms, all_cot, blocks, min(512, edges)
    )
    other = swap(sent)

    def part_of(lo, hi, k):
        at = slice(k * own_atoms, (k + 1) * own_atoms)
        return kept[lo:hi, at] + other[lo:hi, at].astype(F32)

    def scatter(lo, hi):
        total = part_of(lo, hi, 1 % chips)
        for t in range(1, chips):
            total = shift(total.astype(BF16), 1).astype(F32) + part_of(lo, hi, (t + 1) % chips)
        return total

    sums = scatter(0, 2).astype(BF16)
    node = scatter(2, 3).astype(BF16)

    def half_for(k):
        return jnp.where((chip + k) % chips < chips // 2, sums[0], sums[1])

    picked = [half_for(0)] + [shift(half_for(k), k) for k in range(1, chips)]
    picked = jnp.concatenate(picked, axis=0)
    picked_other = swap(picked)
    depth = experts.shape[1]
    own_cols = lax.dynamic_slice_in_dim(all_atoms, (me_edge % chips) * depth, depth, 1).T
    half = chips * own_atoms
    merged_grad = jnp.dot(own_cols[:, :half], picked, preferred_element_type=F32)
    merged_grad = merged_grad + jnp.dot(own_cols[:, half:], picked_other, preferred_element_type=F32)
    send = merged_grad.astype(BF16)
    grads = [merged_grad] + [across(send, k) for k in range(1, systems)]
    expert_grad = expert_grads(place, coef, grads, count)

    over = (((1,), (1,)), ((), ()))
    atom_grad = lax.dot_general(sums[0], weight[:width], over, preferred_element_type=F32)
    atom_grad = atom_grad + lax.dot_general(
        sums[1], weight[width:], over, preferred_element_type=F32
    )
    return node, atom_grad[None], expert_grad


def solution(mesh):
    placed = P("sys", "edge", None)
    return jax.shard_map(
        functools.partial(shards, mesh.shape["sys"], mesh.shape["edge"]),
        mesh=mesh,
        in_specs=(placed, placed, placed, placed, P(), P("sys", "edge"), P("sys", "edge")),
        out_specs=(placed, placed, placed),
        check_vma=False,
    )
```

time: 367 us -> 179 us (0.49)
  other arithmetic: 72.5 us -> 10.8 us
  matrix products: 52.4 us -> 2.54 us
  waiting for transfers between devices: 152 us -> 103 us
  blocking collectives: 40 us -> 0 us
  Pallas kernels: 0 us -> 28.1 us
  local copies, waits for them, and re-layouts: 35.5 us -> 12.8 us
  starting transfers between devices: 0.73 us -> 20.8 us
  between operations: 14.2 us -> 0.95 us
    ppermute x0 -> x28, waiting for transfers between devices: none -> 103 us  [the longest x15 79.7 us: shift(): lax.ppermute(x, 'edge', [(e, (e + 2 * k) % ways) for e in range(ways)])]
    reduce_scatter x3 -> x0, waiting for transfers between devices: 61 us -> none  [the longest x1 34.3 us: shards(): lax.psum_scatter(node_part, 'edge', scatter_dimension=0, tiled=True)]
    scatter-add x3 -> x0, other arithmetic: 59.1 us -> none  [the longest x1 21.4 us: shards(): jax.ops.segment_sum(message.astype(jnp.float32), tgt_idx, num_segments=at...]
    dot_general x5 -> x4, matrix products: 52.4 us -> 2.54 us  [the longest x1 1.33 us: shards(): lax.dot_general(sums[0], weight[:width], over, preferred_element_type=F32)]
    unnamed x7 -> x0, waiting for transfers between devices: 47.9 us -> none
    all_gather x2 -> x0, waiting for transfers between devices: 42.8 us -> none  [the longest x1 42.8 us: shards(): piece = lax.all_gather(merged_grad[None], 'sys', axis=0, tiled=True)]
    all_gather x2 -> x0, blocking collectives: 40 us -> none  [the longest x1 20.9 us: shards(): lax.all_gather(atoms[0], 'edge', axis=0, tiled=True)]
    gather x3 -> x0, local copies, waits for them, and re-layouts: 28.5 us -> none  [the longest x1 9.51 us: shards(): edge_cot = jnp.take(all_cot, tgt_idx, axis=0).astype(jnp.float32)]
  transfers between devices with their start and end apart: 6 -> 28, of which waited for: 4 -> 15; matrix products, arithmetic and copies ran while one was open for 30% -> 11% of each run, Pallas kernels for 0% -> 0%
where the time goes in v1:
time: 179 us
  waiting for transfers between devices  103 us (58%)
  Pallas kernels  28.1 us (16%)
  starting transfers between devices  20.8 us (12%)
  local copies, waits for them, and re-layouts  12.8 us (7%)
  other arithmetic  10.8 us (6%)
  matrix products  2.54 us (1%)
    ppermute x15, waiting for transfers between devices, shift(): lax.ppermute(x, 'edge', [(e, (e + 2 * k) % ways) for e in range(ways)])  79.7 us
    pallas_call x1, Pallas kernels, edge_sums(): pl.pallas_call(functools.partial(edge_kernel, chips), grid=(edges // tile...  22.7 us
    ppermute x6, waiting for transfers between devices, across(): return lax.ppermute(x, 'sys', [(s, s ^ k) for s in range(systems)])  19.9 us
    ppermute x15, starting transfers between devices, shift(): lax.ppermute(x, 'edge', [(e, (e + 2 * k) % ways) for e in range(ways)])  11.6 us
    ppermute x6, starting transfers between devices, across(): return lax.ppermute(x, 'sys', [(s, s ^ k) for s in range(systems)])  8.1 us
    convert_element_type x6, other arithmetic, scatter(): total.astype(BF16)  6.48 us
    unnamed x22, local copies, waits for them, and re-layouts  5.81 us
  transfers between devices with their start and end apart: 28, of which 15 were waited for; matrix products, arithmetic and copies ran while one was open for 11% of the time, Pallas kernels for 0%

profile of v1, /device:TPU:0, one launch (start us, length us, event | category | flops | bytes accessed | tf_op | source)
XLA Modules:
  0.0 178.6 jit_solution(8328261302739437816)
XLA Ops:
  0.7 0.1 pad_add_fusion.1.place_ref
  0.7 1.4 copy-done
  2.2 0.7 copy-done.1
  2.8 2.2 %merge_parts.1 = (f32[224,896]{1,0:T(8,128)S(1)}, bf16[224,896]{1,0:T(8,128)(2,1)S(1)}, bf16[224,896]{1,0:T(8,128)(2,1)S(1)}, bf16[224,896]{1,0:T(8,128)(2,1)S(1)}) custom-call(s32[3]{0:T(128)S(1)} %pad_add_fusion.1.place_ref, f32[4,16]{1,0:T(4,128)S(1)} %copy-done.1, bf16[4,224,896]{2,1,0:T(8,128)(2,1)S(1)} %copy-done), custom_call_target="tpu_custom_call" | custom-call | tf_op jit(solution)/shard_map/merge_parts/pallas_call | solution.py:46
  5.0 3.0 %collective-permute-start.4 = (bf16[224,896]{1,0:T(8,128)(2,1)S(1)}, bf16[224,896]{1,0:T(8,128)(2,1)S(1)}, u32[]{:S(2)}, u32[]{:S(2)}) collective-permute-start(bf16[224,896]{1,0:T(8,128)(2,1)S(1)} %get-tuple-element.11), channel_id=1, source_target_pairs={{0,8},{8,0},{16,24},{24,16},{1,9},{9,1},{17,25},{25,17},{2,10},{10... | collective-permute-start | bytes 1204232 | tf_op jit(solution)/shard_map/ppermute | solution.py:192
  8.0 1.5 collective-permute-start.5
  9.6 1.6 constant_dynamic-update-slice_fusion.1
  11.1 0.7 constant_dynamic-update-slice_fusion
  11.8 2.0 %collective-permute-start = (bf16[2,64,896]{2,1,0:T(8,128)(2,1)S(1)}, bf16[2,64,896]{2,1,0:T(8,128)(2,1)S(1)}, u32[]{:S(2)}, u32[]{:S(2)}) collective-permute-start(bf16[2,64,896]{2,1,0:T(8,128)(2,1)S(1)} %get-tuple-element.24), channel_id=1, source_target_pairs={{0,2},{1,3},{2,4},{3,5},{4,6},{5,7},{6,0},{7,1},{8,10},{9,11},{10,... | collective-permute-start | bytes 688136 | tf_op jit(solution)/shard_map/ppermute | solution.py:198
  13.8 6.8 %collective-permute-done = bf16[2,64,896]{2,1,0:T(8,128)(2,1)S(1)} collective-permute-done((bf16[2,64,896]{2,1,0:T(8,128)(2,1)S(1)}, bf16[2,64,896]{2,1,0:T(8,128)(2,1)S(1)}, u32[]{:S(2)}, u32[]{:S(2)}) %collective-permute-start) | collective-permute-done | bytes 229408 | tf_op jit(solution)/shard_map/ppermute | solution.py:198
  20.6 6.8 %collective-permute-done.5 = bf16[224,896]{1,0:T(8,128)(2,1)S(1)} collective-permute-done((bf16[224,896]{1,0:T(8,128)(2,1)S(1)}, bf16[224,896]{1,0:T(8,128)(2,1)S(1)}, u32[]{:S(2)}, u32[]{:S(2)}) %collective-permute-start.5) | collective-permute-done | bytes 401440 | tf_op jit(solution)/shard_map/ppermute | solution.py:192
  27.4 0.2 add_convert_fusion.refs_0_
  27.6 1.6 collective-permute-start.8
  29.2 1.6 collective-permute-start.2
  30.8 13.6 %collective-permute-done.2 = bf16[2,64,896]{2,1,0:T(8,128)(2,1)S(1)} collective-permute-done((bf16[2,64,896]{2,1,0:T(8,128)(2,1)S(1)}, bf16[2,64,896]{2,1,0:T(8,128)(2,1)S(1)}, u32[]{:S(2)}, u32[]{:S(2)}) %collective-permute-start.2) | collective-permute-done | bytes 229408 | tf_op jit(solution)/shard_map/ppermute | solution.py:198
  44.4 1.0 pad_maximum_fusion
  45.4 0.3 fusion.13
  45.7 13.2 %collective-permute-done.10.refs_4_ = bf16[224,896]{1,0:T(8,128)(2,1)S(1)} collective-permute-done((bf16[224,896]{1,0:T(8,128)(2,1)S(1)}, bf16[224,896]{1,0:T(8,128)(2,1)S(1)}, u32[]{:S(2)}, u32[]{:S(2)}) %collective-permute-start.10) | collective-permute-done | bytes 401440 | tf_op jit(solution)/shard_map/ppermute | solution.py:198
  58.9 0.4 copy.10.cols_ref
  59.3 0.7 constant_dynamic-update-slice_fusion.5
  60.0 0.7 constant_dynamic-update-slice_fusion.4
  60.7 0.7 constant_dynamic-update-slice_fusion.3
  61.4 0.5 collective-permute-start.9
  61.9 9.7 %collective-permute-done.12.refs_6_ = bf16[224,896]{1,0:T(8,128)(2,1)S(1)} collective-permute-done((bf16[224,896]{1,0:T(8,128)(2,1)S(1)}, bf16[224,896]{1,0:T(8,128)(2,1)S(1)}, u32[]{:S(2)}, u32[]{:S(2)}) %collective-permute-start.12) | collective-permute-done | bytes 401440 | tf_op jit(solution)/shard_map/ppermute | solution.py:198
  71.6 2.2 %constant_dynamic-update-slice_fusion.2 = bf16[2,512,896]{2,1,0:T(8,128)(2,1)} fusion(bf16[2,512,896]{2,1,0:T(8,128)(2,1)} %constant_dynamic-update-slice_fusion.3, bf16[2,256,896]{2,1,0:T(8,128)(2,1)} %collective-permute-done.3), kind=kLoop, calls=%fused_computation.45 | loop fusion | bytes 1835008 | tf_op jit(solution)/shard_map/concatenate | solution.py:211
  73.8 2.6 %fusion.26 = (bf16[1,512,896]{2,1,0:T(8,128)(2,1)}, bf16[512,896]{1,0:T(8,128)(2,1)S(1)}, bf16[512,896]{1,0:T(8,128)(2,1)S(1)}) fusion(bf16[2,512,896]{2,1,0:T(8,128)(2,1)} %constant_dynamic-update-slice_fusion.2), kind=kLoop, calls=%fused_computation.79 | loop fusion | bytes 4587520 | tf_op jit(solution)/shard_map/slice | solution.py:212
  76.4 22.7 %edge_sums.1 = (f32[3,256,896]{2,1,0:T(8,128)}, bf16[3,256,896]{2,1,0:T(8,128)(2,1)}, bf16[1792,896]{1,0:T(8,128)(2,1)}) custom-call(s32[3]{0:T(128)S(1)} %pad_add_fusion.1.place_ref, s32[2048,2]{1,0:T(8,128)S(1)} %copy.10.cols_ref, s32[2,2048]{1,0:T(2,128)S(1)} %get-tuple-element.28.rows_ref, bf16[2048,896]{1,0:T(8,128)(2,1)} %bitcast.39, ...), custom_call_target="tpu_custom_call" | custom-call | flops 12918456320 | bytes 7340032 | tf_op jit(solution)/shard_map/edge_sums/pallas_call | solution.py:147
  99.2 0.5 collective-permute-start.14
  99.7 3.0 %collective-permute-done.14 = bf16[3,256,896]{2,1,0:T(8,128)(2,1)S(1)} collective-permute-done((bf16[3,256,896]{2,1,0:T(8,128)(2,1)}, bf16[3,256,896]{2,1,0:T(8,128)(2,1)S(1)}, u32[]{:S(2)}, u32[]{:S(2)}) %collective-permute-start.14) | collective-permute-done | bytes 1376288 | tf_op jit(solution)/shard_map/ppermute | solution.py:195
  102.7 1.4 add_convert_fusion.4
  104.0 0.1 collective-permute-start.18
  104.1 9.7 %collective-permute-done.18 = bf16[2,64,896]{2,1,0:T(8,128)(2,1)S(1)} collective-permute-done((bf16[2,64,896]{2,1,0:T(8,128)(2,1)S(1)}, bf16[2,64,896]{2,1,0:T(8,128)(2,1)S(1)}, u32[]{:S(2)}, u32[]{:S(2)}) %collective-permute-start.18) | collective-permute-done | bytes 229408 | tf_op jit(solution)/shard_map/ppermute | solution.py:198
  113.8 1.1 add_convert_fusion.3
  114.9 0.1 collective-permute-start.19
  115.0 8.8 %collective-permute-done.19 = bf16[2,64,896]{2,1,0:T(8,128)(2,1)S(1)} collective-permute-done((bf16[2,64,896]{2,1,0:T(8,128)(2,1)S(1)}, bf16[2,64,896]{2,1,0:T(8,128)(2,1)S(1)}, u32[]{:S(2)}, u32[]{:S(2)}) %collective-permute-start.19) | collective-permute-done | bytes 229408 | tf_op jit(solution)/shard_map/ppermute | solution.py:198
  123.8 1.2 add_convert_fusion.2
  125.0 0.1 collective-permute-start.20
  125.1 0.9 add_convert_fusion.8
  126.0 0.1 collective-permute-start.15
  126.1 8.2 %collective-permute-done.20 = bf16[2,64,896]{2,1,0:T(8,128)(2,1)S(1)} collective-permute-done((bf16[2,64,896]{2,1,0:T(8,128)(2,1)S(1)}, bf16[2,64,896]{2,1,0:T(8,128)(2,1)S(1)}, u32[]{:S(2)}, u32[]{:S(2)}) %collective-permute-start.20) | collective-permute-done | bytes 229408 | tf_op jit(solution)/shard_map/ppermute | solution.py:198
  134.2 1.0 add_convert_fusion.1
  135.4 0.1 collective-permute-start.22
  135.5 3.7 %collective-permute-start.23 = (bf16[64,896]{1,0:T(8,128)(2,1)S(1)}, bf16[64,896]{1,0:T(8,128)(2,1)S(1)}, u32[]{:S(2)}, u32[]{:S(2)}) collective-permute-start(bf16[64,896]{1,0:T(8,128)(2,1)S(1)} %get-tuple-element.23), channel_id=1, source_target_pairs={{0,6},{1,7},{2,0},{3,1},{4,2},{5,3},{6,4},{7,5},{8,14},{9,15},{10,... | collective-permute-start | bytes 344072 | tf_op jit(solution)/shard_map/ppermute | solution.py:198
  139.2 0.9 add_convert_fusion.7
  140.1 0.6 collective-permute-start.16
  140.7 2.4 %collective-permute-done.21 = bf16[64,896]{1,0:T(8,128)(2,1)S(1)} collective-permute-done((bf16[64,896]{1,0:T(8,128)(2,1)S(1)}, bf16[64,896]{1,0:T(8,128)(2,1)S(1)}, u32[]{:S(2)}, u32[]{:S(2)}) %collective-permute-start.21) | collective-permute-done | bytes 114720 | tf_op jit(solution)/shard_map/ppermute | solution.py:198
  143.2 2.1 %collective-permute-done.22 = bf16[64,896]{1,0:T(8,128)(2,1)S(1)} collective-permute-done((bf16[64,896]{1,0:T(8,128)(2,1)S(1)}, bf16[64,896]{1,0:T(8,128)(2,1)S(1)}, u32[]{:S(2)}, u32[]{:S(2)}) %collective-permute-start.22) | collective-permute-done | bytes 114720 | tf_op jit(solution)/shard_map/ppermute | solution.py:198
  145.3 0.1 collective-permute-start.24
  145.4 1.5 collective-permute-done.16
  146.9 0.9 add_convert_fusion.6
  147.8 1.6 collective-permute-start.17
  149.5 1.1 dynamic-slice_bitcast_fusion
  150.6 3.9 %collective-permute-done.17 = bf16[1,64,896]{2,1,0:T(8,128)(2,1)S(1)} collective-permute-done((bf16[1,64,896]{2,1,0:T(8,128)(2,1)S(1)}, bf16[1,64,896]{2,1,0:T(8,128)(2,1)S(1)}, u32[]{:S(2)}, u32[]{:S(2)}) %collective-permute-start.17) | collective-permute-done | bytes 114720 | tf_op jit(solution)/shard_map/ppermute | solution.py:198
  154.5 1.6 add_convert_fusion.5
  156.1 0.3 fusion.10
  156.4 0.3 fusion.27
  156.7 1.5 collective-permute-start.27
  158.2 1.5 collective-permute-start.26
  159.7 0.6 collective-permute-start.25
  160.3 0.6 fusion
  160.9 1.3 fusion.7
  162.2 7.7 %collective-permute-done.27.refs_3_ = bf16[224,896]{1,0:T(8,128)(2,1)S(1)} collective-permute-done((bf16[224,896]{1,0:T(8,128)(2,1)S(1)}, bf16[224,896]{1,0:T(8,128)(2,1)S(1)}, u32[]{:S(2)}, u32[]{:S(2)}) %collective-permute-start.27) | collective-permute-done | bytes 401440 | tf_op jit(solution)/shard_map/ppermute | solution.py:192
  169.9 5.5 %collective-permute-done.26.refs_2_ = bf16[224,896]{1,0:T(8,128)(2,1)S(1)} collective-permute-done((bf16[224,896]{1,0:T(8,128)(2,1)S(1)}, bf16[224,896]{1,0:T(8,128)(2,1)S(1)}, u32[]{:S(2)}, u32[]{:S(2)}) %collective-permute-start.26) | collective-permute-done | bytes 401440 | tf_op jit(solution)/shard_map/ppermute | solution.py:192
  175.4 3.2 %expert_grads.1 = f32[4,224,896]{2,1,0:T(8,128)} custom-call(s32[3]{0:T(128)S(1)} %pad_add_fusion.1.place_ref, f32[4,16]{1,0:T(4,128)S(1)} %copy-done.2, f32[224,896]{1,0:T(8,128)S(1)} %get-tuple-element.31.refs_0_, bf16[224,896]{1,0:T(8,128)(2,1)S(1)} %collective-permute-done.25.refs_1_, bf16[224,896]{1,0:T(8,128)(2,1)S(1)} %collective-permute-done.26.refs_2_, ...), custom_call_target="tpu_custom_call" | custom-call | tf_op jit(solution)/shard_map/expert_grads/pallas_call | solution.py:80
  (41 shorter events, 0.3 us)
Async XLA Ops:
  0.7 1.4 copy-start
  2.1 0.7 copy-start.1
  2.8 8.3 %copy-start.6 = (bf16[1,64,896]{2,1,0:T(8,128)(2,1)S(1)}, bf16[1,64,896]{2,1,0:T(8,128)(2,1)}, u32[]{:S(2)}) copy-start(bf16[1,64,896]{2,1,0:T(8,128)(2,1)} %param.8) | copy-start | bytes 344068
  5.0 15.6 %collective-permute-start.4 = (bf16[224,896]{1,0:T(8,128)(2,1)S(1)}, bf16[224,896]{1,0:T(8,128)(2,1)S(1)}, u32[]{:S(2)}, u32[]{:S(2)}) collective-permute-start(bf16[224,896]{1,0:T(8,128)(2,1)S(1)} %get-tuple-element.11), channel_id=1, source_target_pairs={{0,8},{8,0},{16,24},{24,16},{1,9},{9,1},{17,25},{25,17},{2,10},{10... | collective-permute-start | bytes 1204232 | tf_op jit(solution)/shard_map/ppermute | solution.py:192
  8.0 19.4 %collective-permute-start.5 = (bf16[224,896]{1,0:T(8,128)(2,1)S(1)}, bf16[224,896]{1,0:T(8,128)(2,1)S(1)}, u32[]{:S(2)}, u32[]{:S(2)}) collective-permute-start(bf16[224,896]{1,0:T(8,128)(2,1)S(1)} %get-tuple-element.12), channel_id=1, source_target_pairs={{0,16},{8,24},{16,0},{24,8},{1,17},{9,25},{17,1},{25,9},{2,18},{10... | collective-permute-start | bytes 1204232 | tf_op jit(solution)/shard_map/ppermute | solution.py:192
  9.5 17.8 %collective-permute-start.6 = (bf16[224,896]{1,0:T(8,128)(2,1)S(1)}, bf16[224,896]{1,0:T(8,128)(2,1)S(1)}, u32[]{:S(2)}, u32[]{:S(2)}) collective-permute-start(bf16[224,896]{1,0:T(8,128)(2,1)S(1)} %get-tuple-element.13), channel_id=1, source_target_pairs={{0,24},{8,16},{16,8},{24,0},{1,25},{9,17},{17,9},{25,1},{2,26},{10... | collective-permute-start | bytes 1204232 | tf_op jit(solution)/shard_map/ppermute | solution.py:192
  11.8 8.8 %collective-permute-start = (bf16[2,64,896]{2,1,0:T(8,128)(2,1)S(1)}, bf16[2,64,896]{2,1,0:T(8,128)(2,1)S(1)}, u32[]{:S(2)}, u32[]{:S(2)}) collective-permute-start(bf16[2,64,896]{2,1,0:T(8,128)(2,1)S(1)} %get-tuple-element.24), channel_id=1, source_target_pairs={{0,2},{1,3},{2,4},{3,5},{4,6},{5,7},{6,0},{7,1},{8,10},{9,11},{10,... | collective-permute-start | bytes 688136 | tf_op jit(solution)/shard_map/ppermute | solution.py:198
  20.6 8.6 %collective-permute-start.1 = (bf16[2,64,896]{2,1,0:T(8,128)(2,1)S(1)}, bf16[2,64,896]{2,1,0:T(8,128)(2,1)S(1)}, u32[]{:S(2)}, u32[]{:S(2)}) collective-permute-start(bf16[2,64,896]{2,1,0:T(8,128)(2,1)S(1)} %collective-permute-done), channel_id=1, source_target_pairs={{0,2},{1,3},{2,4},{3,5},{4,6},{5,7},{6,0},{7,1},{8,10},{9,11},{10,... | collective-permute-start | bytes 688136 | tf_op jit(solution)/shard_map/ppermute | solution.py:198
  27.4 18.0 %copy-start.7 = (s32[1,2048]{1,0:T(1,128)S(1)}, s32[1,2048]{1,0:T(1,128)}, u32[]{:S(2)}) copy-start(s32[1,2048]{1,0:T(1,128)} %param.12) | copy-start | bytes 24580
  27.4 18.0 %copy-start.8 = (s32[1,2048]{1,0:T(1,128)S(1)}, s32[1,2048]{1,0:T(1,128)}, u32[]{:S(2)}) copy-start(s32[1,2048]{1,0:T(1,128)} %param.13) | copy-start | bytes 24580
  27.6 17.8 %collective-permute-start.8 = (bf16[224,896]{1,0:T(8,128)(2,1)S(1)}, bf16[224,896]{1,0:T(8,128)(2,1)S(1)}, u32[]{:S(2)}, u32[]{:S(2)}) collective-permute-start(bf16[224,896]{1,0:T(8,128)(2,1)S(1)} %add_convert_fusion.refs_0_), channel_id=1, source_target_pairs={{0,2},{1,3},{2,4},{3,5},{4,6},{5,7},{6,0},{7,1},{8,10},{9,11},{10,... | collective-permute-start | bytes 1204232 | tf_op jit(solution)/shard_map/ppermute | solution.py:198
  29.2 15.1 %collective-permute-start.2 = (bf16[2,64,896]{2,1,0:T(8,128)(2,1)S(1)}, bf16[2,64,896]{2,1,0:T(8,128)(2,1)S(1)}, u32[]{:S(2)}, u32[]{:S(2)}) collective-permute-start(bf16[2,64,896]{2,1,0:T(8,128)(2,1)S(1)} %collective-permute-done.1), channel_id=1, source_target_pairs={{0,2},{1,3},{2,4},{3,5},{4,6},{5,7},{6,0},{7,1},{8,10},{9,11},{10,... | collective-permute-start | bytes 688136 | tf_op jit(solution)/shard_map/ppermute | solution.py:198
  45.4 26.2 %collective-permute-start.3 = (bf16[2,256,896]{2,1,0:T(8,128)(2,1)}, bf16[2,256,896]{2,1,0:T(8,128)(2,1)}, u32[]{:S(2)}, u32[]{:S(2)}) collective-permute-start(bf16[2,256,896]{2,1,0:T(8,128)(2,1)} %pad_maximum_fusion), channel_id=1, source_target_pairs={{0,1},{1,0},{2,3},{3,2},{4,5},{5,4},{6,7},{7,6},{8,9},{9,8},{10,11... | collective-permute-start | bytes 2752520 | tf_op jit(solution)/shard_map/ppermute | solution.py:195
  45.4 13.5 %collective-permute-start.10 = (bf16[224,896]{1,0:T(8,128)(2,1)S(1)}, bf16[224,896]{1,0:T(8,128)(2,1)S(1)}, u32[]{:S(2)}, u32[]{:S(2)}) collective-permute-start(bf16[224,896]{1,0:T(8,128)(2,1)S(1)} %collective-permute-done.8.refs_2_), channel_id=1, source_target_pairs={{0,2},{1,3},{2,4},{3,5},{4,6},{5,7},{6,0},{7,1},{8,10},{9,11},{10,... | collective-permute-start | bytes 1204232 | tf_op jit(solution)/shard_map/ppermute | solution.py:198
  58.9 12.7 %collective-permute-start.12 = (bf16[224,896]{1,0:T(8,128)(2,1)S(1)}, bf16[224,896]{1,0:T(8,128)(2,1)S(1)}, u32[]{:S(2)}, u32[]{:S(2)}) collective-permute-start(bf16[224,896]{1,0:T(8,128)(2,1)S(1)} %collective-permute-done.10.refs_4_), channel_id=1, source_target_pairs={{0,2},{1,3},{2,4},{3,5},{4,6},{5,7},{6,0},{7,1},{8,10},{9,11},{10,... | collective-permute-start | bytes 1204232 | tf_op jit(solution)/shard_map/ppermute | solution.py:198
  60.0 16.4 %collective-permute-start.7 = (bf16[224,896]{1,0:T(8,128)(2,1)S(1)}, bf16[224,896]{1,0:T(8,128)(2,1)S(1)}, u32[]{:S(2)}, u32[]{:S(2)}) collective-permute-start(bf16[224,896]{1,0:T(8,128)(2,1)S(1)} %add_convert_fusion.refs_0_), channel_id=1, source_target_pairs={{0,1},{1,0},{2,3},{3,2},{4,5},{5,4},{6,7},{7,6},{8,9},{9,8},{10,11... | collective-permute-start | bytes 1204232 | tf_op jit(solution)/shard_map/ppermute | solution.py:195
  61.4 15.0 %collective-permute-start.9 = (bf16[224,896]{1,0:T(8,128)(2,1)S(1)}, bf16[224,896]{1,0:T(8,128)(2,1)S(1)}, u32[]{:S(2)}, u32[]{:S(2)}) collective-permute-start(bf16[224,896]{1,0:T(8,128)(2,1)S(1)} %collective-permute-done.8.refs_2_), channel_id=1, source_target_pairs={{0,1},{1,0},{2,3},{3,2},{4,5},{5,4},{6,7},{7,6},{8,9},{9,8},{10,11... | collective-permute-start | bytes 1204232 | tf_op jit(solution)/shard_map/ppermute | solution.py:195
  61.9 14.5 %collective-permute-start.11 = (bf16[224,896]{1,0:T(8,128)(2,1)S(1)}, bf16[224,896]{1,0:T(8,128)(2,1)S(1)}, u32[]{:S(2)}, u32[]{:S(2)}) collective-permute-start(bf16[224,896]{1,0:T(8,128)(2,1)S(1)} %collective-permute-done.10.refs_4_), channel_id=1, source_target_pairs={{0,1},{1,0},{2,3},{3,2},{4,5},{5,4},{6,7},{7,6},{8,9},{9,8},{10,11... | collective-permute-start | bytes 1204232 | tf_op jit(solution)/shard_map/ppermute | solution.py:195
  71.6 4.8 %collective-permute-start.13 = (bf16[224,896]{1,0:T(8,128)(2,1)S(1)}, bf16[224,896]{1,0:T(8,128)(2,1)S(1)}, u32[]{:S(2)}, u32[]{:S(2)}) collective-permute-start(bf16[224,896]{1,0:T(8,128)(2,1)S(1)} %collective-permute-done.12.refs_6_), channel_id=1, source_target_pairs={{0,1},{1,0},{2,3},{3,2},{4,5},{5,4},{6,7},{7,6},{8,9},{9,8},{10,11... | collective-permute-start | bytes 1204232 | tf_op jit(solution)/shard_map/ppermute | solution.py:195
  99.2 25.9 %copy-start.3 = (f32[3,256,896]{2,1,0:T(8,128)S(1)}, f32[3,256,896]{2,1,0:T(8,128)}, u32[]{:S(2)}) copy-start(f32[3,256,896]{2,1,0:T(8,128)} %get-tuple-element.14) | copy-start | bytes 8257540
  99.2 3.5 %collective-permute-start.14 = (bf16[3,256,896]{2,1,0:T(8,128)(2,1)}, bf16[3,256,896]{2,1,0:T(8,128)(2,1)S(1)}, u32[]{:S(2)}, u32[]{:S(2)}) collective-permute-start(bf16[3,256,896]{2,1,0:T(8,128)(2,1)} %get-tuple-element.15), channel_id=1, source_target_pairs={{0,1},{1,0},{2,3},{3,2},{4,5},{5,4},{6,7},{7,6},{8,9},{9,8},{10,11... | collective-permute-start | bytes 4128776 | tf_op jit(solution)/shard_map/ppermute | solution.py:195
  102.7 11.1 %copy-start.4 = (bf16[3,256,896]{2,1,0:T(8,128)(2,1)}, bf16[3,256,896]{2,1,0:T(8,128)(2,1)S(1)}, u32[]{:S(2)}) copy-start(bf16[3,256,896]{2,1,0:T(8,128)(2,1)S(1)} %collective-permute-done.14) | copy-start | bytes 4128772
  104.0 9.7 %collective-permute-start.18 = (bf16[2,64,896]{2,1,0:T(8,128)(2,1)S(1)}, bf16[2,64,896]{2,1,0:T(8,128)(2,1)S(1)}, u32[]{:S(2)}, u32[]{:S(2)}) collective-permute-start(bf16[2,64,896]{2,1,0:T(8,128)(2,1)S(1)} %add_convert_fusion.4), channel_id=1, source_target_pairs={{0,2},{1,3},{2,4},{3,5},{4,6},{5,7},{6,0},{7,1},{8,10},{9,11},{10,... | collective-permute-start | bytes 688136 | tf_op jit(solution)/shard_map/ppermute | solution.py:198
  114.9 8.9 %collective-permute-start.19 = (bf16[2,64,896]{2,1,0:T(8,128)(2,1)S(1)}, bf16[2,64,896]{2,1,0:T(8,128)(2,1)S(1)}, u32[]{:S(2)}, u32[]{:S(2)}) collective-permute-start(bf16[2,64,896]{2,1,0:T(8,128)(2,1)S(1)} %add_convert_fusion.3), channel_id=1, source_target_pairs={{0,2},{1,3},{2,4},{3,5},{4,6},{5,7},{6,0},{7,1},{8,10},{9,11},{10,... | collective-permute-start | bytes 688136 | tf_op jit(solution)/shard_map/ppermute | solution.py:198
  125.0 9.2 %collective-permute-start.20 = (bf16[2,64,896]{2,1,0:T(8,128)(2,1)S(1)}, bf16[2,64,896]{2,1,0:T(8,128)(2,1)S(1)}, u32[]{:S(2)}, u32[]{:S(2)}) collective-permute-start(bf16[2,64,896]{2,1,0:T(8,128)(2,1)S(1)} %add_convert_fusion.2), channel_id=1, source_target_pairs={{0,2},{1,3},{2,4},{3,5},{4,6},{5,7},{6,0},{7,1},{8,10},{9,11},{10,... | collective-permute-start | bytes 688136 | tf_op jit(solution)/shard_map/ppermute | solution.py:198
  126.0 13.2 %collective-permute-start.15 = (bf16[1,64,896]{2,1,0:T(8,128)(2,1)S(1)}, bf16[1,64,896]{2,1,0:T(8,128)(2,1)S(1)}, u32[]{:S(2)}, u32[]{:S(2)}) collective-permute-start(bf16[1,64,896]{2,1,0:T(8,128)(2,1)S(1)} %add_convert_fusion.8), channel_id=1, source_target_pairs={{0,2},{1,3},{2,4},{3,5},{4,6},{5,7},{6,0},{7,1},{8,10},{9,11},{10,... | collective-permute-start | bytes 344072 | tf_op jit(solution)/shard_map/ppermute | solution.py:198
  135.3 7.9 %collective-permute-start.21 = (bf16[64,896]{1,0:T(8,128)(2,1)S(1)}, bf16[64,896]{1,0:T(8,128)(2,1)S(1)}, u32[]{:S(2)}, u32[]{:S(2)}) collective-permute-start(bf16[64,896]{1,0:T(8,128)(2,1)S(1)} %get-tuple-element.21), channel_id=1, source_target_pairs={{0,2},{1,3},{2,4},{3,5},{4,6},{5,7},{6,0},{7,1},{8,10},{9,11},{10,... | collective-permute-start | bytes 344072 | tf_op jit(solution)/shard_map/ppermute | solution.py:198
  135.4 9.9 %collective-permute-start.22 = (bf16[64,896]{1,0:T(8,128)(2,1)S(1)}, bf16[64,896]{1,0:T(8,128)(2,1)S(1)}, u32[]{:S(2)}, u32[]{:S(2)}) collective-permute-start(bf16[64,896]{1,0:T(8,128)(2,1)S(1)} %get-tuple-element.22), channel_id=1, source_target_pairs={{0,4},{1,5},{2,6},{3,7},{4,0},{5,1},{6,2},{7,3},{8,12},{9,13},{10,... | collective-permute-start | bytes 344072 | tf_op jit(solution)/shard_map/ppermute | solution.py:198
  135.5 9.8 %collective-permute-start.23 = (bf16[64,896]{1,0:T(8,128)(2,1)S(1)}, bf16[64,896]{1,0:T(8,128)(2,1)S(1)}, u32[]{:S(2)}, u32[]{:S(2)}) collective-permute-start(bf16[64,896]{1,0:T(8,128)(2,1)S(1)} %get-tuple-element.23), channel_id=1, source_target_pairs={{0,6},{1,7},{2,0},{3,1},{4,2},{5,3},{6,4},{7,5},{8,14},{9,15},{10,... | collective-permute-start | bytes 344072 | tf_op jit(solution)/shard_map/ppermute | solution.py:198
  140.1 6.8 %collective-permute-start.16 = (bf16[1,64,896]{2,1,0:T(8,128)(2,1)S(1)}, bf16[1,64,896]{2,1,0:T(8,128)(2,1)S(1)}, u32[]{:S(2)}, u32[]{:S(2)}) collective-permute-start(bf16[1,64,896]{2,1,0:T(8,128)(2,1)S(1)} %add_convert_fusion.7), channel_id=1, source_target_pairs={{0,2},{1,3},{2,4},{3,5},{4,6},{5,7},{6,0},{7,1},{8,10},{9,11},{10,... | collective-permute-start | bytes 344072 | tf_op jit(solution)/shard_map/ppermute | solution.py:198
  145.3 10.7 %collective-permute-start.24 = (bf16[256,896]{1,0:T(8,128)(2,1)S(1)}, bf16[256,896]{1,0:T(8,128)(2,1)S(1)}, u32[]{:S(2)}, u32[]{:S(2)}) collective-permute-start(bf16[256,896]{1,0:T(8,128)(2,1)S(1)} %pad_maximum_fusion.1), channel_id=1, source_target_pairs={{0,1},{1,0},{2,3},{3,2},{4,5},{5,4},{6,7},{7,6},{8,9},{9,8},{10,11... | collective-permute-start | bytes 1376264 | tf_op jit(solution)/shard_map/ppermute | solution.py:195
  147.8 6.6 %collective-permute-start.17 = (bf16[1,64,896]{2,1,0:T(8,128)(2,1)S(1)}, bf16[1,64,896]{2,1,0:T(8,128)(2,1)S(1)}, u32[]{:S(2)}, u32[]{:S(2)}) collective-permute-start(bf16[1,64,896]{2,1,0:T(8,128)(2,1)S(1)} %add_convert_fusion.6), channel_id=1, source_target_pairs={{0,2},{1,3},{2,4},{3,5},{4,6},{5,7},{6,0},{7,1},{8,10},{9,11},{10,... | collective-permute-start | bytes 344072 | tf_op jit(solution)/shard_map/ppermute | solution.py:198
  156.1 4.2 %copy-start.5 = (bf16[1792,896]{1,0:T(8,128)(2,1)S(1)}, bf16[1792,896]{1,0:T(8,128)(2,1)}, u32[]{:S(2)}) copy-start(bf16[1792,896]{1,0:T(8,128)(2,1)} %get-tuple-element.16) | copy-start | bytes 9633796
  156.7 13.2 %collective-permute-start.27 = (bf16[224,896]{1,0:T(8,128)(2,1)S(1)}, bf16[224,896]{1,0:T(8,128)(2,1)S(1)}, u32[]{:S(2)}, u32[]{:S(2)}) collective-permute-start(bf16[224,896]{1,0:T(8,128)(2,1)S(1)} %get-tuple-element.30), channel_id=1, source_target_pairs={{0,24},{8,16},{16,8},{24,0},{1,25},{9,17},{17,9},{25,1},{2,26},{10... | collective-permute-start | bytes 1204232 | tf_op jit(solution)/shard_map/ppermute | solution.py:192
  158.2 17.2 %collective-permute-start.26 = (bf16[224,896]{1,0:T(8,128)(2,1)S(1)}, bf16[224,896]{1,0:T(8,128)(2,1)S(1)}, u32[]{:S(2)}, u32[]{:S(2)}) collective-permute-start(bf16[224,896]{1,0:T(8,128)(2,1)S(1)} %get-tuple-element.30), channel_id=1, source_target_pairs={{0,16},{8,24},{16,0},{24,8},{1,17},{9,25},{17,1},{25,9},{2,18},{10... | collective-permute-start | bytes 1204232 | tf_op jit(solution)/shard_map/ppermute | solution.py:192
  159.7 15.7 %collective-permute-start.25 = (bf16[224,896]{1,0:T(8,128)(2,1)S(1)}, bf16[224,896]{1,0:T(8,128)(2,1)S(1)}, u32[]{:S(2)}, u32[]{:S(2)}) collective-permute-start(bf16[224,896]{1,0:T(8,128)(2,1)S(1)} %get-tuple-element.30), channel_id=1, source_target_pairs={{0,8},{8,0},{16,24},{24,16},{1,9},{9,1},{17,25},{25,17},{2,10},{10... | collective-permute-start | bytes 1204232 | tf_op jit(solution)/shard_map/ppermute | solution.py:192
  160.3 15.1 %copy-start.2 = (f32[4,16]{1,0:T(4,128)S(1)}, f32[4,16]{1,0:T(4,128)}, u32[]{:S(2)}) copy-start(f32[4,16]{1,0:T(4,128)} %coef_ref.3) | copy-start | bytes 772

commit v2 on v1

v2 whole, which is shorter than its diff:
```python
import functools

import jax
import jax.numpy as jnp
from jax import lax
from jax.experimental import pallas as pl
from jax.experimental.pallas import tpu as pltpu
from jax.sharding import PartitionSpec as P

F32 = jnp.float32
BF16 = jnp.bfloat16
VMEM_LIMIT = 48 << 20
LANES = 128
PIECES = 2


def whole_vmem():
    return pl.BlockSpec(memory_space=pltpu.VMEM)


def whole_smem():
    return pl.BlockSpec(memory_space=pltpu.SMEM)


def params():
    return pltpu.CompilerParams(vmem_limit_bytes=VMEM_LIMIT)


def column_chunks(width, pieces):
    tiles = width // LANES
    pieces = max(1, min(pieces, tiles))
    ends = [(tiles * (i + 1) + pieces - 1) // pieces for i in range(pieces)]
    starts = [0] + ends[:-1]
    if tiles * LANES != width:
        return [(0, width)]
    return [(lo * LANES, (hi - lo) * LANES) for lo, hi in zip(starts, ends)]


def merge_kernel(chunks, place_ref, coef_ref, experts_ref, *part_refs):
    me = place_ref[0]
    count, rows, _ = experts_ref.shape
    systems = len(part_refs) // len(chunks)
    step = 16
    scales = [[coef_ref[me ^ k, me * count + e] for e in range(count)] for k in range(systems)]

    @pl.loop(0, rows // step)
    def _(i):
        at = pl.ds(pl.multiple_of(i * step, step), step)
        for j, (lo, size) in enumerate(chunks):
            for col in range(0, size, LANES):
                wide = min(LANES, size - col)
                loaded = [
                    experts_ref[e, at, lo + col : lo + col + wide].astype(F32)
                    for e in range(count)
                ]
                for k in range(systems):
                    total = scales[k][0] * loaded[0]
                    for e in range(1, count):
                        total = total + scales[k][e] * loaded[e]
                    ref = part_refs[j * systems + k]
                    ref[at, col : col + wide] = total.astype(ref.dtype)


def merge_parts(place, coef, experts, systems, chunks):
    count, rows, width = experts.shape
    block = rows // 2 if rows % 32 == 0 else rows
    kinds = [BF16 if k else F32 for _ in chunks for k in range(systems)]
    sizes = [size for _, size in chunks for _ in range(systems)]
    return pl.pallas_call(
        functools.partial(merge_kernel, chunks),
        grid=(rows // block,),
        out_shape=[jax.ShapeDtypeStruct((rows, n), kind) for n, kind in zip(sizes, kinds)],
        in_specs=[
            whole_smem(),
            whole_smem(),
            pl.BlockSpec((count, block, width), lambda i: (0, i, 0)),
        ],
        out_specs=[pl.BlockSpec((block, n), lambda i: (i, 0)) for n in sizes],
        compiler_params=params(),
        name="merge_parts",
    )(place, coef, experts)


def expert_kernel(place_ref, coef_ref, *refs):
    me = place_ref[0]
    out_ref = refs[-1]
    count, rows, _ = out_ref.shape
    systems = coef_ref.shape[0]
    grad_refs = refs[:systems]
    step = 16
    scales = [[coef_ref[me ^ k, me * count + e] for e in range(count)] for k in range(systems)]

    @pl.loop(0, rows // step)
    def _(i):
        at = pl.ds(pl.multiple_of(i * step, step), step)
        grads = [ref[at, :].astype(F32) for ref in grad_refs]
        for e in range(count):
            total = scales[0][e] * grads[0]
            for k in range(1, systems):
                total = total + scales[k][e] * grads[k]
            out_ref[e, at, :] = total


def expert_grads(place, coef, grads, count, width, lo, earlier):
    rows, size = grads[0].shape
    tile = LANES if size % LANES == 0 else size
    extra = [] if earlier is None else [earlier]
    return pl.pallas_call(
        expert_kernel,
        grid=(size // tile,),
        out_shape=jax.ShapeDtypeStruct((count, rows, width), F32),
        in_specs=[whole_smem(), whole_smem()]
        + [pl.BlockSpec((rows, tile), lambda i: (0, i))] * len(grads)
        + [pl.BlockSpec(memory_space=pl.ANY)] * len(extra),
        out_specs=pl.BlockSpec((count, rows, tile), lambda i: (0, 0, lo // tile + i)),
        input_output_aliases={2 + len(grads): 0} if extra else {},
        compiler_params=params(),
        name="expert_grads",
    )(place, coef, *grads, *extra)


def prepare_kernel(chunks, cols_ref, rows_ref, radial_ref, near_ref, far_ref, *refs):
    pieces = len(chunks)
    atoms_ref, gather_ref, sum_ref = refs[:3]
    radial_refs, scaled_refs, cot_ref = refs[3 : 3 + pieces], refs[3 + pieces : -1], refs[-1]
    slots, _, block, _ = near_ref.shape
    atoms = atoms_ref.shape[0]
    tile = radial_ref.shape[0]

    @pl.when(pl.program_id(0) == 0)
    def _():
        for side, ref in enumerate((near_ref, far_ref)):
            for k in range(slots):
                at = slice((side * slots + k) * block, (side * slots + k + 1) * block)
                atoms_ref[at, :] = ref[k, 0]
                cot_ref[at, :] = ref[k, 1]

    def hot(index, shape, axis):
        return jnp.where(index == lax.broadcasted_iota(jnp.int32, shape, axis), 1.0, 0.0).astype(BF16)

    gather_ref[:, :atoms] = hot(cols_ref[:, 0:1], (tile, atoms), 1)
    hot_tgt = hot(cols_ref[:, 1:2], (tile, atoms), 1)
    gather_ref[:, atoms:] = hot_tgt
    sum_ref[:atoms, :] = hot(rows_ref[0:1, :], (atoms, tile), 0)
    sum_ref[atoms:, :] = hot(rows_ref[1:2, :], (atoms, tile), 0)
    for j, (lo, size) in enumerate(chunks):
        at = slice(lo, lo + size)
        cot = jnp.dot(hot_tgt, cot_ref[:, at], preferred_element_type=F32)
        radial_refs[j][...] = radial_ref[:, at]
        scaled_refs[j][...] = (cot * radial_ref[:, at].astype(F32)).astype(BF16)


def prepare(chunks, cols, rows, radial, near, far, tile):
    edges, width = radial.shape
    slots, _, block, _ = near.shape
    atoms = 2 * slots * block
    by_edge = lambda n: pl.BlockSpec((tile, n), lambda i: (i, 0))
    by_column = lambda n: pl.BlockSpec((n, tile), lambda i: (0, i))
    per_chunk = [by_edge(size) for _, size in chunks]
    return pl.pallas_call(
        functools.partial(prepare_kernel, chunks),
        grid=(edges // tile,),
        out_shape=[
            jax.ShapeDtypeStruct((atoms, width), BF16),
            jax.ShapeDtypeStruct((edges, 2 * atoms), BF16),
            jax.ShapeDtypeStruct((2 * atoms, edges), BF16),
        ]
        + [jax.ShapeDtypeStruct((edges, size), BF16) for _ in range(2) for _, size in chunks],
        in_specs=[by_edge(2), by_column(2), by_edge(width), whole_vmem(), whole_vmem()],
        out_specs=[
            pl.BlockSpec((atoms, width), lambda i: (0, 0)),
            by_edge(2 * atoms),
            by_column(2 * atoms),
        ]
        + per_chunk * 2,
        scratch_shapes=[pltpu.VMEM((atoms, width), BF16)],
        compiler_params=params(),
        cost_estimate=pl.CostEstimate(
            flops=2 * atoms * width * edges, bytes_accessed=14 * edges * width, transcendentals=0
        ),
        name="prepare",
    )(cols, rows, radial, near, far)


def edge_kernel(
    place_ref, gather_ref, sum_ref, radial_ref, scaled_ref, atoms_ref, near_ref, far_ref, *refs
):
    kept_ref, sent_ref, node_kept_ref, node_sent_ref, weight_ref, proj_ref, acc_ref = refs
    step = pl.program_id(0)
    atoms, width_in = atoms_ref.shape

    @pl.when(step == 0)
    def _():
        core = place_ref[2]
        chips, depth, _ = near_ref.shape
        for chip in range(chips):
            for ref, parity in ((near_ref, core), (far_ref, 1 - core)):
                at = pl.ds(pl.multiple_of((2 * chip + parity) * depth, depth), depth)
                weight_ref[at, :] = ref[chip]
        for half in range(2):
            proj_ref[half * atoms : (half + 1) * atoms, :] = jnp.dot(
                atoms_ref[...],
                weight_ref[half * width_in : (half + 1) * width_in, :],
                preferred_element_type=F32,
            ).astype(BF16)
        acc_ref[...] = jnp.zeros_like(acc_ref)

    pre = jnp.dot(gather_ref[...], proj_ref[...], preferred_element_type=F32)
    sigma = 0.5 + 0.5 * jnp.tanh(0.5 * pre)
    silu = pre * sigma
    message = (silu * radial_ref[...].astype(F32)).astype(BF16)
    slope = sigma + silu * (1.0 - sigma)
    pre_grad = (scaled_ref[...].astype(F32) * slope).astype(BF16)
    acc_ref[0] += jnp.dot(sum_ref[:atoms, :], pre_grad, preferred_element_type=F32)
    acc_ref[1] += jnp.dot(sum_ref[atoms:, :], pre_grad, preferred_element_type=F32)
    acc_ref[2] += jnp.dot(sum_ref[atoms:, :], message, preferred_element_type=F32)

    @pl.when(step == pl.num_programs(0) - 1)
    def _():
        half = atoms // 2
        kept_ref[...] = acc_ref[:2, :half, :]
        sent_ref[...] = acc_ref[:2, half:, :].astype(BF16)
        node_kept_ref[...] = acc_ref[2, :half, :]
        node_sent_ref[...] = acc_ref[2, half:, :].astype(BF16)


def edge_sums(place, gather, sums, radial, scaled, atoms, near, far, tile):
    edges, width = radial.shape
    count, width_in = atoms.shape
    flops = 2 * count * width * (2 * width_in + 5 * edges)
    fixed = lambda *shape: pl.BlockSpec(shape, lambda i: (0,) * len(shape))
    outs = [
        ((2, count // 2, width), F32),
        ((2, count // 2, width), BF16),
        ((count // 2, width), F32),
        ((count // 2, width), BF16),
        ((2 * width_in, width), BF16),
    ]
    return pl.pallas_call(
        edge_kernel,
        grid=(edges // tile,),
        out_shape=[jax.ShapeDtypeStruct(shape, kind) for shape, kind in outs],
        in_specs=[
            whole_smem(),
            pl.BlockSpec((tile, 2 * count), lambda i: (i, 0)),
            pl.BlockSpec((2 * count, tile), lambda i: (0, i)),
            pl.BlockSpec((tile, width), lambda i: (i, 0)),
            pl.BlockSpec((tile, width), lambda i: (i, 0)),
            fixed(count, width_in),
            whole_vmem(),
            whole_vmem(),
        ],
        out_specs=[fixed(*shape) for shape, _ in outs],
        scratch_shapes=[
            pltpu.VMEM((2 * count, width), BF16),
            pltpu.VMEM((3, count, width), F32),
        ],
        compiler_params=params(),
        cost_estimate=pl.CostEstimate(
            flops=flops,
            bytes_accessed=4 * edges * width + 8 * edges * count,
            transcendentals=edges * width,
        ),
        name="edge_sums",
    )(place, gather, sums, radial, scaled, atoms, near, far)


def after(x, *others):
    return lax.optimization_barrier((x, *others))[0]


def shards(systems, ways, pieces, atoms, cotangent, experts, radial, coef, source, target):
    chips = ways // 2
    me_sys = lax.axis_index("sys")
    me_edge = lax.axis_index("edge")
    chip, core = me_edge // 2, me_edge % 2
    place = jnp.stack([me_sys, chip, core]).astype(jnp.int32)
    count, depth, width = experts.shape
    own = atoms.shape[1]
    edges = radial.shape[1]
    tile = min(512, edges)
    chunks = column_chunks(width, pieces)
    lines = [[2 * z + c for z in range(chips)] for c in range(2)]

    def across(x, k):
        return lax.ppermute(x, "sys", [(s, s ^ k) for s in range(systems)])

    def swap(x):
        return lax.ppermute(x, "edge", [(e, e ^ 1) for e in range(ways)])

    def shift(x, k):
        return lax.ppermute(x, "edge", [(e, (e + 2 * k) % ways) for e in range(ways)])

    features = jnp.concatenate([atoms, cotangent], axis=0)
    near = jnp.stack([features] + [shift(features, k) for k in range(1, chips)])
    far = swap(near)

    def slot(index):
        owner, offset = index // own, index % own
        back = (chip - owner // 2 + chips) % chips
        return ((owner % 2) ^ core) * (chips * own) + back * own + offset

    ends = jnp.stack([slot(source[0]), slot(target[0])])
    prepared = prepare(chunks, ends.T, ends, radial[0], near, far, tile)
    all_atoms, hot_gather, hot_sum = prepared[:3]
    radials, scaled = prepared[3 : 3 + len(chunks)], prepared[3 + len(chunks) :]
    own_cols = lax.dynamic_slice_in_dim(all_atoms, (me_edge % chips) * depth, depth, 1).T

    parts = merge_parts(place, coef, experts, systems, chunks)
    weights = []
    for j in range(len(chunks)):
        total = parts[j * systems]
        got = [across(parts[j * systems + k], k) for k in range(1, systems)]
        for part in got:
            total = total + part.astype(F32)
        block = lax.all_gather(total.astype(BF16), "edge", axis_index_groups=lines)
        weights.append((block, swap(block)))

    def slots(kept, other):
        return [
            kept[..., k * own : (k + 1) * own, :]
            + other[..., k * own : (k + 1) * own, :].astype(F32)
            for k in range(chips)
        ]

    def scatter(blocks):
        total = blocks[0]
        for k in range(1, chips):
            total = total + shift(blocks[k].astype(BF16), chips - k).astype(F32)
        return total

    atom_grad, expert_grad, nodes = None, None, []
    over = (((1,), (1,)), ((), ()))
    half = chips * own
    for j, (lo, size) in enumerate(chunks):
        kept, sent, node_kept, node_sent, weight = edge_sums(
            place, hot_gather, hot_sum, radials[j], scaled[j], all_atoms, *weights[j], tile
        )
        sums = scatter(slots(kept, swap(sent))).astype(BF16)
        nodes.append(slots(node_kept, swap(node_sent)))

        def half_for(k):
            return jnp.where((chip + k) % chips < chips // 2, sums[0], sums[1])

        picked = [half_for(0)] + [shift(half_for(k), k) for k in range(1, chips)]
        picked = jnp.concatenate(picked, axis=0)
        picked_other = swap(picked)
        grad = jnp.dot(own_cols[:, :half], picked, preferred_element_type=F32)
        grad = grad + jnp.dot(own_cols[:, half:], picked_other, preferred_element_type=F32)
        send = grad.astype(BF16)
        grads = [grad] + [across(send, k) for k in range(1, systems)]
        expert_grad = expert_grads(place, coef, grads, count, width, lo, expert_grad)
        for i in range(2):
            part = lax.dot_general(
                sums[i], weight[i * width : (i + 1) * width], over, preferred_element_type=F32
            )
            atom_grad = part if atom_grad is None else atom_grad + part

    blocks = [jnp.concatenate(list(x), axis=1) for x in zip(*nodes)]
    blocks = [blocks[0]] + [after(x.astype(BF16), picked) for x in blocks[1:]]
    node = scatter(blocks).astype(BF16)
    return node[None], atom_grad[None], expert_grad


def solution(mesh):
    placed = P("sys", "edge", None)
    return jax.shard_map(
        functools.partial(shards, mesh.shape["sys"], mesh.shape["edge"], PIECES),
        mesh=mesh,
        in_specs=(placed, placed, placed, placed, P(), P("sys", "edge"), P("sys", "edge")),
        out_specs=(placed, placed, placed),
        check_vma=False,
    )
```

time: 179 us -> 178 us (level)
  waiting for transfers between devices: 103 us -> 27.4 us
  blocking collectives: 0 us -> 46.1 us
  starting transfers between devices: 20.8 us -> 52.5 us
  Pallas kernels: 28.1 us -> 40.4 us
  other arithmetic: 10.8 us -> 2.1 us
  local copies, waits for them, and re-layouts: 12.8 us -> 4.73 us
    ppermute x15 -> x18, waiting for transfers between devices: 79.7 us -> 20.6 us  [shift(): lax.ppermute(x, 'edge', [(e, (e + 2 * k) % ways) for e in range(ways)])]
    all_gather x0 -> x2, blocking collectives: none -> 46.1 us  [shards(): block = lax.all_gather(total.astype(BF16), 'edge', axis_index_groups=lines)]
    ppermute x15 -> x18, starting transfers between devices: 11.6 us -> 32 us  [shift(): lax.ppermute(x, 'edge', [(e, (e + 2 * k) % ways) for e in range(ways)])]
    ppermute x6 -> x12, waiting for transfers between devices: 19.9 us -> 5.52 us  [across(): return lax.ppermute(x, 'sys', [(s, s ^ k) for s in range(systems)])]
    pallas_call x3 -> x6, Pallas kernels: 28.1 us -> 40.4 us  [the longest x2 23.7 us: edge_sums(): pl.pallas_call(edge_kernel, grid=(edges // tile,), out_shape=[jax.ShapeDt...]
    ppermute x6 -> x12, starting transfers between devices: 8.1 us -> 18.7 us  [across(): return lax.ppermute(x, 'sys', [(s, s ^ k) for s in range(systems)])]
    convert_element_type x9 -> x6, other arithmetic: 9.3 us -> 0.6 us  [the longest x2 0.23 us: scatter(): total = total + shift(blocks[k].astype(BF16), chips - k).astype(F32)]
    concatenate x2 -> x1, local copies, waits for them, and re-layouts: 2.84 us -> 0.02 us  [shards(): features = jnp.concatenate([atoms, cotangent], axis=0)]
  transfers between devices with their start and end apart: 28 -> 39, of which waited for: 15 -> 15; matrix products, arithmetic and copies ran while one was open for 11% -> 3% of each run, Pallas kernels for 0% -> 20%
where the time goes in v2:
time: 178 us; the launch traced here: 177 us
  starting transfers between devices  52.5 us (29%)
  blocking collectives  46.1 us (26%)
  Pallas kernels  40.4 us (23%)
  waiting for transfers between devices  27.4 us (15%)
  local copies, waits for them, and re-layouts  4.73 us (3%)
  matrix products  3.18 us (2%)
  other arithmetic  2.1 us (1%)
    all_gather x2, blocking collectives, shards(): block = lax.all_gather(total.astype(BF16), 'edge', axis_index_groups=lines)  46.1 us
    ppermute x18, starting transfers between devices, shift(): lax.ppermute(x, 'edge', [(e, (e + 2 * k) % ways) for e in range(ways)])  32 us
    pallas_call x2, Pallas kernels, edge_sums(): pl.pallas_call(edge_kernel, grid=(edges // tile,), out_shape=[jax.ShapeDt...  23.7 us
    ppermute x18, waiting for transfers between devices, shift(): lax.ppermute(x, 'edge', [(e, (e + 2 * k) % ways) for e in range(ways)])  20.6 us
    ppermute x12, starting transfers between devices, across(): return lax.ppermute(x, 'sys', [(s, s ^ k) for s in range(systems)])  18.7 us
    pallas_call x1, Pallas kernels, prepare(): pl.pallas_call(functools.partial(prepare_kernel, chunks), grid=(edges //...  8.98 us
    pallas_call x2, Pallas kernels, expert_grads(): pl.pallas_call(expert_kernel, grid=(size // tile,), out_shape=jax.ShapeDt...  5.88 us
    ppermute x12, waiting for transfers between devices, across(): return lax.ppermute(x, 'sys', [(s, s ^ k) for s in range(systems)])  5.52 us
  transfers between devices with their start and end apart: 39, of which 15 were waited for; matrix products, arithmetic and copies ran while one was open for 3% of the time, Pallas kernels for 20%

profile of v2, /device:TPU:0, one launch (start us, length us, event | category | flops | bytes accessed | tf_op | source)
XLA Modules:
  0.0 177.4 jit_solution(9591692301597548762)
XLA Ops:
  0.7 1.4 copy-done
  2.2 0.7 copy-done.1
  2.8 1.8 %merge_parts.1 = (f32[224,512]{1,0:T(8,128)S(1)}, bf16[224,512]{1,0:T(8,128)(2,1)S(1)}, bf16[224,512]{1,0:T(8,128)(2,1)S(1)}, bf16[224,512]{1,0:T(8,128)(2,1)S(1...) custom-call(s32[3]{0:T(128)S(1)} %pad_add_fusion.1.place_ref, ...), custom_call_target="tpu_custom_call" | custom-call | tf_op jit(solution)/shard_map/merge_parts/pallas_call | solution.py:69
  4.7 4.0 %collective-permute-start.11 = (bf16[224,384]{1,0:T(8,128)(2,1)S(1)}, bf16[224,384]{1,0:T(8,128)(2,1)S(1)}, u32[]{:S(2)}, u32[]{:S(2)}) collective-permute-start(bf16[224,384]{1,0:T(8,128)(2,1)S(1)} %get-tuple-element.47), channel_id=1, source_target_pairs={{0,24},{8,16},{16,8},{24,0},{1,25},{9,17},{17,9},{25,1},{2,26},{10... | collective-permute-start | bytes 516104 | tf_op jit(solution)/shard_map/ppermute | solution.py:286
  8.6 0.5 collective-permute-start.10
  9.3 0.9 constant_dynamic-update-slice_fusion.1
  10.2 4.1 %collective-permute-start.2 = (bf16[2,64,896]{2,1,0:T(8,128)(2,1)S(1)}, bf16[2,64,896]{2,1,0:T(8,128)(2,1)S(1)}, u32[]{:S(2)}, u32[]{:S(2)}) collective-permute-start(bf16[2,64,896]{2,1,0:T(8,128)(2,1)S(1)} %constant_dynamic-update-slice_fusion), channel_id=1, source_target_pairs={{0,6},{1,7},{2,0},{3,1},{4,2},{5,3},{6,4},{7,5},{8,14},{9,15},{10,... | collective-permute-start | bytes 688136 | tf_op jit(solution)/shard_map/ppermute | solution.py:292
  14.3 1.6 collective-permute-start
  15.9 0.8 collective-permute-done.10
  16.7 1.8 %collective-permute-start.6 = (bf16[224,512]{1,0:T(8,128)(2,1)S(1)}, bf16[224,512]{1,0:T(8,128)(2,1)S(1)}, u32[]{:S(2)}, u32[]{:S(2)}) collective-permute-start(bf16[224,512]{1,0:T(8,128)(2,1)S(1)} %get-tuple-element.39), channel_id=1, source_target_pairs={{0,24},{8,16},{16,8},{24,0},{1,25},{9,17},{17,9},{25,1},{2,26},{10... | collective-permute-start | bytes 688136 | tf_op jit(solution)/shard_map/ppermute | solution.py:286
  18.5 1.3 collective-permute-start.5
  19.9 0.4 collective-permute-done.2
  20.4 1.5 collective-permute-start.4
  21.8 26.6 %all-gather.1 = bf16[896,384]{1,0:T(8,128)(2,1)} all-gather(bf16[224,384]{1,0:T(8,128)(2,1)S(1)} %add_convert_fusion.1), channel_id=3, replica_groups={{0,2,4,6},{1,3,5,7},{8,10,12,14},{9,11,13,15},{16,18,20,22},{17,19,21,2..., dimensions={0}, use_global_device_ids=true | all-gather | bytes 860160 | tf_op jit(solution)/shard_map/all_gather | solution.py:316
  48.6 0.5 collective-permute-start.3
  49.3 19.5 %all-gather = bf16[896,512]{1,0:T(8,128)(2,1)S(1)} all-gather(bf16[224,512]{1,0:T(8,128)(2,1)S(1)} %add_convert_fusion), channel_id=2, replica_groups={{0,2,4,6},{1,3,5,7},{8,10,12,14},{9,11,13,15},{16,18,20,22},{17,19,21,2..., dimensions={0}, use_global_device_ids=true | all-gather | bytes 1146880 | tf_op jit(solution)/shard_map/all_gather | solution.py:316
  68.8 0.3 fusion.20
  69.2 0.4 copy.11.cols_ref
  69.7 9.0 %prepare.1 = (bf16[512,896]{1,0:T(8,128)(2,1)S(1)}, bf16[2048,1024]{1,0:T(8,128)(2,1)}, bf16[1024,2048]{1,0:T(8,128)(2,1)}, bf16[2048,512]{1,0:T(8,128)(2,1)}, b...) custom-call(s32[2048,2]{1,0:T(8,128)S(1)} %copy.11.cols_ref, ...), custom_call_target="tpu_custom_call" | custom-call | flops 1879048192 | bytes 25690112 | tf_op jit(solution)/shard_map/prepare/pallas_call | solution.py:160
  78.6 1.2 copy-done.3
  79.8 11.0 %edge_sums.3 = (f32[2,256,384]{2,1,0:T(8,128)S(1)}, bf16[2,256,384]{2,1,0:T(8,128)(2,1)S(1)}, f32[256,384]{1,0:T(8,128)S(1)}, bf16[256,384]{1,0:T(8,128)(2,1)S(1)}, bf16[1792,384]{1,0:T(8,128)(2,1)S(1)}) custom-call(s32[3]{0:T(128)S(1)} %pad_add_fusion.1.place_ref, bf16[2048,1024]{1,0:T(8,128)(2,1)} %get-tuple-element.31.gather_ref, ...), custom_call_target="tpu_custom_call" | custom-call | flops 4731174912 | bytes 11534336 | tf_op jit(solution)/shard_map/edge_sums/pallas_call | solution.py:239
  90.8 0.5 collective-permute-start.13
  91.4 12.7 %edge_sums.2 = (f32[2,256,512]{2,1,0:T(8,128)S(1)}, bf16[2,256,512]{2,1,0:T(8,128)(2,1)S(1)}, f32[256,512]{1,0:T(8,128)S(1)}, bf16[256,512]{1,0:T(8,128)(2,1)S(1)}, bf16[1792,512]{1,0:T(8,128)(2,1)}) custom-call(s32[3]{0:T(128)S(1)} %pad_add_fusion.1.place_ref, bf16[2048,1024]{1,0:T(8,128)(2,1)} %get-tuple-element.31.gather_ref, ...), custom_call_target="tpu_custom_call" | custom-call | flops 6308233216 | bytes 12582912 | tf_op jit(solution)/shard_map/edge_sums/pallas_call | solution.py:239
  104.1 0.5 collective-permute-start.14
  104.8 0.8 collective-permute-done.8
  105.7 0.4 collective-permute-done.14
  106.3 2.2 %collective-permute-start.16 = (bf16[2,64,384]{2,1,0:T(8,128)(2,1)S(1)}, bf16[2,64,384]{2,1,0:T(8,128)(2,1)S(1)}, u32[]{:S(2)}, u32[]{:S(2)}) collective-permute-start(bf16[2,64,384]{2,1,0:T(8,128)(2,1)S(1)} %get-tuple-element.64), channel_id=1, source_target_pairs={{0,4},{1,5},{2,6},{3,7},{4,0},{5,1},{6,2},{7,3},{8,12},{9,13},{10,... | collective-permute-start | bytes 294920 | tf_op jit(solution)/shard_map/ppermute | solution.py:292
  108.6 1.6 collective-permute-start.15
  110.2 3.7 %collective-permute-done.17 = bf16[2,64,384]{2,1,0:T(8,128)(2,1)S(1)} collective-permute-done((bf16[2,64,384]{2,1,0:T(8,128)(2,1)S(1)}, bf16[2,64,384]{2,1,0:T(8,128)(2,1)S(1)}, u32[]{:S(2)}, u32[]{:S(2)}) %collective-permute-start.17) | collective-permute-done | bytes 98336 | tf_op jit(solution)/shard_map/ppermute | solution.py:292
  113.9 3.3 %collective-permute-done.16 = bf16[2,64,384]{2,1,0:T(8,128)(2,1)S(1)} collective-permute-done((bf16[2,64,384]{2,1,0:T(8,128)(2,1)S(1)}, bf16[2,64,384]{2,1,0:T(8,128)(2,1)S(1)}, u32[]{:S(2)}, u32[]{:S(2)}) %collective-permute-start.16) | collective-permute-done | bytes 98336 | tf_op jit(solution)/shard_map/ppermute | solution.py:292
  117.2 2.4 %collective-permute-start.20 = (bf16[64,384]{1,0:T(8,128)(2,1)S(1)}, bf16[64,384]{1,0:T(8,128)(2,1)S(1)}, u32[]{:S(2)}, u32[]{:S(2)}) collective-permute-start(bf16[64,384]{1,0:T(8,128)(2,1)S(1)} %get-tuple-element.80), channel_id=1, source_target_pairs={{0,6},{1,7},{2,0},{3,1},{4,2},{5,3},{6,4},{7,5},{8,14},{9,15},{10,... | collective-permute-start | bytes 147464 | tf_op jit(solution)/shard_map/ppermute | solution.py:292
  119.7 1.0 collective-permute-start.19
  120.6 0.3 fusion.6
  121.1 2.6 %collective-permute-start.27 = (bf16[2,64,512]{2,1,0:T(8,128)(2,1)S(1)}, bf16[2,64,512]{2,1,0:T(8,128)(2,1)S(1)}, u32[]{:S(2)}, u32[]{:S(2)}) collective-permute-start(bf16[2,64,512]{2,1,0:T(8,128)(2,1)S(1)} %get-tuple-element.60), channel_id=1, source_target_pairs={{0,2},{1,3},{2,4},{3,5},{4,6},{5,7},{6,0},{7,1},{8,10},{9,11},{10,... | collective-permute-start | bytes 393224 | tf_op jit(solution)/shard_map/ppermute | solution.py:292
  123.7 1.9 %collective-permute-start.26 = (bf16[2,64,512]{2,1,0:T(8,128)(2,1)S(1)}, bf16[2,64,512]{2,1,0:T(8,128)(2,1)S(1)}, u32[]{:S(2)}, u32[]{:S(2)}) collective-permute-start(bf16[2,64,512]{2,1,0:T(8,128)(2,1)S(1)} %get-tuple-element.61), channel_id=1, source_target_pairs={{0,4},{1,5},{2,6},{3,7},{4,0},{5,1},{6,2},{7,3},{8,12},{9,13},{10,... | collective-permute-start | bytes 393224 | tf_op jit(solution)/shard_map/ppermute | solution.py:292
  125.6 0.6 collective-permute-start.25
  126.1 0.3 fusion.8
  126.5 3.6 %collective-permute-done.19 = bf16[64,384]{1,0:T(8,128)(2,1)S(1)} collective-permute-done((bf16[64,384]{1,0:T(8,128)(2,1)S(1)}, bf16[64,384]{1,0:T(8,128)(2,1)S(1)}, u32[]{:S(2)}, u32[]{:S(2)}) %collective-permute-start.19) | collective-permute-done | bytes 49184 | tf_op jit(solution)/shard_map/ppermute | solution.py:292
  130.2 3.9 %collective-permute-done.26 = bf16[2,64,512]{2,1,0:T(8,128)(2,1)S(1)} collective-permute-done((bf16[2,64,512]{2,1,0:T(8,128)(2,1)S(1)}, bf16[2,64,512]{2,1,0:T(8,128)(2,1)S(1)}, u32[]{:S(2)}, u32[]{:S(2)}) %collective-permute-start.26) | collective-permute-done | bytes 131104 | tf_op jit(solution)/shard_map/ppermute | solution.py:292
  134.3 5.3 %collective-permute-start.34 = (bf16[64,512]{1,0:T(8,128)(2,1)S(1)}, bf16[64,512]{1,0:T(8,128)(2,1)S(1)}, u32[]{:S(2)}, u32[]{:S(2)}) collective-permute-start(bf16[64,512]{1,0:T(8,128)(2,1)S(1)} %get-tuple-element.76), channel_id=1, source_target_pairs={{0,6},{1,7},{2,0},{3,1},{4,2},{5,3},{6,4},{7,5},{8,14},{9,15},{10,... | collective-permute-start | bytes 196616 | tf_op jit(solution)/shard_map/ppermute | solution.py:292
  139.6 1.7 collective-permute-start.33
  141.3 0.4 fusion.3
  141.8 0.3 collective-permute-done.34
  142.1 5.5 %collective-permute-start.22 = (bf16[64,896]{1,0:T(8,128)(2,1)S(1)}, bf16[64,896]{1,0:T(8,128)(2,1)S(1)}, u32[]{:S(2)}, u32[]{:S(2)}) collective-permute-start(bf16[64,896]{1,0:T(8,128)(2,1)S(1)} %pad_maximum_fusion.4), channel_id=1, source_target_pairs={{0,4},{1,5},{2,6},{3,7},{4,0},{5,1},{6,2},{7,3},{8,12},{9,13},{10,... | collective-permute-start | bytes 344072 | tf_op jit(solution)/shard_map/ppermute | solution.py:292
  147.6 2.1 %collective-permute-done.33 = bf16[64,512]{1,0:T(8,128)(2,1)S(1)} collective-permute-done((bf16[64,512]{1,0:T(8,128)(2,1)S(1)}, bf16[64,512]{1,0:T(8,128)(2,1)S(1)}, u32[]{:S(2)}, u32[]{:S(2)}) %collective-permute-start.33) | collective-permute-done | bytes 65568 | tf_op jit(solution)/shard_map/ppermute | solution.py:292
  149.7 1.5 collective-permute-start.21
  151.3 0.8 collective-permute-done.22
  152.1 2.4 %collective-permute-done.21 = bf16[64,896]{1,0:T(8,128)(2,1)S(1)} collective-permute-done((bf16[64,896]{1,0:T(8,128)(2,1)S(1)}, bf16[64,896]{1,0:T(8,128)(2,1)S(1)}, u32[]{:S(2)}, u32[]{:S(2)}) %collective-permute-start.21) | collective-permute-done | bytes 114720 | tf_op jit(solution)/shard_map/ppermute | solution.py:292
  154.5 0.7 fusion.19
  155.2 0.2 fusion.15
  155.7 0.2 fusion.34
  156.0 1.7 collective-permute-start.36
  157.7 1.5 collective-permute-start.37
  159.2 0.3 collective-permute-start.38
  159.5 0.2 fusion.33
  159.8 1.7 collective-permute-start.29
  161.5 1.5 collective-permute-start.30
  163.0 1.5 collective-permute-done.36.refs_1_
  164.5 2.6 %collective-permute-start.31 = (bf16[224,384]{1,0:T(8,128)(2,1)S(1)}, bf16[224,384]{1,0:T(8,128)(2,1)S(1)}, u32[]{:S(2)}, u32[]{:S(2)}) collective-permute-start(bf16[224,384]{1,0:T(8,128)(2,1)S(1)} %get-tuple-element.83), channel_id=1, source_target_pairs={{0,24},{8,16},{16,8},{24,0},{1,25},{9,17},{17,9},{25,1},{2,26},{10... | collective-permute-start | bytes 516104 | tf_op jit(solution)/shard_map/ppermute | solution.py:286
  167.2 1.1 fusion.2
  168.3 2.6 %collective-permute-done.37.refs_2_ = bf16[224,512]{1,0:T(8,128)(2,1)S(1)} collective-permute-done((bf16[224,512]{1,0:T(8,128)(2,1)S(1)}, bf16[224,512]{1,0:T(8,128)(2,1)S(1)}, u32[]{:S(2)}, u32[]{:S(2)}) %collective-permute-start.37) | collective-permute-done | bytes 229408 | tf_op jit(solution)/shard_map/ppermute | solution.py:286
  171.0 3.1 %expert_grads.2.refs_4_ = f32[4,224,896]{2,1,0:T(8,128)} custom-call(s32[3]{0:T(128)S(1)} %pad_add_fusion.1.place_ref, f32[4,16]{1,0:T(4,128)S(1)} %copy-done.2, f32[224,512]{1,0:T(8,128)S(1)} %get-tuple-element.86.refs_0_, bf16[224,512]{1,0:T(8,128)(2,1)S(1)} %collective-permute-done.36.refs_1_, bf16[224,512]{1,0:T(8,128)(2,1)S(1)} %collective-permute-done.37.refs_2_, ...), custom_call_target="tpu_custom_call" | custom-call | tf_op jit(solution)/shard_map/expert_grads/pallas_call | solution.py:108
  174.1 0.6 collective-permute-done.30.refs_2_
  174.7 2.7 %expert_grads.3 = f32[4,224,896]{2,1,0:T(8,128)} custom-call(s32[3]{0:T(128)S(1)} %pad_add_fusion.1.place_ref, f32[4,16]{1,0:T(4,128)S(1)} %copy-done.2, f32[224,384]{1,0:T(8,128)S(1)} %get-tuple-element.84.refs_0_, bf16[224,384]{1,0:T(8,128)(2,1)S(1)} %collective-permute-done.29.refs_1_, ...), custom_call_target="tpu_custom_call", output_to_operand_aliasing={{}: (6, {})} | custom-call | tf_op jit(solution)/shard_map/expert_grads/pallas_call | solution.py:108
  (70 shorter events, 2.0 us)
Async XLA Ops:
  0.7 1.4 copy-start
  2.1 0.7 copy-start.1
  2.8 7.3 %copy-start.5 = (bf16[1,64,896]{2,1,0:T(8,128)(2,1)S(1)}, bf16[1,64,896]{2,1,0:T(8,128)(2,1)}, u32[]{:S(2)}) copy-start(bf16[1,64,896]{2,1,0:T(8,128)(2,1)} %param.8) | copy-start | bytes 344068
  4.7 9.6 %collective-permute-start.11 = (bf16[224,384]{1,0:T(8,128)(2,1)S(1)}, bf16[224,384]{1,0:T(8,128)(2,1)S(1)}, u32[]{:S(2)}, u32[]{:S(2)}) collective-permute-start(bf16[224,384]{1,0:T(8,128)(2,1)S(1)} %get-tuple-element.47), channel_id=1, source_target_pairs={{0,24},{8,16},{16,8},{24,0},{1,25},{9,17},{17,9},{25,1},{2,26},{10... | collective-permute-start | bytes 516104 | tf_op jit(solution)/shard_map/ppermute | solution.py:286
  8.6 8.1 %collective-permute-start.10 = (bf16[224,384]{1,0:T(8,128)(2,1)S(1)}, bf16[224,384]{1,0:T(8,128)(2,1)S(1)}, u32[]{:S(2)}, u32[]{:S(2)}) collective-permute-start(bf16[224,384]{1,0:T(8,128)(2,1)S(1)} %get-tuple-element.46), channel_id=1, source_target_pairs={{0,16},{8,24},{16,0},{24,8},{1,17},{9,25},{17,1},{25,9},{2,18},{10... | collective-permute-start | bytes 516104 | tf_op jit(solution)/shard_map/ppermute | solution.py:286
  9.1 9.4 %collective-permute-start.9 = (bf16[224,384]{1,0:T(8,128)(2,1)S(1)}, bf16[224,384]{1,0:T(8,128)(2,1)S(1)}, u32[]{:S(2)}, u32[]{:S(2)}) collective-permute-start(bf16[224,384]{1,0:T(8,128)(2,1)S(1)} %get-tuple-element.45), channel_id=1, source_target_pairs={{0,8},{8,0},{16,24},{24,16},{1,9},{9,1},{17,25},{25,17},{2,10},{10... | collective-permute-start | bytes 516104 | tf_op jit(solution)/shard_map/ppermute | solution.py:286
  10.2 10.2 %collective-permute-start.2 = (bf16[2,64,896]{2,1,0:T(8,128)(2,1)S(1)}, bf16[2,64,896]{2,1,0:T(8,128)(2,1)S(1)}, u32[]{:S(2)}, u32[]{:S(2)}) collective-permute-start(bf16[2,64,896]{2,1,0:T(8,128)(2,1)S(1)} %constant_dynamic-update-slice_fusion), channel_id=1, source_target_pairs={{0,6},{1,7},{2,0},{3,1},{4,2},{5,3},{6,4},{7,5},{8,14},{9,15},{10,... | collective-permute-start | bytes 688136 | tf_op jit(solution)/shard_map/ppermute | solution.py:292
  14.3 34.2 %collective-permute-start.1 = (bf16[2,64,896]{2,1,0:T(8,128)(2,1)S(1)}, bf16[2,64,896]{2,1,0:T(8,128)(2,1)S(1)}, u32[]{:S(2)}, u32[]{:S(2)}) collective-permute-start(bf16[2,64,896]{2,1,0:T(8,128)(2,1)S(1)} %constant_dynamic-update-slice_fusion), channel_id=1, source_target_pairs={{0,4},{1,5},{2,6},{3,7},{4,0},{5,1},{6,2},{7,3},{8,12},{9,13},{10,... | collective-permute-start | bytes 688136 | tf_op jit(solution)/shard_map/ppermute | solution.py:292
  14.3 34.2 %collective-permute-start = (bf16[2,64,896]{2,1,0:T(8,128)(2,1)S(1)}, bf16[2,64,896]{2,1,0:T(8,128)(2,1)S(1)}, u32[]{:S(2)}, u32[]{:S(2)}) collective-permute-start(bf16[2,64,896]{2,1,0:T(8,128)(2,1)S(1)} %constant_dynamic-update-slice_fusion), channel_id=1, source_target_pairs={{0,2},{1,3},{2,4},{3,5},{4,6},{5,7},{6,0},{7,1},{8,10},{9,11},{10,... | collective-permute-start | bytes 688136 | tf_op jit(solution)/shard_map/ppermute | solution.py:292
  16.7 32.5 %collective-permute-start.6 = (bf16[224,512]{1,0:T(8,128)(2,1)S(1)}, bf16[224,512]{1,0:T(8,128)(2,1)S(1)}, u32[]{:S(2)}, u32[]{:S(2)}) collective-permute-start(bf16[224,512]{1,0:T(8,128)(2,1)S(1)} %get-tuple-element.39), channel_id=1, source_target_pairs={{0,24},{8,16},{16,8},{24,0},{1,25},{9,17},{17,9},{25,1},{2,26},{10... | collective-permute-start | bytes 688136 | tf_op jit(solution)/shard_map/ppermute | solution.py:286
  18.5 30.6 %collective-permute-start.5 = (bf16[224,512]{1,0:T(8,128)(2,1)S(1)}, bf16[224,512]{1,0:T(8,128)(2,1)S(1)}, u32[]{:S(2)}, u32[]{:S(2)}) collective-permute-start(bf16[224,512]{1,0:T(8,128)(2,1)S(1)} %get-tuple-element.38), channel_id=1, source_target_pairs={{0,16},{8,24},{16,0},{24,8},{1,17},{9,25},{17,1},{25,9},{2,18},{10... | collective-permute-start | bytes 688136 | tf_op jit(solution)/shard_map/ppermute | solution.py:286
  20.4 28.8 %collective-permute-start.4 = (bf16[224,512]{1,0:T(8,128)(2,1)S(1)}, bf16[224,512]{1,0:T(8,128)(2,1)S(1)}, u32[]{:S(2)}, u32[]{:S(2)}) collective-permute-start(bf16[224,512]{1,0:T(8,128)(2,1)S(1)} %get-tuple-element.37), channel_id=1, source_target_pairs={{0,8},{8,0},{16,24},{24,16},{1,9},{9,1},{17,25},{25,17},{2,10},{10... | collective-permute-start | bytes 688136 | tf_op jit(solution)/shard_map/ppermute | solution.py:286
  48.4 31.4 %collective-permute-start.12 = (bf16[4,224,384]{2,1,0:T(8,128)(2,1)}, bf16[4,224,384]{2,1,0:T(8,128)(2,1)}, u32[]{:S(2)}, u32[]{:S(2)}) collective-permute-start(bf16[4,224,384]{2,1,0:T(8,128)(2,1)} %bitcast.10.near_ref), channel_id=1, source_target_pairs={{0,1},{1,0},{2,3},{3,2},{4,5},{5,4},{6,7},{7,6},{8,9},{9,8},{10,11... | collective-permute-start | bytes 2064392 | tf_op jit(solution)/shard_map/ppermute | solution.py:289
  48.4 20.4 %copy-start.6 = (s32[1,2048]{1,0:T(1,128)S(1)}, s32[1,2048]{1,0:T(1,128)}, u32[]{:S(2)}) copy-start(s32[1,2048]{1,0:T(1,128)} %param.12) | copy-start | bytes 24580
  48.4 20.4 %copy-start.7 = (s32[1,2048]{1,0:T(1,128)S(1)}, s32[1,2048]{1,0:T(1,128)}, u32[]{:S(2)}) copy-start(s32[1,2048]{1,0:T(1,128)} %param.13) | copy-start | bytes 24580
  48.6 21.0 %collective-permute-start.3 = (bf16[4,2,64,896]{3,2,1,0:T(8,128)(2,1)S(1)}, bf16[4,2,64,896]{3,2,1,0:T(8,128)(2,1)}, u32[]{:S(2)}, u32[]{:S(2)}) collective-permute-start(bf16[4,2,64,896]{3,2,1,0:T(8,128)(2,1)S(1)} %pad_maximum_fusion.near_ref), channel_id=1, source_target_pairs={{0,1},{1,0},{2,3},{3,2},{4,5},{5,4},{6,7},{7,6},{8,9},{9,8},{10,11... | collective-permute-start | bytes 2752520 | tf_op jit(solution)/shard_map/ppermute | solution.py:289
  68.8 22.6 %collective-permute-start.7 = (bf16[4,224,512]{2,1,0:T(8,128)(2,1)S(1)}, bf16[4,224,512]{2,1,0:T(8,128)(2,1)}, u32[]{:S(2)}, u32[]{:S(2)}) collective-permute-start(bf16[4,224,512]{2,1,0:T(8,128)(2,1)S(1)} %bitcast.64), channel_id=1, source_target_pairs={{0,1},{1,0},{2,3},{3,2},{4,5},{5,4},{6,7},{7,6},{8,9},{9,8},{10,11... | collective-permute-start | bytes 2752520 | tf_op jit(solution)/shard_map/ppermute | solution.py:289
  78.6 1.2 copy-start.3
  90.8 14.0 %collective-permute-start.13 = (bf16[256,384]{1,0:T(8,128)(2,1)S(1)}, bf16[256,384]{1,0:T(8,128)(2,1)S(1)}, u32[]{:S(2)}, u32[]{:S(2)}) collective-permute-start(bf16[256,384]{1,0:T(8,128)(2,1)S(1)} %get-tuple-element.49), channel_id=1, source_target_pairs={{0,1},{1,0},{2,3},{3,2},{4,5},{5,4},{6,7},{7,6},{8,9},{9,8},{10,11... | collective-permute-start | bytes 589832 | tf_op jit(solution)/shard_map/ppermute | solution.py:289
  104.1 1.5 collective-permute-start.8
  104.1 2.1 %collective-permute-start.14 = (bf16[2,256,384]{2,1,0:T(8,128)(2,1)S(1)}, bf16[2,256,384]{2,1,0:T(8,128)(2,1)S(1)}, u32[]{:S(2)}, u32[]{:S(2)}) collective-permute-start(bf16[2,256,384]{2,1,0:T(8,128)(2,1)S(1)} %get-tuple-element.51), channel_id=1, source_target_pairs={{0,1},{1,0},{2,3},{3,2},{4,5},{5,4},{6,7},{7,6},{8,9},{9,8},{10,11... | collective-permute-start | bytes 1179656 | tf_op jit(solution)/shard_map/ppermute | solution.py:289
  104.6 16.4 %collective-permute-start.24 = (bf16[2,256,512]{2,1,0:T(8,128)(2,1)S(1)}, bf16[2,256,512]{2,1,0:T(8,128)(2,1)S(1)}, u32[]{:S(2)}, u32[]{:S(2)}) collective-permute-start(bf16[2,256,512]{2,1,0:T(8,128)(2,1)S(1)} %get-tuple-element.56), channel_id=1, source_target_pairs={{0,1},{1,0},{2,3},{3,2},{4,5},{5,4},{6,7},{7,6},{8,9},{9,8},{10,11... | collective-permute-start | bytes 1572872 | tf_op jit(solution)/shard_map/ppermute | solution.py:289
  106.3 7.6 %collective-permute-start.17 = (bf16[2,64,384]{2,1,0:T(8,128)(2,1)S(1)}, bf16[2,64,384]{2,1,0:T(8,128)(2,1)S(1)}, u32[]{:S(2)}, u32[]{:S(2)}) collective-permute-start(bf16[2,64,384]{2,1,0:T(8,128)(2,1)S(1)} %get-tuple-element.63), channel_id=1, source_target_pairs={{0,2},{1,3},{2,4},{3,5},{4,6},{5,7},{6,0},{7,1},{8,10},{9,11},{10,... | collective-permute-start | bytes 294920 | tf_op jit(solution)/shard_map/ppermute | solution.py:292
  106.3 10.8 %collective-permute-start.16 = (bf16[2,64,384]{2,1,0:T(8,128)(2,1)S(1)}, bf16[2,64,384]{2,1,0:T(8,128)(2,1)S(1)}, u32[]{:S(2)}, u32[]{:S(2)}) collective-permute-start(bf16[2,64,384]{2,1,0:T(8,128)(2,1)S(1)} %get-tuple-element.64), channel_id=1, source_target_pairs={{0,4},{1,5},{2,6},{3,7},{4,0},{5,1},{6,2},{7,3},{8,12},{9,13},{10,... | collective-permute-start | bytes 294920 | tf_op jit(solution)/shard_map/ppermute | solution.py:292
  108.6 8.6 %collective-permute-start.15 = (bf16[2,64,384]{2,1,0:T(8,128)(2,1)S(1)}, bf16[2,64,384]{2,1,0:T(8,128)(2,1)S(1)}, u32[]{:S(2)}, u32[]{:S(2)}) collective-permute-start(bf16[2,64,384]{2,1,0:T(8,128)(2,1)S(1)} %get-tuple-element.62), channel_id=1, source_target_pairs={{0,6},{1,7},{2,0},{3,1},{4,2},{5,3},{6,4},{7,5},{8,14},{9,15},{10,... | collective-permute-start | bytes 294920 | tf_op jit(solution)/shard_map/ppermute | solution.py:292
  117.2 8.3 %collective-permute-start.20 = (bf16[64,384]{1,0:T(8,128)(2,1)S(1)}, bf16[64,384]{1,0:T(8,128)(2,1)S(1)}, u32[]{:S(2)}, u32[]{:S(2)}) collective-permute-start(bf16[64,384]{1,0:T(8,128)(2,1)S(1)} %get-tuple-element.80), channel_id=1, source_target_pairs={{0,6},{1,7},{2,0},{3,1},{4,2},{5,3},{6,4},{7,5},{8,14},{9,15},{10,... | collective-permute-start | bytes 147464 | tf_op jit(solution)/shard_map/ppermute | solution.py:292
  119.7 10.4 %collective-permute-start.19 = (bf16[64,384]{1,0:T(8,128)(2,1)S(1)}, bf16[64,384]{1,0:T(8,128)(2,1)S(1)}, u32[]{:S(2)}, u32[]{:S(2)}) collective-permute-start(bf16[64,384]{1,0:T(8,128)(2,1)S(1)} %get-tuple-element.79), channel_id=1, source_target_pairs={{0,4},{1,5},{2,6},{3,7},{4,0},{5,1},{6,2},{7,3},{8,12},{9,13},{10,... | collective-permute-start | bytes 147464 | tf_op jit(solution)/shard_map/ppermute | solution.py:292
  120.6 9.4 %collective-permute-start.18 = (bf16[64,384]{1,0:T(8,128)(2,1)S(1)}, bf16[64,384]{1,0:T(8,128)(2,1)S(1)}, u32[]{:S(2)}, u32[]{:S(2)}) collective-permute-start(bf16[64,384]{1,0:T(8,128)(2,1)S(1)} %get-tuple-element.78), channel_id=1, source_target_pairs={{0,2},{1,3},{2,4},{3,5},{4,6},{5,7},{6,0},{7,1},{8,10},{9,11},{10,... | collective-permute-start | bytes 147464 | tf_op jit(solution)/shard_map/ppermute | solution.py:292
  121.0 20.4 %copy-start.4 = (bf16[1792,512]{1,0:T(8,128)(2,1)S(1)}, bf16[1792,512]{1,0:T(8,128)(2,1)}, u32[]{:S(2)}) copy-start(bf16[1792,512]{1,0:T(8,128)(2,1)} %get-tuple-element.57) | copy-start | bytes 5505028
  121.1 9.1 %collective-permute-start.27 = (bf16[2,64,512]{2,1,0:T(8,128)(2,1)S(1)}, bf16[2,64,512]{2,1,0:T(8,128)(2,1)S(1)}, u32[]{:S(2)}, u32[]{:S(2)}) collective-permute-start(bf16[2,64,512]{2,1,0:T(8,128)(2,1)S(1)} %get-tuple-element.60), channel_id=1, source_target_pairs={{0,2},{1,3},{2,4},{3,5},{4,6},{5,7},{6,0},{7,1},{8,10},{9,11},{10,... | collective-permute-start | bytes 393224 | tf_op jit(solution)/shard_map/ppermute | solution.py:292
  123.7 10.5 %collective-permute-start.26 = (bf16[2,64,512]{2,1,0:T(8,128)(2,1)S(1)}, bf16[2,64,512]{2,1,0:T(8,128)(2,1)S(1)}, u32[]{:S(2)}, u32[]{:S(2)}) collective-permute-start(bf16[2,64,512]{2,1,0:T(8,128)(2,1)S(1)} %get-tuple-element.61), channel_id=1, source_target_pairs={{0,4},{1,5},{2,6},{3,7},{4,0},{5,1},{6,2},{7,3},{8,12},{9,13},{10,... | collective-permute-start | bytes 393224 | tf_op jit(solution)/shard_map/ppermute | solution.py:292
  125.6 8.6 %collective-permute-start.25 = (bf16[2,64,512]{2,1,0:T(8,128)(2,1)S(1)}, bf16[2,64,512]{2,1,0:T(8,128)(2,1)S(1)}, u32[]{:S(2)}, u32[]{:S(2)}) collective-permute-start(bf16[2,64,512]{2,1,0:T(8,128)(2,1)S(1)} %get-tuple-element.59), channel_id=1, source_target_pairs={{0,6},{1,7},{2,0},{3,1},{4,2},{5,3},{6,4},{7,5},{8,14},{9,15},{10,... | collective-permute-start | bytes 393224 | tf_op jit(solution)/shard_map/ppermute | solution.py:292
  130.1 25.1 %collective-permute-start.28 = (bf16[256,384]{1,0:T(8,128)(2,1)S(1)}, bf16[256,384]{1,0:T(8,128)(2,1)S(1)}, u32[]{:S(2)}, u32[]{:S(2)}) collective-permute-start(bf16[256,384]{1,0:T(8,128)(2,1)S(1)} %pad_maximum_fusion.2), channel_id=1, source_target_pairs={{0,1},{1,0},{2,3},{3,2},{4,5},{5,4},{6,7},{7,6},{8,9},{9,8},{10,11... | collective-permute-start | bytes 589832 | tf_op jit(solution)/shard_map/ppermute | solution.py:289
  130.2 21.1 %collective-permute-start.23 = (bf16[64,896]{1,0:T(8,128)(2,1)S(1)}, bf16[64,896]{1,0:T(8,128)(2,1)S(1)}, u32[]{:S(2)}, u32[]{:S(2)}) collective-permute-start(bf16[64,896]{1,0:T(8,128)(2,1)S(1)} %pad_maximum_fusion.5), channel_id=1, source_target_pairs={{0,2},{1,3},{2,4},{3,5},{4,6},{5,7},{6,0},{7,1},{8,10},{9,11},{10,... | collective-permute-start | bytes 344072 | tf_op jit(solution)/shard_map/ppermute | solution.py:292
  134.3 7.8 %collective-permute-start.34 = (bf16[64,512]{1,0:T(8,128)(2,1)S(1)}, bf16[64,512]{1,0:T(8,128)(2,1)S(1)}, u32[]{:S(2)}, u32[]{:S(2)}) collective-permute-start(bf16[64,512]{1,0:T(8,128)(2,1)S(1)} %get-tuple-element.76), channel_id=1, source_target_pairs={{0,6},{1,7},{2,0},{3,1},{4,2},{5,3},{6,4},{7,5},{8,14},{9,15},{10,... | collective-permute-start | bytes 196616 | tf_op jit(solution)/shard_map/ppermute | solution.py:292
  139.6 10.1 %collective-permute-start.33 = (bf16[64,512]{1,0:T(8,128)(2,1)S(1)}, bf16[64,512]{1,0:T(8,128)(2,1)S(1)}, u32[]{:S(2)}, u32[]{:S(2)}) collective-permute-start(bf16[64,512]{1,0:T(8,128)(2,1)S(1)} %get-tuple-element.75), channel_id=1, source_target_pairs={{0,4},{1,5},{2,6},{3,7},{4,0},{5,1},{6,2},{7,3},{8,12},{9,13},{10,... | collective-permute-start | bytes 196616 | tf_op jit(solution)/shard_map/ppermute | solution.py:292
  141.3 9.9 %collective-permute-start.32 = (bf16[64,512]{1,0:T(8,128)(2,1)S(1)}, bf16[64,512]{1,0:T(8,128)(2,1)S(1)}, u32[]{:S(2)}, u32[]{:S(2)}) collective-permute-start(bf16[64,512]{1,0:T(8,128)(2,1)S(1)} %get-tuple-element.74), channel_id=1, source_target_pairs={{0,2},{1,3},{2,4},{3,5},{4,6},{5,7},{6,0},{7,1},{8,10},{9,11},{10,... | collective-permute-start | bytes 196616 | tf_op jit(solution)/shard_map/ppermute | solution.py:292
  142.1 10.0 %collective-permute-start.22 = (bf16[64,896]{1,0:T(8,128)(2,1)S(1)}, bf16[64,896]{1,0:T(8,128)(2,1)S(1)}, u32[]{:S(2)}, u32[]{:S(2)}) collective-permute-start(bf16[64,896]{1,0:T(8,128)(2,1)S(1)} %pad_maximum_fusion.4), channel_id=1, source_target_pairs={{0,4},{1,5},{2,6},{3,7},{4,0},{5,1},{6,2},{7,3},{8,12},{9,13},{10,... | collective-permute-start | bytes 344072 | tf_op jit(solution)/shard_map/ppermute | solution.py:292
  149.7 4.8 %collective-permute-start.21 = (bf16[64,896]{1,0:T(8,128)(2,1)S(1)}, bf16[64,896]{1,0:T(8,128)(2,1)S(1)}, u32[]{:S(2)}, u32[]{:S(2)}) collective-permute-start(bf16[64,896]{1,0:T(8,128)(2,1)S(1)} %pad_maximum_fusion.3), channel_id=1, source_target_pairs={{0,6},{1,7},{2,0},{3,1},{4,2},{5,3},{6,4},{7,5},{8,14},{9,15},{10,... | collective-permute-start | bytes 344072 | tf_op jit(solution)/shard_map/ppermute | solution.py:292
  151.2 4.3 %collective-permute-start.35 = (bf16[256,512]{1,0:T(8,128)(2,1)S(1)}, bf16[256,512]{1,0:T(8,128)(2,1)S(1)}, u32[]{:S(2)}, u32[]{:S(2)}) collective-permute-start(bf16[256,512]{1,0:T(8,128)(2,1)S(1)} %pad_maximum_fusion.1), channel_id=1, source_target_pairs={{0,1},{1,0},{2,3},{3,2},{4,5},{5,4},{6,7},{7,6},{8,9},{9,8},{10,11... | collective-permute-start | bytes 786440 | tf_op jit(solution)/shard_map/ppermute | solution.py:289
  156.0 15.0 %copy-start.2 = (f32[4,16]{1,0:T(4,128)S(1)}, f32[4,16]{1,0:T(4,128)}, u32[]{:S(2)}) copy-start(f32[4,16]{1,0:T(4,128)} %coef_ref.5) | copy-start | bytes 772
  156.0 8.6 %collective-permute-start.36 = (bf16[224,512]{1,0:T(8,128)(2,1)S(1)}, bf16[224,512]{1,0:T(8,128)(2,1)S(1)}, u32[]{:S(2)}, u32[]{:S(2)}) collective-permute-start(bf16[224,512]{1,0:T(8,128)(2,1)S(1)} %get-tuple-element.85), channel_id=1, source_target_pairs={{0,8},{8,0},{16,24},{24,16},{1,9},{9,1},{17,25},{25,17},{2,10},{10... | collective-permute-start | bytes 688136 | tf_op jit(solution)/shard_map/ppermute | solution.py:286
  157.7 13.3 %collective-permute-start.37 = (bf16[224,512]{1,0:T(8,128)(2,1)S(1)}, bf16[224,512]{1,0:T(8,128)(2,1)S(1)}, u32[]{:S(2)}, u32[]{:S(2)}) collective-permute-start(bf16[224,512]{1,0:T(8,128)(2,1)S(1)} %get-tuple-element.85), channel_id=1, source_target_pairs={{0,16},{8,24},{16,0},{24,8},{1,17},{9,25},{17,1},{25,9},{2,18},{10... | collective-permute-start | bytes 688136 | tf_op jit(solution)/shard_map/ppermute | solution.py:286
  159.2 11.8 %collective-permute-start.38 = (bf16[224,512]{1,0:T(8,128)(2,1)S(1)}, bf16[224,512]{1,0:T(8,128)(2,1)S(1)}, u32[]{:S(2)}, u32[]{:S(2)}) collective-permute-start(bf16[224,512]{1,0:T(8,128)(2,1)S(1)} %get-tuple-element.85), channel_id=1, source_target_pairs={{0,24},{8,16},{16,8},{24,0},{1,25},{9,17},{17,9},{25,1},{2,26},{10... | collective-permute-start | bytes 688136 | tf_op jit(solution)/shard_map/ppermute | solution.py:286
  159.8 14.3 %collective-permute-start.29 = (bf16[224,384]{1,0:T(8,128)(2,1)S(1)}, bf16[224,384]{1,0:T(8,128)(2,1)S(1)}, u32[]{:S(2)}, u32[]{:S(2)}) collective-permute-start(bf16[224,384]{1,0:T(8,128)(2,1)S(1)} %get-tuple-element.83), channel_id=1, source_target_pairs={{0,8},{8,0},{16,24},{24,16},{1,9},{9,1},{17,25},{25,17},{2,10},{10... | collective-permute-start | bytes 516104 | tf_op jit(solution)/shard_map/ppermute | solution.py:286
  161.5 13.2 %collective-permute-start.30 = (bf16[224,384]{1,0:T(8,128)(2,1)S(1)}, bf16[224,384]{1,0:T(8,128)(2,1)S(1)}, u32[]{:S(2)}, u32[]{:S(2)}) collective-permute-start(bf16[224,384]{1,0:T(8,128)(2,1)S(1)} %get-tuple-element.83), channel_id=1, source_target_pairs={{0,16},{8,24},{16,0},{24,8},{1,17},{9,25},{17,1},{25,9},{2,18},{10... | collective-permute-start | bytes 516104 | tf_op jit(solution)/shard_map/ppermute | solution.py:286
  164.5 10.1 %collective-permute-start.31 = (bf16[224,384]{1,0:T(8,128)(2,1)S(1)}, bf16[224,384]{1,0:T(8,128)(2,1)S(1)}, u32[]{:S(2)}, u32[]{:S(2)}) collective-permute-start(bf16[224,384]{1,0:T(8,128)(2,1)S(1)} %get-tuple-element.83), channel_id=1, source_target_pairs={{0,24},{8,16},{16,8},{24,0},{1,25},{9,17},{17,9},{25,1},{2,26},{10... | collective-permute-start | bytes 516104 | tf_op jit(solution)/shard_map/ppermute | solution.py:286

commit v3 on v2

--- a/solution.py
+++ b/solution.py
@@ -11,7 +11,7 @@
 BF16 = jnp.bfloat16
 VMEM_LIMIT = 48 << 20
 LANES = 128
-PIECES = 2
+PIECES = 1
 
 
 def whole_vmem():

time: 178 us -> 209 us (1.17)
  waiting for transfers between devices: 27.4 us -> 118 us
  blocking collectives: 46.1 us -> 0 us
  starting transfers between devices: 52.5 us -> 27.4 us
  between operations: 1.13 us -> 14.2 us
  other arithmetic: 2.1 us -> 6.02 us
  Pallas kernels: 40.4 us -> 36.5 us
    all_gather x2 -> x0, blocking collectives: 46.1 us -> none  [shards(): block = lax.all_gather(total.astype(BF16), 'edge', axis_index_groups=lines)]
    all_gather x0 -> x1, waiting for transfers between devices: none -> 38.1 us  [shards(): block = lax.all_gather(total.astype(BF16), 'edge', axis_index_groups=lines)]
    ppermute x18 -> x12, waiting for transfers between devices: 20.6 us -> 47.6 us  [shift(): lax.ppermute(x, 'edge', [(e, (e + 2 * k) % ways) for e in range(ways)])]
    ppermute x12 -> x6, waiting for transfers between devices: 5.52 us -> 27.8 us  [across(): return lax.ppermute(x, 'sys', [(s, s ^ k) for s in range(systems)])]
    ppermute x18 -> x12, starting transfers between devices: 32 us -> 18.1 us  [shift(): lax.ppermute(x, 'edge', [(e, (e + 2 * k) % ways) for e in range(ways)])]
    ppermute x12 -> x6, starting transfers between devices: 18.7 us -> 8.99 us  [across(): return lax.ppermute(x, 'sys', [(s, s ^ k) for s in range(systems)])]
    pallas_call x2 -> x1, Pallas kernels: 23.7 us -> 20.6 us  [edge_sums(): pl.pallas_call(edge_kernel, grid=(edges // tile,), out_shape=[jax.ShapeDt...]
    ppermute x9 -> x5, waiting for transfers between devices: 1.24 us -> 4.08 us  [swap(): return lax.ppermute(x, 'edge', [(e, e ^ 1) for e in range(ways)])]
  transfers between devices with their start and end apart: 39 -> 24, of which waited for: 15 -> 14; matrix products, arithmetic and copies ran while one was open for 3% -> 3% of each run, Pallas kernels for 20% -> 4%
where the time goes in v3:
time: 209 us
  waiting for transfers between devices  118 us (56%)
  Pallas kernels  36.5 us (17%)
  starting transfers between devices  27.4 us (13%)
  between operations  14.2 us (7%)
  other arithmetic  6.02 us (3%)
  local copies, waits for them, and re-layouts  4.77 us (2%)
  matrix products  2.52 us (1%)
    ppermute x12, waiting for transfers between devices, shift(): lax.ppermute(x, 'edge', [(e, (e + 2 * k) % ways) for e in range(ways)])  47.6 us
    all_gather x1, waiting for transfers between devices, shards(): block = lax.all_gather(total.astype(BF16), 'edge', axis_index_groups=lines)  38.1 us
    ppermute x6, waiting for transfers between devices, across(): return lax.ppermute(x, 'sys', [(s, s ^ k) for s in range(systems)])  27.8 us
    pallas_call x1, Pallas kernels, edge_sums(): pl.pallas_call(edge_kernel, grid=(edges // tile,), out_shape=[jax.ShapeDt...  20.6 us
    ppermute x12, starting transfers between devices, shift(): lax.ppermute(x, 'edge', [(e, (e + 2 * k) % ways) for e in range(ways)])  18.1 us
    pallas_call x1, Pallas kernels, prepare(): pl.pallas_call(functools.partial(prepare_kernel, chunks), grid=(edges //...  9.15 us
    ppermute x6, starting transfers between devices, across(): return lax.ppermute(x, 'sys', [(s, s ^ k) for s in range(systems)])  8.99 us
    pallas_call x1, Pallas kernels, expert_grads(): pl.pallas_call(expert_kernel, grid=(size // tile,), out_shape=jax.ShapeDt...  4.95 us
  transfers between devices with their start and end apart: 24, of which 14 were waited for; matrix products, arithmetic and copies ran while one was open for 3% of the time, Pallas kernels for 4%

profile of v3, /device:TPU:0, one launch (start us, length us, event | category | flops | bytes accessed | tf_op | source)
XLA Modules:
  0.0 209.1 jit_solution(3300065945336630962)
XLA Ops:
  7.2 0.0 all-gather.3.cloned.1.call-start
  7.2 0.1 pad_add_fusion.1.place_ref
  7.3 1.4 copy-done
  8.7 0.7 copy-done.1
  9.4 1.8 merge_parts.1
  11.3 3.0 %collective-permute-start.4 = (bf16[224,896]{1,0:T(8,128)(2,1)S(1)}, bf16[224,896]{1,0:T(8,128)(2,1)S(1)}, u32[]{:S(2)}, u32[]{:S(2)}) collective-permute-start(bf16[224,896]{1,0:T(8,128)(2,1)S(1)} %get-tuple-element.26), channel_id=1, source_target_pairs={{0,8},{8,0},{16,24},{24,16},{1,9},{9,1},{17,25},{25,17},{2,10},{10... | collective-permute-start | bytes 1204232 | tf_op jit(solution)/shard_map/ppermute | solution.py:286
  14.3 1.5 collective-permute-start.5
  15.8 0.0 collective-permute-start.6
  15.8 8.6 %collective-permute-done.4 = bf16[224,896]{1,0:T(8,128)(2,1)S(1)} collective-permute-done((bf16[224,896]{1,0:T(8,128)(2,1)S(1)}, bf16[224,896]{1,0:T(8,128)(2,1)S(1)}, u32[]{:S(2)}, u32[]{:S(2)}) %collective-permute-start.4) | collective-permute-done | bytes 401440 | tf_op jit(solution)/shard_map/ppermute | solution.py:286
  24.4 9.2 %collective-permute-done.5 = bf16[224,896]{1,0:T(8,128)(2,1)S(1)} collective-permute-done((bf16[224,896]{1,0:T(8,128)(2,1)S(1)}, bf16[224,896]{1,0:T(8,128)(2,1)S(1)}, u32[]{:S(2)}, u32[]{:S(2)}) %collective-permute-start.5) | collective-permute-done | bytes 401440 | tf_op jit(solution)/shard_map/ppermute | solution.py:286
  33.6 0.9 add_convert_fusion
  34.6 0.0 all-gather.3.cloned.1.call-update
  34.6 38.1 %all-gather.3.cloned.1.call-done = bf16[896,896]{1,0:T(8,128)(2,1)} async-done(((bf16[224,896]{1,0:T(8,128)(2,1)}), bf16[896,896]{1,0:T(8,128)(2,1)}) %all-gather.3.cloned.1.call-update) | async-done | bytes 1605648 | tf_op jit(solution)/shard_map/all_gather | solution.py:316
  72.7 0.0 collective-permute-start.7
  72.7 0.5 collective-permute-start
  73.2 1.4 collective-permute-start.1
  74.6 2.4 %collective-permute-start.2 = (bf16[2,64,896]{2,1,0:T(8,128)(2,1)S(1)}, bf16[2,64,896]{2,1,0:T(8,128)(2,1)S(1)}, u32[]{:S(2)}, u32[]{:S(2)}) collective-permute-start(bf16[2,64,896]{2,1,0:T(8,128)(2,1)S(1)} %constant_dynamic-update-slice_fusion), channel_id=1, source_target_pairs={{0,6},{1,7},{2,0},{3,1},{4,2},{5,3},{6,4},{7,5},{8,14},{9,15},{10,... | collective-permute-start | bytes 688136 | tf_op jit(solution)/shard_map/ppermute | solution.py:292
  77.0 6.1 %collective-permute-done = bf16[2,64,896]{2,1,0:T(8,128)(2,1)S(1)} collective-permute-done((bf16[2,64,896]{2,1,0:T(8,128)(2,1)S(1)}, bf16[2,64,896]{2,1,0:T(8,128)(2,1)S(1)}, u32[]{:S(2)}, u32[]{:S(2)}) %collective-permute-start) | collective-permute-done | bytes 229408 | tf_op jit(solution)/shard_map/ppermute | solution.py:292
  83.1 9.3 %collective-permute-done.1 = bf16[2,64,896]{2,1,0:T(8,128)(2,1)S(1)} collective-permute-done((bf16[2,64,896]{2,1,0:T(8,128)(2,1)S(1)}, bf16[2,64,896]{2,1,0:T(8,128)(2,1)S(1)}, u32[]{:S(2)}, u32[]{:S(2)}) %collective-permute-start.1) | collective-permute-done | bytes 229408 | tf_op jit(solution)/shard_map/ppermute | solution.py:292
  92.4 0.0 collective-permute-done.2
  92.4 0.1 pad_maximum_fusion.near_ref
  92.6 0.1 collective-permute-start.3
  92.7 0.3 fusion.14
  93.0 0.4 copy.10.cols_ref
  93.4 1.7 collective-permute-done.3.far_ref
  95.1 0.9 copy-done.4
  96.1 1.2 copy-done.5
  97.2 9.1 %prepare.1 = (bf16[512,896]{1,0:T(8,128)(2,1)S(1)}, bf16[2048,1024]{1,0:T(8,128)(2,1)}, bf16[1024,2048]{1,0:T(8,128)(2,1)}, bf16[2048,896]{1,0:T(8,128)(2,1)}, bf16[2048,896]{1,0:T(8,128)(2,1)}) custom-call(s32[2048,2]{1,0:T(8,128)S(1)} %copy.10.cols_ref, s32[2,2048]{1,0:T(2,128)S(1)} %get-tuple-element.47.rows_ref, bf16[2048,896]{1,0:T(8,128)(2,1)} %bitcast.46, ...), custom_call_target="tpu_custom_call" | custom-call | flops 1879048192 | bytes 25690112 | tf_op jit(solution)/shard_map/prepare/pallas_call | solution.py:160
  106.4 0.0 collective-permute-done.7.far_ref
  106.4 20.6 %edge_sums.1 = (f32[2,256,896]{2,1,0:T(8,128)}, bf16[2,256,896]{2,1,0:T(8,128)(2,1)S(1)}, f32[256,896]{1,0:T(8,128)S(1)}, bf16[256,896]{1,0:T(8,128)(2,1)S(1)}, bf16[1792,896]{1,0:T(8,128)(2,1)}) custom-call(s32[3]{0:T(128)S(1)} %pad_add_fusion.1.place_ref, bf16[2048,1024]{1,0:T(8,128)(2,1)} %get-tuple-element.20.gather_ref, ...), custom_call_target="tpu_custom_call" | custom-call | flops 11039408128 | bytes 15728640 | tf_op jit(solution)/shard_map/edge_sums/pallas_call | solution.py:239
  127.0 0.1 collective-permute-start.9
  127.1 2.3 %collective-permute-done.9 = bf16[2,256,896]{2,1,0:T(8,128)(2,1)S(1)} collective-permute-done((bf16[2,256,896]{2,1,0:T(8,128)(2,1)S(1)}, bf16[2,256,896]{2,1,0:T(8,128)(2,1)S(1)}, u32[]{:S(2)}, u32[]{:S(2)}) %collective-permute-start.9) | collective-permute-done | bytes 917536 | tf_op jit(solution)/shard_map/ppermute | solution.py:289
  129.4 2.2 %add_convert_fusion.4 = (bf16[2,64,896]{2,1,0:T(8,128)(2,1)}, bf16[2,64,896]{2,1,0:T(8,128)(2,1)}, bf16[2,64,896]{2,1,0:T(8,128)(2,1)}) fusion(f32[2,256,896]{2,1,0:T(8,128)} %get-tuple-element.31, bf16[2,256,896]{2,1,0:T(8,128)(2,1)S(1)} %collective-permute-done.9), kind=kLoop, calls=%fused_computation.13 | loop fusion | flops 1032192 | bytes 2752512 | tf_op jit(solution)/shard_map/convert_element_type | solution.py:329
  131.6 5.3 %collective-permute-start.10 = (bf16[2,64,896]{2,1,0:T(8,128)(2,1)}, bf16[2,64,896]{2,1,0:T(8,128)(2,1)S(1)}, u32[]{:S(2)}, u32[]{:S(2)}) collective-permute-start(bf16[2,64,896]{2,1,0:T(8,128)(2,1)} %get-tuple-element.37), channel_id=1, source_target_pairs={{0,6},{1,7},{2,0},{3,1},{4,2},{5,3},{6,4},{7,5},{8,14},{9,15},{10,... | collective-permute-start | bytes 688136 | tf_op jit(solution)/shard_map/ppermute | solution.py:292
  136.9 0.9 collective-permute-start.11
  137.9 0.0 collective-permute-start.12
  137.9 0.0 collective-permute-start.8
  137.9 5.4 %collective-permute-done.10 = bf16[2,64,896]{2,1,0:T(8,128)(2,1)S(1)} collective-permute-done((bf16[2,64,896]{2,1,0:T(8,128)(2,1)}, bf16[2,64,896]{2,1,0:T(8,128)(2,1)S(1)}, u32[]{:S(2)}, u32[]{:S(2)}) %collective-permute-start.10) | collective-permute-done | bytes 229408 | tf_op jit(solution)/shard_map/ppermute | solution.py:292
  143.3 15.3 %collective-permute-done.11 = bf16[2,64,896]{2,1,0:T(8,128)(2,1)} collective-permute-done((bf16[2,64,896]{2,1,0:T(8,128)(2,1)}, bf16[2,64,896]{2,1,0:T(8,128)(2,1)}, u32[]{:S(2)}, u32[]{:S(2)}) %collective-permute-start.11) | collective-permute-done | bytes 229408 | tf_op jit(solution)/shard_map/ppermute | solution.py:292
  158.6 1.4 add_convert_fusion.1
  160.0 0.1 broadcast_select_fusion.3
  160.1 0.1 collective-permute-start.13
  160.1 1.2 collective-permute-start.14
  161.3 2.8 %collective-permute-start.15 = (bf16[64,896]{1,0:T(8,128)(2,1)S(1)}, bf16[64,896]{1,0:T(8,128)(2,1)S(1)}, u32[]{:S(2)}, u32[]{:S(2)}) collective-permute-start(bf16[64,896]{1,0:T(8,128)(2,1)S(1)} %get-tuple-element.46), channel_id=1, source_target_pairs={{0,6},{1,7},{2,0},{3,1},{4,2},{5,3},{6,4},{7,5},{8,14},{9,15},{10,... | collective-permute-start | bytes 344072 | tf_op jit(solution)/shard_map/ppermute | solution.py:292
  164.2 0.1 dynamic-slice_bitcast_fusion
  164.3 3.7 %collective-permute-done.13 = bf16[64,896]{1,0:T(8,128)(2,1)S(1)} collective-permute-done((bf16[64,896]{1,0:T(8,128)(2,1)S(1)}, bf16[64,896]{1,0:T(8,128)(2,1)S(1)}, u32[]{:S(2)}, u32[]{:S(2)}) %collective-permute-start.13) | collective-permute-done | bytes 114720 | tf_op jit(solution)/shard_map/ppermute | solution.py:292
  168.0 3.3 %collective-permute-done.14 = bf16[64,896]{1,0:T(8,128)(2,1)S(1)} collective-permute-done((bf16[64,896]{1,0:T(8,128)(2,1)S(1)}, bf16[64,896]{1,0:T(8,128)(2,1)S(1)}, u32[]{:S(2)}, u32[]{:S(2)}) %collective-permute-start.14) | collective-permute-done | bytes 114720 | tf_op jit(solution)/shard_map/ppermute | solution.py:292
  171.4 0.1 collective-permute-start.19
  171.5 0.0 collective-permute-done.8
  171.5 0.1 add_convert_fusion.8
  171.6 0.6 fusion
  172.2 2.7 %collective-permute-start.16 = (bf16[64,896]{1,0:T(8,128)(2,1)S(1)}, bf16[64,896]{1,0:T(8,128)(2,1)S(1)}, u32[]{:S(2)}, u32[]{:S(2)}) collective-permute-start(bf16[64,896]{1,0:T(8,128)(2,1)S(1)} %get-tuple-element.33), channel_id=1, source_target_pairs={{0,6},{1,7},{2,0},{3,1},{4,2},{5,3},{6,4},{7,5},{8,14},{9,15},{10,... | collective-permute-start | bytes 344072 | tf_op jit(solution)/shard_map/ppermute | solution.py:292
  174.9 0.8 collective-permute-start.17
  175.7 0.3 fusion.10
  176.0 0.3 fusion.27
  176.4 1.5 collective-permute-start.20
  177.9 1.5 collective-permute-start.21
  179.4 1.4 collective-permute-start.22
  180.8 1.3 fusion.7
  182.1 4.5 %collective-permute-done.17 = bf16[64,896]{1,0:T(8,128)(2,1)S(1)} collective-permute-done((bf16[64,896]{1,0:T(8,128)(2,1)S(1)}, bf16[64,896]{1,0:T(8,128)(2,1)S(1)}, u32[]{:S(2)}, u32[]{:S(2)}) %collective-permute-start.17) | collective-permute-done | bytes 114720 | tf_op jit(solution)/shard_map/ppermute | solution.py:292
  186.6 0.7 fusion.13
  187.3 1.3 collective-permute-done.20.refs_1_
  188.6 8.8 %collective-permute-done.21.refs_2_ = bf16[224,896]{1,0:T(8,128)(2,1)S(1)} collective-permute-done((bf16[224,896]{1,0:T(8,128)(2,1)S(1)}, bf16[224,896]{1,0:T(8,128)(2,1)S(1)}, u32[]{:S(2)}, u32[]{:S(2)}) %collective-permute-start.21) | collective-permute-done | bytes 401440 | tf_op jit(solution)/shard_map/ppermute | solution.py:286
  197.3 5.0 %expert_grads.1 = f32[4,224,896]{2,1,0:T(8,128)} custom-call(s32[3]{0:T(128)S(1)} %pad_add_fusion.1.place_ref, f32[4,16]{1,0:T(4,128)S(1)} %copy-done.2, f32[224,896]{1,0:T(8,128)S(1)} %get-tuple-element.50.refs_0_, bf16[224,896]{1,0:T(8,128)(2,1)S(1)} %collective-permute-done.20.refs_1_, bf16[224,896]{1,0:T(8,128)(2,1)S(1)} %collective-permute-done.21.refs_2_, ...), custom_call_target="tpu_custom_call" | custom-call | tf_op jit(solution)/shard_map/expert_grads/pallas_call | solution.py:108
  (30 shorter events, 0.1 us)
Async XLA Ops:
  7.2 65.5 %all-gather.3.cloned.1.call-start = ((), (), s32[]{:S(2)}) async-start(), calls=%async_computation | async-start | bytes 2007040 | tf_op jit(solution)/shard_map/all_gather | solution.py:316
  7.3 1.4 copy-start
  8.7 0.7 copy-start.1
  9.4 63.3 %copy-start.7 = (bf16[1,64,896]{2,1,0:T(8,128)(2,1)S(1)}, bf16[1,64,896]{2,1,0:T(8,128)(2,1)}, u32[]{:S(2)}) copy-start(bf16[1,64,896]{2,1,0:T(8,128)(2,1)} %param.7) | copy-start | bytes 344068
  9.4 63.3 %copy-start.8 = (bf16[1,64,896]{2,1,0:T(8,128)(2,1)S(1)}, bf16[1,64,896]{2,1,0:T(8,128)(2,1)}, u32[]{:S(2)}) copy-start(bf16[1,64,896]{2,1,0:T(8,128)(2,1)} %param.8) | copy-start | bytes 344068
  9.4 83.3 %copy-start.9 = (s32[1,2048]{1,0:T(1,128)S(1)}, s32[1,2048]{1,0:T(1,128)}, u32[]{:S(2)}) copy-start(s32[1,2048]{1,0:T(1,128)} %param.12) | copy-start | bytes 24580
  9.4 83.3 %copy-start.10 = (s32[1,2048]{1,0:T(1,128)S(1)}, s32[1,2048]{1,0:T(1,128)}, u32[]{:S(2)}) copy-start(s32[1,2048]{1,0:T(1,128)} %param.13) | copy-start | bytes 24580
  11.3 13.1 %collective-permute-start.4 = (bf16[224,896]{1,0:T(8,128)(2,1)S(1)}, bf16[224,896]{1,0:T(8,128)(2,1)S(1)}, u32[]{:S(2)}, u32[]{:S(2)}) collective-permute-start(bf16[224,896]{1,0:T(8,128)(2,1)S(1)} %get-tuple-element.26), channel_id=1, source_target_pairs={{0,8},{8,0},{16,24},{24,16},{1,9},{9,1},{17,25},{25,17},{2,10},{10... | collective-permute-start | bytes 1204232 | tf_op jit(solution)/shard_map/ppermute | solution.py:286
  14.3 19.4 %collective-permute-start.5 = (bf16[224,896]{1,0:T(8,128)(2,1)S(1)}, bf16[224,896]{1,0:T(8,128)(2,1)S(1)}, u32[]{:S(2)}, u32[]{:S(2)}) collective-permute-start(bf16[224,896]{1,0:T(8,128)(2,1)S(1)} %get-tuple-element.27), channel_id=1, source_target_pairs={{0,16},{8,24},{16,0},{24,8},{1,17},{9,25},{17,1},{25,9},{2,18},{10... | collective-permute-start | bytes 1204232 | tf_op jit(solution)/shard_map/ppermute | solution.py:286
  15.8 17.8 %collective-permute-start.6 = (bf16[224,896]{1,0:T(8,128)(2,1)S(1)}, bf16[224,896]{1,0:T(8,128)(2,1)S(1)}, u32[]{:S(2)}, u32[]{:S(2)}) collective-permute-start(bf16[224,896]{1,0:T(8,128)(2,1)S(1)} %get-tuple-element.28), channel_id=1, source_target_pairs={{0,24},{8,16},{16,8},{24,0},{1,25},{9,17},{17,9},{25,1},{2,26},{10... | collective-permute-start | bytes 1204232 | tf_op jit(solution)/shard_map/ppermute | solution.py:286
  72.7 33.7 %collective-permute-start.7 = (bf16[4,224,896]{2,1,0:T(8,128)(2,1)}, bf16[4,224,896]{2,1,0:T(8,128)(2,1)}, u32[]{:S(2)}, u32[]{:S(2)}) collective-permute-start(bf16[4,224,896]{2,1,0:T(8,128)(2,1)} %bitcast.40), channel_id=1, source_target_pairs={{0,1},{1,0},{2,3},{3,2},{4,5},{5,4},{6,7},{7,6},{8,9},{9,8},{10,11... | collective-permute-start | bytes 4816904 | tf_op jit(solution)/shard_map/ppermute | solution.py:289
  72.7 10.4 %collective-permute-start = (bf16[2,64,896]{2,1,0:T(8,128)(2,1)S(1)}, bf16[2,64,896]{2,1,0:T(8,128)(2,1)S(1)}, u32[]{:S(2)}, u32[]{:S(2)}) collective-permute-start(bf16[2,64,896]{2,1,0:T(8,128)(2,1)S(1)} %constant_dynamic-update-slice_fusion), channel_id=1, source_target_pairs={{0,2},{1,3},{2,4},{3,5},{4,6},{5,7},{6,0},{7,1},{8,10},{9,11},{10,... | collective-permute-start | bytes 688136 | tf_op jit(solution)/shard_map/ppermute | solution.py:292
  73.2 19.2 %collective-permute-start.1 = (bf16[2,64,896]{2,1,0:T(8,128)(2,1)S(1)}, bf16[2,64,896]{2,1,0:T(8,128)(2,1)S(1)}, u32[]{:S(2)}, u32[]{:S(2)}) collective-permute-start(bf16[2,64,896]{2,1,0:T(8,128)(2,1)S(1)} %constant_dynamic-update-slice_fusion), channel_id=1, source_target_pairs={{0,4},{1,5},{2,6},{3,7},{4,0},{5,1},{6,2},{7,3},{8,12},{9,13},{10,... | collective-permute-start | bytes 688136 | tf_op jit(solution)/shard_map/ppermute | solution.py:292
  74.6 17.8 %collective-permute-start.2 = (bf16[2,64,896]{2,1,0:T(8,128)(2,1)S(1)}, bf16[2,64,896]{2,1,0:T(8,128)(2,1)S(1)}, u32[]{:S(2)}, u32[]{:S(2)}) collective-permute-start(bf16[2,64,896]{2,1,0:T(8,128)(2,1)S(1)} %constant_dynamic-update-slice_fusion), channel_id=1, source_target_pairs={{0,6},{1,7},{2,0},{3,1},{4,2},{5,3},{6,4},{7,5},{8,14},{9,15},{10,... | collective-permute-start | bytes 688136 | tf_op jit(solution)/shard_map/ppermute | solution.py:292
  92.6 2.5 %collective-permute-start.3 = (bf16[4,2,64,896]{3,2,1,0:T(8,128)(2,1)S(1)}, bf16[4,2,64,896]{3,2,1,0:T(8,128)(2,1)S(1)}, u32[]{:S(2)}, u32[]{:S(2)}) collective-permute-start(bf16[4,2,64,896]{3,2,1,0:T(8,128)(2,1)S(1)} %pad_maximum_fusion.near_ref), channel_id=1, source_target_pairs={{0,1},{1,0},{2,3},{3,2},{4,5},{5,4},{6,7},{7,6},{8,9},{9,8},{10,11... | collective-permute-start | bytes 2752520 | tf_op jit(solution)/shard_map/ppermute | solution.py:289
  95.1 0.9 copy-start.4
  96.1 1.2 copy-start.5
  97.2 9.2 %copy-start.3 = (bf16[896,896]{1,0:T(8,128)(2,1)S(1)}, bf16[896,896]{1,0:T(8,128)(2,1)}, u32[]{:S(2)}) copy-start(bf16[896,896]{1,0:T(8,128)(2,1)} %all-gather.3.cloned.1.call-done) | copy-start | bytes 4816900
  127.0 2.5 %collective-permute-start.9 = (bf16[2,256,896]{2,1,0:T(8,128)(2,1)S(1)}, bf16[2,256,896]{2,1,0:T(8,128)(2,1)S(1)}, u32[]{:S(2)}, u32[]{:S(2)}) collective-permute-start(bf16[2,256,896]{2,1,0:T(8,128)(2,1)S(1)} %get-tuple-element.32), channel_id=1, source_target_pairs={{0,1},{1,0},{2,3},{3,2},{4,5},{5,4},{6,7},{7,6},{8,9},{9,8},{10,11... | collective-permute-start | bytes 2752520 | tf_op jit(solution)/shard_map/ppermute | solution.py:289
  131.6 11.7 %collective-permute-start.10 = (bf16[2,64,896]{2,1,0:T(8,128)(2,1)}, bf16[2,64,896]{2,1,0:T(8,128)(2,1)S(1)}, u32[]{:S(2)}, u32[]{:S(2)}) collective-permute-start(bf16[2,64,896]{2,1,0:T(8,128)(2,1)} %get-tuple-element.37), channel_id=1, source_target_pairs={{0,6},{1,7},{2,0},{3,1},{4,2},{5,3},{6,4},{7,5},{8,14},{9,15},{10,... | collective-permute-start | bytes 688136 | tf_op jit(solution)/shard_map/ppermute | solution.py:292
  136.9 21.6 %collective-permute-start.11 = (bf16[2,64,896]{2,1,0:T(8,128)(2,1)}, bf16[2,64,896]{2,1,0:T(8,128)(2,1)}, u32[]{:S(2)}, u32[]{:S(2)}) collective-permute-start(bf16[2,64,896]{2,1,0:T(8,128)(2,1)} %get-tuple-element.39), channel_id=1, source_target_pairs={{0,4},{1,5},{2,6},{3,7},{4,0},{5,1},{6,2},{7,3},{8,12},{9,13},{10,... | collective-permute-start | bytes 688136 | tf_op jit(solution)/shard_map/ppermute | solution.py:292
  137.9 20.7 %collective-permute-start.12 = (bf16[2,64,896]{2,1,0:T(8,128)(2,1)}, bf16[2,64,896]{2,1,0:T(8,128)(2,1)}, u32[]{:S(2)}, u32[]{:S(2)}) collective-permute-start(bf16[2,64,896]{2,1,0:T(8,128)(2,1)} %get-tuple-element.38), channel_id=1, source_target_pairs={{0,2},{1,3},{2,4},{3,5},{4,6},{5,7},{6,0},{7,1},{8,10},{9,11},{10,... | collective-permute-start | bytes 688136 | tf_op jit(solution)/shard_map/ppermute | solution.py:292
  137.9 33.7 %copy-start.6 = (bf16[1792,896]{1,0:T(8,128)(2,1)S(1)}, bf16[1792,896]{1,0:T(8,128)(2,1)}, u32[]{:S(2)}) copy-start(bf16[1792,896]{1,0:T(8,128)(2,1)} %get-tuple-element.36) | copy-start | bytes 9633796
  137.9 33.6 %collective-permute-start.8 = (bf16[256,896]{1,0:T(8,128)(2,1)S(1)}, bf16[256,896]{1,0:T(8,128)(2,1)S(1)}, u32[]{:S(2)}, u32[]{:S(2)}) collective-permute-start(bf16[256,896]{1,0:T(8,128)(2,1)S(1)} %get-tuple-element.30), channel_id=1, source_target_pairs={{0,1},{1,0},{2,3},{3,2},{4,5},{5,4},{6,7},{7,6},{8,9},{9,8},{10,11... | collective-permute-start | bytes 1376264 | tf_op jit(solution)/shard_map/ppermute | solution.py:289
  160.1 8.0 %collective-permute-start.13 = (bf16[64,896]{1,0:T(8,128)(2,1)S(1)}, bf16[64,896]{1,0:T(8,128)(2,1)S(1)}, u32[]{:S(2)}, u32[]{:S(2)}) collective-permute-start(bf16[64,896]{1,0:T(8,128)(2,1)S(1)} %get-tuple-element.44), channel_id=1, source_target_pairs={{0,2},{1,3},{2,4},{3,5},{4,6},{5,7},{6,0},{7,1},{8,10},{9,11},{10,... | collective-permute-start | bytes 344072 | tf_op jit(solution)/shard_map/ppermute | solution.py:292
  160.1 11.2 %collective-permute-start.14 = (bf16[64,896]{1,0:T(8,128)(2,1)S(1)}, bf16[64,896]{1,0:T(8,128)(2,1)S(1)}, u32[]{:S(2)}, u32[]{:S(2)}) collective-permute-start(bf16[64,896]{1,0:T(8,128)(2,1)S(1)} %get-tuple-element.45), channel_id=1, source_target_pairs={{0,4},{1,5},{2,6},{3,7},{4,0},{5,1},{6,2},{7,3},{8,12},{9,13},{10,... | collective-permute-start | bytes 344072 | tf_op jit(solution)/shard_map/ppermute | solution.py:292
  161.3 10.0 %collective-permute-start.15 = (bf16[64,896]{1,0:T(8,128)(2,1)S(1)}, bf16[64,896]{1,0:T(8,128)(2,1)S(1)}, u32[]{:S(2)}, u32[]{:S(2)}) collective-permute-start(bf16[64,896]{1,0:T(8,128)(2,1)S(1)} %get-tuple-element.46), channel_id=1, source_target_pairs={{0,6},{1,7},{2,0},{3,1},{4,2},{5,3},{6,4},{7,5},{8,14},{9,15},{10,... | collective-permute-start | bytes 344072 | tf_op jit(solution)/shard_map/ppermute | solution.py:292
  171.4 4.3 %collective-permute-start.19 = (bf16[256,896]{1,0:T(8,128)(2,1)S(1)}, bf16[256,896]{1,0:T(8,128)(2,1)S(1)}, u32[]{:S(2)}, u32[]{:S(2)}) collective-permute-start(bf16[256,896]{1,0:T(8,128)(2,1)S(1)} %pad_maximum_fusion.1), channel_id=1, source_target_pairs={{0,1},{1,0},{2,3},{3,2},{4,5},{5,4},{6,7},{7,6},{8,9},{9,8},{10,11... | collective-permute-start | bytes 1376264 | tf_op jit(solution)/shard_map/ppermute | solution.py:289
  172.2 7.2 %collective-permute-start.16 = (bf16[64,896]{1,0:T(8,128)(2,1)S(1)}, bf16[64,896]{1,0:T(8,128)(2,1)S(1)}, u32[]{:S(2)}, u32[]{:S(2)}) collective-permute-start(bf16[64,896]{1,0:T(8,128)(2,1)S(1)} %get-tuple-element.33), channel_id=1, source_target_pairs={{0,6},{1,7},{2,0},{3,1},{4,2},{5,3},{6,4},{7,5},{8,14},{9,15},{10,... | collective-permute-start | bytes 344072 | tf_op jit(solution)/shard_map/ppermute | solution.py:292
  174.9 11.7 %collective-permute-start.17 = (bf16[64,896]{1,0:T(8,128)(2,1)S(1)}, bf16[64,896]{1,0:T(8,128)(2,1)S(1)}, u32[]{:S(2)}, u32[]{:S(2)}) collective-permute-start(bf16[64,896]{1,0:T(8,128)(2,1)S(1)} %get-tuple-element.34), channel_id=1, source_target_pairs={{0,4},{1,5},{2,6},{3,7},{4,0},{5,1},{6,2},{7,3},{8,12},{9,13},{10,... | collective-permute-start | bytes 344072 | tf_op jit(solution)/shard_map/ppermute | solution.py:292
  175.7 21.6 %copy-start.2 = (f32[4,16]{1,0:T(4,128)S(1)}, f32[4,16]{1,0:T(4,128)}, u32[]{:S(2)}) copy-start(f32[4,16]{1,0:T(4,128)} %coef_ref.3) | copy-start | bytes 772
  175.7 10.9 %collective-permute-start.18 = (bf16[64,896]{1,0:T(8,128)(2,1)S(1)}, bf16[64,896]{1,0:T(8,128)(2,1)S(1)}, u32[]{:S(2)}, u32[]{:S(2)}) collective-permute-start(bf16[64,896]{1,0:T(8,128)(2,1)S(1)} %get-tuple-element.35), channel_id=1, source_target_pairs={{0,2},{1,3},{2,4},{3,5},{4,6},{5,7},{6,0},{7,1},{8,10},{9,11},{10,... | collective-permute-start | bytes 344072 | tf_op jit(solution)/shard_map/ppermute | solution.py:292
  176.4 12.2 %collective-permute-start.20 = (bf16[224,896]{1,0:T(8,128)(2,1)S(1)}, bf16[224,896]{1,0:T(8,128)(2,1)S(1)}, u32[]{:S(2)}, u32[]{:S(2)}) collective-permute-start(bf16[224,896]{1,0:T(8,128)(2,1)S(1)} %get-tuple-element.49), channel_id=1, source_target_pairs={{0,8},{8,0},{16,24},{24,16},{1,9},{9,1},{17,25},{25,17},{2,10},{10... | collective-permute-start | bytes 1204232 | tf_op jit(solution)/shard_map/ppermute | solution.py:286
  177.9 19.4 %collective-permute-start.21 = (bf16[224,896]{1,0:T(8,128)(2,1)S(1)}, bf16[224,896]{1,0:T(8,128)(2,1)S(1)}, u32[]{:S(2)}, u32[]{:S(2)}) collective-permute-start(bf16[224,896]{1,0:T(8,128)(2,1)S(1)} %get-tuple-element.49), channel_id=1, source_target_pairs={{0,16},{8,24},{16,0},{24,8},{1,17},{9,25},{17,1},{25,9},{2,18},{10... | collective-permute-start | bytes 1204232 | tf_op jit(solution)/shard_map/ppermute | solution.py:286
  179.4 18.0 %collective-permute-start.22 = (bf16[224,896]{1,0:T(8,128)(2,1)S(1)}, bf16[224,896]{1,0:T(8,128)(2,1)S(1)}, u32[]{:S(2)}, u32[]{:S(2)}) collective-permute-start(bf16[224,896]{1,0:T(8,128)(2,1)S(1)} %get-tuple-element.49), channel_id=1, source_target_pairs={{0,24},{8,16},{16,8},{24,0},{1,25},{9,17},{17,9},{25,1},{2,26},{10... | collective-permute-start | bytes 1204232 | tf_op jit(solution)/shard_map/ppermute | solution.py:286
Sparse Core Ops, SparseCore 0:
  34.7 37.9 all-gather.2

commit v4 on v1

v4 whole, which is shorter than its diff:
```python
import functools

import jax
import jax.numpy as jnp
from jax import lax
from jax.experimental import pallas as pl
from jax.experimental.pallas import tpu as pltpu
from jax.sharding import PartitionSpec as P

F32 = jnp.float32
BF16 = jnp.bfloat16
VMEM_LIMIT = 48 << 20
STEP = 16


def whole_vmem():
    return pl.BlockSpec(memory_space=pltpu.VMEM)


def in_hbm():
    return pl.BlockSpec(memory_space=pltpu.HBM)


def whole_smem():
    return pl.BlockSpec(memory_space=pltpu.SMEM)


def params():
    return pltpu.CompilerParams(vmem_limit_bytes=VMEM_LIMIT)


def row_parts(depth):
    first = -(-depth // (2 * STEP)) * STEP
    return [(0, first), (first, depth - first)]


def merge_kernel(parts, place_ref, coef_ref, experts_ref, *refs):
    part_refs, held_ref, sems = refs[:-2], refs[-2], refs[-1]
    me = place_ref[0]
    count, _, width = experts_ref.shape
    systems = len(part_refs) // len(parts)
    copies = []
    for h, (lo, size) in enumerate(parts):
        at = pl.ds(lo, size)
        copies.append(
            pltpu.make_async_copy(experts_ref.at[:, at, :], held_ref.at[:, at, :], sems.at[h])
        )
        copies[-1].start()
    scales = [[coef_ref[me ^ k, me * count + e] for e in range(count)] for k in range(systems)]
    for h, (lo, size) in enumerate(parts):
        copies[h].wait()

        @pl.loop(0, size // STEP)
        def _(i):
            at = pl.ds(pl.multiple_of(i * STEP, STEP), STEP)
            source = pl.ds(pl.multiple_of(lo + i * STEP, STEP), STEP)
            for col in range(0, width, 128):
                cols = slice(col, min(col + 128, width))
                loaded = [held_ref[e, source, cols].astype(F32) for e in range(count)]
                for k in range(systems):
                    total = scales[k][0] * loaded[0]
                    for e in range(1, count):
                        total = total + scales[k][e] * loaded[e]
                    ref = part_refs[h * systems + k]
                    ref[at, cols] = total.astype(ref.dtype)


def merge_parts(place, coef, experts, systems, parts):
    _, _, width = experts.shape
    outs = [((size, width), BF16 if k else F32) for _, size in parts for k in range(systems)]
    return pl.pallas_call(
        functools.partial(merge_kernel, parts),
        out_shape=[jax.ShapeDtypeStruct(*out) for out in outs],
        in_specs=[whole_smem(), whole_smem(), in_hbm()],
        out_specs=[whole_vmem()] * len(outs),
        scratch_shapes=[
            pltpu.VMEM(experts.shape, BF16),
            pltpu.SemaphoreType.DMA((len(parts),)),
        ],
        compiler_params=params(),
        name="merge_parts",
    )(place, coef, experts)


def merged_grad_kernel(parts, cols_ref, *refs):
    block_refs, out_refs, sums_ref = refs[: -2 * len(parts) - 1], refs[-2 * len(parts) - 1 : -1], refs[-1]
    own = block_refs[0].shape[0]
    for i, ref in enumerate(block_refs):
        sums_ref[i * own : (i + 1) * own, :] = ref[...]
    for h, (lo, size) in enumerate(parts):
        grad = jnp.dot(cols_ref[lo : lo + size, :], sums_ref[...], preferred_element_type=F32)
        out_refs[2 * h][...] = grad
        out_refs[2 * h + 1][...] = grad.astype(BF16)


def merged_grads(cols, blocks, parts):
    own, width = blocks[0].shape
    outs = [((size, width), kind) for _, size in parts for kind in (F32, BF16)]
    return pl.pallas_call(
        functools.partial(merged_grad_kernel, parts),
        out_shape=[jax.ShapeDtypeStruct(*out) for out in outs],
        in_specs=[whole_vmem()] * (1 + len(blocks)),
        out_specs=[whole_vmem()] * len(outs),
        scratch_shapes=[pltpu.VMEM((own * len(blocks), width), BF16)],
        compiler_params=params(),
        name="merged_grads",
    )(cols, *blocks)


def expert_kernel(parts, masks, place_ref, coef_ref, *refs):
    grad_refs, out_ref, held_ref, sems = refs[:-3], refs[-3], refs[-2], refs[-1]
    me = place_ref[0]
    count, _, width = out_ref.shape
    systems = coef_ref.shape[0]
    copies = []
    for h, (lo, size) in enumerate(parts):
        scales = [
            [coef_ref[me ^ mask, me * count + e] for e in range(count)] for mask in masks[h]
        ]

        @pl.loop(0, size // STEP)
        def _(i):
            at = pl.ds(pl.multiple_of(i * STEP, STEP), STEP)
            to = pl.ds(pl.multiple_of(lo + i * STEP, STEP), STEP)
            for col in range(0, width, 128):
                cols = slice(col, min(col + 128, width))
                grads = [ref[at, cols].astype(F32) for ref in grad_refs[h * systems : (h + 1) * systems]]
                for e in range(count):
                    total = scales[0][e] * grads[0]
                    for k in range(1, systems):
                        total = total + scales[k][e] * grads[k]
                    held_ref[e, to, cols] = total

        at = pl.ds(lo, size)
        copies.append(pltpu.make_async_copy(held_ref.at[:, at, :], out_ref.at[:, at, :], sems.at[h]))
        copies[-1].start()
    for copy in copies:
        copy.wait()


def expert_grads(place, coef, grads, masks, shape, parts):
    return pl.pallas_call(
        functools.partial(expert_kernel, parts, masks),
        out_shape=jax.ShapeDtypeStruct(shape, F32),
        in_specs=[whole_smem(), whole_smem()] + [whole_vmem()] * len(grads),
        out_specs=in_hbm(),
        scratch_shapes=[pltpu.VMEM(shape, F32), pltpu.SemaphoreType.DMA((len(parts),))],
        compiler_params=params(),
        name="expert_grads",
    )(place, coef, *grads)


def prepare_kernel(slots, cols_ref, rows_ref, radial_ref, *refs):
    atom_refs, cot_refs = refs[:slots], refs[slots : 2 * slots]
    atoms_ref, gather_ref, sum_ref, scaled_ref, cot_ref = refs[2 * slots :]
    atoms = atoms_ref.shape[0]
    tile = radial_ref.shape[0]

    @pl.when(pl.program_id(0) == 0)
    def _():
        own = atoms // slots
        for k in range(slots):
            at = slice(k * own, (k + 1) * own)
            atoms_ref[at, :] = atom_refs[k][0]
            cot_ref[at, :] = cot_refs[k][0]

    def hot(index, shape, axis):
        return jnp.where(index == lax.broadcasted_iota(jnp.int32, shape, axis), 1.0, 0.0).astype(BF16)

    gather_ref[:, :atoms] = hot(cols_ref[:, 0:1], (tile, atoms), 1)
    hot_tgt = hot(cols_ref[:, 1:2], (tile, atoms), 1)
    gather_ref[:, atoms:] = hot_tgt
    sum_ref[:atoms, :] = hot(rows_ref[0:1, :], (atoms, tile), 0)
    sum_ref[atoms:, :] = hot(rows_ref[1:2, :], (atoms, tile), 0)
    cot = jnp.dot(hot_tgt, cot_ref[...], preferred_element_type=F32)
    scaled_ref[...] = (cot * radial_ref[...].astype(F32)).astype(BF16)


def prepare(cols, rows, radial, atom_blocks, cot_blocks, tile):
    edges, width = radial.shape
    slots = len(atom_blocks)
    atoms = slots * atom_blocks[0].shape[1]
    by_edge = lambda n: pl.BlockSpec((tile, n), lambda i: (i, 0))
    by_column = lambda n: pl.BlockSpec((n, tile), lambda i: (0, i))
    return pl.pallas_call(
        functools.partial(prepare_kernel, slots),
        grid=(edges // tile,),
        out_shape=[
            jax.ShapeDtypeStruct((atoms, width), BF16),
            jax.ShapeDtypeStruct((edges, 2 * atoms), BF16),
            jax.ShapeDtypeStruct((2 * atoms, edges), BF16),
            jax.ShapeDtypeStruct((edges, width), BF16),
        ],
        in_specs=[by_edge(2), by_column(2), by_edge(width)] + [whole_vmem()] * (2 * slots),
        out_specs=[
            pl.BlockSpec((atoms, width), lambda i: (0, 0)),
            by_edge(2 * atoms),
            by_column(2 * atoms),
            by_edge(width),
        ],
        scratch_shapes=[pltpu.VMEM((atoms, width), BF16)],
        compiler_params=params(),
        cost_estimate=pl.CostEstimate(
            flops=2 * atoms * width * edges, bytes_accessed=14 * edges * width, transcendentals=0
        ),
        name="prepare",
    )(cols, rows, radial, *atom_blocks, *cot_blocks)


def edge_kernel(
    chips, parts, place_ref, gather_ref, sum_ref, radial_ref, scaled_ref, atoms_ref, *refs
):
    blocks = 2 * chips * len(parts)
    block_refs = refs[:blocks]
    kept_refs, sent_refs, weight_out = refs[blocks : blocks + 3], refs[blocks + 3 : blocks + 6], refs[blocks + 6]
    weight_ref, proj_ref, acc_ref, sem = refs[blocks + 7 :]
    step = pl.program_id(0)
    atoms, width_in = atoms_ref.shape
    store = pltpu.make_async_copy(weight_ref, weight_out, sem)

    @pl.when(step == 0)
    def _():
        chip, core = place_ref[1], place_ref[2]
        depth = sum(size for _, size in parts)
        for h, (lo, size) in enumerate(parts):
            for k in range(chips):
                source = lax.rem(chip - k + chips, chips)
                for other in range(2):
                    device = 2 * source + (core if other == 0 else 1 - core)
                    at = pl.ds(pl.multiple_of(device * depth + lo, STEP), size)
                    weight_ref[at, :] = block_refs[(h * chips + k) * 2 + other][...]
        store.start()
        for half in range(2):
            proj_ref[half * atoms : (half + 1) * atoms, :] = jnp.dot(
                atoms_ref[...],
                weight_ref[half * width_in : (half + 1) * width_in, :],
                preferred_element_type=F32,
            ).astype(BF16)
        acc_ref[...] = jnp.zeros_like(acc_ref)

    pre = jnp.dot(gather_ref[...], proj_ref[...], preferred_element_type=F32)
    sigma = 0.5 + 0.5 * jnp.tanh(0.5 * pre)
    silu = pre * sigma
    message = (silu * radial_ref[...].astype(F32)).astype(BF16)
    slope = sigma + silu * (1.0 - sigma)
    pre_grad = (scaled_ref[...].astype(F32) * slope).astype(BF16)
    acc_ref[0] += jnp.dot(sum_ref[:atoms, :], pre_grad, preferred_element_type=F32)
    acc_ref[1] += jnp.dot(sum_ref[atoms:, :], pre_grad, preferred_element_type=F32)
    acc_ref[2] += jnp.dot(sum_ref[atoms:, :], message, preferred_element_type=F32)

    @pl.when(step == pl.num_programs(0) - 1)
    def _():
        half = atoms // 2
        for i in range(3):
            kept_refs[i][...] = acc_ref[i, :half, :]
            sent_refs[i][...] = acc_ref[i, half:, :].astype(BF16)
        store.wait()


def edge_sums(chips, parts, place, gather, sums, radial, scaled, atoms, blocks, tile):
    edges, width = radial.shape
    count, width_in = atoms.shape
    flops = 2 * count * width * (2 * width_in + 5 * edges)
    fixed = lambda *shape: pl.BlockSpec(shape, lambda i: (0,) * len(shape))
    halves = [((count // 2, width), F32)] * 3 + [((count // 2, width), BF16)] * 3
    outs = halves + [((2 * width_in, width), BF16)]
    return pl.pallas_call(
        functools.partial(edge_kernel, chips, parts),
        grid=(edges // tile,),
        out_shape=[jax.ShapeDtypeStruct(shape, kind) for shape, kind in outs],
        in_specs=[
            whole_smem(),
            pl.BlockSpec((tile, 2 * count), lambda i: (i, 0)),
            pl.BlockSpec((2 * count, tile), lambda i: (0, i)),
            pl.BlockSpec((tile, width), lambda i: (i, 0)),
            pl.BlockSpec((tile, width), lambda i: (i, 0)),
            fixed(count, width_in),
        ]
        + [whole_vmem()] * len(blocks),
        out_specs=[fixed(*shape) for shape, _ in halves] + [in_hbm()],
        scratch_shapes=[
            pltpu.VMEM((2 * width_in, width), BF16),
            pltpu.VMEM((2 * count, width), BF16),
            pltpu.VMEM((3, count, width), F32),
            pltpu.SemaphoreType.DMA,
        ],
        compiler_params=params(),
        cost_estimate=pl.CostEstimate(
            flops=flops,
            bytes_accessed=4 * edges * width + 8 * edges * count,
            transcendentals=edges * width,
        ),
        name="edge_sums",
    )(place, gather, sums, radial, scaled, atoms, *blocks)


def after(x, *others):
    return lax.optimization_barrier((x, *others))[0]


def shards(systems, ways, atoms, cotangent, experts, radial, coef, source, target):
    chips = ways // 2
    me_sys = lax.axis_index("sys")
    me_edge = lax.axis_index("edge")
    chip, core = me_edge // 2, me_edge % 2
    place = jnp.stack([me_sys, chip, core]).astype(jnp.int32)
    _, depth, width = experts.shape
    own = atoms.shape[1]
    tile = min(512, radial.shape[1])
    parts = row_parts(depth)

    def across(x, k):
        return lax.ppermute(x, "sys", [(s, s ^ k) for s in range(systems)])

    def swap(x):
        return lax.ppermute(x, "edge", [(e, e ^ 1) for e in range(ways)])

    def shift(x, k):
        return lax.ppermute(x, "edge", [(e, (e + 2 * k) % ways) for e in range(ways)])

    def gather(x):
        got = [x]
        for _ in range(chips - 1):
            got.append(shift(got[-1], 1))
        return got

    def both_cores(blocks):
        return blocks + [swap(block) for block in blocks]

    def slot(index):
        owner, offset = index // own, index % own
        back = (chip - owner // 2 + chips) % chips
        return ((owner % 2) ^ core) * (chips * own) + back * own + offset

    atom_blocks, cot_blocks = both_cores(gather(atoms)), both_cores(gather(cotangent))
    ends = jnp.stack([slot(source[0]), slot(target[0])])
    all_atoms, hot_gather, hot_sum, scaled = prepare(
        ends.T, ends, radial[0], atom_blocks, cot_blocks, tile
    )
    own_cols = lax.dynamic_slice_in_dim(all_atoms, (me_edge % chips) * depth, depth, 1).T

    merged = merge_parts(place, coef, experts, systems, parts)
    blocks = []
    for h in range(len(parts)):
        total = merged[h * systems]
        for k in range(1, systems):
            total = total + across(merged[h * systems + k], k).astype(F32)
        for block in gather(total.astype(BF16)):
            blocks += [block, swap(block)]

    *halves, weight = edge_sums(
        chips, parts, place, hot_gather, hot_sum, radial[0], scaled, all_atoms, blocks, tile
    )

    def slots(i):
        kept, other = halves[i], swap(halves[3 + i])
        cut = lambda x, k: x[k * own : (k + 1) * own]
        return [cut(kept, k) + cut(other, k).astype(F32) for k in range(chips)]

    def ring_sum(terms):
        total = terms[1 % chips]
        for t in range(1, chips):
            total = shift(total.astype(BF16), 1).astype(F32) + terms[(t + 1) % chips]
        return total

    sums = [ring_sum(slots(i)).astype(BF16) for i in range(2)]

    def half_for(k):
        return jnp.where((chip + k) % chips < chips // 2, sums[0], sums[1])

    picked = both_cores([half_for(0)] + [shift(half_for(k), k) for k in range(1, chips)])
    grads = merged_grads(own_cols, picked, parts)

    bits = [1 << b for b in range((systems - 1).bit_length())]
    all_grads, all_masks = [], []
    for h, order in enumerate((bits, bits[::-1])):
        held, masks = [grads[2 * h + 1]], [0]
        for bit in order:
            held += [across(x, bit) for x in held]
            masks += [mask ^ bit for mask in masks]
        all_grads += [grads[2 * h]] + held[1:]
        all_masks.append(masks)
    expert_grad = expert_grads(place, coef, all_grads, all_masks, experts.shape, parts)

    node = slots(2)
    total = node[0]
    for k in range(1, chips):
        total = total + shift(after(node[k].astype(BF16), *picked), chips - k).astype(F32)

    over = (((1,), (1,)), ((), ()))
    atom_grad = lax.dot_general(sums[0], weight[:width], over, preferred_element_type=F32)
    atom_grad = atom_grad + lax.dot_general(
        sums[1], weight[width:], over, preferred_element_type=F32
    )
    return total.astype(BF16)[None], atom_grad[None], expert_grad


def solution(mesh):
    placed = P("sys", "edge", None)
    return jax.shard_map(
        functools.partial(shards, mesh.shape["sys"], mesh.shape["edge"]),
        mesh=mesh,
        in_specs=(placed, placed, placed, placed, P(), P("sys", "edge"), P("sys", "edge")),
        out_specs=(placed, placed, placed),
        check_vma=False,
    )
```

time: 179 us -> 192 us (1.073)
  waiting for transfers between devices: 103 us -> 76.2 us
  local copies, waits for them, and re-layouts: 12.8 us -> 31.6 us
  starting transfers between devices: 20.8 us -> 37.9 us
  Pallas kernels: 28.1 us -> 33.1 us
  other arithmetic: 10.8 us -> 8.68 us
    unnamed x22 -> x102, local copies, waits for them, and re-layouts: 5.81 us -> 28.9 us
    ppermute x15 -> x24, waiting for transfers between devices: 79.7 us -> 60 us  [shift(): lax.ppermute(x, 'edge', [(e, (e + 2 * k) % ways) for e in range(ways)])]
    ppermute x15 -> x24, starting transfers between devices: 11.6 us -> 20.4 us  [shift(): lax.ppermute(x, 'edge', [(e, (e + 2 * k) % ways) for e in range(ways)])]
    ppermute x6 -> x12, starting transfers between devices: 8.1 us -> 14.3 us  [across(): return lax.ppermute(x, 'sys', [(s, s ^ k) for s in range(systems)])]
    ppermute x6 -> x12, waiting for transfers between devices: 19.9 us -> 14.7 us  [across(): return lax.ppermute(x, 'sys', [(s, s ^ k) for s in range(systems)])]
    pallas_call x3 -> x5, Pallas kernels: 28.1 us -> 33.1 us  [the longest x1 19.8 us: edge_sums(): pl.pallas_call(functools.partial(edge_kernel, chips, parts), grid=(edges...]
    convert_element_type x8 -> x7, other arithmetic: 9.1 us -> 6.15 us  [the longest x6 6.09 us: ring_sum(): total = shift(total.astype(BF16), 1).astype(F32) + terms[(t + 1) % chips]]
    concatenate x2 -> x0, local copies, waits for them, and re-layouts: 2.84 us -> none  [the longest x1 2.18 us: shards(): features = jnp.concatenate([features, swap(features)], axis=1)]
  transfers between devices with their start and end apart: 28 -> 59, of which waited for: 15 -> 27; matrix products, arithmetic and copies ran while one was open for 11% -> 7% of each run, Pallas kernels for 0% -> 4%
where the time goes in v4:
time: 192 us; the launch traced here: 191 us
  waiting for transfers between devices  76.2 us (40%)
  starting transfers between devices  37.9 us (20%)
  Pallas kernels  33.1 us (17%)
  local copies, waits for them, and re-layouts  31.6 us (16%)
  other arithmetic  8.68 us (5%)
  matrix products  1.92 us (1%)
    ppermute x24, waiting for transfers between devices, shift(): lax.ppermute(x, 'edge', [(e, (e + 2 * k) % ways) for e in range(ways)])  60 us
    unnamed x102, local copies, waits for them, and re-layouts  28.9 us
    ppermute x24, starting transfers between devices, shift(): lax.ppermute(x, 'edge', [(e, (e + 2 * k) % ways) for e in range(ways)])  20.4 us
    pallas_call x1, Pallas kernels, edge_sums(): pl.pallas_call(functools.partial(edge_kernel, chips, parts), grid=(edges...  19.8 us
    ppermute x12, waiting for transfers between devices, across(): return lax.ppermute(x, 'sys', [(s, s ^ k) for s in range(systems)])  14.7 us
    ppermute x12, starting transfers between devices, across(): return lax.ppermute(x, 'sys', [(s, s ^ k) for s in range(systems)])  14.3 us
    pallas_call x1, Pallas kernels, prepare(): pl.pallas_call(functools.partial(prepare_kernel, slots), grid=(edges // t...  8.41 us
    convert_element_type x6, other arithmetic, ring_sum(): total = shift(total.astype(BF16), 1).astype(F32) + terms[(t + 1) % chips]  6.09 us
  transfers between devices with their start and end apart: 59, of which 27 were waited for; matrix products, arithmetic and copies ran while one was open for 7% of the time, Pallas kernels for 4%

profile of v4, /device:TPU:0, one launch (start us, length us, event | category | flops | bytes accessed | tf_op | source)
XLA Modules:
  0.0 190.7 jit_solution(16249554156744319451)
XLA Ops:
  0.8 1.4 copy-done
  2.9 1.7 merge_parts.1
  4.6 3.0 %collective-permute-start.14 = (bf16[112,896]{1,0:T(8,128)(2,1)S(1)}, bf16[112,896]{1,0:T(8,128)(2,1)S(1)}, u32[]{:S(2)}, u32[]{:S(2)}) collective-permute-start(bf16[112,896]{1,0:T(8,128)(2,1)S(1)} %get-tuple-element.34), channel_id=1, source_target_pairs={{0,8},{8,0},{16,24},{24,16},{1,9},{9,1},{17,25},{25,17},{2,10},{10... | collective-permute-start | bytes 602120 | tf_op jit(solution)/shard_map/ppermute | solution.py:313
  7.6 1.5 collective-permute-start.15
  9.2 2.0 %collective-permute-start.7 = (bf16[1,64,896]{2,1,0:T(8,128)(2,1)}, bf16[1,64,896]{2,1,0:T(8,128)(2,1)S(1)}, u32[]{:S(2)}, u32[]{:S(2)}) collective-permute-start(bf16[1,64,896]{2,1,0:T(8,128)(2,1)} %refs_8_.1), channel_id=1, source_target_pairs={{0,2},{1,3},{2,4},{3,5},{4,6},{5,7},{6,0},{7,1},{8,10},{9,11},{10,... | collective-permute-start | bytes 344072 | tf_op jit(solution)/shard_map/ppermute | solution.py:319
  11.2 1.6 collective-permute-start
  13.4 2.1 %collective-permute-start.24 = (bf16[112,896]{1,0:T(8,128)(2,1)S(1)}, bf16[112,896]{1,0:T(8,128)(2,1)S(1)}, u32[]{:S(2)}, u32[]{:S(2)}) collective-permute-start(bf16[112,896]{1,0:T(8,128)(2,1)S(1)} %get-tuple-element.38), channel_id=1, source_target_pairs={{0,8},{8,0},{16,24},{24,16},{1,9},{9,1},{17,25},{25,17},{2,10},{10... | collective-permute-start | bytes 602120 | tf_op jit(solution)/shard_map/ppermute | solution.py:313
  15.5 3.3 %collective-permute-done.15 = bf16[112,896]{1,0:T(8,128)(2,1)S(1)} collective-permute-done((bf16[112,896]{1,0:T(8,128)(2,1)S(1)}, bf16[112,896]{1,0:T(8,128)(2,1)S(1)}, u32[]{:S(2)}, u32[]{:S(2)}) %collective-permute-start.15) | collective-permute-done | bytes 200736 | tf_op jit(solution)/shard_map/ppermute | solution.py:313
  18.7 2.5 %collective-permute-start.25 = (bf16[112,896]{1,0:T(8,128)(2,1)S(1)}, bf16[112,896]{1,0:T(8,128)(2,1)S(1)}, u32[]{:S(2)}, u32[]{:S(2)}) collective-permute-start(bf16[112,896]{1,0:T(8,128)(2,1)S(1)} %get-tuple-element.39), channel_id=1, source_target_pairs={{0,16},{8,24},{16,0},{24,8},{1,17},{9,25},{17,1},{25,9},{2,18},{10... | collective-permute-start | bytes 602120 | tf_op jit(solution)/shard_map/ppermute | solution.py:313
  22.1 2.1 %collective-permute-start.8 = (bf16[1,64,896]{2,1,0:T(8,128)(2,1)S(1)}, bf16[1,64,896]{2,1,0:T(8,128)(2,1)S(1)}, u32[]{:S(2)}, u32[]{:S(2)}) collective-permute-start(bf16[1,64,896]{2,1,0:T(8,128)(2,1)S(1)} %collective-permute-done.7.refs_9_), channel_id=1, source_target_pairs={{0,2},{1,3},{2,4},{3,5},{4,6},{5,7},{6,0},{7,1},{8,10},{9,11},{10,... | collective-permute-start | bytes 344072 | tf_op jit(solution)/shard_map/ppermute | solution.py:319
  24.2 4.3 %collective-permute-done.25 = bf16[112,896]{1,0:T(8,128)(2,1)S(1)} collective-permute-done((bf16[112,896]{1,0:T(8,128)(2,1)S(1)}, bf16[112,896]{1,0:T(8,128)(2,1)S(1)}, u32[]{:S(2)}, u32[]{:S(2)}) %collective-permute-start.25) | collective-permute-done | bytes 200736 | tf_op jit(solution)/shard_map/ppermute | solution.py:313
  28.5 1.4 collective-permute-start.1
  30.7 1.6 collective-permute-start.18
  32.9 1.6 collective-permute-start.28
  34.5 1.8 collective-permute-done.1.refs_2_
  36.9 1.2 collective-permute-start.2
  39.4 7.9 %collective-permute-done.9.refs_11_ = bf16[1,64,896]{2,1,0:T(8,128)(2,1)S(1)} collective-permute-done((bf16[1,64,896]{2,1,0:T(8,128)(2,1)S(1)}, bf16[1,64,896]{2,1,0:T(8,128)(2,1)S(1)}, u32[]{:S(2)}, u32[]{:S(2)}) %collective-permute-start.9) | collective-permute-done | bytes 114720 | tf_op jit(solution)/shard_map/ppermute | solution.py:319
  47.3 2.1 %collective-permute-done.2.refs_3_ = bf16[1,64,896]{2,1,0:T(8,128)(2,1)S(1)} collective-permute-done((bf16[1,64,896]{2,1,0:T(8,128)(2,1)S(1)}, bf16[1,64,896]{2,1,0:T(8,128)(2,1)S(1)}, u32[]{:S(2)}, u32[]{:S(2)}) %collective-permute-start.2) | collective-permute-done | bytes 114720 | tf_op jit(solution)/shard_map/ppermute | solution.py:319
  49.4 1.2 collective-permute-start.30
  55.1 3.8 %collective-permute-done.20.refs_4_ = bf16[112,896]{1,0:T(8,128)(2,1)S(1)} collective-permute-done((bf16[112,896]{1,0:T(8,128)(2,1)S(1)}, bf16[112,896]{1,0:T(8,128)(2,1)S(1)}, u32[]{:S(2)}, u32[]{:S(2)}) %collective-permute-start.20) | collective-permute-done | bytes 200736 | tf_op jit(solution)/shard_map/ppermute | solution.py:319
  59.0 4.0 %collective-permute-done.30.refs_12_ = bf16[112,896]{1,0:T(8,128)(2,1)S(1)} collective-permute-done((bf16[112,896]{1,0:T(8,128)(2,1)S(1)}, bf16[112,896]{1,0:T(8,128)(2,1)S(1)}, u32[]{:S(2)}, u32[]{:S(2)}) %collective-permute-start.30) | collective-permute-done | bytes 200736 | tf_op jit(solution)/shard_map/ppermute | solution.py:319
  65.2 2.1 %collective-permute-done.22.refs_6_ = bf16[112,896]{1,0:T(8,128)(2,1)S(1)} collective-permute-done((bf16[112,896]{1,0:T(8,128)(2,1)S(1)}, bf16[112,896]{1,0:T(8,128)(2,1)S(1)}, u32[]{:S(2)}, u32[]{:S(2)}) %collective-permute-start.22) | collective-permute-done | bytes 200736 | tf_op jit(solution)/shard_map/ppermute | solution.py:319
  67.3 4.3 %collective-permute-done.32.refs_14_ = bf16[112,896]{1,0:T(8,128)(2,1)} collective-permute-done((bf16[112,896]{1,0:T(8,128)(2,1)S(1)}, bf16[112,896]{1,0:T(8,128)(2,1)}, u32[]{:S(2)}, u32[]{:S(2)}) %collective-permute-start.32) | collective-permute-done | bytes 200736 | tf_op jit(solution)/shard_map/ppermute | solution.py:319
  73.8 0.9 copy-done.26
  74.7 0.9 copy-done.28
  75.6 0.9 copy-done.30
  83.7 8.4 %prepare.1 = (bf16[512,896]{1,0:T(8,128)(2,1)S(1)}, bf16[2048,1024]{1,0:T(8,128)(2,1)}, bf16[1024,2048]{1,0:T(8,128)(2,1)}, bf16[2048,896]{1,0:T(8,128)(2,1)}) custom-call(s32[2048,2]{1,0:T(8,128)S(1)} %copy.10.cols_ref, s32[2,2048]{1,0:T(2,128)S(1)} %get-tuple-element.64.rows_ref, bf16[2048,896]{1,0:T(8,128)(2,1)} %bitcast.14, ...), custom_call_target="tpu_custom_call" | custom-call | flops 1879048192 | bytes 25690112 | tf_op jit(solution)/shard_map/prepare/pallas_call | solution.py:185
  92.2 0.9 copy-done.1
  93.1 0.9 copy-done.6
  94.0 0.9 copy-done.8
  95.0 0.9 copy-done.10
  95.9 0.9 copy-done.12
  96.8 0.9 copy-done.14
  97.8 0.9 copy-done.16
  98.7 0.9 copy-done.18
  99.6 19.8 %edge_sums.1 = (f32[256,896]{1,0:T(8,128)S(1)}, f32[256,896]{1,0:T(8,128)}, f32[256,896]{1,0:T(8,128)}, bf16[256,896]{1,0:T(8,128)(2,1)}, bf16[256,896]{1,0:T(8,...) custom-call(s32[3]{0:T(128)S(1)} %pad_add_fusion.1.place_ref, ...), custom_call_target="tpu_custom_call" | custom-call | flops 11039408128 | bytes 15728640 | tf_op jit(solution)/shard_map/edge_sums/pallas_call | solution.py:267
  120.1 1.4 copy.11
  121.8 0.9 add_convert_fusion.12
  122.8 1.2 add_convert_fusion.8
  124.0 6.5 %collective-permute-done.36 = bf16[64,896]{1,0:T(8,128)(2,1)S(1)} collective-permute-done((bf16[64,896]{1,0:T(8,128)(2,1)S(1)}, bf16[64,896]{1,0:T(8,128)(2,1)S(1)}, u32[]{:S(2)}, u32[]{:S(2)}) %collective-permute-start.36) | collective-permute-done | bytes 114720 | tf_op jit(solution)/shard_map/ppermute | solution.py:319
  130.5 0.9 add_convert_fusion.11
  132.4 1.1 add_convert_fusion.7
  133.7 4.9 %collective-permute-done.37 = bf16[64,896]{1,0:T(8,128)(2,1)S(1)} collective-permute-done((bf16[64,896]{1,0:T(8,128)(2,1)S(1)}, bf16[64,896]{1,0:T(8,128)(2,1)S(1)}, u32[]{:S(2)}, u32[]{:S(2)}) %collective-permute-start.37) | collective-permute-done | bytes 114720 | tf_op jit(solution)/shard_map/ppermute | solution.py:319
  138.6 0.9 add_convert_fusion.10
  139.6 1.0 collective-permute-done.41
  140.6 1.1 add_convert_fusion.6
  141.7 1.0 dynamic-slice_bitcast_fusion.cols_ref
  142.7 4.5 %collective-permute-done.38 = bf16[64,896]{1,0:T(8,128)(2,1)S(1)} collective-permute-done((bf16[64,896]{1,0:T(8,128)(2,1)S(1)}, bf16[64,896]{1,0:T(8,128)(2,1)S(1)}, u32[]{:S(2)}, u32[]{:S(2)}) %collective-permute-start.38) | collective-permute-done | bytes 114720 | tf_op jit(solution)/shard_map/ppermute | solution.py:319
  147.2 1.4 collective-permute-done.42
  148.6 1.2 broadcast_select_fusion
  149.9 1.2 collective-permute-start.44
  151.2 2.6 %collective-permute-start.45 = (bf16[64,896]{1,0:T(8,128)(2,1)S(1)}, bf16[64,896]{1,0:T(8,128)(2,1)S(1)}, u32[]{:S(2)}, u32[]{:S(2)}) collective-permute-start(bf16[64,896]{1,0:T(8,128)(2,1)S(1)} %get-tuple-element.55), channel_id=1, source_target_pairs={{0,6},{1,7},{2,0},{3,1},{4,2},{5,3},{6,4},{7,5},{8,14},{9,15},{10,... | collective-permute-start | bytes 344072 | tf_op jit(solution)/shard_map/ppermute | solution.py:319
  153.9 3.9 %collective-permute-done.43.refs_1_ = bf16[64,896]{1,0:T(8,128)(2,1)S(1)} collective-permute-done((bf16[64,896]{1,0:T(8,128)(2,1)S(1)}, bf16[64,896]{1,0:T(8,128)(2,1)S(1)}, u32[]{:S(2)}, u32[]{:S(2)}) %collective-permute-start.43) | collective-permute-done | bytes 114720 | tf_op jit(solution)/shard_map/ppermute | solution.py:319
  157.8 3.1 %collective-permute-done.44.refs_2_ = bf16[64,896]{1,0:T(8,128)(2,1)S(1)} collective-permute-done((bf16[64,896]{1,0:T(8,128)(2,1)S(1)}, bf16[64,896]{1,0:T(8,128)(2,1)S(1)}, u32[]{:S(2)}, u32[]{:S(2)}) %collective-permute-start.44) | collective-permute-done | bytes 114720 | tf_op jit(solution)/shard_map/ppermute | solution.py:319
  163.0 1.3 collective-permute-start.56
  164.3 1.7 collective-permute-start.50
  166.0 1.7 collective-permute-start.51
  167.7 1.3 fusion.7
  170.3 7.3 %collective-permute-done.51 = bf16[64,896]{1,0:T(8,128)(2,1)S(1)} collective-permute-done((bf16[64,896]{1,0:T(8,128)(2,1)S(1)}, bf16[64,896]{1,0:T(8,128)(2,1)S(1)}, u32[]{:S(2)}, u32[]{:S(2)}) %collective-permute-start.51) | collective-permute-done | bytes 114720 | tf_op jit(solution)/shard_map/ppermute | solution.py:319
  177.7 1.6 collective-permute-start.57
  179.3 1.1 collective-permute-start.55
  181.4 4.1 %collective-permute-done.57.refs_6_ = bf16[112,896]{1,0:T(8,128)(2,1)S(1)} collective-permute-done((bf16[112,896]{1,0:T(8,128)(2,1)S(1)}, bf16[112,896]{1,0:T(8,128)(2,1)S(1)}, u32[]{:S(2)}, u32[]{:S(2)}) %collective-permute-start.57) | collective-permute-done | bytes 200736 | tf_op jit(solution)/shard_map/ppermute | solution.py:313
  185.6 2.2 %collective-permute-done.58.refs_7_ = bf16[112,896]{1,0:T(8,128)(2,1)S(1)} collective-permute-done((bf16[112,896]{1,0:T(8,128)(2,1)S(1)}, bf16[112,896]{1,0:T(8,128)(2,1)S(1)}, u32[]{:S(2)}, u32[]{:S(2)}) %collective-permute-start.58) | collective-permute-done | bytes 200736 | tf_op jit(solution)/shard_map/ppermute | solution.py:313
  187.8 2.8 %expert_grads.1 = f32[4,224,896]{2,1,0:T(8,128)} custom-call(s32[3]{0:T(128)S(1)} %pad_add_fusion.1.place_ref, f32[4,16]{1,0:T(4,128)S(1)} %copy-done.4, f32[112,896]{1,0:T(8,128)S(1)} %get-tuple-element.51.refs_0_, bf16[112,896]{1,0:T(8,128)(2,1)S(1)} %collective-permute-done.53.refs_1_, bf16[112,896]{1,0:T(8,128)(2,1)S(1)} %collective-permute-done.54.refs_2_, ...), custom_call_target="tpu_custom_call" | custom-call | tf_op jit(solution)/shard_map/expert_grads/pallas_call | solution.py:142
  (181 shorter events, 29.0 us)
Async XLA Ops:
  0.6 62.4 %copy-start.49 = (s32[1,2048]{1,0:T(1,128)S(1)}, s32[1,2048]{1,0:T(1,128)}, u32[]{:S(2)}) copy-start(s32[1,2048]{1,0:T(1,128)} %param.12) | copy-start | bytes 24580
  0.6 62.4 %copy-start.50 = (s32[1,2048]{1,0:T(1,128)S(1)}, s32[1,2048]{1,0:T(1,128)}, u32[]{:S(2)}) copy-start(s32[1,2048]{1,0:T(1,128)} %param.13) | copy-start | bytes 24580
  2.9 69.2 %copy-start.19 = (bf16[1,64,896]{2,1,0:T(8,128)(2,1)S(1)}, bf16[1,64,896]{2,1,0:T(8,128)(2,1)}, u32[]{:S(2)}) copy-start(bf16[1,64,896]{2,1,0:T(8,128)(2,1)} %refs_0_.1) | copy-start | bytes 344068
  2.9 69.2 %copy-start.20 = (bf16[1,64,896]{2,1,0:T(8,128)(2,1)S(1)}, bf16[1,64,896]{2,1,0:T(8,128)(2,1)}, u32[]{:S(2)}) copy-start(bf16[1,64,896]{2,1,0:T(8,128)(2,1)} %refs_8_.1) | copy-start | bytes 344068
  4.6 8.8 %collective-permute-start.14 = (bf16[112,896]{1,0:T(8,128)(2,1)S(1)}, bf16[112,896]{1,0:T(8,128)(2,1)S(1)}, u32[]{:S(2)}, u32[]{:S(2)}) collective-permute-start(bf16[112,896]{1,0:T(8,128)(2,1)S(1)} %get-tuple-element.34), channel_id=1, source_target_pairs={{0,8},{8,0},{16,24},{24,16},{1,9},{9,1},{17,25},{25,17},{2,10},{10... | collective-permute-start | bytes 602120 | tf_op jit(solution)/shard_map/ppermute | solution.py:313
  7.6 11.1 %collective-permute-start.15 = (bf16[112,896]{1,0:T(8,128)(2,1)S(1)}, bf16[112,896]{1,0:T(8,128)(2,1)S(1)}, u32[]{:S(2)}, u32[]{:S(2)}) collective-permute-start(bf16[112,896]{1,0:T(8,128)(2,1)S(1)} %get-tuple-element.35), channel_id=1, source_target_pairs={{0,16},{8,24},{16,0},{24,8},{1,17},{9,25},{17,1},{25,9},{2,18},{10... | collective-permute-start | bytes 602120 | tf_op jit(solution)/shard_map/ppermute | solution.py:313
  9.1 12.1 %collective-permute-start.16 = (bf16[112,896]{1,0:T(8,128)(2,1)S(1)}, bf16[112,896]{1,0:T(8,128)(2,1)S(1)}, u32[]{:S(2)}, u32[]{:S(2)}) collective-permute-start(bf16[112,896]{1,0:T(8,128)(2,1)S(1)} %get-tuple-element.36), channel_id=1, source_target_pairs={{0,24},{8,16},{16,8},{24,0},{1,25},{9,17},{17,9},{25,1},{2,26},{10... | collective-permute-start | bytes 602120 | tf_op jit(solution)/shard_map/ppermute | solution.py:313
  9.2 12.2 %collective-permute-start.7 = (bf16[1,64,896]{2,1,0:T(8,128)(2,1)}, bf16[1,64,896]{2,1,0:T(8,128)(2,1)S(1)}, u32[]{:S(2)}, u32[]{:S(2)}) collective-permute-start(bf16[1,64,896]{2,1,0:T(8,128)(2,1)} %refs_8_.1), channel_id=1, source_target_pairs={{0,2},{1,3},{2,4},{3,5},{4,6},{5,7},{6,0},{7,1},{8,10},{9,11},{10,... | collective-permute-start | bytes 344072 | tf_op jit(solution)/shard_map/ppermute | solution.py:319
  11.2 10.2 %collective-permute-start = (bf16[1,64,896]{2,1,0:T(8,128)(2,1)}, bf16[1,64,896]{2,1,0:T(8,128)(2,1)S(1)}, u32[]{:S(2)}, u32[]{:S(2)}) collective-permute-start(bf16[1,64,896]{2,1,0:T(8,128)(2,1)} %refs_0_.1), channel_id=1, source_target_pairs={{0,2},{1,3},{2,4},{3,5},{4,6},{5,7},{6,0},{7,1},{8,10},{9,11},{10,... | collective-permute-start | bytes 344072 | tf_op jit(solution)/shard_map/ppermute | solution.py:319
  13.4 8.6 %collective-permute-start.24 = (bf16[112,896]{1,0:T(8,128)(2,1)S(1)}, bf16[112,896]{1,0:T(8,128)(2,1)S(1)}, u32[]{:S(2)}, u32[]{:S(2)}) collective-permute-start(bf16[112,896]{1,0:T(8,128)(2,1)S(1)} %get-tuple-element.38), channel_id=1, source_target_pairs={{0,8},{8,0},{16,24},{24,16},{1,9},{9,1},{17,25},{25,17},{2,10},{10... | collective-permute-start | bytes 602120 | tf_op jit(solution)/shard_map/ppermute | solution.py:313
  18.7 9.7 %collective-permute-start.25 = (bf16[112,896]{1,0:T(8,128)(2,1)S(1)}, bf16[112,896]{1,0:T(8,128)(2,1)S(1)}, u32[]{:S(2)}, u32[]{:S(2)}) collective-permute-start(bf16[112,896]{1,0:T(8,128)(2,1)S(1)} %get-tuple-element.39), channel_id=1, source_target_pairs={{0,16},{8,24},{16,0},{24,8},{1,17},{9,25},{17,1},{25,9},{2,18},{10... | collective-permute-start | bytes 602120 | tf_op jit(solution)/shard_map/ppermute | solution.py:313
  21.2 7.3 %collective-permute-start.26 = (bf16[112,896]{1,0:T(8,128)(2,1)S(1)}, bf16[112,896]{1,0:T(8,128)(2,1)S(1)}, u32[]{:S(2)}, u32[]{:S(2)}) collective-permute-start(bf16[112,896]{1,0:T(8,128)(2,1)S(1)} %get-tuple-element.40), channel_id=1, source_target_pairs={{0,24},{8,16},{16,8},{24,0},{1,25},{9,17},{17,9},{25,1},{2,26},{10... | collective-permute-start | bytes 602120 | tf_op jit(solution)/shard_map/ppermute | solution.py:313
  21.4 8.7 %collective-permute-start.10 = (bf16[1,64,896]{2,1,0:T(8,128)(2,1)}, bf16[1,64,896]{2,1,0:T(8,128)(2,1)S(1)}, u32[]{:S(2)}, u32[]{:S(2)}) collective-permute-start(bf16[1,64,896]{2,1,0:T(8,128)(2,1)} %refs_8_.1), channel_id=1, source_target_pairs={{0,1},{1,0},{2,3},{3,2},{4,5},{5,4},{6,7},{7,6},{8,9},{9,8},{10,11... | collective-permute-start | bytes 344072 | tf_op jit(solution)/shard_map/ppermute | solution.py:316
  21.5 10.8 %collective-permute-start.3 = (bf16[1,64,896]{2,1,0:T(8,128)(2,1)}, bf16[1,64,896]{2,1,0:T(8,128)(2,1)S(1)}, u32[]{:S(2)}, u32[]{:S(2)}) collective-permute-start(bf16[1,64,896]{2,1,0:T(8,128)(2,1)} %refs_0_.1), channel_id=1, source_target_pairs={{0,1},{1,0},{2,3},{3,2},{4,5},{5,4},{6,7},{7,6},{8,9},{9,8},{10,11... | collective-permute-start | bytes 344072 | tf_op jit(solution)/shard_map/ppermute | solution.py:316
  22.1 12.4 %collective-permute-start.8 = (bf16[1,64,896]{2,1,0:T(8,128)(2,1)S(1)}, bf16[1,64,896]{2,1,0:T(8,128)(2,1)S(1)}, u32[]{:S(2)}, u32[]{:S(2)}) collective-permute-start(bf16[1,64,896]{2,1,0:T(8,128)(2,1)S(1)} %collective-permute-done.7.refs_9_), channel_id=1, source_target_pairs={{0,2},{1,3},{2,4},{3,5},{4,6},{5,7},{6,0},{7,1},{8,10},{9,11},{10,... | collective-permute-start | bytes 344072 | tf_op jit(solution)/shard_map/ppermute | solution.py:319
  28.5 7.8 %collective-permute-start.11 = (bf16[1,64,896]{2,1,0:T(8,128)(2,1)S(1)}, bf16[1,64,896]{2,1,0:T(8,128)(2,1)S(1)}, u32[]{:S(2)}, u32[]{:S(2)}) collective-permute-start(bf16[1,64,896]{2,1,0:T(8,128)(2,1)S(1)} %collective-permute-done.7.refs_9_), channel_id=1, source_target_pairs={{0,1},{1,0},{2,3},{3,2},{4,5},{5,4},{6,7},{7,6},{8,9},{9,8},{10,11... | collective-permute-start | bytes 344072 | tf_op jit(solution)/shard_map/ppermute | solution.py:316
  28.5 7.7 %collective-permute-start.1 = (bf16[1,64,896]{2,1,0:T(8,128)(2,1)S(1)}, bf16[1,64,896]{2,1,0:T(8,128)(2,1)S(1)}, u32[]{:S(2)}, u32[]{:S(2)}) collective-permute-start(bf16[1,64,896]{2,1,0:T(8,128)(2,1)S(1)} %collective-permute-done.refs_1_), channel_id=1, source_target_pairs={{0,2},{1,3},{2,4},{3,5},{4,6},{5,7},{6,0},{7,1},{8,10},{9,11},{10,... | collective-permute-start | bytes 344072 | tf_op jit(solution)/shard_map/ppermute | solution.py:319
  30.7 18.7 %collective-permute-start.18 = (bf16[112,896]{1,0:T(8,128)(2,1)S(1)}, bf16[112,896]{1,0:T(8,128)(2,1)S(1)}, u32[]{:S(2)}, u32[]{:S(2)}) collective-permute-start(bf16[112,896]{1,0:T(8,128)(2,1)S(1)} %add_convert_fusion.1.refs_0_), channel_id=1, source_target_pairs={{0,2},{1,3},{2,4},{3,5},{4,6},{5,7},{6,0},{7,1},{8,10},{9,11},{10,... | collective-permute-start | bytes 602120 | tf_op jit(solution)/shard_map/ppermute | solution.py:319
  32.9 16.5 %collective-permute-start.28 = (bf16[112,896]{1,0:T(8,128)(2,1)S(1)}, bf16[112,896]{1,0:T(8,128)(2,1)S(1)}, u32[]{:S(2)}, u32[]{:S(2)}) collective-permute-start(bf16[112,896]{1,0:T(8,128)(2,1)S(1)} %add_convert_fusion.refs_8_), channel_id=1, source_target_pairs={{0,2},{1,3},{2,4},{3,5},{4,6},{5,7},{6,0},{7,1},{8,10},{9,11},{10,... | collective-permute-start | bytes 602120 | tf_op jit(solution)/shard_map/ppermute | solution.py:319
  34.5 3.6 %collective-permute-start.4 = (bf16[1,64,896]{2,1,0:T(8,128)(2,1)S(1)}, bf16[1,64,896]{2,1,0:T(8,128)(2,1)S(1)}, u32[]{:S(2)}, u32[]{:S(2)}) collective-permute-start(bf16[1,64,896]{2,1,0:T(8,128)(2,1)S(1)} %collective-permute-done.refs_1_), channel_id=1, source_target_pairs={{0,1},{1,0},{2,3},{3,2},{4,5},{5,4},{6,7},{7,6},{8,9},{9,8},{10,11... | collective-permute-start | bytes 344072 | tf_op jit(solution)/shard_map/ppermute | solution.py:316
  36.2 11.1 %collective-permute-start.9 = (bf16[1,64,896]{2,1,0:T(8,128)(2,1)S(1)}, bf16[1,64,896]{2,1,0:T(8,128)(2,1)S(1)}, u32[]{:S(2)}, u32[]{:S(2)}) collective-permute-start(bf16[1,64,896]{2,1,0:T(8,128)(2,1)S(1)} %collective-permute-done.8.refs_10_), channel_id=1, source_target_pairs={{0,2},{1,3},{2,4},{3,5},{4,6},{5,7},{6,0},{7,1},{8,10},{9,11},{10,... | collective-permute-start | bytes 344072 | tf_op jit(solution)/shard_map/ppermute | solution.py:319
  36.9 12.5 %collective-permute-start.2 = (bf16[1,64,896]{2,1,0:T(8,128)(2,1)S(1)}, bf16[1,64,896]{2,1,0:T(8,128)(2,1)S(1)}, u32[]{:S(2)}, u32[]{:S(2)}) collective-permute-start(bf16[1,64,896]{2,1,0:T(8,128)(2,1)S(1)} %collective-permute-done.1.refs_2_), channel_id=1, source_target_pairs={{0,2},{1,3},{2,4},{3,5},{4,6},{5,7},{6,0},{7,1},{8,10},{9,11},{10,... | collective-permute-start | bytes 344072 | tf_op jit(solution)/shard_map/ppermute | solution.py:319
  38.7 11.8 %collective-permute-start.12 = (bf16[1,64,896]{2,1,0:T(8,128)(2,1)S(1)}, bf16[1,64,896]{2,1,0:T(8,128)(2,1)S(1)}, u32[]{:S(2)}, u32[]{:S(2)}) collective-permute-start(bf16[1,64,896]{2,1,0:T(8,128)(2,1)S(1)} %collective-permute-done.8.refs_10_), channel_id=1, source_target_pairs={{0,1},{1,0},{2,3},{3,2},{4,5},{5,4},{6,7},{7,6},{8,9},{9,8},{10,11... | collective-permute-start | bytes 344072 | tf_op jit(solution)/shard_map/ppermute | solution.py:316
  47.3 6.7 %collective-permute-start.17 = (bf16[112,896]{1,0:T(8,128)(2,1)S(1)}, bf16[112,896]{1,0:T(8,128)(2,1)S(1)}, u32[]{:S(2)}, u32[]{:S(2)}) collective-permute-start(bf16[112,896]{1,0:T(8,128)(2,1)S(1)} %add_convert_fusion.1.refs_0_), channel_id=1, source_target_pairs={{0,1},{1,0},{2,3},{3,2},{4,5},{5,4},{6,7},{7,6},{8,9},{9,8},{10,11... | collective-permute-start | bytes 602120 | tf_op jit(solution)/shard_map/ppermute | solution.py:316
  49.4 5.6 %collective-permute-start.27 = (bf16[112,896]{1,0:T(8,128)(2,1)S(1)}, bf16[112,896]{1,0:T(8,128)(2,1)S(1)}, u32[]{:S(2)}, u32[]{:S(2)}) collective-permute-start(bf16[112,896]{1,0:T(8,128)(2,1)S(1)} %add_convert_fusion.refs_8_), channel_id=1, source_target_pairs={{0,1},{1,0},{2,3},{3,2},{4,5},{5,4},{6,7},{7,6},{8,9},{9,8},{10,11... | collective-permute-start | bytes 602120 | tf_op jit(solution)/shard_map/ppermute | solution.py:316
  49.4 9.6 %collective-permute-start.20 = (bf16[112,896]{1,0:T(8,128)(2,1)S(1)}, bf16[112,896]{1,0:T(8,128)(2,1)S(1)}, u32[]{:S(2)}, u32[]{:S(2)}) collective-permute-start(bf16[112,896]{1,0:T(8,128)(2,1)S(1)} %collective-permute-done.18.refs_2_), channel_id=1, source_target_pairs={{0,2},{1,3},{2,4},{3,5},{4,6},{5,7},{6,0},{7,1},{8,10},{9,11},{10,... | collective-permute-start | bytes 602120 | tf_op jit(solution)/shard_map/ppermute | solution.py:319
  49.4 42.7 %copy-start.5 = (bf16[112,896]{1,0:T(8,128)(2,1)}, bf16[112,896]{1,0:T(8,128)(2,1)S(1)}, u32[]{:S(2)}) copy-start(bf16[112,896]{1,0:T(8,128)(2,1)S(1)} %collective-permute-done.28.refs_10_) | copy-start | bytes 602116
  49.4 13.6 %collective-permute-start.30 = (bf16[112,896]{1,0:T(8,128)(2,1)S(1)}, bf16[112,896]{1,0:T(8,128)(2,1)S(1)}, u32[]{:S(2)}, u32[]{:S(2)}) collective-permute-start(bf16[112,896]{1,0:T(8,128)(2,1)S(1)} %collective-permute-done.28.refs_10_), channel_id=1, source_target_pairs={{0,2},{1,3},{2,4},{3,5},{4,6},{5,7},{6,0},{7,1},{8,10},{9,11},{10,... | collective-permute-start | bytes 602120 | tf_op jit(solution)/shard_map/ppermute | solution.py:319
  51.2 1.3 collective-permute-start.5
  53.2 10.2 %collective-permute-start.13 = (bf16[1,64,896]{2,1,0:T(8,128)(2,1)S(1)}, bf16[1,64,896]{2,1,0:T(8,128)(2,1)S(1)}, u32[]{:S(2)}, u32[]{:S(2)}) collective-permute-start(bf16[1,64,896]{2,1,0:T(8,128)(2,1)S(1)} %collective-permute-done.9.refs_11_), channel_id=1, source_target_pairs={{0,1},{1,0},{2,3},{3,2},{4,5},{5,4},{6,7},{7,6},{8,9},{9,8},{10,11... | collective-permute-start | bytes 344072 | tf_op jit(solution)/shard_map/ppermute | solution.py:316
  54.0 10.0 %collective-permute-start.6 = (bf16[1,64,896]{2,1,0:T(8,128)(2,1)S(1)}, bf16[1,64,896]{2,1,0:T(8,128)(2,1)S(1)}, u32[]{:S(2)}, u32[]{:S(2)}) collective-permute-start(bf16[1,64,896]{2,1,0:T(8,128)(2,1)S(1)} %collective-permute-done.2.refs_3_), channel_id=1, source_target_pairs={{0,1},{1,0},{2,3},{3,2},{4,5},{5,4},{6,7},{7,6},{8,9},{9,8},{10,11... | collective-permute-start | bytes 344072 | tf_op jit(solution)/shard_map/ppermute | solution.py:316
  55.0 10.2 %collective-permute-start.19 = (bf16[112,896]{1,0:T(8,128)(2,1)S(1)}, bf16[112,896]{1,0:T(8,128)(2,1)S(1)}, u32[]{:S(2)}, u32[]{:S(2)}) collective-permute-start(bf16[112,896]{1,0:T(8,128)(2,1)S(1)} %collective-permute-done.18.refs_2_), channel_id=1, source_target_pairs={{0,1},{1,0},{2,3},{3,2},{4,5},{5,4},{6,7},{7,6},{8,9},{9,8},{10,11... | collective-permute-start | bytes 602120 | tf_op jit(solution)/shard_map/ppermute | solution.py:316
  59.0 8.3 %collective-permute-start.22 = (bf16[112,896]{1,0:T(8,128)(2,1)S(1)}, bf16[112,896]{1,0:T(8,128)(2,1)S(1)}, u32[]{:S(2)}, u32[]{:S(2)}) collective-permute-start(bf16[112,896]{1,0:T(8,128)(2,1)S(1)} %collective-permute-done.20.refs_4_), channel_id=1, source_target_pairs={{0,2},{1,3},{2,4},{3,5},{4,6},{5,7},{6,0},{7,1},{8,10},{9,11},{10,... | collective-permute-start | bytes 602120 | tf_op jit(solution)/shard_map/ppermute | solution.py:319
  63.0 8.6 %collective-permute-start.32 = (bf16[112,896]{1,0:T(8,128)(2,1)S(1)}, bf16[112,896]{1,0:T(8,128)(2,1)}, u32[]{:S(2)}, u32[]{:S(2)}) collective-permute-start(bf16[112,896]{1,0:T(8,128)(2,1)S(1)} %collective-permute-done.30.refs_12_), channel_id=1, source_target_pairs={{0,2},{1,3},{2,4},{3,5},{4,6},{5,7},{6,0},{7,1},{8,10},{9,11},{10,... | collective-permute-start | bytes 602120 | tf_op jit(solution)/shard_map/ppermute | solution.py:319
  64.0 29.1 %collective-permute-start.29 = (bf16[112,896]{1,0:T(8,128)(2,1)S(1)}, bf16[112,896]{1,0:T(8,128)(2,1)}, u32[]{:S(2)}, u32[]{:S(2)}) collective-permute-start(bf16[112,896]{1,0:T(8,128)(2,1)S(1)} %collective-permute-done.28.refs_10_), channel_id=1, source_target_pairs={{0,1},{1,0},{2,3},{3,2},{4,5},{5,4},{6,7},{7,6},{8,9},{9,8},{10,11... | collective-permute-start | bytes 602120 | tf_op jit(solution)/shard_map/ppermute | solution.py:316
  64.6 28.4 %collective-permute-start.21 = (bf16[112,896]{1,0:T(8,128)(2,1)S(1)}, bf16[112,896]{1,0:T(8,128)(2,1)}, u32[]{:S(2)}, u32[]{:S(2)}) collective-permute-start(bf16[112,896]{1,0:T(8,128)(2,1)S(1)} %collective-permute-done.20.refs_4_), channel_id=1, source_target_pairs={{0,1},{1,0},{2,3},{3,2},{4,5},{5,4},{6,7},{7,6},{8,9},{9,8},{10,11... | collective-permute-start | bytes 602120 | tf_op jit(solution)/shard_map/ppermute | solution.py:316
  65.2 27.9 %collective-permute-start.31 = (bf16[112,896]{1,0:T(8,128)(2,1)S(1)}, bf16[112,896]{1,0:T(8,128)(2,1)}, u32[]{:S(2)}, u32[]{:S(2)}) collective-permute-start(bf16[112,896]{1,0:T(8,128)(2,1)S(1)} %collective-permute-done.30.refs_12_), channel_id=1, source_target_pairs={{0,1},{1,0},{2,3},{3,2},{4,5},{5,4},{6,7},{7,6},{8,9},{9,8},{10,11... | collective-permute-start | bytes 602120 | tf_op jit(solution)/shard_map/ppermute | solution.py:316
  67.3 25.8 %collective-permute-start.23 = (bf16[112,896]{1,0:T(8,128)(2,1)S(1)}, bf16[112,896]{1,0:T(8,128)(2,1)}, u32[]{:S(2)}, u32[]{:S(2)}) collective-permute-start(bf16[112,896]{1,0:T(8,128)(2,1)S(1)} %collective-permute-done.22.refs_6_), channel_id=1, source_target_pairs={{0,1},{1,0},{2,3},{3,2},{4,5},{5,4},{6,7},{7,6},{8,9},{9,8},{10,11... | collective-permute-start | bytes 602120 | tf_op jit(solution)/shard_map/ppermute | solution.py:316
  71.6 21.5 %collective-permute-start.33 = (bf16[112,896]{1,0:T(8,128)(2,1)}, bf16[112,896]{1,0:T(8,128)(2,1)}, u32[]{:S(2)}, u32[]{:S(2)}) collective-permute-start(bf16[112,896]{1,0:T(8,128)(2,1)} %collective-permute-done.32.refs_14_), channel_id=1, source_target_pairs={{0,1},{1,0},{2,3},{3,2},{4,5},{5,4},{6,7},{7,6},{8,9},{9,8},{10,11... | collective-permute-start | bytes 602120 | tf_op jit(solution)/shard_map/ppermute | solution.py:316
  119.4 2.4 %collective-permute-start.35 = (bf16[256,896]{1,0:T(8,128)(2,1)}, bf16[256,896]{1,0:T(8,128)(2,1)}, u32[]{:S(2)}, u32[]{:S(2)}) collective-permute-start(bf16[256,896]{1,0:T(8,128)(2,1)} %get-tuple-element.44), channel_id=1, source_target_pairs={{0,1},{1,0},{2,3},{3,2},{4,5},{5,4},{6,7},{7,6},{8,9},{9,8},{10,11... | collective-permute-start | bytes 1376264 | tf_op jit(solution)/shard_map/ppermute | solution.py:316
  120.0 2.8 %collective-permute-start.39 = (bf16[256,896]{1,0:T(8,128)(2,1)S(1)}, bf16[256,896]{1,0:T(8,128)(2,1)}, u32[]{:S(2)}, u32[]{:S(2)}) collective-permute-start(bf16[256,896]{1,0:T(8,128)(2,1)S(1)} %get-tuple-element.46), channel_id=1, source_target_pairs={{0,1},{1,0},{2,3},{3,2},{4,5},{5,4},{6,7},{7,6},{8,9},{9,8},{10,11... | collective-permute-start | bytes 1376264 | tf_op jit(solution)/shard_map/ppermute | solution.py:316
  122.7 7.8 %collective-permute-start.36 = (bf16[64,896]{1,0:T(8,128)(2,1)S(1)}, bf16[64,896]{1,0:T(8,128)(2,1)S(1)}, u32[]{:S(2)}, u32[]{:S(2)}) collective-permute-start(bf16[64,896]{1,0:T(8,128)(2,1)S(1)} %add_convert_fusion.12), channel_id=1, source_target_pairs={{0,2},{1,3},{2,4},{3,5},{4,6},{5,7},{6,0},{7,1},{8,10},{9,11},{10,... | collective-permute-start | bytes 344072 | tf_op jit(solution)/shard_map/ppermute | solution.py:319
  124.0 8.5 %collective-permute-start.40 = (bf16[64,896]{1,0:T(8,128)(2,1)S(1)}, bf16[64,896]{1,0:T(8,128)(2,1)S(1)}, u32[]{:S(2)}, u32[]{:S(2)}) collective-permute-start(bf16[64,896]{1,0:T(8,128)(2,1)S(1)} %add_convert_fusion.8), channel_id=1, source_target_pairs={{0,2},{1,3},{2,4},{3,5},{4,6},{5,7},{6,0},{7,1},{8,10},{9,11},{10,... | collective-permute-start | bytes 344072 | tf_op jit(solution)/shard_map/ppermute | solution.py:319
  131.5 7.1 %collective-permute-start.37 = (bf16[64,896]{1,0:T(8,128)(2,1)S(1)}, bf16[64,896]{1,0:T(8,128)(2,1)S(1)}, u32[]{:S(2)}, u32[]{:S(2)}) collective-permute-start(bf16[64,896]{1,0:T(8,128)(2,1)S(1)} %add_convert_fusion.11), channel_id=1, source_target_pairs={{0,2},{1,3},{2,4},{3,5},{4,6},{5,7},{6,0},{7,1},{8,10},{9,11},{10,... | collective-permute-start | bytes 344072 | tf_op jit(solution)/shard_map/ppermute | solution.py:319
  133.5 7.1 %collective-permute-start.41 = (bf16[64,896]{1,0:T(8,128)(2,1)S(1)}, bf16[64,896]{1,0:T(8,128)(2,1)S(1)}, u32[]{:S(2)}, u32[]{:S(2)}) collective-permute-start(bf16[64,896]{1,0:T(8,128)(2,1)S(1)} %add_convert_fusion.7), channel_id=1, source_target_pairs={{0,2},{1,3},{2,4},{3,5},{4,6},{5,7},{6,0},{7,1},{8,10},{9,11},{10,... | collective-permute-start | bytes 344072 | tf_op jit(solution)/shard_map/ppermute | solution.py:319
  139.5 7.7 %collective-permute-start.38 = (bf16[64,896]{1,0:T(8,128)(2,1)S(1)}, bf16[64,896]{1,0:T(8,128)(2,1)S(1)}, u32[]{:S(2)}, u32[]{:S(2)}) collective-permute-start(bf16[64,896]{1,0:T(8,128)(2,1)S(1)} %add_convert_fusion.10), channel_id=1, source_target_pairs={{0,2},{1,3},{2,4},{3,5},{4,6},{5,7},{6,0},{7,1},{8,10},{9,11},{10,... | collective-permute-start | bytes 344072 | tf_op jit(solution)/shard_map/ppermute | solution.py:319
  141.6 7.0 %collective-permute-start.42 = (bf16[64,896]{1,0:T(8,128)(2,1)S(1)}, bf16[64,896]{1,0:T(8,128)(2,1)S(1)}, u32[]{:S(2)}, u32[]{:S(2)}) collective-permute-start(bf16[64,896]{1,0:T(8,128)(2,1)S(1)} %add_convert_fusion.6), channel_id=1, source_target_pairs={{0,2},{1,3},{2,4},{3,5},{4,6},{5,7},{6,0},{7,1},{8,10},{9,11},{10,... | collective-permute-start | bytes 344072 | tf_op jit(solution)/shard_map/ppermute | solution.py:319
  142.7 11.1 %collective-permute-start.34 = (bf16[256,896]{1,0:T(8,128)(2,1)S(1)}, bf16[256,896]{1,0:T(8,128)(2,1)S(1)}, u32[]{:S(2)}, u32[]{:S(2)}) collective-permute-start(bf16[256,896]{1,0:T(8,128)(2,1)S(1)} %get-tuple-element.42), channel_id=1, source_target_pairs={{0,1},{1,0},{2,3},{3,2},{4,5},{5,4},{6,7},{7,6},{8,9},{9,8},{10,11... | collective-permute-start | bytes 1376264 | tf_op jit(solution)/shard_map/ppermute | solution.py:316
  149.9 8.0 %collective-permute-start.43 = (bf16[64,896]{1,0:T(8,128)(2,1)S(1)}, bf16[64,896]{1,0:T(8,128)(2,1)S(1)}, u32[]{:S(2)}, u32[]{:S(2)}) collective-permute-start(bf16[64,896]{1,0:T(8,128)(2,1)S(1)} %get-tuple-element.62), channel_id=1, source_target_pairs={{0,2},{1,3},{2,4},{3,5},{4,6},{5,7},{6,0},{7,1},{8,10},{9,11},{10,... | collective-permute-start | bytes 344072 | tf_op jit(solution)/shard_map/ppermute | solution.py:319
  149.9 11.1 %collective-permute-start.44 = (bf16[64,896]{1,0:T(8,128)(2,1)S(1)}, bf16[64,896]{1,0:T(8,128)(2,1)S(1)}, u32[]{:S(2)}, u32[]{:S(2)}) collective-permute-start(bf16[64,896]{1,0:T(8,128)(2,1)S(1)} %get-tuple-element.61), channel_id=1, source_target_pairs={{0,4},{1,5},{2,6},{3,7},{4,0},{5,1},{6,2},{7,3},{8,12},{9,13},{10,... | collective-permute-start | bytes 344072 | tf_op jit(solution)/shard_map/ppermute | solution.py:319
  151.2 9.8 %collective-permute-start.45 = (bf16[64,896]{1,0:T(8,128)(2,1)S(1)}, bf16[64,896]{1,0:T(8,128)(2,1)S(1)}, u32[]{:S(2)}, u32[]{:S(2)}) collective-permute-start(bf16[64,896]{1,0:T(8,128)(2,1)S(1)} %get-tuple-element.55), channel_id=1, source_target_pairs={{0,6},{1,7},{2,0},{3,1},{4,2},{5,3},{6,4},{7,5},{8,14},{9,15},{10,... | collective-permute-start | bytes 344072 | tf_op jit(solution)/shard_map/ppermute | solution.py:319
  153.8 8.3 %collective-permute-start.46 = (bf16[64,896]{1,0:T(8,128)(2,1)S(1)}, bf16[64,896]{1,0:T(8,128)(2,1)S(1)}, u32[]{:S(2)}, u32[]{:S(2)}) collective-permute-start(bf16[64,896]{1,0:T(8,128)(2,1)S(1)} %get-tuple-element.63.refs_0_), channel_id=1, source_target_pairs={{0,1},{1,0},{2,3},{3,2},{4,5},{5,4},{6,7},{7,6},{8,9},{9,8},{10,11... | collective-permute-start | bytes 344072 | tf_op jit(solution)/shard_map/ppermute | solution.py:316
  157.8 4.3 %collective-permute-start.47 = (bf16[64,896]{1,0:T(8,128)(2,1)S(1)}, bf16[64,896]{1,0:T(8,128)(2,1)S(1)}, u32[]{:S(2)}, u32[]{:S(2)}) collective-permute-start(bf16[64,896]{1,0:T(8,128)(2,1)S(1)} %collective-permute-done.43.refs_1_), channel_id=1, source_target_pairs={{0,1},{1,0},{2,3},{3,2},{4,5},{5,4},{6,7},{7,6},{8,9},{9,8},{10,11... | collective-permute-start | bytes 344072 | tf_op jit(solution)/shard_map/ppermute | solution.py:316
  161.0 1.3 collective-permute-start.48
  161.0 1.5 collective-permute-start.49
  162.9 16.4 %collective-permute-start.53 = (bf16[112,896]{1,0:T(8,128)(2,1)S(1)}, bf16[112,896]{1,0:T(8,128)(2,1)S(1)}, u32[]{:S(2)}, u32[]{:S(2)}) collective-permute-start(bf16[112,896]{1,0:T(8,128)(2,1)S(1)} %get-tuple-element.52), channel_id=1, source_target_pairs={{0,8},{8,0},{16,24},{24,16},{1,9},{9,1},{17,25},{25,17},{2,10},{10... | collective-permute-start | bytes 602120 | tf_op jit(solution)/shard_map/ppermute | solution.py:313
  163.0 17.4 %collective-permute-start.56 = (bf16[112,896]{1,0:T(8,128)(2,1)S(1)}, bf16[112,896]{1,0:T(8,128)(2,1)S(1)}, u32[]{:S(2)}, u32[]{:S(2)}) collective-permute-start(bf16[112,896]{1,0:T(8,128)(2,1)S(1)} %get-tuple-element.54), channel_id=1, source_target_pairs={{0,16},{8,24},{16,0},{24,8},{1,17},{9,25},{17,1},{25,9},{2,18},{10... | collective-permute-start | bytes 602120 | tf_op jit(solution)/shard_map/ppermute | solution.py:313
  164.3 5.2 %collective-permute-start.50 = (bf16[64,896]{1,0:T(8,128)(2,1)S(1)}, bf16[64,896]{1,0:T(8,128)(2,1)S(1)}, u32[]{:S(2)}, u32[]{:S(2)}) collective-permute-start(bf16[64,896]{1,0:T(8,128)(2,1)S(1)} %get-tuple-element.47), channel_id=1, source_target_pairs={{0,6},{1,7},{2,0},{3,1},{4,2},{5,3},{6,4},{7,5},{8,14},{9,15},{10,... | collective-permute-start | bytes 344072 | tf_op jit(solution)/shard_map/ppermute | solution.py:319
  166.0 11.7 %collective-permute-start.51 = (bf16[64,896]{1,0:T(8,128)(2,1)S(1)}, bf16[64,896]{1,0:T(8,128)(2,1)S(1)}, u32[]{:S(2)}, u32[]{:S(2)}) collective-permute-start(bf16[64,896]{1,0:T(8,128)(2,1)S(1)} %get-tuple-element.48), channel_id=1, source_target_pairs={{0,4},{1,5},{2,6},{3,7},{4,0},{5,1},{6,2},{7,3},{8,12},{9,13},{10,... | collective-permute-start | bytes 344072 | tf_op jit(solution)/shard_map/ppermute | solution.py:319
  167.7 13.1 %collective-permute-start.52 = (bf16[64,896]{1,0:T(8,128)(2,1)S(1)}, bf16[64,896]{1,0:T(8,128)(2,1)S(1)}, u32[]{:S(2)}, u32[]{:S(2)}) collective-permute-start(bf16[64,896]{1,0:T(8,128)(2,1)S(1)} %get-tuple-element.49), channel_id=1, source_target_pairs={{0,2},{1,3},{2,4},{3,5},{4,6},{5,7},{6,0},{7,1},{8,10},{9,11},{10,... | collective-permute-start | bytes 344072 | tf_op jit(solution)/shard_map/ppermute | solution.py:319
  169.5 11.9 %collective-permute-start.54 = (bf16[112,896]{1,0:T(8,128)(2,1)S(1)}, bf16[112,896]{1,0:T(8,128)(2,1)S(1)}, u32[]{:S(2)}, u32[]{:S(2)}) collective-permute-start(bf16[112,896]{1,0:T(8,128)(2,1)S(1)} %get-tuple-element.52), channel_id=1, source_target_pairs={{0,16},{8,24},{16,0},{24,8},{1,17},{9,25},{17,1},{25,9},{2,18},{10... | collective-permute-start | bytes 602120 | tf_op jit(solution)/shard_map/ppermute | solution.py:313
  177.7 7.9 %collective-permute-start.57 = (bf16[112,896]{1,0:T(8,128)(2,1)S(1)}, bf16[112,896]{1,0:T(8,128)(2,1)S(1)}, u32[]{:S(2)}, u32[]{:S(2)}) collective-permute-start(bf16[112,896]{1,0:T(8,128)(2,1)S(1)} %get-tuple-element.54), channel_id=1, source_target_pairs={{0,8},{8,0},{16,24},{24,16},{1,9},{9,1},{17,25},{25,17},{2,10},{10... | collective-permute-start | bytes 602120 | tf_op jit(solution)/shard_map/ppermute | solution.py:313
  179.3 6.3 %collective-permute-start.55 = (bf16[112,896]{1,0:T(8,128)(2,1)S(1)}, bf16[112,896]{1,0:T(8,128)(2,1)S(1)}, u32[]{:S(2)}, u32[]{:S(2)}) collective-permute-start(bf16[112,896]{1,0:T(8,128)(2,1)S(1)} %collective-permute-done.53.refs_1_), channel_id=1, source_target_pairs={{0,16},{8,24},{16,0},{24,8},{1,17},{9,25},{17,1},{25,9},{2,18},{10... | collective-permute-start | bytes 602120 | tf_op jit(solution)/shard_map/ppermute | solution.py:313
  180.4 7.4 %collective-permute-start.58 = (bf16[112,896]{1,0:T(8,128)(2,1)S(1)}, bf16[112,896]{1,0:T(8,128)(2,1)S(1)}, u32[]{:S(2)}, u32[]{:S(2)}) collective-permute-start(bf16[112,896]{1,0:T(8,128)(2,1)S(1)} %collective-permute-done.56.refs_5_), channel_id=1, source_target_pairs={{0,8},{8,0},{16,24},{24,16},{1,9},{9,1},{17,25},{25,17},{2,10},{10... | collective-permute-start | bytes 602120 | tf_op jit(solution)/shard_map/ppermute | solution.py:313
  (46 other events, 361.1 us)

commit v5 on v4

--- a/solution.py
+++ b/solution.py
@@ -34,11 +34,15 @@
     return [(0, first), (first, depth - first)]
 
 
-def merge_kernel(parts, place_ref, coef_ref, experts_ref, *refs):
-    part_refs, held_ref, sems = refs[:-2], refs[-2], refs[-1]
+def merge_kernel(parts, place_ref, coef_ref, experts_ref, atoms_ref, cot_ref, both_ref, *refs):
+    part_refs, held_ref, sems, both_sem = refs[:-3], refs[-3], refs[-2], refs[-1]
     me = place_ref[0]
     count, _, width = experts_ref.shape
     systems = len(part_refs) // len(parts)
+    joins = [
+        pltpu.make_async_copy(ref.at[0], both_ref.at[i], both_sem.at[i])
+        for i, ref in enumerate((atoms_ref, cot_ref))
+    ]
     copies = []
     for h, (lo, size) in enumerate(parts):
         at = pl.ds(lo, size)
@@ -46,6 +50,8 @@
             pltpu.make_async_copy(experts_ref.at[:, at, :], held_ref.at[:, at, :], sems.at[h])
         )
         copies[-1].start()
+    for join in joins:
+        join.start()
     scales = [[coef_ref[me ^ k, me * count + e] for e in range(count)] for k in range(systems)]
     for h, (lo, size) in enumerate(parts):
         copies[h].wait()
@@ -63,23 +69,27 @@
                         total = total + scales[k][e] * loaded[e]
                     ref = part_refs[h * systems + k]
                     ref[at, cols] = total.astype(ref.dtype)
-
-
-def merge_parts(place, coef, experts, systems, parts):
+    for join in joins:
+        join.wait()
+
+
+def merge_parts(place, coef, experts, atoms, cotangent, systems, parts):
     _, _, width = experts.shape
-    outs = [((size, width), BF16 if k else F32) for _, size in parts for k in range(systems)]
+    outs = [((2, *atoms.shape[1:]), BF16)]
+    outs += [((size, width), BF16 if k else F32) for _, size in parts for k in range(systems)]
     return pl.pallas_call(
         functools.partial(merge_kernel, parts),
         out_shape=[jax.ShapeDtypeStruct(*out) for out in outs],
-        in_specs=[whole_smem(), whole_smem(), in_hbm()],
-        out_specs=[whole_vmem()] * len(outs),
+        in_specs=[whole_smem(), whole_smem()] + [in_hbm()] * 3,
+        out_specs=[in_hbm()] + [whole_vmem()] * (len(outs) - 1),
         scratch_shapes=[
             pltpu.VMEM(experts.shape, BF16),
             pltpu.SemaphoreType.DMA((len(parts),)),
+            pltpu.SemaphoreType.DMA((2,)),
         ],
         compiler_params=params(),
         name="merge_parts",
-    )(place, coef, experts)
+    )(place, coef, experts, atoms, cotangent)
 
 
 def merged_grad_kernel(parts, cols_ref, *refs):
@@ -107,7 +117,7 @@
     )(cols, *blocks)
 
 
-def expert_kernel(parts, masks, place_ref, coef_ref, *refs):
+def expert_kernel(parts, place_ref, coef_ref, *refs):
     grad_refs, out_ref, held_ref, sems = refs[:-3], refs[-3], refs[-2], refs[-1]
     me = place_ref[0]
     count, _, width = out_ref.shape
@@ -115,7 +125,7 @@
     copies = []
     for h, (lo, size) in enumerate(parts):
         scales = [
-            [coef_ref[me ^ mask, me * count + e] for e in range(count)] for mask in masks[h]
+            [coef_ref[me ^ k, me * count + e] for e in range(count)] for k in range(systems)
         ]
 
         @pl.loop(0, size // STEP)
@@ -138,9 +148,9 @@
         copy.wait()
 
 
-def expert_grads(place, coef, grads, masks, shape, parts):
-    return pl.pallas_call(
-        functools.partial(expert_kernel, parts, masks),
+def expert_grads(place, coef, grads, shape, parts):
+    return pl.pallas_call(
+        functools.partial(expert_kernel, parts),
         out_shape=jax.ShapeDtypeStruct(shape, F32),
         in_specs=[whole_smem(), whole_smem()] + [whole_vmem()] * len(grads),
         out_specs=in_hbm(),
@@ -150,61 +160,107 @@
     )(place, coef, *grads)
 
 
-def prepare_kernel(slots, cols_ref, rows_ref, radial_ref, *refs):
-    atom_refs, cot_refs = refs[:slots], refs[slots : 2 * slots]
-    atoms_ref, gather_ref, sum_ref, scaled_ref, cot_ref = refs[2 * slots :]
-    atoms = atoms_ref.shape[0]
-    tile = radial_ref.shape[0]
-
-    @pl.when(pl.program_id(0) == 0)
+def hot_kernel(cols_ref, rows_ref, across_ref, down_ref, gather_ref, sum_ref, token_ref):
+    atoms = down_ref.shape[0]
+
+    def hot(same):
+        return jnp.where(same, 1.0, 0.0).astype(BF16)
+
+    for i in range(2):
+        at = slice(i * atoms, (i + 1) * atoms)
+        gather_ref[:, at] = hot(cols_ref[:, i : i + 1] == across_ref[...])
+        sum_ref[at, :] = hot(down_ref[...] == rows_ref[i : i + 1, :])
+    token_ref[...] = jnp.zeros_like(token_ref)
+
+
+def hot_ends(cols, rows, order, tile):
+    edges, atoms = cols.shape[0], order.shape[0]
+    fixed = lambda *shape: pl.BlockSpec(shape, lambda i: (0, 0))
+    return pl.pallas_call(
+        hot_kernel,
+        grid=(edges // tile,),
+        out_shape=[
+            jax.ShapeDtypeStruct((edges, 2 * atoms), BF16),
+            jax.ShapeDtypeStruct((2 * atoms, edges), BF16),
+            jax.ShapeDtypeStruct((8, 128), F32),
+        ],
+        in_specs=[
+            pl.BlockSpec((tile, 2), lambda i: (i, 0)),
+            pl.BlockSpec((2, tile), lambda i: (0, i)),
+            fixed(1, atoms),
+            fixed(atoms, 1),
+        ],
+        out_specs=[
+            pl.BlockSpec((tile, 2 * atoms), lambda i: (i, 0)),
+            pl.BlockSpec((2 * atoms, tile), lambda i: (0, i)),
+            fixed(8, 128),
+        ],
+        compiler_params=params(),
+        cost_estimate=pl.CostEstimate(
+            flops=16 * edges * atoms, bytes_accessed=8 * edges * atoms, transcendentals=0
+        ),
+        name="hot_ends",
+    )(cols, rows, order[None, :], order[:, None])
+
+
+def scale_kernel(slots, gather_ref, radial_ref, *refs):
+    block_refs = refs[:slots]
+    atoms_out, scaled_ref, atoms_ref, cot_ref, sems = refs[slots:]
+    step = pl.program_id(0)
+    own = block_refs[0].shape[1]
+    store = pltpu.make_async_copy(atoms_ref, atoms_out, sems.at[2 * slots])
+
+    @pl.when(step == 0)
     def _():
-        own = atoms // slots
-        for k in range(slots):
-            at = slice(k * own, (k + 1) * own)
-            atoms_ref[at, :] = atom_refs[k][0]
-            cot_ref[at, :] = cot_refs[k][0]
-
-    def hot(index, shape, axis):
-        return jnp.where(index == lax.broadcasted_iota(jnp.int32, shape, axis), 1.0, 0.0).astype(BF16)
-
-    gather_ref[:, :atoms] = hot(cols_ref[:, 0:1], (tile, atoms), 1)
-    hot_tgt = hot(cols_ref[:, 1:2], (tile, atoms), 1)
-    gather_ref[:, atoms:] = hot_tgt
-    sum_ref[:atoms, :] = hot(rows_ref[0:1, :], (atoms, tile), 0)
-    sum_ref[atoms:, :] = hot(rows_ref[1:2, :], (atoms, tile), 0)
-    cot = jnp.dot(hot_tgt, cot_ref[...], preferred_element_type=F32)
+        loads = []
+        for k, ref in enumerate(block_refs):
+            at = pl.ds(k * own, own)
+            for i, to in enumerate((atoms_ref, cot_ref)):
+                loads.append(pltpu.make_async_copy(ref.at[i], to.at[at], sems.at[2 * k + i]))
+                loads[-1].start()
+        for load in loads:
+            load.wait()
+        store.start()
+
+    cot = jnp.dot(gather_ref[...], cot_ref[...], preferred_element_type=F32)
     scaled_ref[...] = (cot * radial_ref[...].astype(F32)).astype(BF16)
 
-
-def prepare(cols, rows, radial, atom_blocks, cot_blocks, tile):
+    @pl.when(step == pl.num_programs(0) - 1)
+    def _():
+        store.wait()
+
+
+def scaled_edges(hot_gather, radial, blocks, tile):
     edges, width = radial.shape
-    slots = len(atom_blocks)
-    atoms = slots * atom_blocks[0].shape[1]
-    by_edge = lambda n: pl.BlockSpec((tile, n), lambda i: (i, 0))
-    by_column = lambda n: pl.BlockSpec((n, tile), lambda i: (0, i))
-    return pl.pallas_call(
-        functools.partial(prepare_kernel, slots),
+    atoms = hot_gather.shape[1] // 2
+    slots = len(blocks)
+    return pl.pallas_call(
+        functools.partial(scale_kernel, slots),
         grid=(edges // tile,),
         out_shape=[
             jax.ShapeDtypeStruct((atoms, width), BF16),
-            jax.ShapeDtypeStruct((edges, 2 * atoms), BF16),
-            jax.ShapeDtypeStruct((2 * atoms, edges), BF16),
             jax.ShapeDtypeStruct((edges, width), BF16),
         ],
-        in_specs=[by_edge(2), by_column(2), by_edge(width)] + [whole_vmem()] * (2 * slots),
+        in_specs=[
+            pl.BlockSpec((tile, atoms), lambda i: (i, 1)),
+            pl.BlockSpec((tile, width), lambda i: (i, 0)),
+        ]
+        + [in_hbm()] * slots,
         out_specs=[
-            pl.BlockSpec((atoms, width), lambda i: (0, 0)),
-            by_edge(2 * atoms),
-            by_column(2 * atoms),
-            by_edge(width),
-        ],
-        scratch_shapes=[pltpu.VMEM((atoms, width), BF16)],
+            in_hbm(),
+            pl.BlockSpec((tile, width), lambda i: (i, 0)),
+        ],
+        scratch_shapes=[
+            pltpu.VMEM((atoms, width), BF16),
+            pltpu.VMEM((atoms, width), BF16),
+            pltpu.SemaphoreType.DMA((2 * slots + 1,)),
+        ],
         compiler_params=params(),
         cost_estimate=pl.CostEstimate(
-            flops=2 * atoms * width * edges, bytes_accessed=14 * edges * width, transcendentals=0
+            flops=2 * atoms * width * edges, bytes_accessed=6 * edges * width, transcendentals=0
         ),
-        name="prepare",
-    )(cols, rows, radial, *atom_blocks, *cot_blocks)
+        name="scaled_edges",
+    )(hot_gather, radial, *blocks)
 
 
 def edge_kernel(
@@ -213,7 +269,7 @@
     blocks = 2 * chips * len(parts)
     block_refs = refs[:blocks]
     kept_refs, sent_refs, weight_out = refs[blocks : blocks + 3], refs[blocks + 3 : blocks + 6], refs[blocks + 6]
-    weight_ref, proj_ref, acc_ref, sem = refs[blocks + 7 :]
+    weight_ref, proj_ref, acc_ref, sem, sems = refs[blocks + 7 :]
     step = pl.program_id(0)
     atoms, width_in = atoms_ref.shape
     store = pltpu.make_async_copy(weight_ref, weight_out, sem)
@@ -222,13 +278,20 @@
     def _():
         chip, core = place_ref[1], place_ref[2]
         depth = sum(size for _, size in parts)
+        loads = []
         for h, (lo, size) in enumerate(parts):
             for k in range(chips):
                 source = lax.rem(chip - k + chips, chips)
                 for other in range(2):
                     device = 2 * source + (core if other == 0 else 1 - core)
                     at = pl.ds(pl.multiple_of(device * depth + lo, STEP), size)
-                    weight_ref[at, :] = block_refs[(h * chips + k) * 2 + other][...]
+                    i = (h * chips + k) * 2 + other
+                    loads.append(
+                        pltpu.make_async_copy(block_refs[i], weight_ref.at[at], sems.at[i])
+                    )
+                    loads[-1].start()
+        for load in loads:
+            load.wait()
         store.start()
         for half in range(2):
             proj_ref[half * atoms : (half + 1) * atoms, :] = jnp.dot(
@@ -276,13 +339,14 @@
             pl.BlockSpec((tile, width), lambda i: (i, 0)),
             fixed(count, width_in),
         ]
-        + [whole_vmem()] * len(blocks),
+        + [in_hbm()] * len(blocks),
         out_specs=[fixed(*shape) for shape, _ in halves] + [in_hbm()],
         scratch_shapes=[
             pltpu.VMEM((2 * width_in, width), BF16),
             pltpu.VMEM((2 * count, width), BF16),
             pltpu.VMEM((3, count, width), F32),
             pltpu.SemaphoreType.DMA,
+            pltpu.SemaphoreType.DMA((len(blocks),)),
         ],
         compiler_params=params(),
         cost_estimate=pl.CostEstimate(
@@ -318,35 +382,31 @@
     def shift(x, k):
         return lax.ppermute(x, "edge", [(e, (e + 2 * k) % ways) for e in range(ways)])
 
-    def gather(x):
-        got = [x]
-        for _ in range(chips - 1):
-            got.append(shift(got[-1], 1))
-        return got
-
     def both_cores(blocks):
         return blocks + [swap(block) for block in blocks]
 
-    def slot(index):
-        owner, offset = index // own, index % own
-        back = (chip - owner // 2 + chips) % chips
-        return ((owner % 2) ^ core) * (chips * own) + back * own + offset
-
-    atom_blocks, cot_blocks = both_cores(gather(atoms)), both_cores(gather(cotangent))
-    ends = jnp.stack([slot(source[0]), slot(target[0])])
-    all_atoms, hot_gather, hot_sum, scaled = prepare(
-        ends.T, ends, radial[0], atom_blocks, cot_blocks, tile
-    )
+    merged = merge_parts(place, coef, experts, atoms, cotangent, systems, parts)
+    features, *merged = merged
+    features = both_cores([features] + [shift(features, k) for k in range(1, chips)])
+
+    at = jnp.arange(ways * own, dtype=jnp.int32)
+    side, back, offset = at // (chips * own), at // own % chips, at % own
+    order = (2 * ((chip - back + chips) % chips) + (core ^ side)) * own + offset
+    ends = jnp.concatenate([source, target])
+    hot_gather, hot_sum, hot_token = hot_ends(ends.T, ends, order, tile)
+    all_atoms, scaled = scaled_edges(hot_gather, radial[0], features, tile)
     own_cols = lax.dynamic_slice_in_dim(all_atoms, (me_edge % chips) * depth, depth, 1).T
 
-    merged = merge_parts(place, coef, experts, systems, parts)
     blocks = []
     for h in range(len(parts)):
-        total = merged[h * systems]
+        total = merged[h * systems] + (hot_token[0, 0] if h == 0 else 0.0)
         for k in range(1, systems):
             total = total + across(merged[h * systems + k], k).astype(F32)
-        for block in gather(total.astype(BF16)):
-            blocks += [block, swap(block)]
+        held = total.astype(BF16)
+        for k in range(chips):
+            if k:
+                held = shift(held, 1)
+            blocks += [held, swap(held)]
 
     *halves, weight = edge_sums(
         chips, parts, place, hot_gather, hot_sum, radial[0], scaled, all_atoms, blocks, tile
@@ -371,16 +431,11 @@
     picked = both_cores([half_for(0)] + [shift(half_for(k), k) for k in range(1, chips)])
     grads = merged_grads(own_cols, picked, parts)
 
-    bits = [1 << b for b in range((systems - 1).bit_length())]
-    all_grads, all_masks = [], []
-    for h, order in enumerate((bits, bits[::-1])):
-        held, masks = [grads[2 * h + 1]], [0]
-        for bit in order:
-            held += [across(x, bit) for x in held]
-            masks += [mask ^ bit for mask in masks]
-        all_grads += [grads[2 * h]] + held[1:]
-        all_masks.append(masks)
-    expert_grad = expert_grads(place, coef, all_grads, all_masks, experts.shape, parts)
+    all_grads = []
+    for h in range(len(parts)):
+        send = grads[2 * h + 1]
+        all_grads += [grads[2 * h]] + [across(send, k) for k in range(1, systems)]
+    expert_grad = expert_grads(place, coef, all_grads, experts.shape, parts)
 
     node = slots(2)
     total = node[0]

time: 192 us -> 173 us (0.901)
  local copies, waits for them, and re-layouts: 31.6 us -> 10 us
  Pallas kernels: 33.1 us -> 42.7 us
  starting transfers between devices: 37.9 us -> 32.9 us
  waiting for transfers between devices: 76.2 us -> 72.3 us
  other arithmetic: 8.68 us -> 11.2 us
    unnamed x102 -> x20, local copies, waits for them, and re-layouts: 28.9 us -> 6.85 us
    ppermute x24 -> x21, starting transfers between devices: 20.4 us -> 15.9 us  [shift(): lax.ppermute(x, 'edge', [(e, (e + 2 * k) % ways) for e in range(ways)])]
    pallas_call x1, Pallas kernels: 19.8 us -> 24.2 us  [edge_sums(): pl.pallas_call(functools.partial(edge_kernel, chips, parts), grid=(edges...]
    pallas_call x2 -> x3, Pallas kernels: 11.2 us -> 15.2 us  [the longest x1 9.05 us: scaled_edges(): pl.pallas_call(functools.partial(scale_kernel, slots), grid=(edges // til...]
    ppermute x12, waiting for transfers between devices: 14.7 us -> 11.8 us  [across(): return lax.ppermute(x, 'sys', [(s, s ^ k) for s in range(systems)])]
    ppermute x24 -> x21, waiting for transfers between devices: 60 us -> 60 us  [shift(): lax.ppermute(x, 'edge', [(e, (e + 2 * k) % ways) for e in range(ways)])]
  transfers between devices with their start and end apart: 59 -> 52, of which waited for: 27 -> 23; matrix products, arithmetic and copies ran while one was open for 7% -> 9% of each run, Pallas kernels for 4% -> 7%
where the time goes in v5:
time: 173 us; the launch traced here: 172 us
  waiting for transfers between devices  72.3 us (42%)
  Pallas kernels  42.7 us (25%)
  starting transfers between devices  32.9 us (19%)
  other arithmetic  11.2 us (6%)
  local copies, waits for them, and re-layouts  10 us (6%)
  matrix products  1.92 us (1%)
    ppermute x21, waiting for transfers between devices, shift(): lax.ppermute(x, 'edge', [(e, (e + 2 * k) % ways) for e in range(ways)])  60 us
    pallas_call x1, Pallas kernels, edge_sums(): pl.pallas_call(functools.partial(edge_kernel, chips, parts), grid=(edges...  24.2 us
    ppermute x21, starting transfers between devices, shift(): lax.ppermute(x, 'edge', [(e, (e + 2 * k) % ways) for e in range(ways)])  15.9 us
    ppermute x12, starting transfers between devices, across(): return lax.ppermute(x, 'sys', [(s, s ^ k) for s in range(systems)])  14 us
    ppermute x12, waiting for transfers between devices, across(): return lax.ppermute(x, 'sys', [(s, s ^ k) for s in range(systems)])  11.8 us
    pallas_call x1, Pallas kernels, scaled_edges(): pl.pallas_call(functools.partial(scale_kernel, slots), grid=(edges // til...  9.05 us
    unnamed x20, local copies, waits for them, and re-layouts  6.85 us
    convert_element_type x6, other arithmetic, ring_sum(): total = shift(total.astype(BF16), 1).astype(F32) + terms[(t + 1) % chips]  6.21 us
  transfers between devices with their start and end apart: 52, of which 23 were waited for; matrix products, arithmetic and copies ran while one was open for 9% of the time, Pallas kernels for 7%

profile of v5, /device:TPU:0, one launch (start us, length us, event | category | flops | bytes accessed | tf_op | source)
XLA Modules:
  0.0 172.1 jit_solution(10123408170036735476)
XLA Ops:
  0.7 1.4 copy-done.1
  2.2 0.9 copy-done.4
  3.0 0.9 copy-done.5
  3.9 0.7 copy-done.6
  4.6 2.8 %merge_parts.1 = (bf16[2,64,896]{2,1,0:T(8,128)(2,1)S(1)}, f32[112,896]{1,0:T(8,128)S(1)}, bf16[112,896]{1,0:T(8,128)(2,1)}, bf16[112,896]{1,0:T(8,128)(2,1)}, b...) custom-call(s32[3]{0:T(128)S(1)} %pad_add_fusion.1.place_ref, ...), custom_call_target="tpu_custom_call" | custom-call | tf_op jit(solution)/shard_map/merge_parts/pallas_call | solution.py:80
  7.4 3.1 %collective-permute-start = (bf16[2,64,896]{2,1,0:T(8,128)(2,1)S(1)}, bf16[2,64,896]{2,1,0:T(8,128)(2,1)S(1)}, u32[]{:S(2)}, u32[]{:S(2)}) collective-permute-start(bf16[2,64,896]{2,1,0:T(8,128)(2,1)S(1)} %get-tuple-element.33.refs_0_), channel_id=1, source_target_pairs={{0,2},{1,3},{2,4},{3,5},{4,6},{5,7},{6,0},{7,1},{8,10},{9,11},{10,... | collective-permute-start | bytes 688136 | tf_op jit(solution)/shard_map/ppermute | solution.py:383
  10.5 2.6 %collective-permute-start.1 = (bf16[2,64,896]{2,1,0:T(8,128)(2,1)S(1)}, bf16[2,64,896]{2,1,0:T(8,128)(2,1)S(1)}, u32[]{:S(2)}, u32[]{:S(2)}) collective-permute-start(bf16[2,64,896]{2,1,0:T(8,128)(2,1)S(1)} %get-tuple-element.33.refs_0_), channel_id=1, source_target_pairs={{0,4},{1,5},{2,6},{3,7},{4,0},{5,1},{6,2},{7,3},{8,12},{9,13},{10,... | collective-permute-start | bytes 688136 | tf_op jit(solution)/shard_map/ppermute | solution.py:383
  13.1 1.5 collective-permute-start.7
  14.6 1.5 collective-permute-start.8
  16.6 0.7 pad_add_fusion
  18.0 3.4 %hot_ends.1 = (bf16[2048,1024]{1,0:T(8,128)(2,1)S(1)}, bf16[1024,2048]{1,0:T(8,128)(2,1)}, f32[8,128]{1,0:T(8,128)S(1)}) custom-call(s32[2048,2]{1,0:T(8,128)S(1)} %copy.13.cols_ref, s32[2,2048]{1,0:T(2,128)S(1)} %get-tuple-element.68.rows_ref, s32[1,512]{1,0:T(1,128)S(1)} %fusion.29.across_ref, s32[512,1]{1,0:T(8,128)S(1)} %fusion.23.down_ref), custom_call_target="tpu_custom_call" | custom-call | flops 16777216 | bytes 8388608 | tf_op jit(solution)/shard_map/hot_ends/pallas_call | solution.py:179
  21.3 2.0 %copy-done = bf16[2048,1024]{1,0:T(8,128)(2,1)} copy-done((bf16[2048,1024]{1,0:T(8,128)(2,1)}, bf16[2048,1024]{1,0:T(8,128)(2,1)S(1)}, u32[]{:S(2)}) %copy-start) | copy-done | bytes 4194328
  23.3 0.5 slice.81
  23.9 1.5 collective-permute-start.17
  25.4 1.5 collective-permute-start.18
  27.4 1.9 %add_convert_fusion.1.refs_0_ = bf16[112,896]{1,0:T(8,128)(2,1)S(1)} fusion(bf16[112,896]{1,0:T(8,128)(2,1)} %collective-permute-done.9, bf16[112,896]{1,0:T(8,128)(2,1)} %collective-permute-done.8, bf16[112,896]{1,0:T(8,128)(2,1)} %collective-permute-done.7, f32[112,896]{1,0:T(8,128)S(1)} %get-tuple-element.36, f32[]{:T(128)} %bitcast.5), kind=kLoop, calls=%fused_computation.14 | loop fusion | flops 802816 | bytes 1204228 | tf_op jit(solution)/shard_map/convert_element_type | solution.py:405
  29.2 2.4 %collective-permute-done.17 = bf16[112,896]{1,0:T(8,128)(2,1)S(1)} collective-permute-done((bf16[112,896]{1,0:T(8,128)(2,1)S(1)}, bf16[112,896]{1,0:T(8,128)(2,1)S(1)}, u32[]{:S(2)}, u32[]{:S(2)}) %collective-permute-start.17) | collective-permute-done | bytes 200736 | tf_op jit(solution)/shard_map/ppermute | solution.py:377
  31.6 1.3 collective-permute-start.2
  32.9 2.0 %collective-permute-done.18 = bf16[112,896]{1,0:T(8,128)(2,1)S(1)} collective-permute-done((bf16[112,896]{1,0:T(8,128)(2,1)S(1)}, bf16[112,896]{1,0:T(8,128)(2,1)S(1)}, u32[]{:S(2)}, u32[]{:S(2)}) %collective-permute-start.18) | collective-permute-done | bytes 200736 | tf_op jit(solution)/shard_map/ppermute | solution.py:377
  35.4 0.6 collective-permute-start.21
  36.0 1.6 collective-permute-done.2.refs_3_
  38.1 6.4 %collective-permute-done.11.refs_2_ = bf16[112,896]{1,0:T(8,128)(2,1)S(1)} collective-permute-done((bf16[112,896]{1,0:T(8,128)(2,1)S(1)}, bf16[112,896]{1,0:T(8,128)(2,1)S(1)}, u32[]{:S(2)}, u32[]{:S(2)}) %collective-permute-start.11) | collective-permute-done | bytes 200736 | tf_op jit(solution)/shard_map/ppermute | solution.py:383
  44.6 4.0 %collective-permute-done.21.refs_10_ = bf16[112,896]{1,0:T(8,128)(2,1)S(1)} collective-permute-done((bf16[112,896]{1,0:T(8,128)(2,1)S(1)}, bf16[112,896]{1,0:T(8,128)(2,1)S(1)}, u32[]{:S(2)}, u32[]{:S(2)}) %collective-permute-start.21) | collective-permute-done | bytes 200736 | tf_op jit(solution)/shard_map/ppermute | solution.py:383
  49.2 3.7 %collective-permute-done.13.refs_4_ = bf16[112,896]{1,0:T(8,128)(2,1)S(1)} collective-permute-done((bf16[112,896]{1,0:T(8,128)(2,1)S(1)}, bf16[112,896]{1,0:T(8,128)(2,1)S(1)}, u32[]{:S(2)}, u32[]{:S(2)}) %collective-permute-start.13) | collective-permute-done | bytes 200736 | tf_op jit(solution)/shard_map/ppermute | solution.py:383
  52.9 5.4 %collective-permute-done.23.refs_12_ = bf16[112,896]{1,0:T(8,128)(2,1)S(1)} collective-permute-done((bf16[112,896]{1,0:T(8,128)(2,1)S(1)}, bf16[112,896]{1,0:T(8,128)(2,1)S(1)}, u32[]{:S(2)}, u32[]{:S(2)}) %collective-permute-start.23) | collective-permute-done | bytes 200736 | tf_op jit(solution)/shard_map/ppermute | solution.py:383
  58.9 3.4 %collective-permute-done.15.refs_6_ = bf16[112,896]{1,0:T(8,128)(2,1)S(1)} collective-permute-done((bf16[112,896]{1,0:T(8,128)(2,1)S(1)}, bf16[112,896]{1,0:T(8,128)(2,1)S(1)}, u32[]{:S(2)}, u32[]{:S(2)}) %collective-permute-start.15) | collective-permute-done | bytes 200736 | tf_op jit(solution)/shard_map/ppermute | solution.py:383
  62.3 3.5 %collective-permute-done.25.refs_14_ = bf16[112,896]{1,0:T(8,128)(2,1)S(1)} collective-permute-done((bf16[112,896]{1,0:T(8,128)(2,1)S(1)}, bf16[112,896]{1,0:T(8,128)(2,1)S(1)}, u32[]{:S(2)}, u32[]{:S(2)}) %collective-permute-start.25) | collective-permute-done | bytes 200736 | tf_op jit(solution)/shard_map/ppermute | solution.py:383
  65.8 9.0 %scaled_edges.1 = (bf16[512,896]{1,0:T(8,128)(2,1)S(1)}, bf16[2048,896]{1,0:T(8,128)(2,1)}) custom-call(bf16[2048,1024]{1,0:T(8,128)(2,1)} %copy-done, bf16[2048,896]{1,0:T(8,128)(2,1)} %bitcast.15, bf16[2,64,896]{2,1,0:T(8,128)(2,1)S(1)} %get-tuple-element.33.refs_0_, bf16[2,64,896]{2,1,0:T(8,128)(2,1)S(1)} %collective-permute-done.refs_1_, ...), custom_call_target="tpu_custom_call" | custom-call | flops 1879048192 | bytes 11010048 | tf_op jit(solution)/shard_map/scaled_edges/pallas_call | solution.py:237
  74.9 0.9 copy-done.2
  75.8 24.2 %edge_sums.1 = (f32[256,896]{1,0:T(8,128)S(1)}, f32[256,896]{1,0:T(8,128)}, f32[256,896]{1,0:T(8,128)}, bf16[256,896]{1,0:T(8,128)(2,1)S(1)}, bf16[256,896]{1,0:...) custom-call(s32[3]{0:T(128)S(1)} %pad_add_fusion.1.place_ref, bf16[2048,1024]{1,0:T(8,128)(2,1)} %copy-done, ...), custom_call_target="tpu_custom_call" | custom-call | flops 11039408128 | bytes 15728640 | tf_op jit(solution)/shard_map/edge_sums/pallas_call | solution.py:330
  100.1 0.6 collective-permute-start.28
  100.8 1.3 copy.14
  102.3 1.0 add_convert_fusion.12
  103.4 1.2 add_convert_fusion.8
  105.0 6.1 %collective-permute-done.29 = bf16[64,896]{1,0:T(8,128)(2,1)S(1)} collective-permute-done((bf16[64,896]{1,0:T(8,128)(2,1)S(1)}, bf16[64,896]{1,0:T(8,128)(2,1)S(1)}, u32[]{:S(2)}, u32[]{:S(2)}) %collective-permute-start.29) | collective-permute-done | bytes 114720 | tf_op jit(solution)/shard_map/ppermute | solution.py:383
  111.1 0.9 add_convert_fusion.11
  112.1 0.9 collective-permute-done.33
  113.0 1.1 add_convert_fusion.7
  114.1 5.3 %collective-permute-done.30 = bf16[64,896]{1,0:T(8,128)(2,1)S(1)} collective-permute-done((bf16[64,896]{1,0:T(8,128)(2,1)S(1)}, bf16[64,896]{1,0:T(8,128)(2,1)S(1)}, u32[]{:S(2)}, u32[]{:S(2)}) %collective-permute-start.30) | collective-permute-done | bytes 114720 | tf_op jit(solution)/shard_map/ppermute | solution.py:383
  119.4 0.9 add_convert_fusion.10
  120.4 0.7 collective-permute-done.34
  121.1 1.1 add_convert_fusion.6
  122.3 1.0 dynamic-slice_bitcast_fusion.cols_ref
  123.3 4.7 %collective-permute-done.31 = bf16[64,896]{1,0:T(8,128)(2,1)S(1)} collective-permute-done((bf16[64,896]{1,0:T(8,128)(2,1)S(1)}, bf16[64,896]{1,0:T(8,128)(2,1)S(1)}, u32[]{:S(2)}, u32[]{:S(2)}) %collective-permute-start.31) | collective-permute-done | bytes 114720 | tf_op jit(solution)/shard_map/ppermute | solution.py:383
  128.1 1.4 collective-permute-done.35
  129.5 1.2 broadcast_select_fusion
  130.7 1.2 collective-permute-start.37
  132.0 2.6 %collective-permute-start.38 = (bf16[64,896]{1,0:T(8,128)(2,1)S(1)}, bf16[64,896]{1,0:T(8,128)(2,1)S(1)}, u32[]{:S(2)}, u32[]{:S(2)}) collective-permute-start(bf16[64,896]{1,0:T(8,128)(2,1)S(1)} %get-tuple-element.59), channel_id=1, source_target_pairs={{0,6},{1,7},{2,0},{3,1},{4,2},{5,3},{6,4},{7,5},{8,14},{9,15},{10,... | collective-permute-start | bytes 344072 | tf_op jit(solution)/shard_map/ppermute | solution.py:383
  134.7 3.9 %collective-permute-done.36.refs_1_ = bf16[64,896]{1,0:T(8,128)(2,1)S(1)} collective-permute-done((bf16[64,896]{1,0:T(8,128)(2,1)S(1)}, bf16[64,896]{1,0:T(8,128)(2,1)S(1)}, u32[]{:S(2)}, u32[]{:S(2)}) %collective-permute-start.36) | collective-permute-done | bytes 114720 | tf_op jit(solution)/shard_map/ppermute | solution.py:383
  138.6 3.1 %collective-permute-done.37.refs_2_ = bf16[64,896]{1,0:T(8,128)(2,1)S(1)} collective-permute-done((bf16[64,896]{1,0:T(8,128)(2,1)S(1)}, bf16[64,896]{1,0:T(8,128)(2,1)S(1)}, u32[]{:S(2)}, u32[]{:S(2)}) %collective-permute-start.37) | collective-permute-done | bytes 114720 | tf_op jit(solution)/shard_map/ppermute | solution.py:383
  142.3 0.6 fusion
  144.0 1.6 collective-permute-start.43
  145.6 1.7 collective-permute-start.44
  147.3 1.3 fusion.7
  148.7 1.5 collective-permute-start.47
  150.2 1.7 collective-permute-start.48
  151.9 5.8 %collective-permute-done.44 = bf16[64,896]{1,0:T(8,128)(2,1)S(1)} collective-permute-done((bf16[64,896]{1,0:T(8,128)(2,1)S(1)}, bf16[64,896]{1,0:T(8,128)(2,1)S(1)}, u32[]{:S(2)}, u32[]{:S(2)}) %collective-permute-start.44) | collective-permute-done | bytes 114720 | tf_op jit(solution)/shard_map/ppermute | solution.py:383
  157.7 1.7 collective-permute-start.49
  159.4 1.2 collective-permute-start.50
  160.6 0.6 collective-permute-start.51
  161.2 0.7 fusion.28
  161.9 3.6 %collective-permute-done.49.refs_5_ = bf16[112,896]{1,0:T(8,128)(2,1)S(1)} collective-permute-done((bf16[112,896]{1,0:T(8,128)(2,1)S(1)}, bf16[112,896]{1,0:T(8,128)(2,1)S(1)}, u32[]{:S(2)}, u32[]{:S(2)}) %collective-permute-start.49) | collective-permute-done | bytes 200736 | tf_op jit(solution)/shard_map/ppermute | solution.py:377
  165.6 3.8 %collective-permute-done.50.refs_6_ = bf16[112,896]{1,0:T(8,128)(2,1)S(1)} collective-permute-done((bf16[112,896]{1,0:T(8,128)(2,1)S(1)}, bf16[112,896]{1,0:T(8,128)(2,1)S(1)}, u32[]{:S(2)}, u32[]{:S(2)}) %collective-permute-start.50) | collective-permute-done | bytes 200736 | tf_op jit(solution)/shard_map/ppermute | solution.py:377
  169.3 2.8 %expert_grads.1 = f32[4,224,896]{2,1,0:T(8,128)} custom-call(s32[3]{0:T(128)S(1)} %pad_add_fusion.1.place_ref, f32[4,16]{1,0:T(4,128)S(1)} %copy-done.7, f32[112,896]{1,0:T(8,128)S(1)} %get-tuple-element.55.refs_0_, bf16[112,896]{1,0:T(8,128)(2,1)S(1)} %collective-permute-done.46.refs_1_, bf16[112,896]{1,0:T(8,128)(2,1)S(1)} %collective-permute-done.47.refs_2_, ...), custom_call_target="tpu_custom_call" | custom-call | tf_op jit(solution)/shard_map/expert_grads/pallas_call | solution.py:152
  (88 shorter events, 6.8 us)
Async XLA Ops:
  0.7 1.4 copy-start.1
  2.1 0.9 copy-start.4
  3.0 0.9 copy-start.5
  3.9 0.7 copy-start.6
  7.4 28.0 %collective-permute-start = (bf16[2,64,896]{2,1,0:T(8,128)(2,1)S(1)}, bf16[2,64,896]{2,1,0:T(8,128)(2,1)S(1)}, u32[]{:S(2)}, u32[]{:S(2)}) collective-permute-start(bf16[2,64,896]{2,1,0:T(8,128)(2,1)S(1)} %get-tuple-element.33.refs_0_), channel_id=1, source_target_pairs={{0,2},{1,3},{2,4},{3,5},{4,6},{5,7},{6,0},{7,1},{8,10},{9,11},{10,... | collective-permute-start | bytes 688136 | tf_op jit(solution)/shard_map/ppermute | solution.py:383
  10.5 25.5 %collective-permute-start.1 = (bf16[2,64,896]{2,1,0:T(8,128)(2,1)S(1)}, bf16[2,64,896]{2,1,0:T(8,128)(2,1)S(1)}, u32[]{:S(2)}, u32[]{:S(2)}) collective-permute-start(bf16[2,64,896]{2,1,0:T(8,128)(2,1)S(1)} %get-tuple-element.33.refs_0_), channel_id=1, source_target_pairs={{0,4},{1,5},{2,6},{3,7},{4,0},{5,1},{6,2},{7,3},{8,12},{9,13},{10,... | collective-permute-start | bytes 688136 | tf_op jit(solution)/shard_map/ppermute | solution.py:383
  13.1 10.7 %collective-permute-start.7 = (bf16[112,896]{1,0:T(8,128)(2,1)}, bf16[112,896]{1,0:T(8,128)(2,1)}, u32[]{:S(2)}, u32[]{:S(2)}) collective-permute-start(bf16[112,896]{1,0:T(8,128)(2,1)} %get-tuple-element.38), channel_id=1, source_target_pairs={{0,8},{8,0},{16,24},{24,16},{1,9},{9,1},{17,25},{25,17},{2,10},{10... | collective-permute-start | bytes 602120 | tf_op jit(solution)/shard_map/ppermute | solution.py:377
  14.6 10.8 %collective-permute-start.8 = (bf16[112,896]{1,0:T(8,128)(2,1)}, bf16[112,896]{1,0:T(8,128)(2,1)}, u32[]{:S(2)}, u32[]{:S(2)}) collective-permute-start(bf16[112,896]{1,0:T(8,128)(2,1)} %get-tuple-element.39), channel_id=1, source_target_pairs={{0,16},{8,24},{16,0},{24,8},{1,17},{9,25},{17,1},{25,9},{2,18},{10... | collective-permute-start | bytes 602120 | tf_op jit(solution)/shard_map/ppermute | solution.py:377
  16.1 10.8 %collective-permute-start.9 = (bf16[112,896]{1,0:T(8,128)(2,1)S(1)}, bf16[112,896]{1,0:T(8,128)(2,1)}, u32[]{:S(2)}, u32[]{:S(2)}) collective-permute-start(bf16[112,896]{1,0:T(8,128)(2,1)S(1)} %get-tuple-element.40), channel_id=1, source_target_pairs={{0,24},{8,16},{16,8},{24,0},{1,25},{9,17},{17,9},{25,1},{2,26},{10... | collective-permute-start | bytes 602120 | tf_op jit(solution)/shard_map/ppermute | solution.py:377
  21.3 2.0 %copy-start = (bf16[2048,1024]{1,0:T(8,128)(2,1)}, bf16[2048,1024]{1,0:T(8,128)(2,1)S(1)}, u32[]{:S(2)}) copy-start(bf16[2048,1024]{1,0:T(8,128)(2,1)S(1)} %get-tuple-element.31.gather_ref) | copy-start | bytes 12582916
  23.9 7.7 %collective-permute-start.17 = (bf16[112,896]{1,0:T(8,128)(2,1)S(1)}, bf16[112,896]{1,0:T(8,128)(2,1)S(1)}, u32[]{:S(2)}, u32[]{:S(2)}) collective-permute-start(bf16[112,896]{1,0:T(8,128)(2,1)S(1)} %get-tuple-element.42), channel_id=1, source_target_pairs={{0,8},{8,0},{16,24},{24,16},{1,9},{9,1},{17,25},{25,17},{2,10},{10... | collective-permute-start | bytes 602120 | tf_op jit(solution)/shard_map/ppermute | solution.py:377
  25.4 9.6 %collective-permute-start.18 = (bf16[112,896]{1,0:T(8,128)(2,1)S(1)}, bf16[112,896]{1,0:T(8,128)(2,1)S(1)}, u32[]{:S(2)}, u32[]{:S(2)}) collective-permute-start(bf16[112,896]{1,0:T(8,128)(2,1)S(1)} %get-tuple-element.43), channel_id=1, source_target_pairs={{0,16},{8,24},{16,0},{24,8},{1,17},{9,25},{17,1},{25,9},{2,18},{10... | collective-permute-start | bytes 602120 | tf_op jit(solution)/shard_map/ppermute | solution.py:377
  26.9 8.1 %collective-permute-start.19 = (bf16[112,896]{1,0:T(8,128)(2,1)S(1)}, bf16[112,896]{1,0:T(8,128)(2,1)S(1)}, u32[]{:S(2)}, u32[]{:S(2)}) collective-permute-start(bf16[112,896]{1,0:T(8,128)(2,1)S(1)} %get-tuple-element.44), channel_id=1, source_target_pairs={{0,24},{8,16},{16,8},{24,0},{1,25},{9,17},{17,9},{25,1},{2,26},{10... | collective-permute-start | bytes 602120 | tf_op jit(solution)/shard_map/ppermute | solution.py:377
  31.6 6.0 %collective-permute-start.2 = (bf16[2,64,896]{2,1,0:T(8,128)(2,1)S(1)}, bf16[2,64,896]{2,1,0:T(8,128)(2,1)S(1)}, u32[]{:S(2)}, u32[]{:S(2)}) collective-permute-start(bf16[2,64,896]{2,1,0:T(8,128)(2,1)S(1)} %get-tuple-element.33.refs_0_), channel_id=1, source_target_pairs={{0,6},{1,7},{2,0},{3,1},{4,2},{5,3},{6,4},{7,5},{8,14},{9,15},{10,... | collective-permute-start | bytes 688136 | tf_op jit(solution)/shard_map/ppermute | solution.py:383
  35.0 2.7 %collective-permute-start.3 = (bf16[2,64,896]{2,1,0:T(8,128)(2,1)S(1)}, bf16[2,64,896]{2,1,0:T(8,128)(2,1)S(1)}, u32[]{:S(2)}, u32[]{:S(2)}) collective-permute-start(bf16[2,64,896]{2,1,0:T(8,128)(2,1)S(1)} %get-tuple-element.33.refs_0_), channel_id=1, source_target_pairs={{0,1},{1,0},{2,3},{3,2},{4,5},{5,4},{6,7},{7,6},{8,9},{9,8},{10,11... | collective-permute-start | bytes 688136 | tf_op jit(solution)/shard_map/ppermute | solution.py:380
  35.0 9.6 %collective-permute-start.11 = (bf16[112,896]{1,0:T(8,128)(2,1)S(1)}, bf16[112,896]{1,0:T(8,128)(2,1)S(1)}, u32[]{:S(2)}, u32[]{:S(2)}) collective-permute-start(bf16[112,896]{1,0:T(8,128)(2,1)S(1)} %add_convert_fusion.1.refs_0_), channel_id=1, source_target_pairs={{0,2},{1,3},{2,4},{3,5},{4,6},{5,7},{6,0},{7,1},{8,10},{9,11},{10,... | collective-permute-start | bytes 602120 | tf_op jit(solution)/shard_map/ppermute | solution.py:383
  35.4 13.1 %collective-permute-start.21 = (bf16[112,896]{1,0:T(8,128)(2,1)S(1)}, bf16[112,896]{1,0:T(8,128)(2,1)S(1)}, u32[]{:S(2)}, u32[]{:S(2)}) collective-permute-start(bf16[112,896]{1,0:T(8,128)(2,1)S(1)} %add_convert_fusion.refs_8_), channel_id=1, source_target_pairs={{0,2},{1,3},{2,4},{3,5},{4,6},{5,7},{6,0},{7,1},{8,10},{9,11},{10,... | collective-permute-start | bytes 602120 | tf_op jit(solution)/shard_map/ppermute | solution.py:383
  36.0 12.6 %collective-permute-start.10 = (bf16[112,896]{1,0:T(8,128)(2,1)S(1)}, bf16[112,896]{1,0:T(8,128)(2,1)S(1)}, u32[]{:S(2)}, u32[]{:S(2)}) collective-permute-start(bf16[112,896]{1,0:T(8,128)(2,1)S(1)} %add_convert_fusion.1.refs_0_), channel_id=1, source_target_pairs={{0,1},{1,0},{2,3},{3,2},{4,5},{5,4},{6,7},{7,6},{8,9},{9,8},{10,11... | collective-permute-start | bytes 602120 | tf_op jit(solution)/shard_map/ppermute | solution.py:380
  37.6 11.0 %collective-permute-start.20 = (bf16[112,896]{1,0:T(8,128)(2,1)S(1)}, bf16[112,896]{1,0:T(8,128)(2,1)S(1)}, u32[]{:S(2)}, u32[]{:S(2)}) collective-permute-start(bf16[112,896]{1,0:T(8,128)(2,1)S(1)} %add_convert_fusion.refs_8_), channel_id=1, source_target_pairs={{0,1},{1,0},{2,3},{3,2},{4,5},{5,4},{6,7},{7,6},{8,9},{9,8},{10,11... | collective-permute-start | bytes 602120 | tf_op jit(solution)/shard_map/ppermute | solution.py:380
  37.6 11.5 %collective-permute-start.4 = (bf16[2,64,896]{2,1,0:T(8,128)(2,1)S(1)}, bf16[2,64,896]{2,1,0:T(8,128)(2,1)S(1)}, u32[]{:S(2)}, u32[]{:S(2)}) collective-permute-start(bf16[2,64,896]{2,1,0:T(8,128)(2,1)S(1)} %collective-permute-done.refs_1_), channel_id=1, source_target_pairs={{0,1},{1,0},{2,3},{3,2},{4,5},{5,4},{6,7},{7,6},{8,9},{9,8},{10,11... | collective-permute-start | bytes 688136 | tf_op jit(solution)/shard_map/ppermute | solution.py:380
  44.6 8.3 %collective-permute-start.13 = (bf16[112,896]{1,0:T(8,128)(2,1)S(1)}, bf16[112,896]{1,0:T(8,128)(2,1)S(1)}, u32[]{:S(2)}, u32[]{:S(2)}) collective-permute-start(bf16[112,896]{1,0:T(8,128)(2,1)S(1)} %collective-permute-done.11.refs_2_), channel_id=1, source_target_pairs={{0,2},{1,3},{2,4},{3,5},{4,6},{5,7},{6,0},{7,1},{8,10},{9,11},{10,... | collective-permute-start | bytes 602120 | tf_op jit(solution)/shard_map/ppermute | solution.py:383
  48.6 9.7 %collective-permute-start.23 = (bf16[112,896]{1,0:T(8,128)(2,1)S(1)}, bf16[112,896]{1,0:T(8,128)(2,1)S(1)}, u32[]{:S(2)}, u32[]{:S(2)}) collective-permute-start(bf16[112,896]{1,0:T(8,128)(2,1)S(1)} %collective-permute-done.21.refs_10_), channel_id=1, source_target_pairs={{0,2},{1,3},{2,4},{3,5},{4,6},{5,7},{6,0},{7,1},{8,10},{9,11},{10,... | collective-permute-start | bytes 602120 | tf_op jit(solution)/shard_map/ppermute | solution.py:383
  48.6 9.7 %collective-permute-start.5 = (bf16[2,64,896]{2,1,0:T(8,128)(2,1)S(1)}, bf16[2,64,896]{2,1,0:T(8,128)(2,1)S(1)}, u32[]{:S(2)}, u32[]{:S(2)}) collective-permute-start(bf16[2,64,896]{2,1,0:T(8,128)(2,1)S(1)} %collective-permute-done.1.refs_2_), channel_id=1, source_target_pairs={{0,1},{1,0},{2,3},{3,2},{4,5},{5,4},{6,7},{7,6},{8,9},{9,8},{10,11... | collective-permute-start | bytes 688136 | tf_op jit(solution)/shard_map/ppermute | solution.py:380
  48.6 9.7 %collective-permute-start.6 = (bf16[2,64,896]{2,1,0:T(8,128)(2,1)S(1)}, bf16[2,64,896]{2,1,0:T(8,128)(2,1)S(1)}, u32[]{:S(2)}, u32[]{:S(2)}) collective-permute-start(bf16[2,64,896]{2,1,0:T(8,128)(2,1)S(1)} %collective-permute-done.2.refs_3_), channel_id=1, source_target_pairs={{0,1},{1,0},{2,3},{3,2},{4,5},{5,4},{6,7},{7,6},{8,9},{9,8},{10,11... | collective-permute-start | bytes 688136 | tf_op jit(solution)/shard_map/ppermute | solution.py:380
  49.1 9.7 %collective-permute-start.12 = (bf16[112,896]{1,0:T(8,128)(2,1)S(1)}, bf16[112,896]{1,0:T(8,128)(2,1)S(1)}, u32[]{:S(2)}, u32[]{:S(2)}) collective-permute-start(bf16[112,896]{1,0:T(8,128)(2,1)S(1)} %collective-permute-done.11.refs_2_), channel_id=1, source_target_pairs={{0,1},{1,0},{2,3},{3,2},{4,5},{5,4},{6,7},{7,6},{8,9},{9,8},{10,11... | collective-permute-start | bytes 602120 | tf_op jit(solution)/shard_map/ppermute | solution.py:380
  52.9 9.4 %collective-permute-start.15 = (bf16[112,896]{1,0:T(8,128)(2,1)S(1)}, bf16[112,896]{1,0:T(8,128)(2,1)S(1)}, u32[]{:S(2)}, u32[]{:S(2)}) collective-permute-start(bf16[112,896]{1,0:T(8,128)(2,1)S(1)} %collective-permute-done.13.refs_4_), channel_id=1, source_target_pairs={{0,2},{1,3},{2,4},{3,5},{4,6},{5,7},{6,0},{7,1},{8,10},{9,11},{10,... | collective-permute-start | bytes 602120 | tf_op jit(solution)/shard_map/ppermute | solution.py:383
  58.3 7.5 %collective-permute-start.25 = (bf16[112,896]{1,0:T(8,128)(2,1)S(1)}, bf16[112,896]{1,0:T(8,128)(2,1)S(1)}, u32[]{:S(2)}, u32[]{:S(2)}) collective-permute-start(bf16[112,896]{1,0:T(8,128)(2,1)S(1)} %collective-permute-done.23.refs_12_), channel_id=1, source_target_pairs={{0,2},{1,3},{2,4},{3,5},{4,6},{5,7},{6,0},{7,1},{8,10},{9,11},{10,... | collective-permute-start | bytes 602120 | tf_op jit(solution)/shard_map/ppermute | solution.py:383
  58.3 17.5 %collective-permute-start.22 = (bf16[112,896]{1,0:T(8,128)(2,1)S(1)}, bf16[112,896]{1,0:T(8,128)(2,1)S(1)}, u32[]{:S(2)}, u32[]{:S(2)}) collective-permute-start(bf16[112,896]{1,0:T(8,128)(2,1)S(1)} %collective-permute-done.21.refs_10_), channel_id=1, source_target_pairs={{0,1},{1,0},{2,3},{3,2},{4,5},{5,4},{6,7},{7,6},{8,9},{9,8},{10,11... | collective-permute-start | bytes 602120 | tf_op jit(solution)/shard_map/ppermute | solution.py:380
  58.3 17.5 %collective-permute-start.14 = (bf16[112,896]{1,0:T(8,128)(2,1)S(1)}, bf16[112,896]{1,0:T(8,128)(2,1)S(1)}, u32[]{:S(2)}, u32[]{:S(2)}) collective-permute-start(bf16[112,896]{1,0:T(8,128)(2,1)S(1)} %collective-permute-done.13.refs_4_), channel_id=1, source_target_pairs={{0,1},{1,0},{2,3},{3,2},{4,5},{5,4},{6,7},{7,6},{8,9},{9,8},{10,11... | collective-permute-start | bytes 602120 | tf_op jit(solution)/shard_map/ppermute | solution.py:380
  58.8 17.0 %collective-permute-start.24 = (bf16[112,896]{1,0:T(8,128)(2,1)S(1)}, bf16[112,896]{1,0:T(8,128)(2,1)S(1)}, u32[]{:S(2)}, u32[]{:S(2)}) collective-permute-start(bf16[112,896]{1,0:T(8,128)(2,1)S(1)} %collective-permute-done.23.refs_12_), channel_id=1, source_target_pairs={{0,1},{1,0},{2,3},{3,2},{4,5},{5,4},{6,7},{7,6},{8,9},{9,8},{10,11... | collective-permute-start | bytes 602120 | tf_op jit(solution)/shard_map/ppermute | solution.py:380
  62.3 13.5 %collective-permute-start.16 = (bf16[112,896]{1,0:T(8,128)(2,1)S(1)}, bf16[112,896]{1,0:T(8,128)(2,1)S(1)}, u32[]{:S(2)}, u32[]{:S(2)}) collective-permute-start(bf16[112,896]{1,0:T(8,128)(2,1)S(1)} %collective-permute-done.15.refs_6_), channel_id=1, source_target_pairs={{0,1},{1,0},{2,3},{3,2},{4,5},{5,4},{6,7},{7,6},{8,9},{9,8},{10,11... | collective-permute-start | bytes 602120 | tf_op jit(solution)/shard_map/ppermute | solution.py:380
  65.8 10.0 %collective-permute-start.26 = (bf16[112,896]{1,0:T(8,128)(2,1)S(1)}, bf16[112,896]{1,0:T(8,128)(2,1)S(1)}, u32[]{:S(2)}, u32[]{:S(2)}) collective-permute-start(bf16[112,896]{1,0:T(8,128)(2,1)S(1)} %collective-permute-done.25.refs_14_), channel_id=1, source_target_pairs={{0,1},{1,0},{2,3},{3,2},{4,5},{5,4},{6,7},{7,6},{8,9},{9,8},{10,11... | collective-permute-start | bytes 602120 | tf_op jit(solution)/shard_map/ppermute | solution.py:380
  74.9 0.9 copy-start.2
  75.8 24.9 %copy-start.3 = (bf16[512,896]{1,0:T(8,128)(2,1)S(1)}, bf16[512,896]{1,0:T(8,128)(2,1)}, u32[]{:S(2)}) copy-start(bf16[512,896]{1,0:T(8,128)(2,1)} %copy-done.2) | copy-start | bytes 2752516
  100.1 2.2 %collective-permute-start.28 = (bf16[256,896]{1,0:T(8,128)(2,1)S(1)}, bf16[256,896]{1,0:T(8,128)(2,1)}, u32[]{:S(2)}, u32[]{:S(2)}) collective-permute-start(bf16[256,896]{1,0:T(8,128)(2,1)S(1)} %get-tuple-element.48), channel_id=1, source_target_pairs={{0,1},{1,0},{2,3},{3,2},{4,5},{5,4},{6,7},{7,6},{8,9},{9,8},{10,11... | collective-permute-start | bytes 1376264 | tf_op jit(solution)/shard_map/ppermute | solution.py:380
  100.7 2.7 %collective-permute-start.32 = (bf16[256,896]{1,0:T(8,128)(2,1)S(1)}, bf16[256,896]{1,0:T(8,128)(2,1)}, u32[]{:S(2)}, u32[]{:S(2)}) collective-permute-start(bf16[256,896]{1,0:T(8,128)(2,1)S(1)} %get-tuple-element.50), channel_id=1, source_target_pairs={{0,1},{1,0},{2,3},{3,2},{4,5},{5,4},{6,7},{7,6},{8,9},{9,8},{10,11... | collective-permute-start | bytes 1376264 | tf_op jit(solution)/shard_map/ppermute | solution.py:380
  102.1 32.5 %copy-start.9 = (f32[256,896]{1,0:T(8,128)S(1)}, f32[256,896]{1,0:T(8,128)}, u32[]{:S(2)}) copy-start(f32[256,896]{1,0:T(8,128)} %get-tuple-element.45) | copy-start | bytes 2752516
  103.3 7.8 %collective-permute-start.29 = (bf16[64,896]{1,0:T(8,128)(2,1)S(1)}, bf16[64,896]{1,0:T(8,128)(2,1)S(1)}, u32[]{:S(2)}, u32[]{:S(2)}) collective-permute-start(bf16[64,896]{1,0:T(8,128)(2,1)S(1)} %add_convert_fusion.12), channel_id=1, source_target_pairs={{0,2},{1,3},{2,4},{3,5},{4,6},{5,7},{6,0},{7,1},{8,10},{9,11},{10,... | collective-permute-start | bytes 344072 | tf_op jit(solution)/shard_map/ppermute | solution.py:383
  103.4 38.9 %copy-start.8 = (bf16[1792,896]{1,0:T(8,128)(2,1)S(1)}, bf16[1792,896]{1,0:T(8,128)(2,1)}, u32[]{:S(2)}) copy-start(bf16[1792,896]{1,0:T(8,128)(2,1)} %get-tuple-element.54) | copy-start | bytes 9633796
  104.6 8.4 %collective-permute-start.33 = (bf16[64,896]{1,0:T(8,128)(2,1)S(1)}, bf16[64,896]{1,0:T(8,128)(2,1)S(1)}, u32[]{:S(2)}, u32[]{:S(2)}) collective-permute-start(bf16[64,896]{1,0:T(8,128)(2,1)S(1)} %add_convert_fusion.8), channel_id=1, source_target_pairs={{0,2},{1,3},{2,4},{3,5},{4,6},{5,7},{6,0},{7,1},{8,10},{9,11},{10,... | collective-permute-start | bytes 344072 | tf_op jit(solution)/shard_map/ppermute | solution.py:383
  112.0 7.4 %collective-permute-start.30 = (bf16[64,896]{1,0:T(8,128)(2,1)S(1)}, bf16[64,896]{1,0:T(8,128)(2,1)S(1)}, u32[]{:S(2)}, u32[]{:S(2)}) collective-permute-start(bf16[64,896]{1,0:T(8,128)(2,1)S(1)} %add_convert_fusion.11), channel_id=1, source_target_pairs={{0,2},{1,3},{2,4},{3,5},{4,6},{5,7},{6,0},{7,1},{8,10},{9,11},{10,... | collective-permute-start | bytes 344072 | tf_op jit(solution)/shard_map/ppermute | solution.py:383
  114.0 7.1 %collective-permute-start.34 = (bf16[64,896]{1,0:T(8,128)(2,1)S(1)}, bf16[64,896]{1,0:T(8,128)(2,1)S(1)}, u32[]{:S(2)}, u32[]{:S(2)}) collective-permute-start(bf16[64,896]{1,0:T(8,128)(2,1)S(1)} %add_convert_fusion.7), channel_id=1, source_target_pairs={{0,2},{1,3},{2,4},{3,5},{4,6},{5,7},{6,0},{7,1},{8,10},{9,11},{10,... | collective-permute-start | bytes 344072 | tf_op jit(solution)/shard_map/ppermute | solution.py:383
  120.4 7.7 %collective-permute-start.31 = (bf16[64,896]{1,0:T(8,128)(2,1)S(1)}, bf16[64,896]{1,0:T(8,128)(2,1)S(1)}, u32[]{:S(2)}, u32[]{:S(2)}) collective-permute-start(bf16[64,896]{1,0:T(8,128)(2,1)S(1)} %add_convert_fusion.10), channel_id=1, source_target_pairs={{0,2},{1,3},{2,4},{3,5},{4,6},{5,7},{6,0},{7,1},{8,10},{9,11},{10,... | collective-permute-start | bytes 344072 | tf_op jit(solution)/shard_map/ppermute | solution.py:383
  122.2 7.2 %collective-permute-start.35 = (bf16[64,896]{1,0:T(8,128)(2,1)S(1)}, bf16[64,896]{1,0:T(8,128)(2,1)S(1)}, u32[]{:S(2)}, u32[]{:S(2)}) collective-permute-start(bf16[64,896]{1,0:T(8,128)(2,1)S(1)} %add_convert_fusion.6), channel_id=1, source_target_pairs={{0,2},{1,3},{2,4},{3,5},{4,6},{5,7},{6,0},{7,1},{8,10},{9,11},{10,... | collective-permute-start | bytes 344072 | tf_op jit(solution)/shard_map/ppermute | solution.py:383
  123.2 11.3 %collective-permute-start.27 = (bf16[256,896]{1,0:T(8,128)(2,1)S(1)}, bf16[256,896]{1,0:T(8,128)(2,1)S(1)}, u32[]{:S(2)}, u32[]{:S(2)}) collective-permute-start(bf16[256,896]{1,0:T(8,128)(2,1)S(1)} %get-tuple-element.46), channel_id=1, source_target_pairs={{0,1},{1,0},{2,3},{3,2},{4,5},{5,4},{6,7},{7,6},{8,9},{9,8},{10,11... | collective-permute-start | bytes 1376264 | tf_op jit(solution)/shard_map/ppermute | solution.py:380
  130.7 8.0 %collective-permute-start.36 = (bf16[64,896]{1,0:T(8,128)(2,1)S(1)}, bf16[64,896]{1,0:T(8,128)(2,1)S(1)}, u32[]{:S(2)}, u32[]{:S(2)}) collective-permute-start(bf16[64,896]{1,0:T(8,128)(2,1)S(1)} %get-tuple-element.66), channel_id=1, source_target_pairs={{0,2},{1,3},{2,4},{3,5},{4,6},{5,7},{6,0},{7,1},{8,10},{9,11},{10,... | collective-permute-start | bytes 344072 | tf_op jit(solution)/shard_map/ppermute | solution.py:383
  130.7 11.0 %collective-permute-start.37 = (bf16[64,896]{1,0:T(8,128)(2,1)S(1)}, bf16[64,896]{1,0:T(8,128)(2,1)S(1)}, u32[]{:S(2)}, u32[]{:S(2)}) collective-permute-start(bf16[64,896]{1,0:T(8,128)(2,1)S(1)} %get-tuple-element.65), channel_id=1, source_target_pairs={{0,4},{1,5},{2,6},{3,7},{4,0},{5,1},{6,2},{7,3},{8,12},{9,13},{10,... | collective-permute-start | bytes 344072 | tf_op jit(solution)/shard_map/ppermute | solution.py:383
  132.0 9.8 %collective-permute-start.38 = (bf16[64,896]{1,0:T(8,128)(2,1)S(1)}, bf16[64,896]{1,0:T(8,128)(2,1)S(1)}, u32[]{:S(2)}, u32[]{:S(2)}) collective-permute-start(bf16[64,896]{1,0:T(8,128)(2,1)S(1)} %get-tuple-element.59), channel_id=1, source_target_pairs={{0,6},{1,7},{2,0},{3,1},{4,2},{5,3},{6,4},{7,5},{8,14},{9,15},{10,... | collective-permute-start | bytes 344072 | tf_op jit(solution)/shard_map/ppermute | solution.py:383
  134.6 34.7 %copy-start.7 = (f32[4,16]{1,0:T(4,128)S(1)}, f32[4,16]{1,0:T(4,128)}, u32[]{:S(2)}) copy-start(f32[4,16]{1,0:T(4,128)} %coef_ref.3) | copy-start | bytes 772
  134.7 8.2 %collective-permute-start.39 = (bf16[64,896]{1,0:T(8,128)(2,1)S(1)}, bf16[64,896]{1,0:T(8,128)(2,1)S(1)}, u32[]{:S(2)}, u32[]{:S(2)}) collective-permute-start(bf16[64,896]{1,0:T(8,128)(2,1)S(1)} %get-tuple-element.67.refs_0_), channel_id=1, source_target_pairs={{0,1},{1,0},{2,3},{3,2},{4,5},{5,4},{6,7},{7,6},{8,9},{9,8},{10,11... | collective-permute-start | bytes 344072 | tf_op jit(solution)/shard_map/ppermute | solution.py:380
  138.6 4.2 %collective-permute-start.40 = (bf16[64,896]{1,0:T(8,128)(2,1)S(1)}, bf16[64,896]{1,0:T(8,128)(2,1)S(1)}, u32[]{:S(2)}, u32[]{:S(2)}) collective-permute-start(bf16[64,896]{1,0:T(8,128)(2,1)S(1)} %collective-permute-done.36.refs_1_), channel_id=1, source_target_pairs={{0,1},{1,0},{2,3},{3,2},{4,5},{5,4},{6,7},{7,6},{8,9},{9,8},{10,11... | collective-permute-start | bytes 344072 | tf_op jit(solution)/shard_map/ppermute | solution.py:380
  141.7 1.3 collective-permute-start.41
  141.7 1.5 collective-permute-start.42
  143.7 17.0 %collective-permute-start.46 = (bf16[112,896]{1,0:T(8,128)(2,1)S(1)}, bf16[112,896]{1,0:T(8,128)(2,1)S(1)}, u32[]{:S(2)}, u32[]{:S(2)}) collective-permute-start(bf16[112,896]{1,0:T(8,128)(2,1)S(1)} %get-tuple-element.56), channel_id=1, source_target_pairs={{0,8},{8,0},{16,24},{24,16},{1,9},{9,1},{17,25},{25,17},{2,10},{10... | collective-permute-start | bytes 602120 | tf_op jit(solution)/shard_map/ppermute | solution.py:377
  144.0 6.2 %collective-permute-start.43 = (bf16[64,896]{1,0:T(8,128)(2,1)S(1)}, bf16[64,896]{1,0:T(8,128)(2,1)S(1)}, u32[]{:S(2)}, u32[]{:S(2)}) collective-permute-start(bf16[64,896]{1,0:T(8,128)(2,1)S(1)} %get-tuple-element.51), channel_id=1, source_target_pairs={{0,6},{1,7},{2,0},{3,1},{4,2},{5,3},{6,4},{7,5},{8,14},{9,15},{10,... | collective-permute-start | bytes 344072 | tf_op jit(solution)/shard_map/ppermute | solution.py:383
  145.6 12.1 %collective-permute-start.44 = (bf16[64,896]{1,0:T(8,128)(2,1)S(1)}, bf16[64,896]{1,0:T(8,128)(2,1)S(1)}, u32[]{:S(2)}, u32[]{:S(2)}) collective-permute-start(bf16[64,896]{1,0:T(8,128)(2,1)S(1)} %get-tuple-element.52), channel_id=1, source_target_pairs={{0,4},{1,5},{2,6},{3,7},{4,0},{5,1},{6,2},{7,3},{8,12},{9,13},{10,... | collective-permute-start | bytes 344072 | tf_op jit(solution)/shard_map/ppermute | solution.py:383
  147.3 12.0 %collective-permute-start.45 = (bf16[64,896]{1,0:T(8,128)(2,1)S(1)}, bf16[64,896]{1,0:T(8,128)(2,1)S(1)}, u32[]{:S(2)}, u32[]{:S(2)}) collective-permute-start(bf16[64,896]{1,0:T(8,128)(2,1)S(1)} %get-tuple-element.53), channel_id=1, source_target_pairs={{0,2},{1,3},{2,4},{3,5},{4,6},{5,7},{6,0},{7,1},{8,10},{9,11},{10,... | collective-permute-start | bytes 344072 | tf_op jit(solution)/shard_map/ppermute | solution.py:383
  148.7 13.3 %collective-permute-start.47 = (bf16[112,896]{1,0:T(8,128)(2,1)S(1)}, bf16[112,896]{1,0:T(8,128)(2,1)S(1)}, u32[]{:S(2)}, u32[]{:S(2)}) collective-permute-start(bf16[112,896]{1,0:T(8,128)(2,1)S(1)} %get-tuple-element.56), channel_id=1, source_target_pairs={{0,16},{8,24},{16,0},{24,8},{1,17},{9,25},{17,1},{25,9},{2,18},{10... | collective-permute-start | bytes 602120 | tf_op jit(solution)/shard_map/ppermute | solution.py:377
  150.2 11.7 %collective-permute-start.48 = (bf16[112,896]{1,0:T(8,128)(2,1)S(1)}, bf16[112,896]{1,0:T(8,128)(2,1)S(1)}, u32[]{:S(2)}, u32[]{:S(2)}) collective-permute-start(bf16[112,896]{1,0:T(8,128)(2,1)S(1)} %get-tuple-element.56), channel_id=1, source_target_pairs={{0,24},{8,16},{16,8},{24,0},{1,25},{9,17},{17,9},{25,1},{2,26},{10... | collective-permute-start | bytes 602120 | tf_op jit(solution)/shard_map/ppermute | solution.py:377
  157.7 7.8 %collective-permute-start.49 = (bf16[112,896]{1,0:T(8,128)(2,1)S(1)}, bf16[112,896]{1,0:T(8,128)(2,1)S(1)}, u32[]{:S(2)}, u32[]{:S(2)}) collective-permute-start(bf16[112,896]{1,0:T(8,128)(2,1)S(1)} %get-tuple-element.58), channel_id=1, source_target_pairs={{0,8},{8,0},{16,24},{24,16},{1,9},{9,1},{17,25},{25,17},{2,10},{10... | collective-permute-start | bytes 602120 | tf_op jit(solution)/shard_map/ppermute | solution.py:377
  159.4 10.0 %collective-permute-start.50 = (bf16[112,896]{1,0:T(8,128)(2,1)S(1)}, bf16[112,896]{1,0:T(8,128)(2,1)S(1)}, u32[]{:S(2)}, u32[]{:S(2)}) collective-permute-start(bf16[112,896]{1,0:T(8,128)(2,1)S(1)} %get-tuple-element.58), channel_id=1, source_target_pairs={{0,16},{8,24},{16,0},{24,8},{1,17},{9,25},{17,1},{25,9},{2,18},{10... | collective-permute-start | bytes 602120 | tf_op jit(solution)/shard_map/ppermute | solution.py:377
  160.6 8.7 %collective-permute-start.51 = (bf16[112,896]{1,0:T(8,128)(2,1)S(1)}, bf16[112,896]{1,0:T(8,128)(2,1)S(1)}, u32[]{:S(2)}, u32[]{:S(2)}) collective-permute-start(bf16[112,896]{1,0:T(8,128)(2,1)S(1)} %get-tuple-element.58), channel_id=1, source_target_pairs={{0,24},{8,16},{16,8},{24,0},{1,25},{9,17},{17,9},{25,1},{2,26},{10... | collective-permute-start | bytes 602120 | tf_op jit(solution)/shard_map/ppermute | solution.py:377

commit v6 on v5

v6 whole, which is shorter than its diff:
```python
import functools

import jax
import jax.numpy as jnp
from jax import lax
from jax.experimental import pallas as pl
from jax.experimental.pallas import tpu as pltpu
from jax.sharding import PartitionSpec as P

F32 = jnp.float32
BF16 = jnp.bfloat16
LARGE = 60 << 20
SMALL = 24 << 20
STEP = 16


def whole_vmem():
    return pl.BlockSpec(memory_space=pltpu.VMEM)


def in_hbm():
    return pl.BlockSpec(memory_space=pltpu.HBM)


def whole_smem():
    return pl.BlockSpec(memory_space=pltpu.SMEM)


def params(limit=LARGE):
    return pltpu.CompilerParams(vmem_limit_bytes=limit)


def row_parts(depth):
    first = -(-depth // (2 * STEP)) * STEP
    return [(0, first), (first, depth - first)]


def merge_kernel(lo, pairs, place_ref, coef_ref, experts_ref, *refs):
    systems, count = coef_ref.shape[0], experts_ref.shape[0]
    pair_refs, part_refs = refs[:pairs], refs[-systems - 3 : -3]
    held_ref, sem, pair_sems = refs[-3:]
    me = place_ref[0]
    size, width = part_refs[0].shape
    load = pltpu.make_async_copy(experts_ref.at[:, pl.ds(lo, size), :], held_ref, sem)
    load.start()
    joins = []
    if pairs:
        both_ref = refs[-systems - 4]
        for i, ref in enumerate(pair_refs[:2]):
            joins.append(pltpu.make_async_copy(ref.at[0], both_ref.at[i], pair_sems.at[i]))
            joins[-1].start()
    scales = [[coef_ref[me ^ k, me * count + e] for e in range(count)] for k in range(systems)]
    load.wait()

    @pl.loop(0, size // STEP)
    def _(i):
        at = pl.ds(pl.multiple_of(i * STEP, STEP), STEP)
        for col in range(0, width, 128):
            cols = slice(col, min(col + 128, width))
            loaded = [held_ref[e, at, cols].astype(F32) for e in range(count)]
            for k in range(systems):
                total = scales[k][0] * loaded[0]
                for e in range(1, count):
                    total = total + scales[k][e] * loaded[e]
                part_refs[k][at, cols] = total.astype(part_refs[k].dtype)

    for join in joins:
        join.wait()


def merge_part(place, coef, experts, systems, part, joined=()):
    count, _, width = experts.shape
    lo, size = part
    outs = [((2, *joined[0].shape[1:]), BF16)] if joined else []
    outs += [((size, width), BF16 if k else F32) for k in range(systems)]
    return pl.pallas_call(
        functools.partial(merge_kernel, lo, len(joined)),
        out_shape=[jax.ShapeDtypeStruct(*out) for out in outs],
        in_specs=[whole_smem(), whole_smem()] + [in_hbm()] * (1 + len(joined)),
        out_specs=([in_hbm()] if joined else []) + [whole_vmem()] * systems,
        scratch_shapes=[
            pltpu.VMEM((count, size, width), BF16),
            pltpu.SemaphoreType.DMA,
            pltpu.SemaphoreType.DMA((2,)),
        ],
        compiler_params=params(),
        name="merge_part",
    )(place, coef, experts, *joined)


def merged_grad_kernel(cols_ref, *refs):
    block_refs, grad_ref, sent_ref, sums_ref = refs[:-3], refs[-3], refs[-2], refs[-1]
    own = block_refs[0].shape[0]
    for i, ref in enumerate(block_refs):
        sums_ref[i * own : (i + 1) * own, :] = ref[...]
    grad = jnp.dot(cols_ref[...], sums_ref[...], preferred_element_type=F32)
    grad_ref[...] = grad
    sent_ref[...] = grad.astype(BF16)


def merged_grads(cols, blocks):
    own, width = blocks[0].shape
    return pl.pallas_call(
        merged_grad_kernel,
        out_shape=[jax.ShapeDtypeStruct((cols.shape[0], width), kind) for kind in (F32, BF16)],
        in_specs=[whole_vmem()] * (1 + len(blocks)),
        out_specs=[whole_vmem()] * 2,
        scratch_shapes=[pltpu.VMEM((own * len(blocks), width), BF16)],
        compiler_params=params(SMALL),
        name="merged_grads",
    )(cols, *blocks)


def expert_kernel(parts, place_ref, coef_ref, *refs):
    grad_refs, out_ref, held_ref, sems = refs[:-3], refs[-3], refs[-2], refs[-1]
    me = place_ref[0]
    count, _, width = out_ref.shape
    systems = coef_ref.shape[0]
    copies = []
    scales = [[coef_ref[me ^ k, me * count + e] for e in range(count)] for k in range(systems)]
    for h, (lo, size) in enumerate(parts):

        @pl.loop(0, size // STEP)
        def _(i):
            at = pl.ds(pl.multiple_of(lo + i * STEP, STEP), STEP)
            for col in range(0, width, 128):
                cols = slice(col, min(col + 128, width))
                grads = [ref[at, cols].astype(F32) for ref in grad_refs]
                for e in range(count):
                    total = scales[0][e] * grads[0]
                    for k in range(1, systems):
                        total = total + scales[k][e] * grads[k]
                    held_ref[e, at, cols] = total

        at = pl.ds(lo, size)
        copies.append(pltpu.make_async_copy(held_ref.at[:, at, :], out_ref.at[:, at, :], sems.at[h]))
        copies[-1].start()
    for copy in copies:
        copy.wait()


def expert_grads(place, coef, grads, shape, parts):
    return pl.pallas_call(
        functools.partial(expert_kernel, parts),
        out_shape=jax.ShapeDtypeStruct(shape, F32),
        in_specs=[whole_smem(), whole_smem()] + [whole_vmem()] * len(grads),
        out_specs=in_hbm(),
        scratch_shapes=[pltpu.VMEM(shape, F32), pltpu.SemaphoreType.DMA((len(parts),))],
        compiler_params=params(SMALL),
        name="expert_grads",
    )(place, coef, *grads)


def hot_kernel(cols_ref, rows_ref, across_ref, down_ref, _, gather_ref, sum_ref, token_ref):
    atoms = down_ref.shape[0]

    def hot(same):
        return jnp.where(same, 1.0, 0.0).astype(BF16)

    for i in range(2):
        at = slice(i * atoms, (i + 1) * atoms)
        gather_ref[:, at] = hot(cols_ref[:, i : i + 1] == across_ref[...])
        sum_ref[at, :] = hot(down_ref[...] == rows_ref[i : i + 1, :])
    token_ref[...] = jnp.zeros_like(token_ref)


def hot_ends(cols, rows, order, earlier, tile):
    edges, atoms = cols.shape[0], order.shape[0]
    fixed = lambda *shape: pl.BlockSpec(shape, lambda i: (0, 0))
    return pl.pallas_call(
        hot_kernel,
        grid=(edges // tile,),
        out_shape=[
            jax.ShapeDtypeStruct((edges, 2 * atoms), BF16),
            jax.ShapeDtypeStruct((2 * atoms, edges), BF16),
            jax.ShapeDtypeStruct((8, 128), F32),
        ],
        in_specs=[
            pl.BlockSpec((tile, 2), lambda i: (i, 0)),
            pl.BlockSpec((2, tile), lambda i: (0, i)),
            fixed(1, atoms),
            fixed(atoms, 1),
            in_hbm(),
        ],
        out_specs=[
            pl.BlockSpec((tile, 2 * atoms), lambda i: (i, 0)),
            pl.BlockSpec((2 * atoms, tile), lambda i: (0, i)),
            fixed(8, 128),
        ],
        compiler_params=params(),
        cost_estimate=pl.CostEstimate(
            flops=16 * edges * atoms, bytes_accessed=8 * edges * atoms, transcendentals=0
        ),
        name="hot_ends",
    )(cols, rows, order[None, :], order[:, None], earlier)


def scale_kernel(slots, gather_ref, radial_ref, *refs):
    block_refs = refs[:slots]
    atoms_out, scaled_ref, token_ref, atoms_ref, cot_ref, sems = refs[slots:]
    step = pl.program_id(0)
    own = block_refs[0].shape[1]
    store = pltpu.make_async_copy(atoms_ref, atoms_out, sems.at[2 * slots])

    @pl.when(step == 0)
    def _():
        loads = []
        for k, ref in enumerate(block_refs):
            at = pl.ds(k * own, own)
            for i, to in enumerate((atoms_ref, cot_ref)):
                loads.append(pltpu.make_async_copy(ref.at[i], to.at[at], sems.at[2 * k + i]))
                loads[-1].start()
        for load in loads:
            load.wait()
        store.start()

    cot = jnp.dot(gather_ref[...], cot_ref[...], preferred_element_type=F32)
    scaled_ref[...] = (cot * radial_ref[...].astype(F32)).astype(BF16)
    token_ref[...] = jnp.zeros_like(token_ref)

    @pl.when(step == pl.num_programs(0) - 1)
    def _():
        store.wait()


def scaled_edges(hot_gather, radial, blocks, tile):
    edges, width = radial.shape
    atoms = hot_gather.shape[1] // 2
    slots = len(blocks)
    return pl.pallas_call(
        functools.partial(scale_kernel, slots),
        grid=(edges // tile,),
        out_shape=[
            jax.ShapeDtypeStruct((atoms, width), BF16),
            jax.ShapeDtypeStruct((edges, width), BF16),
            jax.ShapeDtypeStruct((8, 128), F32),
        ],
        in_specs=[
            pl.BlockSpec((tile, atoms), lambda i: (i, 1)),
            pl.BlockSpec((tile, width), lambda i: (i, 0)),
        ]
        + [in_hbm()] * slots,
        out_specs=[
            in_hbm(),
            pl.BlockSpec((tile, width), lambda i: (i, 0)),
            pl.BlockSpec((8, 128), lambda i: (0, 0)),
        ],
        scratch_shapes=[
            pltpu.VMEM((atoms, width), BF16),
            pltpu.VMEM((atoms, width), BF16),
            pltpu.SemaphoreType.DMA((2 * slots + 1,)),
        ],
        compiler_params=params(),
        cost_estimate=pl.CostEstimate(
            flops=2 * atoms * width * edges, bytes_accessed=6 * edges * width, transcendentals=0
        ),
        name="scaled_edges",
    )(hot_gather, radial, *blocks)


def edge_kernel(
    chips, parts, place_ref, gather_ref, sum_ref, radial_ref, scaled_ref, atoms_hbm, _, *refs
):
    blocks = 2 * chips * len(parts)
    block_refs, kept_refs, sent_refs = refs[:blocks], refs[blocks : blocks + 3], refs[blocks + 3 : blocks + 6]
    weight_out, atoms_ref, weight_ref, proj_ref, value_ref, acc_ref, sem, sems = refs[blocks + 6 :]
    step, last = pl.program_id(0), pl.num_programs(0) - 1
    atoms, width_in = atoms_ref.shape
    width = radial_ref.shape[1]
    store = pltpu.make_async_copy(weight_ref, weight_out, sem)

    def messages():
        pre = jnp.dot(gather_ref[...], proj_ref[...], preferred_element_type=F32)
        sigma = 0.5 + 0.5 * jnp.tanh(0.5 * pre)
        silu = pre * sigma
        slope = sigma + silu * (1.0 - sigma)
        to = lax.rem(step, 2)
        value_ref[to, :, :width] = (scaled_ref[...].astype(F32) * slope).astype(BF16)
        value_ref[to, :, width:] = (silu * radial_ref[...].astype(F32)).astype(BF16)

    def add_up():
        at = lax.rem(step + 1, 2)
        acc_ref[:, :width] += jnp.dot(
            sum_ref[:atoms, :], value_ref[at, :, :width], preferred_element_type=F32
        )
        acc_ref[:, width:] += jnp.dot(
            sum_ref[atoms:, :], value_ref[at], preferred_element_type=F32
        )

    @pl.when(step == 0)
    def _():
        chip, core = place_ref[1], place_ref[2]
        depth = sum(size for _, size in parts)
        loads = [pltpu.make_async_copy(atoms_hbm, atoms_ref, sems.at[blocks])]
        for h, (lo, size) in enumerate(parts):
            for k in range(chips):
                source = lax.rem(chip - k + chips, chips)
                for other in range(2):
                    device = 2 * source + (core if other == 0 else 1 - core)
                    at = pl.ds(pl.multiple_of(device * depth + lo, STEP), size)
                    i = (h * chips + k) * 2 + other
                    loads.append(
                        pltpu.make_async_copy(block_refs[i], weight_ref.at[at], sems.at[i])
                    )
        for load in loads:
            load.start()
        acc_ref[...] = jnp.zeros_like(acc_ref)
        for load in loads:
            load.wait()
        store.start()
        for half in range(2):
            proj_ref[half * atoms : (half + 1) * atoms, :] = jnp.dot(
                atoms_ref[...],
                weight_ref[half * width_in : (half + 1) * width_in, :],
                preferred_element_type=F32,
            ).astype(BF16)
        messages()

    @pl.when(jnp.logical_and(step > 0, step < last))
    def _():
        add_up()
        messages()

    @pl.when(step == last)
    def _():
        add_up()
        half = atoms // 2
        for i in range(3):
            cols = slice(i * width, (i + 1) * width)
            kept_refs[i][...] = acc_ref[:half, cols]
            sent_refs[i][...] = acc_ref[half:, cols].astype(BF16)
        store.wait()


def edge_sums(chips, parts, place, gather, sums, radial, scaled, atoms, earlier, blocks, tile):
    edges, width = radial.shape
    count, width_in = atoms.shape
    flops = 2 * count * width * (2 * width_in + 5 * edges)
    fixed = lambda *shape: pl.BlockSpec(shape, lambda i: (0,) * len(shape))
    halves = [((count // 2, width), F32)] * 3 + [((count // 2, width), BF16)] * 3
    outs = halves + [((2 * width_in, width), BF16)]
    steps = edges // tile
    return pl.pallas_call(
        functools.partial(edge_kernel, chips, parts),
        grid=(steps + 1,),
        out_shape=[jax.ShapeDtypeStruct(shape, kind) for shape, kind in outs],
        in_specs=[
            whole_smem(),
            pl.BlockSpec((tile, 2 * count), lambda i: (jnp.minimum(i, steps - 1), 0)),
            pl.BlockSpec((2 * count, tile), lambda i: (0, jnp.maximum(i - 1, 0))),
            pl.BlockSpec((tile, width), lambda i: (jnp.minimum(i, steps - 1), 0)),
            pl.BlockSpec((tile, width), lambda i: (jnp.minimum(i, steps - 1), 0)),
        ]
        + [in_hbm()] * (2 + len(blocks)),
        out_specs=[fixed(*shape) for shape, _ in halves] + [in_hbm()],
        scratch_shapes=[
            pltpu.VMEM((count, width_in), BF16),
            pltpu.VMEM((2 * width_in, width), BF16),
            pltpu.VMEM((2 * count, width), BF16),
            pltpu.VMEM((2, tile, 2 * width), BF16),
            pltpu.VMEM((count, 3 * width), F32),
            pltpu.SemaphoreType.DMA,
            pltpu.SemaphoreType.DMA((len(blocks) + 1,)),
        ],
        compiler_params=params(),
        cost_estimate=pl.CostEstimate(
            flops=flops,
            bytes_accessed=4 * edges * width + 8 * edges * count,
            transcendentals=edges * width,
        ),
        name="edge_sums",
    )(place, gather, sums, radial, scaled, atoms, earlier, *blocks)


def after(x, *others):
    return lax.optimization_barrier((x, *others))[0]


def shards(systems, ways, atoms, cotangent, experts, radial, coef, source, target):
    chips = ways // 2
    me_sys = lax.axis_index("sys")
    me_edge = lax.axis_index("edge")
    chip, core = me_edge // 2, me_edge % 2
    place = jnp.stack([me_sys, chip, core]).astype(jnp.int32)
    _, depth, width = experts.shape
    own = atoms.shape[1]
    tile = min(512, radial.shape[1])
    parts = row_parts(depth)

    def across(x, k):
        return lax.ppermute(x, "sys", [(s, s ^ k) for s in range(systems)])

    def swap(x):
        return lax.ppermute(x, "edge", [(e, e ^ 1) for e in range(ways)])

    def shift(x, k):
        return lax.ppermute(x, "edge", [(e, (e + 2 * k) % ways) for e in range(ways)])

    def both_cores(blocks):
        return blocks + [swap(block) for block in blocks]

    merged = [merge_part(place, coef, experts, systems, parts[0])]
    joined = (atoms, cotangent, merged[0][0])
    features, *second = merge_part(place, coef, experts, systems, parts[1], joined)
    merged.append(second)
    features = both_cores([features] + [shift(features, k) for k in range(1, chips)])

    at = jnp.arange(ways * own, dtype=jnp.int32)
    side, back, offset = at // (chips * own), at // own % chips, at % own
    order = (2 * ((chip - back + chips) % chips) + (core ^ side)) * own + offset
    ends = jnp.concatenate([source, target])
    hot_gather, hot_sum, hot_token = hot_ends(ends.T, ends, order, second[0], tile)
    all_atoms, scaled, scaled_token = scaled_edges(hot_gather, radial[0], features, tile)
    own_cols = lax.dynamic_slice_in_dim(all_atoms, (me_edge % chips) * depth, depth, 1).T

    blocks = []
    for h in range(len(parts)):
        total = merged[h][0] + (hot_token[0, 0] if h == 0 else 0.0)
        for k in range(1, systems):
            total = total + across(merged[h][k], k).astype(F32)
        held = total.astype(BF16)
        for k in range(chips):
            if h and k == chips - 1:
                held = held + scaled_token[0, 0].astype(BF16)
            if k:
                held = shift(held, 1)
            blocks += [held, swap(held)]

    *halves, weight = edge_sums(
        chips, parts, place, hot_gather, hot_sum, radial[0], scaled, all_atoms, own_cols, blocks, tile
    )

    def slots(i):
        kept, other = halves[i], swap(halves[3 + i])
        cut = lambda x, k: x[k * own : (k + 1) * own]
        return [cut(kept, k) + cut(other, k).astype(F32) for k in range(chips)]

    def ring_sum(terms):
        total = terms[1 % chips]
        for t in range(1, chips):
            total = shift(total.astype(BF16), 1).astype(F32) + terms[(t + 1) % chips]
        return total

    sums = [ring_sum(slots(i)).astype(BF16) for i in range(2)]

    def half_for(k):
        return jnp.where((chip + k) % chips < chips // 2, sums[0], sums[1])

    picked = both_cores([half_for(0)] + [shift(half_for(k), k) for k in range(1, chips)])
    grad, send = merged_grads(own_cols, picked)

    grads = [grad] + [across(send, k) for k in range(1, systems)]
    expert_grad = expert_grads(place, coef, grads, experts.shape, parts)

    node = slots(2)
    total = node[0]
    for k in range(1, chips):
        total = total + shift(after(node[k].astype(BF16), *picked), chips - k).astype(F32)

    over = (((1,), (1,)), ((), ()))
    atom_grad = lax.dot_general(sums[0], weight[:width], over, preferred_element_type=F32)
    atom_grad = atom_grad + lax.dot_general(
        sums[1], weight[width:], over, preferred_element_type=F32
    )
    return total.astype(BF16)[None], atom_grad[None], expert_grad


def solution(mesh):
    placed = P("sys", "edge", None)
    return jax.shard_map(
        functools.partial(shards, mesh.shape["sys"], mesh.shape["edge"]),
        mesh=mesh,
        in_specs=(placed, placed, placed, placed, P(), P("sys", "edge"), P("sys", "edge")),
        out_specs=(placed, placed, placed),
        check_vma=False,
    )
```

time: 173 us -> 182 us (1.052)
  Pallas kernels: 42.7 us -> 52.1 us
  waiting for transfers between devices: 72.3 us -> 65.5 us
  other arithmetic: 11.2 us -> 16.7 us
  starting transfers between devices: 32.9 us -> 36.6 us
  local copies, waits for them, and re-layouts: 10 us -> 6.77 us
    ppermute x21, waiting for transfers between devices: 60 us -> 51.4 us  [shift(): lax.ppermute(x, 'edge', [(e, (e + 2 * k) % ways) for e in range(ways)])]
    pallas_call x3 -> x4, Pallas kernels: 27.5 us -> 35.7 us  [the longest x1 22 us: edge_sums(): pl.pallas_call(functools.partial(edge_kernel, chips, parts), grid=(steps...]
    ppermute x21, starting transfers between devices: 15.9 us -> 23.1 us  [shift(): lax.ppermute(x, 'edge', [(e, (e + 2 * k) % ways) for e in range(ways)])]
    unnamed x20 -> x70, local copies, waits for them, and re-layouts: 6.85 us -> 1.48 us
    ppermute x12 -> x9, starting transfers between devices: 14 us -> 10.5 us  [across(): return lax.ppermute(x, 'sys', [(s, s ^ k) for s in range(systems)])]
    pallas_call x1, Pallas kernels: 3.37 us -> 5.68 us  [hot_ends(): pl.pallas_call(hot_kernel, grid=(edges // tile,), out_shape=[jax.ShapeDty...]
    ppermute x12 -> x9, waiting for transfers between devices: 11.8 us -> 12.5 us  [across(): return lax.ppermute(x, 'sys', [(s, s ^ k) for s in range(systems)])]
  transfers between devices with their start and end apart: 52 -> 49, of which waited for: 23 -> 16; matrix products, arithmetic and copies ran while one was open for 9% -> 13% of each run, Pallas kernels for 7% -> 8%
where the time goes in v6:
time: 182 us; the launch traced here: 181 us
  waiting for transfers between devices  65.5 us (36%)
  Pallas kernels  52.1 us (29%)
  starting transfers between devices  36.6 us (20%)
  other arithmetic  16.7 us (9%)
  local copies, waits for them, and re-layouts  6.77 us (4%)
  matrix products  1.92 us (1%)
    ppermute x21, waiting for transfers between devices, shift(): lax.ppermute(x, 'edge', [(e, (e + 2 * k) % ways) for e in range(ways)])  51.4 us
    ppermute x21, starting transfers between devices, shift(): lax.ppermute(x, 'edge', [(e, (e + 2 * k) % ways) for e in range(ways)])  23.1 us
    pallas_call x1, Pallas kernels, edge_sums(): pl.pallas_call(functools.partial(edge_kernel, chips, parts), grid=(steps...  22 us
    pallas_call x2, Pallas kernels, merge_part(): pl.pallas_call(functools.partial(merge_kernel, lo, len(joined)), out_shap...  13.2 us
    ppermute x9, waiting for transfers between devices, across(): return lax.ppermute(x, 'sys', [(s, s ^ k) for s in range(systems)])  12.5 us
    ppermute x9, starting transfers between devices, across(): return lax.ppermute(x, 'sys', [(s, s ^ k) for s in range(systems)])  10.5 us
    pallas_call x1, Pallas kernels, scaled_edges(): pl.pallas_call(functools.partial(scale_kernel, slots), grid=(edges // til...  7.98 us
    convert_element_type x6, other arithmetic, ring_sum(): total = shift(total.astype(BF16), 1).astype(F32) + terms[(t + 1) % chips]  7.53 us
  transfers between devices with their start and end apart: 49, of which 16 were waited for; matrix products, arithmetic and copies ran while one was open for 13% of the time, Pallas kernels for 8%

profile of v6, /device:TPU:0, one launch (start us, length us, event | category | flops | bytes accessed | tf_op | source)
XLA Modules:
  0.0 181.0 jit_solution(14443525531210781707)
XLA Ops:
  0.7 0.6 pad_add_fusion.1.place_ref
  1.2 3.4 %merge_part.2 = (f32[112,896]{1,0:T(8,128)}, bf16[112,896]{1,0:T(8,128)(2,1)}, bf16[112,896]{1,0:T(8,128)(2,1)}, bf16[112,896]{1,0:T(8,128)(2,1)}) custom-call(s32[3]{0:T(128)} %pad_add_fusion.1.place_ref, f32[4,16]{1,0:T(4,128)} %coef_ref.5, bf16[4,224,896]{2,1,0:T(8,128)(2,1)} %experts_ref.3), custom_call_target="tpu_custom_call" | custom-call | tf_op jit(solution)/shard_map/merge_part/pallas_call | solution.py:76
  4.6 9.9 %merge_part.3 = (bf16[2,64,896]{2,1,0:T(8,128)(2,1)}, f32[112,896]{1,0:T(8,128)}, bf16[112,896]{1,0:T(8,128)(2,1)}, bf16[112,896]{1,0:T(8,128)(2,1)}, bf16[112,896]{1,0:T(8,128)(2,1)}) custom-call(s32[3]{0:T(128)} %pad_add_fusion.1.place_ref, f32[4,16]{1,0:T(4,128)} %coef_ref.5, bf16[4,224,896]{2,1,0:T(8,128)(2,1)} %experts_ref.3, ...), custom_call_target="tpu_custom_call" | custom-call | tf_op jit(solution)/shard_map/merge_part/pallas_call | solution.py:76
  14.5 3.1 %collective-permute-start = (bf16[2,64,896]{2,1,0:T(8,128)(2,1)}, bf16[2,64,896]{2,1,0:T(8,128)(2,1)S(1)}, u32[]{:S(2)}, u32[]{:S(2)}) collective-permute-start(bf16[2,64,896]{2,1,0:T(8,128)(2,1)} %get-tuple-element.34.refs_0_), channel_id=1, source_target_pairs={{0,2},{1,3},{2,4},{3,5},{4,6},{5,7},{6,0},{7,1},{8,10},{9,11},{10,... | collective-permute-start | bytes 688136 | tf_op jit(solution)/shard_map/ppermute | solution.py:397
  17.6 1.5 collective-permute-start.17
  19.1 1.5 collective-permute-start.18
  21.1 1.5 collective-permute-start.7
  22.6 0.6 pad_add_fusion
  23.2 1.3 copy.13.cols_ref
  24.6 0.6 fusion.29.across_ref
  25.1 0.9 fusion.23.down_ref
  26.1 5.7 %hot_ends.1 = (bf16[2048,1024]{1,0:T(8,128)(2,1)}, bf16[1024,2048]{1,0:T(8,128)(2,1)}, f32[8,128]{1,0:T(8,128)}) custom-call(s32[2048,2]{1,0:T(8,128)} %copy.13.cols_ref, s32[2,2048]{1,0:T(2,128)} %get-tuple-element.66.rows_ref, s32[1,512]{1,0:T(1,128)} %fusion.29.across_ref, s32[512,1]{1,0:T(8,128)} %fusion.23.down_ref, f32[112,896]{1,0:T(8,128)} %get-tuple-element.31._), custom_call_target="tpu_custom_call" | custom-call | flops 16777216 | bytes 8388608 | tf_op jit(solution)/shard_map/hot_ends/pallas_call | solution.py:170
  31.8 1.2 slice.85
  32.9 2.6 %collective-permute-start.1 = (bf16[2,64,896]{2,1,0:T(8,128)(2,1)}, bf16[2,64,896]{2,1,0:T(8,128)(2,1)S(1)}, u32[]{:S(2)}, u32[]{:S(2)}) collective-permute-start(bf16[2,64,896]{2,1,0:T(8,128)(2,1)} %get-tuple-element.34.refs_0_), channel_id=1, source_target_pairs={{0,4},{1,5},{2,6},{3,7},{4,0},{5,1},{6,2},{7,3},{8,12},{9,13},{10,... | collective-permute-start | bytes 688136 | tf_op jit(solution)/shard_map/ppermute | solution.py:397
  35.5 1.3 collective-permute-start.2
  36.9 1.5 collective-permute-start.8
  39.0 7.0 %collective-permute-done.8 = bf16[112,896]{1,0:T(8,128)(2,1)S(1)} collective-permute-done((bf16[112,896]{1,0:T(8,128)(2,1)S(1)}, bf16[112,896]{1,0:T(8,128)(2,1)S(1)}, u32[]{:S(2)}, u32[]{:S(2)}) %collective-permute-start.8) | collective-permute-done | bytes 200736 | tf_op jit(solution)/shard_map/ppermute | solution.py:391
  46.0 0.7 collective-permute-start.21
  47.4 0.8 add_convert_fusion.1.refs_0_
  48.2 3.9 %collective-permute-start.11 = (bf16[112,896]{1,0:T(8,128)(2,1)S(1)}, bf16[112,896]{1,0:T(8,128)(2,1)S(1)}, u32[]{:S(2)}, u32[]{:S(2)}) collective-permute-start(bf16[112,896]{1,0:T(8,128)(2,1)S(1)} %add_convert_fusion.1.refs_0_), channel_id=1, source_target_pairs={{0,2},{1,3},{2,4},{3,5},{4,6},{5,7},{6,0},{7,1},{8,10},{9,11},{10,... | collective-permute-start | bytes 602120 | tf_op jit(solution)/shard_map/ppermute | solution.py:397
  52.1 3.0 %collective-permute-done.21.refs_10_ = bf16[112,896]{1,0:T(8,128)(2,1)S(1)} collective-permute-done((bf16[112,896]{1,0:T(8,128)(2,1)S(1)}, bf16[112,896]{1,0:T(8,128)(2,1)S(1)}, u32[]{:S(2)}, u32[]{:S(2)}) %collective-permute-start.21) | collective-permute-done | bytes 200736 | tf_op jit(solution)/shard_map/ppermute | solution.py:397
  55.2 5.4 %collective-permute-done.11.refs_2_ = bf16[112,896]{1,0:T(8,128)(2,1)S(1)} collective-permute-done((bf16[112,896]{1,0:T(8,128)(2,1)S(1)}, bf16[112,896]{1,0:T(8,128)(2,1)S(1)}, u32[]{:S(2)}, u32[]{:S(2)}) %collective-permute-start.11) | collective-permute-done | bytes 200736 | tf_op jit(solution)/shard_map/ppermute | solution.py:397
  61.9 8.0 %scaled_edges.1 = (bf16[512,896]{1,0:T(8,128)(2,1)}, bf16[2048,896]{1,0:T(8,128)(2,1)}, f32[8,128]{1,0:T(8,128)}) custom-call(bf16[2048,1024]{1,0:T(8,128)(2,1)} %get-tuple-element.32.gather_ref, bf16[2048,896]{1,0:T(8,128)(2,1)} %bitcast.16, bf16[2,64,896]{2,1,0:T(8,128)(2,1)} %get-tuple-element.34.refs_0_, bf16[2,64,896]{2,1,0:T(8,128)(2,1)} %copy-done.9, ...), custom_call_target="tpu_custom_call" | custom-call | flops 1879048192 | bytes 11010048 | tf_op jit(solution)/shard_map/scaled_edges/pallas_call | solution.py:230
  69.9 0.7 convert.3
  71.1 0.7 broadcast_add_fusion
  71.8 0.8 collective-permute-start.25
  72.6 2.3 %collective-permute-start.15 = (bf16[112,896]{1,0:T(8,128)(2,1)S(1)}, bf16[112,896]{1,0:T(8,128)(2,1)S(1)}, u32[]{:S(2)}, u32[]{:S(2)}) collective-permute-start(bf16[112,896]{1,0:T(8,128)(2,1)S(1)} %collective-permute-done.13.refs_4_), channel_id=1, source_target_pairs={{0,2},{1,3},{2,4},{3,5},{4,6},{5,7},{6,0},{7,1},{8,10},{9,11},{10,... | collective-permute-start | bytes 602120 | tf_op jit(solution)/shard_map/ppermute | solution.py:397
  75.6 5.9 %collective-permute-done.25.refs_14_ = bf16[112,896]{1,0:T(8,128)(2,1)S(1)} collective-permute-done((bf16[112,896]{1,0:T(8,128)(2,1)S(1)}, bf16[112,896]{1,0:T(8,128)(2,1)S(1)}, u32[]{:S(2)}, u32[]{:S(2)}) %collective-permute-start.25) | collective-permute-done | bytes 200736 | tf_op jit(solution)/shard_map/ppermute | solution.py:397
  81.5 3.4 %collective-permute-done.15.refs_6_ = bf16[112,896]{1,0:T(8,128)(2,1)S(1)} collective-permute-done((bf16[112,896]{1,0:T(8,128)(2,1)S(1)}, bf16[112,896]{1,0:T(8,128)(2,1)S(1)}, u32[]{:S(2)}, u32[]{:S(2)}) %collective-permute-start.15) | collective-permute-done | bytes 200736 | tf_op jit(solution)/shard_map/ppermute | solution.py:397
  85.0 1.5 copy.14
  86.5 0.7 dynamic-slice_bitcast_fusion._.cols_ref
  87.4 0.5 copy-done.29
  88.1 22.0 %edge_sums.1 = (f32[256,896]{1,0:T(8,128)}, f32[256,896]{1,0:T(8,128)}, f32[256,896]{1,0:T(8,128)}, bf16[256,896]{1,0:T(8,128)(2,1)}, bf16[256,896]{1,0:T(8,128)...) custom-call(s32[3]{0:T(128)} %pad_add_fusion.1.place_ref, bf16[2048,1024]{1,0:T(8,128)(2,1)} %get-tuple-element.32.gather_ref, ...), custom_call_target="tpu_custom_call" | custom-call | flops 11039408128 | bytes 15728640 | tf_op jit(solution)/shard_map/edge_sums/pallas_call | solution.py:343
  110.7 1.6 collective-permute-done.28
  112.3 1.2 add_convert_fusion.12
  113.6 1.1 add_convert_fusion.8
  114.7 1.1 collective-permute-start.33
  115.8 5.5 %collective-permute-done.29 = bf16[64,896]{1,0:T(8,128)(2,1)S(1)} collective-permute-done((bf16[64,896]{1,0:T(8,128)(2,1)S(1)}, bf16[64,896]{1,0:T(8,128)(2,1)S(1)}, u32[]{:S(2)}, u32[]{:S(2)}) %collective-permute-start.29) | collective-permute-done | bytes 114720 | tf_op jit(solution)/shard_map/ppermute | solution.py:397
  121.3 1.0 add_convert_fusion.11
  122.4 0.8 collective-permute-done.33
  123.2 1.0 add_convert_fusion.7
  124.3 5.5 %collective-permute-done.30 = bf16[64,896]{1,0:T(8,128)(2,1)S(1)} collective-permute-done((bf16[64,896]{1,0:T(8,128)(2,1)S(1)}, bf16[64,896]{1,0:T(8,128)(2,1)S(1)}, u32[]{:S(2)}, u32[]{:S(2)}) %collective-permute-start.30) | collective-permute-done | bytes 114720 | tf_op jit(solution)/shard_map/ppermute | solution.py:397
  129.7 1.6 add_convert_fusion.10
  131.4 1.6 add_convert_fusion.6
  133.0 6.3 %collective-permute-done.31 = bf16[64,896]{1,0:T(8,128)(2,1)S(1)} collective-permute-done((bf16[64,896]{1,0:T(8,128)(2,1)}, bf16[64,896]{1,0:T(8,128)(2,1)S(1)}, u32[]{:S(2)}, u32[]{:S(2)}) %collective-permute-start.31) | collective-permute-done | bytes 114720 | tf_op jit(solution)/shard_map/ppermute | solution.py:397
  139.4 1.4 collective-permute-done.35
  140.7 1.3 broadcast_select_fusion
  142.2 1.8 collective-permute-start.37
  143.9 2.1 %collective-permute-start.38 = (bf16[64,896]{1,0:T(8,128)(2,1)S(1)}, bf16[64,896]{1,0:T(8,128)(2,1)S(1)}, u32[]{:S(2)}, u32[]{:S(2)}) collective-permute-start(bf16[64,896]{1,0:T(8,128)(2,1)S(1)} %get-tuple-element.57), channel_id=1, source_target_pairs={{0,6},{1,7},{2,0},{3,1},{4,2},{5,3},{6,4},{7,5},{8,14},{9,15},{10,... | collective-permute-start | bytes 344072 | tf_op jit(solution)/shard_map/ppermute | solution.py:397
  146.0 4.1 %collective-permute-done.36.refs_1_ = bf16[64,896]{1,0:T(8,128)(2,1)S(1)} collective-permute-done((bf16[64,896]{1,0:T(8,128)(2,1)S(1)}, bf16[64,896]{1,0:T(8,128)(2,1)S(1)}, u32[]{:S(2)}, u32[]{:S(2)}) %collective-permute-start.36) | collective-permute-done | bytes 114720 | tf_op jit(solution)/shard_map/ppermute | solution.py:397
  150.0 3.0 %collective-permute-done.37.refs_2_ = bf16[64,896]{1,0:T(8,128)(2,1)S(1)} collective-permute-done((bf16[64,896]{1,0:T(8,128)(2,1)S(1)}, bf16[64,896]{1,0:T(8,128)(2,1)S(1)}, u32[]{:S(2)}, u32[]{:S(2)}) %collective-permute-start.37) | collective-permute-done | bytes 114720 | tf_op jit(solution)/shard_map/ppermute | solution.py:397
  153.5 1.2 add_convert_fusion.13
  154.8 1.6 collective-permute-start.43
  156.5 0.6 fusion
  157.5 0.6 collective-permute-start.46
  158.1 1.5 collective-permute-start.47
  159.6 1.4 collective-permute-start.48
  161.1 1.4 collective-permute-start.44
  162.5 1.3 fusion.7
  163.8 7.0 %collective-permute-done.44 = bf16[64,896]{1,0:T(8,128)(2,1)S(1)} collective-permute-done((bf16[64,896]{1,0:T(8,128)(2,1)S(1)}, bf16[64,896]{1,0:T(8,128)(2,1)S(1)}, u32[]{:S(2)}, u32[]{:S(2)}) %collective-permute-start.44) | collective-permute-done | bytes 114720 | tf_op jit(solution)/shard_map/ppermute | solution.py:397
  170.8 1.7 fusion.28
  172.5 3.9 %collective-permute-done.47.refs_2_ = bf16[224,896]{1,0:T(8,128)(2,1)S(1)} collective-permute-done((bf16[224,896]{1,0:T(8,128)(2,1)S(1)}, bf16[224,896]{1,0:T(8,128)(2,1)S(1)}, u32[]{:S(2)}, u32[]{:S(2)}) %collective-permute-start.47) | collective-permute-done | bytes 401440 | tf_op jit(solution)/shard_map/ppermute | solution.py:391
  176.4 1.6 collective-permute-done.48.refs_3_
  178.1 2.8 %expert_grads.1 = f32[4,224,896]{2,1,0:T(8,128)} custom-call(s32[3]{0:T(128)S(1)} %copy-done.2, f32[4,16]{1,0:T(4,128)S(1)} %copy-done.1, f32[224,896]{1,0:T(8,128)S(1)} %get-tuple-element.55.refs_0_, bf16[224,896]{1,0:T(8,128)(2,1)S(1)} %collective-permute-done.46.refs_1_, bf16[224,896]{1,0:T(8,128)(2,1)S(1)} %collective-permute-done.47.refs_2_, ...), custom_call_target="tpu_custom_call" | custom-call | tf_op jit(solution)/shard_map/expert_grads/pallas_call | solution.py:143
  (136 shorter events, 6.4 us)
Async XLA Ops:
  0.6 22.0 %copy-start.20 = (s32[1,2048]{1,0:T(1,128)S(1)}, s32[1,2048]{1,0:T(1,128)}, u32[]{:S(2)}) copy-start(s32[1,2048]{1,0:T(1,128)} %param.12) | copy-start | bytes 24580
  0.6 22.0 %copy-start.19 = (s32[1,2048]{1,0:T(1,128)S(1)}, s32[1,2048]{1,0:T(1,128)}, u32[]{:S(2)}) copy-start(s32[1,2048]{1,0:T(1,128)} %param.13) | copy-start | bytes 24580
  4.6 32.3 %copy-start.33 = (bf16[112,896]{1,0:T(8,128)(2,1)S(1)}, bf16[112,896]{1,0:T(8,128)(2,1)}, u32[]{:S(2)}) copy-start(bf16[112,896]{1,0:T(8,128)(2,1)} %get-tuple-element.39) | copy-start | bytes 602116
  4.6 33.8 %copy-start.31 = (bf16[112,896]{1,0:T(8,128)(2,1)S(1)}, bf16[112,896]{1,0:T(8,128)(2,1)}, u32[]{:S(2)}) copy-start(bf16[112,896]{1,0:T(8,128)(2,1)} %get-tuple-element.40) | copy-start | bytes 602116
  4.6 42.8 %copy-start.5 = (f32[112,896]{1,0:T(8,128)S(1)}, f32[112,896]{1,0:T(8,128)}, u32[]{:S(2)}) copy-start(f32[112,896]{1,0:T(8,128)} %get-tuple-element.30.refs_2_) | copy-start | bytes 1204228
  14.5 24.4 %copy-start.4 = (f32[112,896]{1,0:T(8,128)S(1)}, f32[112,896]{1,0:T(8,128)}, u32[]{:S(2)}) copy-start(f32[112,896]{1,0:T(8,128)} %get-tuple-element.31._) | copy-start | bytes 1204228
  14.5 31.4 %copy-start.8 = (bf16[2,64,896]{2,1,0:T(8,128)(2,1)S(1)}, bf16[2,64,896]{2,1,0:T(8,128)(2,1)}, u32[]{:S(2)}) copy-start(bf16[2,64,896]{2,1,0:T(8,128)(2,1)} %get-tuple-element.34.refs_0_) | copy-start | bytes 688132
  14.5 32.2 %collective-permute-start = (bf16[2,64,896]{2,1,0:T(8,128)(2,1)}, bf16[2,64,896]{2,1,0:T(8,128)(2,1)S(1)}, u32[]{:S(2)}, u32[]{:S(2)}) collective-permute-start(bf16[2,64,896]{2,1,0:T(8,128)(2,1)} %get-tuple-element.34.refs_0_), channel_id=1, source_target_pairs={{0,2},{1,3},{2,4},{3,5},{4,6},{5,7},{6,0},{7,1},{8,10},{9,11},{10,... | collective-permute-start | bytes 688136 | tf_op jit(solution)/shard_map/ppermute | solution.py:397
  17.6 15.3 %collective-permute-start.17 = (bf16[112,896]{1,0:T(8,128)(2,1)}, bf16[112,896]{1,0:T(8,128)(2,1)S(1)}, u32[]{:S(2)}, u32[]{:S(2)}) collective-permute-start(bf16[112,896]{1,0:T(8,128)(2,1)} %get-tuple-element.41), channel_id=1, source_target_pairs={{0,8},{8,0},{16,24},{24,16},{1,9},{9,1},{17,25},{25,17},{2,10},{10... | collective-permute-start | bytes 602120 | tf_op jit(solution)/shard_map/ppermute | solution.py:391
  19.1 16.4 %collective-permute-start.18 = (bf16[112,896]{1,0:T(8,128)(2,1)}, bf16[112,896]{1,0:T(8,128)(2,1)S(1)}, u32[]{:S(2)}, u32[]{:S(2)}) collective-permute-start(bf16[112,896]{1,0:T(8,128)(2,1)} %get-tuple-element.42), channel_id=1, source_target_pairs={{0,16},{8,24},{16,0},{24,8},{1,17},{9,25},{17,1},{25,9},{2,18},{10... | collective-permute-start | bytes 602120 | tf_op jit(solution)/shard_map/ppermute | solution.py:391
  20.6 16.3 %collective-permute-start.19 = (bf16[112,896]{1,0:T(8,128)(2,1)}, bf16[112,896]{1,0:T(8,128)(2,1)S(1)}, u32[]{:S(2)}, u32[]{:S(2)}) collective-permute-start(bf16[112,896]{1,0:T(8,128)(2,1)} %get-tuple-element.43), channel_id=1, source_target_pairs={{0,24},{8,16},{16,8},{24,0},{1,25},{9,17},{17,9},{25,1},{2,26},{10... | collective-permute-start | bytes 602120 | tf_op jit(solution)/shard_map/ppermute | solution.py:391
  21.1 17.3 %collective-permute-start.7 = (bf16[112,896]{1,0:T(8,128)(2,1)}, bf16[112,896]{1,0:T(8,128)(2,1)S(1)}, u32[]{:S(2)}, u32[]{:S(2)}) collective-permute-start(bf16[112,896]{1,0:T(8,128)(2,1)} %get-tuple-element.38), channel_id=1, source_target_pairs={{0,8},{8,0},{16,24},{24,16},{1,9},{9,1},{17,25},{25,17},{2,10},{10... | collective-permute-start | bytes 602120 | tf_op jit(solution)/shard_map/ppermute | solution.py:391
  32.9 13.9 %collective-permute-start.1 = (bf16[2,64,896]{2,1,0:T(8,128)(2,1)}, bf16[2,64,896]{2,1,0:T(8,128)(2,1)S(1)}, u32[]{:S(2)}, u32[]{:S(2)}) collective-permute-start(bf16[2,64,896]{2,1,0:T(8,128)(2,1)} %get-tuple-element.34.refs_0_), channel_id=1, source_target_pairs={{0,4},{1,5},{2,6},{3,7},{4,0},{5,1},{6,2},{7,3},{8,12},{9,13},{10,... | collective-permute-start | bytes 688136 | tf_op jit(solution)/shard_map/ppermute | solution.py:397
  35.5 11.7 %collective-permute-start.2 = (bf16[2,64,896]{2,1,0:T(8,128)(2,1)}, bf16[2,64,896]{2,1,0:T(8,128)(2,1)S(1)}, u32[]{:S(2)}, u32[]{:S(2)}) collective-permute-start(bf16[2,64,896]{2,1,0:T(8,128)(2,1)} %get-tuple-element.34.refs_0_), channel_id=1, source_target_pairs={{0,6},{1,7},{2,0},{3,1},{4,2},{5,3},{6,4},{7,5},{8,14},{9,15},{10,... | collective-permute-start | bytes 688136 | tf_op jit(solution)/shard_map/ppermute | solution.py:397
  36.9 9.1 %collective-permute-start.8 = (bf16[112,896]{1,0:T(8,128)(2,1)S(1)}, bf16[112,896]{1,0:T(8,128)(2,1)S(1)}, u32[]{:S(2)}, u32[]{:S(2)}) collective-permute-start(bf16[112,896]{1,0:T(8,128)(2,1)S(1)} %copy-done.33), channel_id=1, source_target_pairs={{0,16},{8,24},{16,0},{24,8},{1,17},{9,25},{17,1},{25,9},{2,18},{10... | collective-permute-start | bytes 602120 | tf_op jit(solution)/shard_map/ppermute | solution.py:391
  38.4 7.6 %collective-permute-start.9 = (bf16[112,896]{1,0:T(8,128)(2,1)S(1)}, bf16[112,896]{1,0:T(8,128)(2,1)S(1)}, u32[]{:S(2)}, u32[]{:S(2)}) collective-permute-start(bf16[112,896]{1,0:T(8,128)(2,1)S(1)} %copy-done.31), channel_id=1, source_target_pairs={{0,24},{8,16},{16,8},{24,0},{1,25},{9,17},{17,9},{25,1},{2,26},{10... | collective-permute-start | bytes 602120 | tf_op jit(solution)/shard_map/ppermute | solution.py:391
  39.0 30.9 %copy-start.16 = (bf16[112,896]{1,0:T(8,128)(2,1)}, bf16[112,896]{1,0:T(8,128)(2,1)S(1)}, u32[]{:S(2)}) copy-start(bf16[112,896]{1,0:T(8,128)(2,1)S(1)} %add_convert_fusion.refs_8_) | copy-start | bytes 602116
  46.0 2.2 %collective-permute-start.3 = (bf16[2,64,896]{2,1,0:T(8,128)(2,1)S(1)}, bf16[2,64,896]{2,1,0:T(8,128)(2,1)S(1)}, u32[]{:S(2)}, u32[]{:S(2)}) collective-permute-start(bf16[2,64,896]{2,1,0:T(8,128)(2,1)S(1)} %copy-done.8), channel_id=1, source_target_pairs={{0,1},{1,0},{2,3},{3,2},{4,5},{5,4},{6,7},{7,6},{8,9},{9,8},{10,11... | collective-permute-start | bytes 688136 | tf_op jit(solution)/shard_map/ppermute | solution.py:394
  46.0 9.2 %collective-permute-start.21 = (bf16[112,896]{1,0:T(8,128)(2,1)S(1)}, bf16[112,896]{1,0:T(8,128)(2,1)S(1)}, u32[]{:S(2)}, u32[]{:S(2)}) collective-permute-start(bf16[112,896]{1,0:T(8,128)(2,1)S(1)} %add_convert_fusion.refs_8_), channel_id=1, source_target_pairs={{0,2},{1,3},{2,4},{3,5},{4,6},{5,7},{6,0},{7,1},{8,10},{9,11},{10,... | collective-permute-start | bytes 602120 | tf_op jit(solution)/shard_map/ppermute | solution.py:397
  46.7 13.9 %collective-permute-start.4 = (bf16[2,64,896]{2,1,0:T(8,128)(2,1)S(1)}, bf16[2,64,896]{2,1,0:T(8,128)(2,1)S(1)}, u32[]{:S(2)}, u32[]{:S(2)}) collective-permute-start(bf16[2,64,896]{2,1,0:T(8,128)(2,1)S(1)} %collective-permute-done.refs_1_), channel_id=1, source_target_pairs={{0,1},{1,0},{2,3},{3,2},{4,5},{5,4},{6,7},{7,6},{8,9},{9,8},{10,11... | collective-permute-start | bytes 688136 | tf_op jit(solution)/shard_map/ppermute | solution.py:394
  46.9 14.3 %collective-permute-start.5 = (bf16[2,64,896]{2,1,0:T(8,128)(2,1)S(1)}, bf16[2,64,896]{2,1,0:T(8,128)(2,1)S(1)}, u32[]{:S(2)}, u32[]{:S(2)}) collective-permute-start(bf16[2,64,896]{2,1,0:T(8,128)(2,1)S(1)} %collective-permute-done.1.refs_2_), channel_id=1, source_target_pairs={{0,1},{1,0},{2,3},{3,2},{4,5},{5,4},{6,7},{7,6},{8,9},{9,8},{10,11... | collective-permute-start | bytes 688136 | tf_op jit(solution)/shard_map/ppermute | solution.py:394
  47.2 13.9 %collective-permute-start.6 = (bf16[2,64,896]{2,1,0:T(8,128)(2,1)S(1)}, bf16[2,64,896]{2,1,0:T(8,128)(2,1)S(1)}, u32[]{:S(2)}, u32[]{:S(2)}) collective-permute-start(bf16[2,64,896]{2,1,0:T(8,128)(2,1)S(1)} %collective-permute-done.2.refs_3_), channel_id=1, source_target_pairs={{0,1},{1,0},{2,3},{3,2},{4,5},{5,4},{6,7},{7,6},{8,9},{9,8},{10,11... | collective-permute-start | bytes 688136 | tf_op jit(solution)/shard_map/ppermute | solution.py:394
  48.2 39.1 %copy-start.18 = (bf16[112,896]{1,0:T(8,128)(2,1)}, bf16[112,896]{1,0:T(8,128)(2,1)S(1)}, u32[]{:S(2)}) copy-start(bf16[112,896]{1,0:T(8,128)(2,1)S(1)} %add_convert_fusion.1.refs_0_) | copy-start | bytes 602116
  48.2 12.4 %collective-permute-start.11 = (bf16[112,896]{1,0:T(8,128)(2,1)S(1)}, bf16[112,896]{1,0:T(8,128)(2,1)S(1)}, u32[]{:S(2)}, u32[]{:S(2)}) collective-permute-start(bf16[112,896]{1,0:T(8,128)(2,1)S(1)} %add_convert_fusion.1.refs_0_), channel_id=1, source_target_pairs={{0,2},{1,3},{2,4},{3,5},{4,6},{5,7},{6,0},{7,1},{8,10},{9,11},{10,... | collective-permute-start | bytes 602120 | tf_op jit(solution)/shard_map/ppermute | solution.py:397
  55.2 32.1 %copy-start.21 = (bf16[112,896]{1,0:T(8,128)(2,1)}, bf16[112,896]{1,0:T(8,128)(2,1)S(1)}, u32[]{:S(2)}) copy-start(bf16[112,896]{1,0:T(8,128)(2,1)S(1)} %collective-permute-done.21.refs_10_) | copy-start | bytes 602116
  55.2 16.0 %collective-permute-start.23 = (bf16[112,896]{1,0:T(8,128)(2,1)S(1)}, bf16[112,896]{1,0:T(8,128)(2,1)S(1)}, u32[]{:S(2)}, u32[]{:S(2)}) collective-permute-start(bf16[112,896]{1,0:T(8,128)(2,1)S(1)} %collective-permute-done.21.refs_10_), channel_id=1, source_target_pairs={{0,2},{1,3},{2,4},{3,5},{4,6},{5,7},{6,0},{7,1},{8,10},{9,11},{10,... | collective-permute-start | bytes 602120 | tf_op jit(solution)/shard_map/ppermute | solution.py:397
  60.6 26.7 %copy-start.22 = (bf16[112,896]{1,0:T(8,128)(2,1)}, bf16[112,896]{1,0:T(8,128)(2,1)S(1)}, u32[]{:S(2)}) copy-start(bf16[112,896]{1,0:T(8,128)(2,1)S(1)} %collective-permute-done.11.refs_2_) | copy-start | bytes 602116
  60.6 14.4 %collective-permute-start.10 = (bf16[112,896]{1,0:T(8,128)(2,1)S(1)}, bf16[112,896]{1,0:T(8,128)(2,1)S(1)}, u32[]{:S(2)}, u32[]{:S(2)}) collective-permute-start(bf16[112,896]{1,0:T(8,128)(2,1)S(1)} %add_convert_fusion.1.refs_0_), channel_id=1, source_target_pairs={{0,1},{1,0},{2,3},{3,2},{4,5},{5,4},{6,7},{7,6},{8,9},{9,8},{10,11... | collective-permute-start | bytes 602120 | tf_op jit(solution)/shard_map/ppermute | solution.py:394
  60.6 14.3 %collective-permute-start.20 = (bf16[112,896]{1,0:T(8,128)(2,1)S(1)}, bf16[112,896]{1,0:T(8,128)(2,1)S(1)}, u32[]{:S(2)}, u32[]{:S(2)}) collective-permute-start(bf16[112,896]{1,0:T(8,128)(2,1)S(1)} %add_convert_fusion.refs_8_), channel_id=1, source_target_pairs={{0,1},{1,0},{2,3},{3,2},{4,5},{5,4},{6,7},{7,6},{8,9},{9,8},{10,11... | collective-permute-start | bytes 602120 | tf_op jit(solution)/shard_map/ppermute | solution.py:394
  61.1 11.5 %collective-permute-start.13 = (bf16[112,896]{1,0:T(8,128)(2,1)S(1)}, bf16[112,896]{1,0:T(8,128)(2,1)S(1)}, u32[]{:S(2)}, u32[]{:S(2)}) collective-permute-start(bf16[112,896]{1,0:T(8,128)(2,1)S(1)} %collective-permute-done.11.refs_2_), channel_id=1, source_target_pairs={{0,2},{1,3},{2,4},{3,5},{4,6},{5,7},{6,0},{7,1},{8,10},{9,11},{10,... | collective-permute-start | bytes 602120 | tf_op jit(solution)/shard_map/ppermute | solution.py:397
  61.2 14.3 %collective-permute-start.12 = (bf16[112,896]{1,0:T(8,128)(2,1)S(1)}, bf16[112,896]{1,0:T(8,128)(2,1)S(1)}, u32[]{:S(2)}, u32[]{:S(2)}) collective-permute-start(bf16[112,896]{1,0:T(8,128)(2,1)S(1)} %collective-permute-done.11.refs_2_), channel_id=1, source_target_pairs={{0,1},{1,0},{2,3},{3,2},{4,5},{5,4},{6,7},{7,6},{8,9},{9,8},{10,11... | collective-permute-start | bytes 602120 | tf_op jit(solution)/shard_map/ppermute | solution.py:394
  71.8 9.7 %collective-permute-start.25 = (bf16[112,896]{1,0:T(8,128)(2,1)S(1)}, bf16[112,896]{1,0:T(8,128)(2,1)S(1)}, u32[]{:S(2)}, u32[]{:S(2)}) collective-permute-start(bf16[112,896]{1,0:T(8,128)(2,1)S(1)} %broadcast_add_fusion), channel_id=1, source_target_pairs={{0,2},{1,3},{2,4},{3,5},{4,6},{5,7},{6,0},{7,1},{8,10},{9,11},{10,... | collective-permute-start | bytes 602120 | tf_op jit(solution)/shard_map/ppermute | solution.py:397
  72.6 12.3 %collective-permute-start.15 = (bf16[112,896]{1,0:T(8,128)(2,1)S(1)}, bf16[112,896]{1,0:T(8,128)(2,1)S(1)}, u32[]{:S(2)}, u32[]{:S(2)}) collective-permute-start(bf16[112,896]{1,0:T(8,128)(2,1)S(1)} %collective-permute-done.13.refs_4_), channel_id=1, source_target_pairs={{0,2},{1,3},{2,4},{3,5},{4,6},{5,7},{6,0},{7,1},{8,10},{9,11},{10,... | collective-permute-start | bytes 602120 | tf_op jit(solution)/shard_map/ppermute | solution.py:397
  75.0 12.2 %collective-permute-start.22 = (bf16[112,896]{1,0:T(8,128)(2,1)S(1)}, bf16[112,896]{1,0:T(8,128)(2,1)S(1)}, u32[]{:S(2)}, u32[]{:S(2)}) collective-permute-start(bf16[112,896]{1,0:T(8,128)(2,1)S(1)} %collective-permute-done.21.refs_10_), channel_id=1, source_target_pairs={{0,1},{1,0},{2,3},{3,2},{4,5},{5,4},{6,7},{7,6},{8,9},{9,8},{10,11... | collective-permute-start | bytes 602120 | tf_op jit(solution)/shard_map/ppermute | solution.py:394
  75.0 12.2 %collective-permute-start.14 = (bf16[112,896]{1,0:T(8,128)(2,1)S(1)}, bf16[112,896]{1,0:T(8,128)(2,1)S(1)}, u32[]{:S(2)}, u32[]{:S(2)}) collective-permute-start(bf16[112,896]{1,0:T(8,128)(2,1)S(1)} %collective-permute-done.13.refs_4_), channel_id=1, source_target_pairs={{0,1},{1,0},{2,3},{3,2},{4,5},{5,4},{6,7},{7,6},{8,9},{9,8},{10,11... | collective-permute-start | bytes 602120 | tf_op jit(solution)/shard_map/ppermute | solution.py:394
  75.5 11.7 %collective-permute-start.24 = (bf16[112,896]{1,0:T(8,128)(2,1)S(1)}, bf16[112,896]{1,0:T(8,128)(2,1)S(1)}, u32[]{:S(2)}, u32[]{:S(2)}) collective-permute-start(bf16[112,896]{1,0:T(8,128)(2,1)S(1)} %collective-permute-done.23.refs_12_), channel_id=1, source_target_pairs={{0,1},{1,0},{2,3},{3,2},{4,5},{5,4},{6,7},{7,6},{8,9},{9,8},{10,11... | collective-permute-start | bytes 602120 | tf_op jit(solution)/shard_map/ppermute | solution.py:394
  81.5 5.7 %collective-permute-start.26 = (bf16[112,896]{1,0:T(8,128)(2,1)S(1)}, bf16[112,896]{1,0:T(8,128)(2,1)S(1)}, u32[]{:S(2)}, u32[]{:S(2)}) collective-permute-start(bf16[112,896]{1,0:T(8,128)(2,1)S(1)} %collective-permute-done.25.refs_14_), channel_id=1, source_target_pairs={{0,1},{1,0},{2,3},{3,2},{4,5},{5,4},{6,7},{7,6},{8,9},{9,8},{10,11... | collective-permute-start | bytes 602120 | tf_op jit(solution)/shard_map/ppermute | solution.py:394
  85.0 2.3 %collective-permute-start.16 = (bf16[112,896]{1,0:T(8,128)(2,1)S(1)}, bf16[112,896]{1,0:T(8,128)(2,1)}, u32[]{:S(2)}, u32[]{:S(2)}) collective-permute-start(bf16[112,896]{1,0:T(8,128)(2,1)S(1)} %collective-permute-done.15.refs_6_), channel_id=1, source_target_pairs={{0,1},{1,0},{2,3},{3,2},{4,5},{5,4},{6,7},{7,6},{8,9},{9,8},{10,11... | collective-permute-start | bytes 602120 | tf_op jit(solution)/shard_map/ppermute | solution.py:394
  110.2 2.1 %collective-permute-start.28 = (bf16[256,896]{1,0:T(8,128)(2,1)}, bf16[256,896]{1,0:T(8,128)(2,1)S(1)}, u32[]{:S(2)}, u32[]{:S(2)}) collective-permute-start(bf16[256,896]{1,0:T(8,128)(2,1)} %get-tuple-element.48), channel_id=1, source_target_pairs={{0,1},{1,0},{2,3},{3,2},{4,5},{5,4},{6,7},{7,6},{8,9},{9,8},{10,11... | collective-permute-start | bytes 1376264 | tf_op jit(solution)/shard_map/ppermute | solution.py:394
  110.6 2.9 %collective-permute-start.32 = (bf16[256,896]{1,0:T(8,128)(2,1)}, bf16[256,896]{1,0:T(8,128)(2,1)S(1)}, u32[]{:S(2)}, u32[]{:S(2)}) collective-permute-start(bf16[256,896]{1,0:T(8,128)(2,1)} %get-tuple-element.50), channel_id=1, source_target_pairs={{0,1},{1,0},{2,3},{3,2},{4,5},{5,4},{6,7},{7,6},{8,9},{9,8},{10,11... | collective-permute-start | bytes 1376264 | tf_op jit(solution)/shard_map/ppermute | solution.py:394
  112.3 44.2 %copy-start.3 = (bf16[1792,896]{1,0:T(8,128)(2,1)S(1)}, bf16[1792,896]{1,0:T(8,128)(2,1)}, u32[]{:S(2)}) copy-start(bf16[1792,896]{1,0:T(8,128)(2,1)} %get-tuple-element.54) | copy-start | bytes 9633796
  113.5 7.8 %collective-permute-start.29 = (bf16[64,896]{1,0:T(8,128)(2,1)S(1)}, bf16[64,896]{1,0:T(8,128)(2,1)S(1)}, u32[]{:S(2)}, u32[]{:S(2)}) collective-permute-start(bf16[64,896]{1,0:T(8,128)(2,1)S(1)} %add_convert_fusion.12), channel_id=1, source_target_pairs={{0,2},{1,3},{2,4},{3,5},{4,6},{5,7},{6,0},{7,1},{8,10},{9,11},{10,... | collective-permute-start | bytes 344072 | tf_op jit(solution)/shard_map/ppermute | solution.py:397
  114.7 8.5 %collective-permute-start.33 = (bf16[64,896]{1,0:T(8,128)(2,1)S(1)}, bf16[64,896]{1,0:T(8,128)(2,1)S(1)}, u32[]{:S(2)}, u32[]{:S(2)}) collective-permute-start(bf16[64,896]{1,0:T(8,128)(2,1)S(1)} %add_convert_fusion.8), channel_id=1, source_target_pairs={{0,2},{1,3},{2,4},{3,5},{4,6},{5,7},{6,0},{7,1},{8,10},{9,11},{10,... | collective-permute-start | bytes 344072 | tf_op jit(solution)/shard_map/ppermute | solution.py:397
  122.3 7.4 %collective-permute-start.30 = (bf16[64,896]{1,0:T(8,128)(2,1)S(1)}, bf16[64,896]{1,0:T(8,128)(2,1)S(1)}, u32[]{:S(2)}, u32[]{:S(2)}) collective-permute-start(bf16[64,896]{1,0:T(8,128)(2,1)S(1)} %add_convert_fusion.11), channel_id=1, source_target_pairs={{0,2},{1,3},{2,4},{3,5},{4,6},{5,7},{6,0},{7,1},{8,10},{9,11},{10,... | collective-permute-start | bytes 344072 | tf_op jit(solution)/shard_map/ppermute | solution.py:397
  124.2 32.9 %copy-start = (bf16[224,512]{1,0:T(8,128)(2,1)S(1)}, bf16[224,512]{1,0:T(8,128)(2,1)}, u32[]{:S(2)}) copy-start(bf16[224,512]{1,0:T(8,128)(2,1)} %dynamic-slice_bitcast_fusion._.cols_ref) | copy-start | bytes 688132
  124.2 7.2 %collective-permute-start.34 = (bf16[64,896]{1,0:T(8,128)(2,1)S(1)}, bf16[64,896]{1,0:T(8,128)(2,1)S(1)}, u32[]{:S(2)}, u32[]{:S(2)}) collective-permute-start(bf16[64,896]{1,0:T(8,128)(2,1)S(1)} %add_convert_fusion.7), channel_id=1, source_target_pairs={{0,2},{1,3},{2,4},{3,5},{4,6},{5,7},{6,0},{7,1},{8,10},{9,11},{10,... | collective-permute-start | bytes 344072 | tf_op jit(solution)/shard_map/ppermute | solution.py:397
  131.4 8.0 %collective-permute-start.31 = (bf16[64,896]{1,0:T(8,128)(2,1)}, bf16[64,896]{1,0:T(8,128)(2,1)S(1)}, u32[]{:S(2)}, u32[]{:S(2)}) collective-permute-start(bf16[64,896]{1,0:T(8,128)(2,1)} %add_convert_fusion.10), channel_id=1, source_target_pairs={{0,2},{1,3},{2,4},{3,5},{4,6},{5,7},{6,0},{7,1},{8,10},{9,11},{10,... | collective-permute-start | bytes 344072 | tf_op jit(solution)/shard_map/ppermute | solution.py:397
  133.0 7.7 %collective-permute-start.35 = (bf16[64,896]{1,0:T(8,128)(2,1)}, bf16[64,896]{1,0:T(8,128)(2,1)}, u32[]{:S(2)}, u32[]{:S(2)}) collective-permute-start(bf16[64,896]{1,0:T(8,128)(2,1)} %add_convert_fusion.6), channel_id=1, source_target_pairs={{0,2},{1,3},{2,4},{3,5},{4,6},{5,7},{6,0},{7,1},{8,10},{9,11},{10,... | collective-permute-start | bytes 344072 | tf_op jit(solution)/shard_map/ppermute | solution.py:397
  133.0 20.5 %collective-permute-start.27 = (bf16[256,896]{1,0:T(8,128)(2,1)}, bf16[256,896]{1,0:T(8,128)(2,1)S(1)}, u32[]{:S(2)}, u32[]{:S(2)}) collective-permute-start(bf16[256,896]{1,0:T(8,128)(2,1)} %get-tuple-element.46), channel_id=1, source_target_pairs={{0,1},{1,0},{2,3},{3,2},{4,5},{5,4},{6,7},{7,6},{8,9},{9,8},{10,11... | collective-permute-start | bytes 1376264 | tf_op jit(solution)/shard_map/ppermute | solution.py:394
  142.1 7.9 %collective-permute-start.36 = (bf16[64,896]{1,0:T(8,128)(2,1)S(1)}, bf16[64,896]{1,0:T(8,128)(2,1)S(1)}, u32[]{:S(2)}, u32[]{:S(2)}) collective-permute-start(bf16[64,896]{1,0:T(8,128)(2,1)S(1)} %get-tuple-element.64), channel_id=1, source_target_pairs={{0,2},{1,3},{2,4},{3,5},{4,6},{5,7},{6,0},{7,1},{8,10},{9,11},{10,... | collective-permute-start | bytes 344072 | tf_op jit(solution)/shard_map/ppermute | solution.py:397
  142.2 10.9 %collective-permute-start.37 = (bf16[64,896]{1,0:T(8,128)(2,1)S(1)}, bf16[64,896]{1,0:T(8,128)(2,1)S(1)}, u32[]{:S(2)}, u32[]{:S(2)}) collective-permute-start(bf16[64,896]{1,0:T(8,128)(2,1)S(1)} %get-tuple-element.63), channel_id=1, source_target_pairs={{0,4},{1,5},{2,6},{3,7},{4,0},{5,1},{6,2},{7,3},{8,12},{9,13},{10,... | collective-permute-start | bytes 344072 | tf_op jit(solution)/shard_map/ppermute | solution.py:397
  143.9 9.1 %collective-permute-start.38 = (bf16[64,896]{1,0:T(8,128)(2,1)S(1)}, bf16[64,896]{1,0:T(8,128)(2,1)S(1)}, u32[]{:S(2)}, u32[]{:S(2)}) collective-permute-start(bf16[64,896]{1,0:T(8,128)(2,1)S(1)} %get-tuple-element.57), channel_id=1, source_target_pairs={{0,6},{1,7},{2,0},{3,1},{4,2},{5,3},{6,4},{7,5},{8,14},{9,15},{10,... | collective-permute-start | bytes 344072 | tf_op jit(solution)/shard_map/ppermute | solution.py:397
  146.0 8.8 %collective-permute-start.39 = (bf16[64,896]{1,0:T(8,128)(2,1)S(1)}, bf16[64,896]{1,0:T(8,128)(2,1)S(1)}, u32[]{:S(2)}, u32[]{:S(2)}) collective-permute-start(bf16[64,896]{1,0:T(8,128)(2,1)S(1)} %get-tuple-element.65.refs_0_), channel_id=1, source_target_pairs={{0,1},{1,0},{2,3},{3,2},{4,5},{5,4},{6,7},{7,6},{8,9},{9,8},{10,11... | collective-permute-start | bytes 344072 | tf_op jit(solution)/shard_map/ppermute | solution.py:394
  150.0 4.8 %collective-permute-start.40 = (bf16[64,896]{1,0:T(8,128)(2,1)S(1)}, bf16[64,896]{1,0:T(8,128)(2,1)S(1)}, u32[]{:S(2)}, u32[]{:S(2)}) collective-permute-start(bf16[64,896]{1,0:T(8,128)(2,1)S(1)} %collective-permute-done.36.refs_1_), channel_id=1, source_target_pairs={{0,1},{1,0},{2,3},{3,2},{4,5},{5,4},{6,7},{7,6},{8,9},{9,8},{10,11... | collective-permute-start | bytes 344072 | tf_op jit(solution)/shard_map/ppermute | solution.py:394
  153.0 1.8 collective-permute-start.41
  153.0 1.8 %collective-permute-start.42 = (bf16[64,896]{1,0:T(8,128)(2,1)S(1)}, bf16[64,896]{1,0:T(8,128)(2,1)S(1)}, u32[]{:S(2)}, u32[]{:S(2)}) collective-permute-start(bf16[64,896]{1,0:T(8,128)(2,1)S(1)} %collective-permute-done.38.refs_3_), channel_id=1, source_target_pairs={{0,1},{1,0},{2,3},{3,2},{4,5},{5,4},{6,7},{7,6},{8,9},{9,8},{10,11... | collective-permute-start | bytes 344072 | tf_op jit(solution)/shard_map/ppermute | solution.py:394
  154.8 23.3 %copy-start.1 = (f32[4,16]{1,0:T(4,128)S(1)}, f32[4,16]{1,0:T(4,128)}, u32[]{:S(2)}) copy-start(f32[4,16]{1,0:T(4,128)} %coef_ref.5) | copy-start | bytes 772
  154.8 23.3 %copy-start.2 = (s32[3]{0:T(128)S(1)}, s32[3]{0:T(128)}, u32[]{:S(2)}) copy-start(s32[3]{0:T(128)} %pad_add_fusion.1.place_ref) | copy-start | bytes 40
  154.8 7.7 %collective-permute-start.43 = (bf16[64,896]{1,0:T(8,128)(2,1)S(1)}, bf16[64,896]{1,0:T(8,128)(2,1)S(1)}, u32[]{:S(2)}, u32[]{:S(2)}) collective-permute-start(bf16[64,896]{1,0:T(8,128)(2,1)S(1)} %get-tuple-element.51), channel_id=1, source_target_pairs={{0,6},{1,7},{2,0},{3,1},{4,2},{5,3},{6,4},{7,5},{8,14},{9,15},{10,... | collective-permute-start | bytes 344072 | tf_op jit(solution)/shard_map/ppermute | solution.py:397
  157.5 15.0 %collective-permute-start.46 = (bf16[224,896]{1,0:T(8,128)(2,1)S(1)}, bf16[224,896]{1,0:T(8,128)(2,1)S(1)}, u32[]{:S(2)}, u32[]{:S(2)}) collective-permute-start(bf16[224,896]{1,0:T(8,128)(2,1)S(1)} %get-tuple-element.56), channel_id=1, source_target_pairs={{0,8},{8,0},{16,24},{24,16},{1,9},{9,1},{17,25},{25,17},{2,10},{10... | collective-permute-start | bytes 1204232 | tf_op jit(solution)/shard_map/ppermute | solution.py:391
  158.1 18.3 %collective-permute-start.47 = (bf16[224,896]{1,0:T(8,128)(2,1)S(1)}, bf16[224,896]{1,0:T(8,128)(2,1)S(1)}, u32[]{:S(2)}, u32[]{:S(2)}) collective-permute-start(bf16[224,896]{1,0:T(8,128)(2,1)S(1)} %get-tuple-element.56), channel_id=1, source_target_pairs={{0,16},{8,24},{16,0},{24,8},{1,17},{9,25},{17,1},{25,9},{2,18},{10... | collective-permute-start | bytes 1204232 | tf_op jit(solution)/shard_map/ppermute | solution.py:391
  159.6 18.4 %collective-permute-start.48 = (bf16[224,896]{1,0:T(8,128)(2,1)S(1)}, bf16[224,896]{1,0:T(8,128)(2,1)S(1)}, u32[]{:S(2)}, u32[]{:S(2)}) collective-permute-start(bf16[224,896]{1,0:T(8,128)(2,1)S(1)} %get-tuple-element.56), channel_id=1, source_target_pairs={{0,24},{8,16},{16,8},{24,0},{1,25},{9,17},{17,9},{25,1},{2,26},{10... | collective-permute-start | bytes 1204232 | tf_op jit(solution)/shard_map/ppermute | solution.py:391
  161.1 9.8 %collective-permute-start.44 = (bf16[64,896]{1,0:T(8,128)(2,1)S(1)}, bf16[64,896]{1,0:T(8,128)(2,1)S(1)}, u32[]{:S(2)}, u32[]{:S(2)}) collective-permute-start(bf16[64,896]{1,0:T(8,128)(2,1)S(1)} %get-tuple-element.52), channel_id=1, source_target_pairs={{0,4},{1,5},{2,6},{3,7},{4,0},{5,1},{6,2},{7,3},{8,12},{9,13},{10,... | collective-permute-start | bytes 344072 | tf_op jit(solution)/shard_map/ppermute | solution.py:397
  162.5 8.3 %collective-permute-start.45 = (bf16[64,896]{1,0:T(8,128)(2,1)S(1)}, bf16[64,896]{1,0:T(8,128)(2,1)S(1)}, u32[]{:S(2)}, u32[]{:S(2)}) collective-permute-start(bf16[64,896]{1,0:T(8,128)(2,1)S(1)} %get-tuple-element.53), channel_id=1, source_target_pairs={{0,2},{1,3},{2,4},{3,5},{4,6},{5,7},{6,0},{7,1},{8,10},{9,11},{10,... | collective-permute-start | bytes 344072 | tf_op jit(solution)/shard_map/ppermute | solution.py:397
  (20 other events, 170.2 us)

commit v7 on v6

--- a/solution.py
+++ b/solution.py
@@ -35,80 +35,111 @@
     return [(0, first), (first, depth - first)]
 
 
-def merge_kernel(lo, pairs, place_ref, coef_ref, experts_ref, *refs):
+def merge_kernel(parts, place_ref, coef_ref, experts_ref, *refs):
+    part_refs, held_ref, sems = refs[:-2], refs[-2], refs[-1]
     systems, count = coef_ref.shape[0], experts_ref.shape[0]
-    pair_refs, part_refs = refs[:pairs], refs[-systems - 3 : -3]
-    held_ref, sem, pair_sems = refs[-3:]
+    width = experts_ref.shape[2]
     me = place_ref[0]
-    size, width = part_refs[0].shape
-    load = pltpu.make_async_copy(experts_ref.at[:, pl.ds(lo, size), :], held_ref, sem)
-    load.start()
-    joins = []
-    if pairs:
-        both_ref = refs[-systems - 4]
-        for i, ref in enumerate(pair_refs[:2]):
-            joins.append(pltpu.make_async_copy(ref.at[0], both_ref.at[i], pair_sems.at[i]))
-            joins[-1].start()
+    loads = []
+    for h, (lo, size) in enumerate(parts):
+        at = pl.ds(lo, size)
+        loads.append(
+            pltpu.make_async_copy(experts_ref.at[:, at, :], held_ref.at[:, at, :], sems.at[h])
+        )
+        loads[-1].start()
     scales = [[coef_ref[me ^ k, me * count + e] for e in range(count)] for k in range(systems)]
-    load.wait()
-
-    @pl.loop(0, size // STEP)
-    def _(i):
-        at = pl.ds(pl.multiple_of(i * STEP, STEP), STEP)
-        for col in range(0, width, 128):
-            cols = slice(col, min(col + 128, width))
-            loaded = [held_ref[e, at, cols].astype(F32) for e in range(count)]
-            for k in range(systems):
-                total = scales[k][0] * loaded[0]
-                for e in range(1, count):
-                    total = total + scales[k][e] * loaded[e]
-                part_refs[k][at, cols] = total.astype(part_refs[k].dtype)
-
-    for join in joins:
-        join.wait()
-
-
-def merge_part(place, coef, experts, systems, part, joined=()):
-    count, _, width = experts.shape
-    lo, size = part
-    outs = [((2, *joined[0].shape[1:]), BF16)] if joined else []
-    outs += [((size, width), BF16 if k else F32) for k in range(systems)]
-    return pl.pallas_call(
-        functools.partial(merge_kernel, lo, len(joined)),
-        out_shape=[jax.ShapeDtypeStruct(*out) for out in outs],
-        in_specs=[whole_smem(), whole_smem()] + [in_hbm()] * (1 + len(joined)),
-        out_specs=([in_hbm()] if joined else []) + [whole_vmem()] * systems,
+    for h, (lo, size) in enumerate(parts):
+        loads[h].wait()
+
+        @pl.loop(0, size // STEP)
+        def _(i):
+            at = pl.ds(pl.multiple_of(lo + i * STEP, STEP), STEP)
+            for col in range(0, width, 128):
+                cols = slice(col, min(col + 128, width))
+                loaded = [held_ref[e, at, cols].astype(F32) for e in range(count)]
+                for k in range(systems):
+                    total = scales[k][0] * loaded[0]
+                    for e in range(1, count):
+                        total = total + scales[k][e] * loaded[e]
+                    part_refs[k][at, cols] = total.astype(part_refs[k].dtype)
+
+
+def merge_parts(place, coef, experts, parts):
+    _, depth, width = experts.shape
+    systems = coef.shape[0]
+    return pl.pallas_call(
+        functools.partial(merge_kernel, parts),
+        out_shape=[
+            jax.ShapeDtypeStruct((depth, width), BF16 if k else F32) for k in range(systems)
+        ],
+        in_specs=[whole_smem(), whole_smem(), in_hbm()],
+        out_specs=[whole_vmem()] * systems,
         scratch_shapes=[
-            pltpu.VMEM((count, size, width), BF16),
-            pltpu.SemaphoreType.DMA,
-            pltpu.SemaphoreType.DMA((2,)),
+            pltpu.VMEM(experts.shape, BF16),
+            pltpu.SemaphoreType.DMA((len(parts),)),
         ],
         compiler_params=params(),
-        name="merge_part",
-    )(place, coef, experts, *joined)
-
-
-def merged_grad_kernel(cols_ref, *refs):
-    block_refs, grad_ref, sent_ref, sums_ref = refs[:-3], refs[-3], refs[-2], refs[-1]
-    own = block_refs[0].shape[0]
+        name="merge_parts",
+    )(place, coef, experts)
+
+
+def merged_grad_kernel(place_ref, cols_ref, *refs):
+    block_refs, grad_ref, sent_ref, token_ref, sums_ref = refs[:-4], *refs[-4:]
+    size = block_refs[0].shape[0]
+    pieces = len(block_refs) // 2
     for i, ref in enumerate(block_refs):
-        sums_ref[i * own : (i + 1) * own, :] = ref[...]
+        piece = lax.rem(place_ref[1] + pieces - i % pieces, pieces)
+        at = pl.ds(pl.multiple_of((i // pieces * pieces + piece) * size, size), size)
+        sums_ref[at, :] = ref[...]
     grad = jnp.dot(cols_ref[...], sums_ref[...], preferred_element_type=F32)
     grad_ref[...] = grad
     sent_ref[...] = grad.astype(BF16)
-
-
-def merged_grads(cols, blocks):
-    own, width = blocks[0].shape
+    token_ref[...] = jnp.zeros_like(token_ref)
+
+
+def merged_grads(place, cols, blocks):
+    size, width = blocks[0].shape
     return pl.pallas_call(
         merged_grad_kernel,
-        out_shape=[jax.ShapeDtypeStruct((cols.shape[0], width), kind) for kind in (F32, BF16)],
-        in_specs=[whole_vmem()] * (1 + len(blocks)),
-        out_specs=[whole_vmem()] * 2,
-        scratch_shapes=[pltpu.VMEM((own * len(blocks), width), BF16)],
+        out_shape=[jax.ShapeDtypeStruct((cols.shape[0], width), kind) for kind in (F32, BF16)]
+        + [jax.ShapeDtypeStruct((8, 128), F32)],
+        in_specs=[whole_smem()] + [whole_vmem()] * (1 + len(blocks)),
+        out_specs=[whole_vmem()] * 3,
+        scratch_shapes=[pltpu.VMEM((size * len(blocks), width), BF16)],
         compiler_params=params(SMALL),
         name="merged_grads",
-    )(cols, *blocks)
+    )(place, cols, *blocks)
+
+
+def atom_grad_kernel(chips, place_ref, sums_ref, weight_hbm, first_ref, second_ref, weight_ref, sem):
+    half = place_ref[1] // (chips // 2)
+    rows, own = weight_ref.shape[0], first_ref.shape[0]
+    at = pl.ds(pl.multiple_of(half * rows, rows), rows)
+    load = pltpu.make_async_copy(weight_hbm.at[at], weight_ref, sem)
+    load.start()
+    load.wait()
+    for side, ref in ((half, first_ref), (1 - half, second_ref)):
+        block = sums_ref[pl.ds(pl.multiple_of(side * own, own), own), :]
+        ref[...] = lax.dot_general(
+            block, weight_ref[...], (((1,), (1,)), ((), ())), preferred_element_type=F32
+        ).astype(BF16)
+
+
+def atom_grads(chips, place, sums, weight):
+    own, width = sums.shape[0] // 2, sums.shape[1]
+    rows = weight.shape[0] // 2
+    return pl.pallas_call(
+        functools.partial(atom_grad_kernel, chips),
+        out_shape=[jax.ShapeDtypeStruct((own, rows), BF16)] * 2,
+        in_specs=[whole_smem(), whole_vmem(), in_hbm()],
+        out_specs=[whole_vmem()] * 2,
+        scratch_shapes=[pltpu.VMEM((rows, width), BF16), pltpu.SemaphoreType.DMA],
+        compiler_params=params(SMALL),
+        cost_estimate=pl.CostEstimate(
+            flops=4 * own * rows * width, bytes_accessed=2 * rows * width, transcendentals=0
+        ),
+        name="atom_grads",
+    )(place, sums, weight)
 
 
 def expert_kernel(parts, place_ref, coef_ref, *refs):
@@ -195,7 +226,7 @@
     )(cols, rows, order[None, :], order[:, None], earlier)
 
 
-def scale_kernel(slots, gather_ref, radial_ref, *refs):
+def scale_kernel(slots, place_ref, gather_ref, radial_ref, *refs):
     block_refs = refs[:slots]
     atoms_out, scaled_ref, token_ref, atoms_ref, cot_ref, sems = refs[slots:]
     step = pl.program_id(0)
@@ -205,8 +236,10 @@
     @pl.when(step == 0)
     def _():
         loads = []
+        chips = slots // 2
         for k, ref in enumerate(block_refs):
-            at = pl.ds(k * own, own)
+            back = lax.rem(place_ref[1] - k % chips + chips, chips)
+            at = pl.ds(pl.multiple_of((k // chips * chips + back) * own, own), own)
             for i, to in enumerate((atoms_ref, cot_ref)):
                 loads.append(pltpu.make_async_copy(ref.at[i], to.at[at], sems.at[2 * k + i]))
                 loads[-1].start()
@@ -223,7 +256,7 @@
         store.wait()
 
 
-def scaled_edges(hot_gather, radial, blocks, tile):
+def scaled_edges(place, hot_gather, radial, blocks, tile):
     edges, width = radial.shape
     atoms = hot_gather.shape[1] // 2
     slots = len(blocks)
@@ -236,6 +269,7 @@
             jax.ShapeDtypeStruct((8, 128), F32),
         ],
         in_specs=[
+            whole_smem(),
             pl.BlockSpec((tile, atoms), lambda i: (i, 1)),
             pl.BlockSpec((tile, width), lambda i: (i, 0)),
         ]
@@ -255,15 +289,16 @@
             flops=2 * atoms * width * edges, bytes_accessed=6 * edges * width, transcendentals=0
         ),
         name="scaled_edges",
-    )(hot_gather, radial, *blocks)
+    )(place, hot_gather, radial, *blocks)
 
 
 def edge_kernel(
-    chips, parts, place_ref, gather_ref, sum_ref, radial_ref, scaled_ref, atoms_hbm, _, *refs
+    chips, place_ref, gather_ref, sum_ref, radial_ref, scaled_ref, atoms_hbm, _, *refs
 ):
-    blocks = 2 * chips * len(parts)
-    block_refs, kept_refs, sent_refs = refs[:blocks], refs[blocks : blocks + 3], refs[blocks + 3 : blocks + 6]
-    weight_out, atoms_ref, weight_ref, proj_ref, value_ref, acc_ref, sem, sems = refs[blocks + 6 :]
+    blocks = 2 * chips
+    block_refs = refs[:blocks]
+    kept_ref, sent_ref, node_kept_ref, node_sent_ref, weight_out = refs[blocks : blocks + 5]
+    atoms_ref, weight_ref, proj_ref, value_ref, acc_ref, sem, sems = refs[blocks + 5 :]
     step, last = pl.program_id(0), pl.num_programs(0) - 1
     atoms, width_in = atoms_ref.shape
     width = radial_ref.shape[1]
@@ -290,18 +325,13 @@
     @pl.when(step == 0)
     def _():
         chip, core = place_ref[1], place_ref[2]
-        depth = sum(size for _, size in parts)
+        depth = block_refs[0].shape[0]
         loads = [pltpu.make_async_copy(atoms_hbm, atoms_ref, sems.at[blocks])]
-        for h, (lo, size) in enumerate(parts):
-            for k in range(chips):
-                source = lax.rem(chip - k + chips, chips)
-                for other in range(2):
-                    device = 2 * source + (core if other == 0 else 1 - core)
-                    at = pl.ds(pl.multiple_of(device * depth + lo, STEP), size)
-                    i = (h * chips + k) * 2 + other
-                    loads.append(
-                        pltpu.make_async_copy(block_refs[i], weight_ref.at[at], sems.at[i])
-                    )
+        for i, ref in enumerate(block_refs):
+            source = lax.rem(chip - i // 2 + chips, chips)
+            device = 2 * source + (1 - core if i % 2 else core)
+            at = pl.ds(pl.multiple_of(device * depth, STEP), depth)
+            loads.append(pltpu.make_async_copy(ref, weight_ref.at[at], sems.at[i]))
         for load in loads:
             load.start()
         acc_ref[...] = jnp.zeros_like(acc_ref)
@@ -324,24 +354,36 @@
     @pl.when(step == last)
     def _():
         add_up()
-        half = atoms // 2
-        for i in range(3):
-            cols = slice(i * width, (i + 1) * width)
-            kept_refs[i][...] = acc_ref[:half, cols]
-            sent_refs[i][...] = acc_ref[half:, cols].astype(BF16)
+        side = atoms // 2
+        for k in range(chips):
+            chip = lax.rem(place_ref[1] + k, chips)
+            cols = pl.ds(pl.multiple_of(chip // (chips // 2) * width, width), width)
+            size = kept_ref.shape[1]
+            row = lax.rem(chip, chips // 2) * size
+            kept_ref[k] = acc_ref[pl.ds(pl.multiple_of(row, size), size), cols]
+            sent_ref[k] = acc_ref[pl.ds(pl.multiple_of(side + row, size), size), cols].astype(BF16)
+            cols = slice(2 * width, 3 * width)
+            size = node_kept_ref.shape[1]
+            row = chip * size
+            node_kept_ref[k] = acc_ref[pl.ds(pl.multiple_of(row, size), size), cols]
+            node_sent_ref[k] = acc_ref[pl.ds(pl.multiple_of(side + row, size), size), cols].astype(
+                BF16
+            )
         store.wait()
 
 
-def edge_sums(chips, parts, place, gather, sums, radial, scaled, atoms, earlier, blocks, tile):
+def edge_sums(chips, place, gather, sums, radial, scaled, atoms, earlier, blocks, tile):
     edges, width = radial.shape
     count, width_in = atoms.shape
     flops = 2 * count * width * (2 * width_in + 5 * edges)
     fixed = lambda *shape: pl.BlockSpec(shape, lambda i: (0,) * len(shape))
-    halves = [((count // 2, width), F32)] * 3 + [((count // 2, width), BF16)] * 3
+    sums_shape = (chips, count // chips, width)
+    node_shape = (chips, count // 2 // chips, width)
+    halves = [(sums_shape, F32), (sums_shape, BF16), (node_shape, F32), (node_shape, BF16)]
     outs = halves + [((2 * width_in, width), BF16)]
     steps = edges // tile
     return pl.pallas_call(
-        functools.partial(edge_kernel, chips, parts),
+        functools.partial(edge_kernel, chips),
         grid=(steps + 1,),
         out_shape=[jax.ShapeDtypeStruct(shape, kind) for shape, kind in outs],
         in_specs=[
@@ -372,10 +414,6 @@
     )(place, gather, sums, radial, scaled, atoms, earlier, *blocks)
 
 
-def after(x, *others):
-    return lax.optimization_barrier((x, *others))[0]
-
-
 def shards(systems, ways, atoms, cotangent, experts, radial, coef, source, target):
     chips = ways // 2
     me_sys = lax.axis_index("sys")
@@ -399,70 +437,61 @@
     def both_cores(blocks):
         return blocks + [swap(block) for block in blocks]
 
-    merged = [merge_part(place, coef, experts, systems, parts[0])]
-    joined = (atoms, cotangent, merged[0][0])
-    features, *second = merge_part(place, coef, experts, systems, parts[1], joined)
-    merged.append(second)
-    features = both_cores([features] + [shift(features, k) for k in range(1, chips)])
+    merged = merge_parts(place, coef, experts, parts)
+    pair = jnp.concatenate([atoms, cotangent], axis=0)
+    features = both_cores([pair] + [shift(pair, k) for k in range(1, chips)])
 
     at = jnp.arange(ways * own, dtype=jnp.int32)
-    side, back, offset = at // (chips * own), at // own % chips, at % own
-    order = (2 * ((chip - back + chips) % chips) + (core ^ side)) * own + offset
+    side, z, offset = at // (chips * own), at // own % chips, at % own
+    order = (2 * z + (core ^ side)) * own + offset
     ends = jnp.concatenate([source, target])
-    hot_gather, hot_sum, hot_token = hot_ends(ends.T, ends, order, second[0], tile)
-    all_atoms, scaled, scaled_token = scaled_edges(hot_gather, radial[0], features, tile)
+    hot_gather, hot_sum, hot_token = hot_ends(ends.T, ends, order, pair, tile)
+    all_atoms, scaled, scaled_token = scaled_edges(place, hot_gather, radial[0], features, tile)
     own_cols = lax.dynamic_slice_in_dim(all_atoms, (me_edge % chips) * depth, depth, 1).T
 
+    total = merged[0] + hot_token[0, 0]
+    for k in range(1, systems):
+        total = total + across(merged[k], k).astype(F32)
+    held = total.astype(BF16)
     blocks = []
-    for h in range(len(parts)):
-        total = merged[h][0] + (hot_token[0, 0] if h == 0 else 0.0)
-        for k in range(1, systems):
-            total = total + across(merged[h][k], k).astype(F32)
-        held = total.astype(BF16)
-        for k in range(chips):
-            if h and k == chips - 1:
-                held = held + scaled_token[0, 0].astype(BF16)
-            if k:
-                held = shift(held, 1)
-            blocks += [held, swap(held)]
-
-    *halves, weight = edge_sums(
-        chips, parts, place, hot_gather, hot_sum, radial[0], scaled, all_atoms, own_cols, blocks, tile
+    for k in range(chips):
+        if k == chips - 1:
+            held = held + scaled_token[0, 0].astype(BF16)
+        if k:
+            held = shift(held, 1)
+        blocks += [held, swap(held)]
+
+    kept, sent, node_kept, node_sent, weight = edge_sums(
+        chips, place, hot_gather, hot_sum, radial[0], scaled, all_atoms, own_cols, blocks, tile
     )
 
-    def slots(i):
-        kept, other = halves[i], swap(halves[3 + i])
-        cut = lambda x, k: x[k * own : (k + 1) * own]
-        return [cut(kept, k) + cut(other, k).astype(F32) for k in range(chips)]
-
-    def ring_sum(terms):
-        total = terms[1 % chips]
-        for t in range(1, chips):
-            total = shift(total.astype(BF16), 1).astype(F32) + terms[(t + 1) % chips]
-        return total
-
-    sums = [ring_sum(slots(i)).astype(BF16) for i in range(2)]
-
-    def half_for(k):
-        return jnp.where((chip + k) % chips < chips // 2, sums[0], sums[1])
-
-    picked = both_cores([half_for(0)] + [shift(half_for(k), k) for k in range(1, chips)])
-    grad, send = merged_grads(own_cols, picked)
-
+    def reduce(kept, other, zero):
+        terms = [kept[k] + other[k].astype(F32) + zero for k in range(chips)]
+        total = terms[0]
+        for k in range(1, chips):
+            total = total + shift(terms[k].astype(BF16), k).astype(F32)
+        return total.astype(BF16)
+
+    shares = chips // 2
+    sums = reduce(kept, swap(sent), 0.0)
+
+    def share(x, j):
+        to = [z // shares * shares + (z + j) % shares for z in range(chips)]
+        return lax.ppermute(x, "edge", [(2 * z + c, 2 * to[z] + c) for z in range(chips) for c in range(2)])
+
+    picked = both_cores([sums] + [share(sums, j) for j in range(1, shares)])
+    grad, send, grad_token = merged_grads(place, own_cols, picked)
     grads = [grad] + [across(send, k) for k in range(1, systems)]
     expert_grad = expert_grads(place, coef, grads, experts.shape, parts)
 
-    node = slots(2)
-    total = node[0]
-    for k in range(1, chips):
-        total = total + shift(after(node[k].astype(BF16), *picked), chips - k).astype(F32)
-
-    over = (((1,), (1,)), ((), ()))
-    atom_grad = lax.dot_general(sums[0], weight[:width], over, preferred_element_type=F32)
-    atom_grad = atom_grad + lax.dot_general(
-        sums[1], weight[width:], over, preferred_element_type=F32
-    )
-    return total.astype(BF16)[None], atom_grad[None], expert_grad
+    atom_grad = 0.0
+    for flip, term in enumerate(atom_grads(chips, place, sums, weight)):
+        to = [2 * (z % shares) + (z // shares ^ flip) for z in range(chips)]
+        pairs = [(2 * z + c, 2 * to[z] + c) for z in range(chips) for c in range(2)]
+        atom_grad = atom_grad + lax.ppermute(term, "edge", pairs).astype(F32)
+
+    node = reduce(node_kept, swap(node_sent), grad_token[0, 0])
+    return node[None], atom_grad[None], expert_grad
 
 
 def solution(mesh):

time: 182 us -> 177 us (0.973)
  waiting for transfers between devices: 65.5 us -> 86.1 us
  starting transfers between devices: 36.6 us -> 23.1 us
  Pallas kernels: 52.1 us -> 45.6 us
  other arithmetic: 16.7 us -> 11 us
  local copies, waits for them, and re-layouts: 6.77 us -> 9.27 us
  matrix products: 1.92 us -> 0 us
    ppermute x21 -> x12, starting transfers between devices: 23.1 us -> 10.3 us  [shift(): lax.ppermute(x, 'edge', [(e, (e + 2 * k) % ways) for e in range(ways)])]
    ppermute x21 -> x12, waiting for transfers between devices: 51.4 us -> 61.9 us  [shift(): lax.ppermute(x, 'edge', [(e, (e + 2 * k) % ways) for e in range(ways)])]
    ppermute x0 -> x3, waiting for transfers between devices: none -> 10.4 us  [the longest x1 6.45 us: share(): lax.ppermute(x, 'edge', [(2 * z + c, 2 * to[z] + c) for z in range(chips)...]
    pallas_call x3, Pallas kernels: 35.2 us -> 28.2 us  [the longest x1 22.3 us: edge_sums(): pl.pallas_call(functools.partial(edge_kernel, chips), grid=(steps + 1,),...]
    convert_element_type x7 -> x3, other arithmetic: 8.77 us -> 3.32 us  [the longest x2 2.16 us: reduce(): total = total + shift(terms[k].astype(BF16), k).astype(F32)]
    ppermute x0 -> x3, starting transfers between devices: none -> 2.49 us  [the longest x2 2.42 us: shards(): atom_grad = atom_grad + lax.ppermute(term, 'edge', pairs).astype(F32)]
    ppermute x9 -> x6, starting transfers between devices: 10.5 us -> 8.08 us  [across(): return lax.ppermute(x, 'sys', [(s, s ^ k) for s in range(systems)])]
    ppermute x9 -> x6, waiting for transfers between devices: 12.5 us -> 10.2 us  [across(): return lax.ppermute(x, 'sys', [(s, s ^ k) for s in range(systems)])]
  transfers between devices with their start and end apart: 49 -> 33, of which waited for: 16 -> 15; matrix products, arithmetic and copies ran while one was open for 13% -> 8% of each run, Pallas kernels for 8% -> 9%
where the time goes in v7:
time: 177 us; the launch traced here: 176 us
  waiting for transfers between devices  86.1 us (49%)
  Pallas kernels  45.6 us (26%)
  starting transfers between devices  23.1 us (13%)
  other arithmetic  11 us (6%)
  local copies, waits for them, and re-layouts  9.27 us (5%)
    ppermute x12, waiting for transfers between devices, shift(): lax.ppermute(x, 'edge', [(e, (e + 2 * k) % ways) for e in range(ways)])  61.9 us
    pallas_call x1, Pallas kernels, edge_sums(): pl.pallas_call(functools.partial(edge_kernel, chips), grid=(steps + 1,),...  22.3 us
    ppermute x12, starting transfers between devices, shift(): lax.ppermute(x, 'edge', [(e, (e + 2 * k) % ways) for e in range(ways)])  10.3 us
    ppermute x6, waiting for transfers between devices, across(): return lax.ppermute(x, 'sys', [(s, s ^ k) for s in range(systems)])  10.2 us
    ppermute x6, starting transfers between devices, across(): return lax.ppermute(x, 'sys', [(s, s ^ k) for s in range(systems)])  8.08 us
    pallas_call x1, Pallas kernels, scaled_edges(): pl.pallas_call(functools.partial(scale_kernel, slots), grid=(edges // til...  7.96 us
    ppermute x1, waiting for transfers between devices, share(): lax.ppermute(x, 'edge', [(2 * z + c, 2 * to[z] + c) for z in range(chips)...  6.45 us
    pallas_call x1, Pallas kernels, hot_ends(): pl.pallas_call(hot_kernel, grid=(edges // tile,), out_shape=[jax.ShapeDty...  5.67 us
  transfers between devices with their start and end apart: 33, of which 15 were waited for; matrix products, arithmetic and copies ran while one was open for 8% of the time, Pallas kernels for 9%

profile of v7, /device:TPU:0, one launch (start us, length us, event | category | flops | bytes accessed | tf_op | source)
XLA Modules:
  0.0 176.2 jit_solution(9705135891671447690)
XLA Ops:
  0.6 0.6 pad_add_fusion.1.place_ref
  1.3 4.1 %merge_parts.1 = (f32[224,896]{1,0:T(8,128)}, bf16[224,896]{1,0:T(8,128)(2,1)}, bf16[224,896]{1,0:T(8,128)(2,1)}, bf16[224,896]{1,0:T(8,128)(2,1)}) custom-call(s32[3]{0:T(128)} %pad_add_fusion.1.place_ref, f32[4,16]{1,0:T(4,128)} %coef_ref.3, bf16[4,224,896]{2,1,0:T(8,128)(2,1)} %experts_ref.1), custom_call_target="tpu_custom_call" | custom-call | tf_op jit(solution)/shard_map/merge_parts/pallas_call | solution.py:70
  5.4 3.0 %collective-permute-start.7 = (bf16[224,896]{1,0:T(8,128)(2,1)}, bf16[224,896]{1,0:T(8,128)(2,1)S(1)}, u32[]{:S(2)}, u32[]{:S(2)}) collective-permute-start(bf16[224,896]{1,0:T(8,128)(2,1)} %get-tuple-element.29), channel_id=1, source_target_pairs={{0,8},{8,0},{16,24},{24,16},{1,9},{9,1},{17,25},{25,17},{2,10},{10... | collective-permute-start | bytes 1204232 | tf_op jit(solution)/shard_map/ppermute | solution.py:429
  8.4 1.5 collective-permute-start.8
  9.9 1.3 pad_add_fusion
  11.3 0.6 fusion.28.across_ref
  11.9 1.3 copy.13.cols_ref
  13.2 0.9 constant_dynamic-update-slice_fusion.1
  14.2 0.9 constant_dynamic-update-slice_fusion._.refs_0_
  15.1 0.8 fusion.13.down_ref
  15.9 5.7 %hot_ends.1 = (bf16[2048,1024]{1,0:T(8,128)(2,1)}, bf16[1024,2048]{1,0:T(8,128)(2,1)}, f32[8,128]{1,0:T(8,128)}) custom-call(s32[2048,2]{1,0:T(8,128)} %copy.13.cols_ref, s32[2,2048]{1,0:T(2,128)} %get-tuple-element.49.rows_ref, s32[1,512]{1,0:T(1,128)} %fusion.28.across_ref, s32[512,1]{1,0:T(8,128)} %fusion.13.down_ref, bf16[2,64,896]{2,1,0:T(8,128)(2,1)} %copy-done.4), custom_call_target="tpu_custom_call" | custom-call | flops 16777216 | bytes 8388608 | tf_op jit(solution)/shard_map/hot_ends/pallas_call | solution.py:201
  21.5 1.2 slice.58
  22.7 5.2 %collective-permute-done.8 = bf16[224,896]{1,0:T(8,128)(2,1)S(1)} collective-permute-done((bf16[224,896]{1,0:T(8,128)(2,1)}, bf16[224,896]{1,0:T(8,128)(2,1)S(1)}, u32[]{:S(2)}, u32[]{:S(2)}) %collective-permute-start.8) | collective-permute-done | bytes 401440 | tf_op jit(solution)/shard_map/ppermute | solution.py:429
  28.0 0.9 add_convert_fusion.refs_0_
  28.8 1.6 collective-permute-start.11
  30.5 2.2 %collective-permute-start.2 = (bf16[2,64,896]{2,1,0:T(8,128)(2,1)}, bf16[2,64,896]{2,1,0:T(8,128)(2,1)S(1)}, u32[]{:S(2)}, u32[]{:S(2)}) collective-permute-start(bf16[2,64,896]{2,1,0:T(8,128)(2,1)} %copy-done.4), channel_id=1, source_target_pairs={{0,6},{1,7},{2,0},{3,1},{4,2},{5,3},{6,4},{7,5},{8,14},{9,15},{10,... | collective-permute-start | bytes 688136 | tf_op jit(solution)/shard_map/ppermute | solution.py:435
  32.7 0.8 collective-permute-start.1
  33.5 1.6 collective-permute-start
  35.1 10.2 %collective-permute-done.2.refs_3_ = bf16[2,64,896]{2,1,0:T(8,128)(2,1)S(1)} collective-permute-done((bf16[2,64,896]{2,1,0:T(8,128)(2,1)}, bf16[2,64,896]{2,1,0:T(8,128)(2,1)S(1)}, u32[]{:S(2)}, u32[]{:S(2)}) %collective-permute-start.2) | collective-permute-done | bytes 229408 | tf_op jit(solution)/shard_map/ppermute | solution.py:435
  45.3 15.1 %collective-permute-done.1.refs_2_ = bf16[2,64,896]{2,1,0:T(8,128)(2,1)S(1)} collective-permute-done((bf16[2,64,896]{2,1,0:T(8,128)(2,1)}, bf16[2,64,896]{2,1,0:T(8,128)(2,1)S(1)}, u32[]{:S(2)}, u32[]{:S(2)}) %collective-permute-start.1) | collective-permute-done | bytes 229408 | tf_op jit(solution)/shard_map/ppermute | solution.py:435
  60.4 0.5 collective-permute-start.4
  60.9 0.9 collective-permute-done.5.refs_6_
  61.9 0.3 collective-permute-done.4.refs_5_
  62.2 0.3 copy-done.14
  62.5 0.3 copy-done.15
  62.9 8.0 %scaled_edges.1 = (bf16[512,896]{1,0:T(8,128)(2,1)}, bf16[2048,896]{1,0:T(8,128)(2,1)}, f32[8,128]{1,0:T(8,128)}) custom-call(s32[3]{0:T(128)} %pad_add_fusion.1.place_ref, bf16[2048,1024]{1,0:T(8,128)(2,1)} %get-tuple-element.23.gather_ref, bf16[2048,896]{1,0:T(8,128)(2,1)} %bitcast.45, bf16[2,64,896]{2,1,0:T(8,128)(2,1)} %copy-done.4, ...), custom_call_target="tpu_custom_call" | custom-call | flops 1879048192 | bytes 11010048 | tf_op jit(solution)/shard_map/scaled_edges/pallas_call | solution.py:263
  70.8 0.7 convert.3
  71.5 0.5 slice.59
  72.0 1.9 %collective-permute-done.13.refs_4_ = bf16[224,896]{1,0:T(8,128)(2,1)S(1)} collective-permute-done((bf16[224,896]{1,0:T(8,128)(2,1)S(1)}, bf16[224,896]{1,0:T(8,128)(2,1)S(1)}, u32[]{:S(2)}, u32[]{:S(2)}) %collective-permute-start.13) | collective-permute-done | bytes 401440 | tf_op jit(solution)/shard_map/ppermute | solution.py:435
  74.0 0.7 broadcast_add_fusion
  74.8 0.5 collective-permute-start.12
  75.3 0.1 collective-permute-start.14
  75.4 11.6 %collective-permute-done.15.refs_6_ = bf16[224,896]{1,0:T(8,128)(2,1)S(1)} collective-permute-done((bf16[224,896]{1,0:T(8,128)(2,1)S(1)}, bf16[224,896]{1,0:T(8,128)(2,1)S(1)}, u32[]{:S(2)}, u32[]{:S(2)}) %collective-permute-start.15) | collective-permute-done | bytes 401440 | tf_op jit(solution)/shard_map/ppermute | solution.py:435
  87.0 1.6 copy.14
  88.6 0.7 dynamic-slice_bitcast_fusion._.cols_ref
  89.3 0.7 copy-done.19
  90.0 0.2 copy-done.20
  90.2 22.3 %edge_sums.1 = (f32[4,128,896]{2,1,0:T(8,128)}, bf16[4,128,896]{2,1,0:T(8,128)(2,1)}, f32[4,64,896]{2,1,0:T(8,128)}, bf16[4,64,896]{2,1,0:T(8,128)(2,1)}, bf16[1792,896]{1,0:T(8,128)(2,1)}) custom-call(s32[3]{0:T(128)} %pad_add_fusion.1.place_ref, bf16[2048,1024]{1,0:T(8,128)(2,1)} %get-tuple-element.23.gather_ref, ...), custom_call_target="tpu_custom_call" | custom-call | flops 11039408128 | bytes 15728640 | tf_op jit(solution)/shard_map/edge_sums/pallas_call | solution.py:385
  112.5 0.4 collective-permute-start.18
  112.9 2.3 %collective-permute-done.18 = bf16[4,128,896]{2,1,0:T(8,128)(2,1)S(1)} collective-permute-done((bf16[4,128,896]{2,1,0:T(8,128)(2,1)}, bf16[4,128,896]{2,1,0:T(8,128)(2,1)S(1)}, u32[]{:S(2)}, u32[]{:S(2)}) %collective-permute-start.18) | collective-permute-done | bytes 917536 | tf_op jit(solution)/shard_map/ppermute | solution.py:432
  115.2 1.4 fusion.18
  116.7 3.8 %collective-permute-start.21 = (bf16[128,896]{1,0:T(8,128)(2,1)S(1)}, bf16[128,896]{1,0:T(8,128)(2,1)S(1)}, u32[]{:S(2)}, u32[]{:S(2)}) collective-permute-start(bf16[128,896]{1,0:T(8,128)(2,1)S(1)} %get-tuple-element.44), channel_id=1, source_target_pairs={{0,6},{1,7},{2,0},{3,1},{4,2},{5,3},{6,4},{7,5},{8,14},{9,15},{10,... | collective-permute-start | bytes 688136 | tf_op jit(solution)/shard_map/ppermute | solution.py:435
  120.6 6.4 %collective-permute-done.19 = bf16[128,896]{1,0:T(8,128)(2,1)S(1)} collective-permute-done((bf16[128,896]{1,0:T(8,128)(2,1)S(1)}, bf16[128,896]{1,0:T(8,128)(2,1)S(1)}, u32[]{:S(2)}, u32[]{:S(2)}) %collective-permute-start.19) | collective-permute-done | bytes 229408 | tf_op jit(solution)/shard_map/ppermute | solution.py:435
  127.0 6.5 %collective-permute-done.21 = bf16[128,896]{1,0:T(8,128)(2,1)S(1)} collective-permute-done((bf16[128,896]{1,0:T(8,128)(2,1)S(1)}, bf16[128,896]{1,0:T(8,128)(2,1)S(1)}, u32[]{:S(2)}, u32[]{:S(2)}) %collective-permute-start.21) | collective-permute-done | bytes 229408 | tf_op jit(solution)/shard_map/ppermute | solution.py:435
  133.5 4.0 %collective-permute-done.20 = bf16[128,896]{1,0:T(8,128)(2,1)S(1)} collective-permute-done((bf16[128,896]{1,0:T(8,128)(2,1)S(1)}, bf16[128,896]{1,0:T(8,128)(2,1)S(1)}, u32[]{:S(2)}, u32[]{:S(2)}) %collective-permute-start.20) | collective-permute-done | bytes 229408 | tf_op jit(solution)/shard_map/ppermute | solution.py:435
  137.5 1.2 fusion.6.refs_0_.sums_ref
  138.9 0.5 collective-permute-start.23
  139.4 6.5 %collective-permute-done.22.refs_1_ = bf16[128,896]{1,0:T(8,128)(2,1)S(1)} collective-permute-done((bf16[128,896]{1,0:T(8,128)(2,1)S(1)}, bf16[128,896]{1,0:T(8,128)(2,1)S(1)}, u32[]{:S(2)}, u32[]{:S(2)}) %collective-permute-start.22) | collective-permute-done | bytes 229408 | tf_op jit(solution)/shard_map/ppermute | solution.py:480
  145.8 1.8 %atom_grads.1 = (bf16[64,896]{1,0:T(8,128)(2,1)S(1)}, bf16[64,896]{1,0:T(8,128)(2,1)S(1)}) custom-call(s32[3]{0:T(128)S(1)} %copy-done.2, bf16[128,896]{1,0:T(8,128)(2,1)S(1)} %fusion.6.refs_0_.sums_ref, bf16[1792,896]{1,0:T(8,128)(2,1)S(1)} %copy-done), custom_call_target="tpu_custom_call" | custom-call | flops 205520896 | bytes 1605632 | tf_op jit(solution)/shard_map/atom_grads/pallas_call | solution.py:131
  147.7 0.7 collective-permute-start.28
  148.4 1.8 collective-permute-start.29
  150.1 1.0 merged_grads.1
  151.2 0.5 slice.70
  151.7 0.7 fusion.24
  152.4 0.1 collective-permute-start.25
  152.5 1.5 collective-permute-start.32
  154.0 1.5 collective-permute-start.31
  155.5 0.6 collective-permute-start.30
  156.0 3.9 %collective-permute-done.29 = bf16[64,896]{1,0:T(8,128)(2,1)S(1)} collective-permute-done((bf16[64,896]{1,0:T(8,128)(2,1)S(1)}, bf16[64,896]{1,0:T(8,128)(2,1)S(1)}, u32[]{:S(2)}, u32[]{:S(2)}) %collective-permute-start.29) | collective-permute-done | bytes 114720 | tf_op jit(solution)/shard_map/ppermute | solution.py:491
  160.1 0.7 add_bitcast_fusion
  160.8 6.2 %collective-permute-done.27 = bf16[64,896]{1,0:T(8,128)(2,1)S(1)} collective-permute-done((bf16[64,896]{1,0:T(8,128)(2,1)S(1)}, bf16[64,896]{1,0:T(8,128)(2,1)S(1)}, u32[]{:S(2)}, u32[]{:S(2)}) %collective-permute-start.27) | collective-permute-done | bytes 114720 | tf_op jit(solution)/shard_map/ppermute | solution.py:435
  167.0 1.4 fusion.27
  168.4 5.0 %collective-permute-done.31.refs_2_ = bf16[224,896]{1,0:T(8,128)(2,1)S(1)} collective-permute-done((bf16[224,896]{1,0:T(8,128)(2,1)S(1)}, bf16[224,896]{1,0:T(8,128)(2,1)S(1)}, u32[]{:S(2)}, u32[]{:S(2)}) %collective-permute-start.31) | collective-permute-done | bytes 401440 | tf_op jit(solution)/shard_map/ppermute | solution.py:429
  173.3 2.8 %expert_grads.1 = f32[4,224,896]{2,1,0:T(8,128)} custom-call(s32[3]{0:T(128)S(1)} %copy-done.2, f32[4,16]{1,0:T(4,128)S(1)} %copy-done.3, f32[224,896]{1,0:T(8,128)S(1)} %get-tuple-element.41.refs_0_, bf16[224,896]{1,0:T(8,128)(2,1)S(1)} %collective-permute-done.30.refs_1_, bf16[224,896]{1,0:T(8,128)(2,1)S(1)} %collective-permute-done.31.refs_2_, ...), custom_call_target="tpu_custom_call" | custom-call | tf_op jit(solution)/shard_map/expert_grads/pallas_call | solution.py:174
  (71 shorter events, 0.6 us)
Async XLA Ops:
  5.4 22.6 %copy-start.6 = (f32[224,896]{1,0:T(8,128)S(1)}, f32[224,896]{1,0:T(8,128)}, u32[]{:S(2)}) copy-start(f32[224,896]{1,0:T(8,128)} %get-tuple-element.27) | copy-start | bytes 2408452
  5.4 17.3 %collective-permute-start.7 = (bf16[224,896]{1,0:T(8,128)(2,1)}, bf16[224,896]{1,0:T(8,128)(2,1)S(1)}, u32[]{:S(2)}, u32[]{:S(2)}) collective-permute-start(bf16[224,896]{1,0:T(8,128)(2,1)} %get-tuple-element.29), channel_id=1, source_target_pairs={{0,8},{8,0},{16,24},{24,16},{1,9},{9,1},{17,25},{25,17},{2,10},{10... | collective-permute-start | bytes 1204232 | tf_op jit(solution)/shard_map/ppermute | solution.py:429
  8.4 19.6 %collective-permute-start.8 = (bf16[224,896]{1,0:T(8,128)(2,1)}, bf16[224,896]{1,0:T(8,128)(2,1)S(1)}, u32[]{:S(2)}, u32[]{:S(2)}) collective-permute-start(bf16[224,896]{1,0:T(8,128)(2,1)} %get-tuple-element.30), channel_id=1, source_target_pairs={{0,16},{8,24},{16,0},{24,8},{1,17},{9,25},{17,1},{25,9},{2,18},{10... | collective-permute-start | bytes 1204232 | tf_op jit(solution)/shard_map/ppermute | solution.py:429
  9.9 18.0 %collective-permute-start.9 = (bf16[224,896]{1,0:T(8,128)(2,1)}, bf16[224,896]{1,0:T(8,128)(2,1)S(1)}, u32[]{:S(2)}, u32[]{:S(2)}) collective-permute-start(bf16[224,896]{1,0:T(8,128)(2,1)} %get-tuple-element.31), channel_id=1, source_target_pairs={{0,24},{8,16},{16,8},{24,0},{1,25},{9,17},{17,9},{25,1},{2,26},{10... | collective-permute-start | bytes 1204232 | tf_op jit(solution)/shard_map/ppermute | solution.py:429
  15.1 0.8 copy-start.4
  28.8 45.9 %copy-start.8 = (bf16[224,896]{1,0:T(8,128)(2,1)}, bf16[224,896]{1,0:T(8,128)(2,1)S(1)}, u32[]{:S(2)}) copy-start(bf16[224,896]{1,0:T(8,128)(2,1)S(1)} %add_convert_fusion.refs_0_) | copy-start | bytes 1204228
  28.8 32.0 %collective-permute-start.11 = (bf16[224,896]{1,0:T(8,128)(2,1)S(1)}, bf16[224,896]{1,0:T(8,128)(2,1)S(1)}, u32[]{:S(2)}, u32[]{:S(2)}) collective-permute-start(bf16[224,896]{1,0:T(8,128)(2,1)S(1)} %add_convert_fusion.refs_0_), channel_id=1, source_target_pairs={{0,2},{1,3},{2,4},{3,5},{4,6},{5,7},{6,0},{7,1},{8,10},{9,11},{10,... | collective-permute-start | bytes 1204232 | tf_op jit(solution)/shard_map/ppermute | solution.py:435
  30.5 14.8 %collective-permute-start.2 = (bf16[2,64,896]{2,1,0:T(8,128)(2,1)}, bf16[2,64,896]{2,1,0:T(8,128)(2,1)S(1)}, u32[]{:S(2)}, u32[]{:S(2)}) collective-permute-start(bf16[2,64,896]{2,1,0:T(8,128)(2,1)} %copy-done.4), channel_id=1, source_target_pairs={{0,6},{1,7},{2,0},{3,1},{4,2},{5,3},{6,4},{7,5},{8,14},{9,15},{10,... | collective-permute-start | bytes 688136 | tf_op jit(solution)/shard_map/ppermute | solution.py:435
  32.7 27.6 %collective-permute-start.1 = (bf16[2,64,896]{2,1,0:T(8,128)(2,1)}, bf16[2,64,896]{2,1,0:T(8,128)(2,1)S(1)}, u32[]{:S(2)}, u32[]{:S(2)}) collective-permute-start(bf16[2,64,896]{2,1,0:T(8,128)(2,1)} %copy-done.4), channel_id=1, source_target_pairs={{0,4},{1,5},{2,6},{3,7},{4,0},{5,1},{6,2},{7,3},{8,12},{9,13},{10,... | collective-permute-start | bytes 688136 | tf_op jit(solution)/shard_map/ppermute | solution.py:435
  33.5 26.9 %collective-permute-start = (bf16[2,64,896]{2,1,0:T(8,128)(2,1)}, bf16[2,64,896]{2,1,0:T(8,128)(2,1)S(1)}, u32[]{:S(2)}, u32[]{:S(2)}) collective-permute-start(bf16[2,64,896]{2,1,0:T(8,128)(2,1)} %copy-done.4), channel_id=1, source_target_pairs={{0,2},{1,3},{2,4},{3,5},{4,6},{5,7},{6,0},{7,1},{8,10},{9,11},{10,... | collective-permute-start | bytes 688136 | tf_op jit(solution)/shard_map/ppermute | solution.py:435
  35.1 25.8 %collective-permute-start.3 = (bf16[2,64,896]{2,1,0:T(8,128)(2,1)}, bf16[2,64,896]{2,1,0:T(8,128)(2,1)S(1)}, u32[]{:S(2)}, u32[]{:S(2)}) collective-permute-start(bf16[2,64,896]{2,1,0:T(8,128)(2,1)} %copy-done.4), channel_id=1, source_target_pairs={{0,1},{1,0},{2,3},{3,2},{4,5},{5,4},{6,7},{7,6},{8,9},{9,8},{10,11... | collective-permute-start | bytes 688136 | tf_op jit(solution)/shard_map/ppermute | solution.py:432
  45.3 16.9 %copy-start.9 = (bf16[2,64,896]{2,1,0:T(8,128)(2,1)}, bf16[2,64,896]{2,1,0:T(8,128)(2,1)S(1)}, u32[]{:S(2)}) copy-start(bf16[2,64,896]{2,1,0:T(8,128)(2,1)S(1)} %collective-permute-done.2.refs_3_) | copy-start | bytes 688132
  45.3 15.6 %collective-permute-start.6 = (bf16[2,64,896]{2,1,0:T(8,128)(2,1)S(1)}, bf16[2,64,896]{2,1,0:T(8,128)(2,1)S(1)}, u32[]{:S(2)}, u32[]{:S(2)}) collective-permute-start(bf16[2,64,896]{2,1,0:T(8,128)(2,1)S(1)} %collective-permute-done.2.refs_3_), channel_id=1, source_target_pairs={{0,1},{1,0},{2,3},{3,2},{4,5},{5,4},{6,7},{7,6},{8,9},{9,8},{10,11... | collective-permute-start | bytes 688136 | tf_op jit(solution)/shard_map/ppermute | solution.py:432
  60.4 1.8 %copy-start.10 = (bf16[2,64,896]{2,1,0:T(8,128)(2,1)}, bf16[2,64,896]{2,1,0:T(8,128)(2,1)S(1)}, u32[]{:S(2)}) copy-start(bf16[2,64,896]{2,1,0:T(8,128)(2,1)S(1)} %collective-permute-done.1.refs_2_) | copy-start | bytes 688132
  60.4 1.5 collective-permute-start.5
  60.4 1.8 %copy-start.11 = (bf16[2,64,896]{2,1,0:T(8,128)(2,1)}, bf16[2,64,896]{2,1,0:T(8,128)(2,1)S(1)}, u32[]{:S(2)}) copy-start(bf16[2,64,896]{2,1,0:T(8,128)(2,1)S(1)} %collective-permute-done.refs_1_) | copy-start | bytes 688132
  60.4 1.8 %collective-permute-start.4 = (bf16[2,64,896]{2,1,0:T(8,128)(2,1)S(1)}, bf16[2,64,896]{2,1,0:T(8,128)(2,1)S(1)}, u32[]{:S(2)}, u32[]{:S(2)}) collective-permute-start(bf16[2,64,896]{2,1,0:T(8,128)(2,1)S(1)} %collective-permute-done.refs_1_), channel_id=1, source_target_pairs={{0,1},{1,0},{2,3},{3,2},{4,5},{5,4},{6,7},{7,6},{8,9},{9,8},{10,11... | collective-permute-start | bytes 688136 | tf_op jit(solution)/shard_map/ppermute | solution.py:432
  60.9 28.4 %copy-start.17 = (bf16[224,896]{1,0:T(8,128)(2,1)}, bf16[224,896]{1,0:T(8,128)(2,1)S(1)}, u32[]{:S(2)}) copy-start(bf16[224,896]{1,0:T(8,128)(2,1)S(1)} %collective-permute-done.11.refs_2_) | copy-start | bytes 1204228
  60.9 13.1 %collective-permute-start.13 = (bf16[224,896]{1,0:T(8,128)(2,1)S(1)}, bf16[224,896]{1,0:T(8,128)(2,1)S(1)}, u32[]{:S(2)}, u32[]{:S(2)}) collective-permute-start(bf16[224,896]{1,0:T(8,128)(2,1)S(1)} %collective-permute-done.11.refs_2_), channel_id=1, source_target_pairs={{0,2},{1,3},{2,4},{3,5},{4,6},{5,7},{6,0},{7,1},{8,10},{9,11},{10,... | collective-permute-start | bytes 1204232 | tf_op jit(solution)/shard_map/ppermute | solution.py:435
  60.9 1.3 copy-start.12
  60.9 1.3 copy-start.13
  61.9 0.7 copy-start.14
  62.2 0.7 copy-start.15
  74.0 15.4 %copy-start.7 = (bf16[224,896]{1,0:T(8,128)(2,1)}, bf16[224,896]{1,0:T(8,128)(2,1)S(1)}, u32[]{:S(2)}) copy-start(bf16[224,896]{1,0:T(8,128)(2,1)S(1)} %collective-permute-done.13.refs_4_) | copy-start | bytes 1204228
  74.7 12.3 %collective-permute-start.15 = (bf16[224,896]{1,0:T(8,128)(2,1)S(1)}, bf16[224,896]{1,0:T(8,128)(2,1)S(1)}, u32[]{:S(2)}, u32[]{:S(2)}) collective-permute-start(bf16[224,896]{1,0:T(8,128)(2,1)S(1)} %broadcast_add_fusion), channel_id=1, source_target_pairs={{0,2},{1,3},{2,4},{3,5},{4,6},{5,7},{6,0},{7,1},{8,10},{9,11},{10,... | collective-permute-start | bytes 1204232 | tf_op jit(solution)/shard_map/ppermute | solution.py:435
  74.7 14.5 %collective-permute-start.10 = (bf16[224,896]{1,0:T(8,128)(2,1)S(1)}, bf16[224,896]{1,0:T(8,128)(2,1)S(1)}, u32[]{:S(2)}, u32[]{:S(2)}) collective-permute-start(bf16[224,896]{1,0:T(8,128)(2,1)S(1)} %add_convert_fusion.refs_0_), channel_id=1, source_target_pairs={{0,1},{1,0},{2,3},{3,2},{4,5},{5,4},{6,7},{7,6},{8,9},{9,8},{10,11... | collective-permute-start | bytes 1204232 | tf_op jit(solution)/shard_map/ppermute | solution.py:432
  74.8 14.5 %collective-permute-start.12 = (bf16[224,896]{1,0:T(8,128)(2,1)S(1)}, bf16[224,896]{1,0:T(8,128)(2,1)S(1)}, u32[]{:S(2)}, u32[]{:S(2)}) collective-permute-start(bf16[224,896]{1,0:T(8,128)(2,1)S(1)} %collective-permute-done.11.refs_2_), channel_id=1, source_target_pairs={{0,1},{1,0},{2,3},{3,2},{4,5},{5,4},{6,7},{7,6},{8,9},{9,8},{10,11... | collective-permute-start | bytes 1204232 | tf_op jit(solution)/shard_map/ppermute | solution.py:432
  75.3 14.0 %collective-permute-start.14 = (bf16[224,896]{1,0:T(8,128)(2,1)S(1)}, bf16[224,896]{1,0:T(8,128)(2,1)}, u32[]{:S(2)}, u32[]{:S(2)}) collective-permute-start(bf16[224,896]{1,0:T(8,128)(2,1)S(1)} %collective-permute-done.13.refs_4_), channel_id=1, source_target_pairs={{0,1},{1,0},{2,3},{3,2},{4,5},{5,4},{6,7},{7,6},{8,9},{9,8},{10,11... | collective-permute-start | bytes 1204232 | tf_op jit(solution)/shard_map/ppermute | solution.py:432
  86.9 2.4 %copy-start.18 = (bf16[224,896]{1,0:T(8,128)(2,1)}, bf16[224,896]{1,0:T(8,128)(2,1)S(1)}, u32[]{:S(2)}) copy-start(bf16[224,896]{1,0:T(8,128)(2,1)S(1)} %collective-permute-done.15.refs_6_) | copy-start | bytes 1204228
  87.0 2.4 %collective-permute-start.16 = (bf16[224,896]{1,0:T(8,128)(2,1)S(1)}, bf16[224,896]{1,0:T(8,128)(2,1)}, u32[]{:S(2)}, u32[]{:S(2)}) collective-permute-start(bf16[224,896]{1,0:T(8,128)(2,1)S(1)} %collective-permute-done.15.refs_6_), channel_id=1, source_target_pairs={{0,1},{1,0},{2,3},{3,2},{4,5},{5,4},{6,7},{7,6},{8,9},{9,8},{10,11... | collective-permute-start | bytes 1204232 | tf_op jit(solution)/shard_map/ppermute | solution.py:432
  89.3 0.7 copy-start.19
  89.3 0.9 copy-start.20
  112.4 26.3 %copy-start.16 = (bf16[4,64,896]{2,1,0:T(8,128)(2,1)S(1)}, bf16[4,64,896]{2,1,0:T(8,128)(2,1)}, u32[]{:S(2)}) copy-start(bf16[4,64,896]{2,1,0:T(8,128)(2,1)} %get-tuple-element.34) | copy-start | bytes 1376260
  112.5 33.4 %copy-start = (bf16[1792,896]{1,0:T(8,128)(2,1)S(1)}, bf16[1792,896]{1,0:T(8,128)(2,1)}, u32[]{:S(2)}) copy-start(bf16[1792,896]{1,0:T(8,128)(2,1)} %get-tuple-element.38.weight_hbm) | copy-start | bytes 9633796
  112.5 33.4 %copy-start.2 = (s32[3]{0:T(128)S(1)}, s32[3]{0:T(128)}, u32[]{:S(2)}) copy-start(s32[3]{0:T(128)} %pad_add_fusion.1.place_ref) | copy-start | bytes 40
  112.5 2.7 %collective-permute-start.18 = (bf16[4,128,896]{2,1,0:T(8,128)(2,1)}, bf16[4,128,896]{2,1,0:T(8,128)(2,1)S(1)}, u32[]{:S(2)}, u32[]{:S(2)}) collective-permute-start(bf16[4,128,896]{2,1,0:T(8,128)(2,1)} %get-tuple-element.36), channel_id=1, source_target_pairs={{0,1},{1,0},{2,3},{3,2},{4,5},{5,4},{6,7},{7,6},{8,9},{9,8},{10,11... | collective-permute-start | bytes 2752520 | tf_op jit(solution)/shard_map/ppermute | solution.py:432
  116.7 33.5 %copy-start.1 = (bf16[224,512]{1,0:T(8,128)(2,1)S(1)}, bf16[224,512]{1,0:T(8,128)(2,1)}, u32[]{:S(2)}) copy-start(bf16[224,512]{1,0:T(8,128)(2,1)} %dynamic-slice_bitcast_fusion._.cols_ref) | copy-start | bytes 688132
  116.7 35.0 %copy-start.5 = (f32[4,64,896]{2,1,0:T(8,128)S(1)}, f32[4,64,896]{2,1,0:T(8,128)}, u32[]{:S(2)}) copy-start(f32[4,64,896]{2,1,0:T(8,128)} %get-tuple-element.33) | copy-start | bytes 2752516
  116.7 10.3 %collective-permute-start.19 = (bf16[128,896]{1,0:T(8,128)(2,1)S(1)}, bf16[128,896]{1,0:T(8,128)(2,1)S(1)}, u32[]{:S(2)}, u32[]{:S(2)}) collective-permute-start(bf16[128,896]{1,0:T(8,128)(2,1)S(1)} %get-tuple-element.43), channel_id=1, source_target_pairs={{0,2},{1,3},{2,4},{3,5},{4,6},{5,7},{6,0},{7,1},{8,10},{9,11},{10,... | collective-permute-start | bytes 688136 | tf_op jit(solution)/shard_map/ppermute | solution.py:435
  116.7 16.8 %collective-permute-start.21 = (bf16[128,896]{1,0:T(8,128)(2,1)S(1)}, bf16[128,896]{1,0:T(8,128)(2,1)S(1)}, u32[]{:S(2)}, u32[]{:S(2)}) collective-permute-start(bf16[128,896]{1,0:T(8,128)(2,1)S(1)} %get-tuple-element.44), channel_id=1, source_target_pairs={{0,6},{1,7},{2,0},{3,1},{4,2},{5,3},{6,4},{7,5},{8,14},{9,15},{10,... | collective-permute-start | bytes 688136 | tf_op jit(solution)/shard_map/ppermute | solution.py:435
  120.6 17.0 %collective-permute-start.20 = (bf16[128,896]{1,0:T(8,128)(2,1)S(1)}, bf16[128,896]{1,0:T(8,128)(2,1)S(1)}, u32[]{:S(2)}, u32[]{:S(2)}) collective-permute-start(bf16[128,896]{1,0:T(8,128)(2,1)S(1)} %get-tuple-element.45), channel_id=1, source_target_pairs={{0,4},{1,5},{2,6},{3,7},{4,0},{5,1},{6,2},{7,3},{8,12},{9,13},{10,... | collective-permute-start | bytes 688136 | tf_op jit(solution)/shard_map/ppermute | solution.py:435
  138.7 7.1 %collective-permute-start.22 = (bf16[128,896]{1,0:T(8,128)(2,1)S(1)}, bf16[128,896]{1,0:T(8,128)(2,1)S(1)}, u32[]{:S(2)}, u32[]{:S(2)}) collective-permute-start(bf16[128,896]{1,0:T(8,128)(2,1)S(1)} %fusion.6.refs_0_.sums_ref), channel_id=1, source_target_pairs={{0,2},{1,3},{2,0},{3,1},{4,6},{5,7},{6,4},{7,5},{8,10},{9,11},{10,... | collective-permute-start | bytes 688136 | tf_op jit(solution)/shard_map/ppermute | solution.py:480
  138.8 12.9 %collective-permute-start.17 = (bf16[4,64,896]{2,1,0:T(8,128)(2,1)S(1)}, bf16[4,64,896]{2,1,0:T(8,128)(2,1)S(1)}, u32[]{:S(2)}, u32[]{:S(2)}) collective-permute-start(bf16[4,64,896]{2,1,0:T(8,128)(2,1)S(1)} %copy-done.16), channel_id=1, source_target_pairs={{0,1},{1,0},{2,3},{3,2},{4,5},{5,4},{6,7},{7,6},{8,9},{9,8},{10,11... | collective-permute-start | bytes 1376264 | tf_op jit(solution)/shard_map/ppermute | solution.py:432
  138.9 11.2 %collective-permute-start.23 = (bf16[128,896]{1,0:T(8,128)(2,1)S(1)}, bf16[128,896]{1,0:T(8,128)(2,1)S(1)}, u32[]{:S(2)}, u32[]{:S(2)}) collective-permute-start(bf16[128,896]{1,0:T(8,128)(2,1)S(1)} %fusion.6.refs_0_.sums_ref), channel_id=1, source_target_pairs={{0,1},{1,0},{2,3},{3,2},{4,5},{5,4},{6,7},{7,6},{8,9},{9,8},{10,11... | collective-permute-start | bytes 688136 | tf_op jit(solution)/shard_map/ppermute | solution.py:432
  145.8 4.3 %collective-permute-start.24 = (bf16[128,896]{1,0:T(8,128)(2,1)S(1)}, bf16[128,896]{1,0:T(8,128)(2,1)S(1)}, u32[]{:S(2)}, u32[]{:S(2)}) collective-permute-start(bf16[128,896]{1,0:T(8,128)(2,1)S(1)} %collective-permute-done.22.refs_1_), channel_id=1, source_target_pairs={{0,1},{1,0},{2,3},{3,2},{4,5},{5,4},{6,7},{7,6},{8,9},{9,8},{10,11... | collective-permute-start | bytes 688136 | tf_op jit(solution)/shard_map/ppermute | solution.py:432
  145.8 27.5 %copy-start.3 = (f32[4,16]{1,0:T(4,128)S(1)}, f32[4,16]{1,0:T(4,128)}, u32[]{:S(2)}) copy-start(f32[4,16]{1,0:T(4,128)} %coef_ref.3) | copy-start | bytes 772
  147.7 7.8 %collective-permute-start.28 = (bf16[64,896]{1,0:T(8,128)(2,1)S(1)}, bf16[64,896]{1,0:T(8,128)(2,1)S(1)}, u32[]{:S(2)}, u32[]{:S(2)}) collective-permute-start(bf16[64,896]{1,0:T(8,128)(2,1)S(1)} %get-tuple-element.39), channel_id=1, source_target_pairs={{0,0},{1,1},{2,4},{3,5},{4,2},{5,3},{6,6},{7,7},{8,8},{9,9},{10,12... | collective-permute-start | bytes 344072 | tf_op jit(solution)/shard_map/ppermute | solution.py:491
  148.4 11.6 %collective-permute-start.29 = (bf16[64,896]{1,0:T(8,128)(2,1)S(1)}, bf16[64,896]{1,0:T(8,128)(2,1)S(1)}, u32[]{:S(2)}, u32[]{:S(2)}) collective-permute-start(bf16[64,896]{1,0:T(8,128)(2,1)S(1)} %get-tuple-element.40), channel_id=1, source_target_pairs={{0,2},{1,3},{2,6},{3,7},{4,0},{5,1},{6,4},{7,5},{8,10},{9,11},{10,... | collective-permute-start | bytes 344072 | tf_op jit(solution)/shard_map/ppermute | solution.py:491
  152.4 7.6 %collective-permute-start.25 = (bf16[64,896]{1,0:T(8,128)(2,1)S(1)}, bf16[64,896]{1,0:T(8,128)(2,1)S(1)}, u32[]{:S(2)}, u32[]{:S(2)}) collective-permute-start(bf16[64,896]{1,0:T(8,128)(2,1)S(1)} %get-tuple-element.46), channel_id=1, source_target_pairs={{0,2},{1,3},{2,4},{3,5},{4,6},{5,7},{6,0},{7,1},{8,10},{9,11},{10,... | collective-permute-start | bytes 344072 | tf_op jit(solution)/shard_map/ppermute | solution.py:435
  152.5 15.8 %collective-permute-start.32 = (bf16[224,896]{1,0:T(8,128)(2,1)S(1)}, bf16[224,896]{1,0:T(8,128)(2,1)S(1)}, u32[]{:S(2)}, u32[]{:S(2)}) collective-permute-start(bf16[224,896]{1,0:T(8,128)(2,1)S(1)} %get-tuple-element.42), channel_id=1, source_target_pairs={{0,24},{8,16},{16,8},{24,0},{1,25},{9,17},{17,9},{25,1},{2,26},{10... | collective-permute-start | bytes 1204232 | tf_op jit(solution)/shard_map/ppermute | solution.py:429
  154.0 19.3 %collective-permute-start.31 = (bf16[224,896]{1,0:T(8,128)(2,1)S(1)}, bf16[224,896]{1,0:T(8,128)(2,1)S(1)}, u32[]{:S(2)}, u32[]{:S(2)}) collective-permute-start(bf16[224,896]{1,0:T(8,128)(2,1)S(1)} %get-tuple-element.42), channel_id=1, source_target_pairs={{0,16},{8,24},{16,0},{24,8},{1,17},{9,25},{17,1},{25,9},{2,18},{10... | collective-permute-start | bytes 1204232 | tf_op jit(solution)/shard_map/ppermute | solution.py:429
  155.5 17.8 %collective-permute-start.30 = (bf16[224,896]{1,0:T(8,128)(2,1)S(1)}, bf16[224,896]{1,0:T(8,128)(2,1)S(1)}, u32[]{:S(2)}, u32[]{:S(2)}) collective-permute-start(bf16[224,896]{1,0:T(8,128)(2,1)S(1)} %get-tuple-element.42), channel_id=1, source_target_pairs={{0,8},{8,0},{16,24},{24,16},{1,9},{9,1},{17,25},{25,17},{2,10},{10... | collective-permute-start | bytes 1204232 | tf_op jit(solution)/shard_map/ppermute | solution.py:429
  160.0 7.0 %collective-permute-start.27 = (bf16[64,896]{1,0:T(8,128)(2,1)S(1)}, bf16[64,896]{1,0:T(8,128)(2,1)S(1)}, u32[]{:S(2)}, u32[]{:S(2)}) collective-permute-start(bf16[64,896]{1,0:T(8,128)(2,1)S(1)} %get-tuple-element.47), channel_id=1, source_target_pairs={{0,6},{1,7},{2,0},{3,1},{4,2},{5,3},{6,4},{7,5},{8,14},{9,15},{10,... | collective-permute-start | bytes 344072 | tf_op jit(solution)/shard_map/ppermute | solution.py:435
  160.0 7.0 %collective-permute-start.26 = (bf16[64,896]{1,0:T(8,128)(2,1)S(1)}, bf16[64,896]{1,0:T(8,128)(2,1)S(1)}, u32[]{:S(2)}, u32[]{:S(2)}) collective-permute-start(bf16[64,896]{1,0:T(8,128)(2,1)S(1)} %get-tuple-element.48), channel_id=1, source_target_pairs={{0,4},{1,5},{2,6},{3,7},{4,0},{5,1},{6,2},{7,3},{8,12},{9,13},{10,... | collective-permute-start | bytes 344072 | tf_op jit(solution)/shard_map/ppermute | solution.py:435

commit v8 on v7

--- a/solution.py
+++ b/solution.py
@@ -83,6 +83,41 @@
     )(place, coef, experts)
 
 
+def join_kernel(atoms_ref, cot_ref, _, both_ref):
+    both_ref[0] = atoms_ref[0]
+    both_ref[1] = cot_ref[0]
+
+
+def join(atoms, cotangent, earlier):
+    return pl.pallas_call(
+        join_kernel,
+        out_shape=jax.ShapeDtypeStruct((2, *atoms.shape[1:]), BF16),
+        in_specs=[whole_vmem(), whole_vmem(), in_hbm()],
+        out_specs=whole_vmem(),
+        compiler_params=params(SMALL),
+        name="join",
+    )(atoms, cotangent, earlier)
+
+
+def rows_kernel(count, *refs):
+    out_ref = refs[-1]
+    total = refs[0][...]
+    for ref in refs[1:count]:
+        total = total + ref[...].astype(F32)
+    out_ref[...] = total.astype(BF16)
+
+
+def weight_rows(parts, earlier):
+    return pl.pallas_call(
+        functools.partial(rows_kernel, len(parts)),
+        out_shape=jax.ShapeDtypeStruct(parts[0].shape, BF16),
+        in_specs=[whole_vmem()] * len(parts) + [in_hbm()] * len(earlier),
+        out_specs=whole_vmem(),
+        compiler_params=params(SMALL),
+        name="weight_rows",
+    )(*parts, *earlier)
+
+
 def merged_grad_kernel(place_ref, cols_ref, *refs):
     block_refs, grad_ref, sent_ref, token_ref, sums_ref = refs[:-4], *refs[-4:]
     size = block_refs[0].shape[0]
@@ -102,7 +137,7 @@
     return pl.pallas_call(
         merged_grad_kernel,
         out_shape=[jax.ShapeDtypeStruct((cols.shape[0], width), kind) for kind in (F32, BF16)]
-        + [jax.ShapeDtypeStruct((8, 128), F32)],
+        + [jax.ShapeDtypeStruct((1, width), F32)],
         in_specs=[whole_smem()] + [whole_vmem()] * (1 + len(blocks)),
         out_specs=[whole_vmem()] * 3,
         scratch_shapes=[pltpu.VMEM((size * len(blocks), width), BF16)],
@@ -111,7 +146,9 @@
     )(place, cols, *blocks)
 
 
-def atom_grad_kernel(chips, place_ref, sums_ref, weight_hbm, first_ref, second_ref, weight_ref, sem):
+def atom_grad_kernel(
+    chips, place_ref, sums_ref, weight_hbm, first_ref, second_ref, token_ref, weight_ref, sem
+):
     half = place_ref[1] // (chips // 2)
     rows, own = weight_ref.shape[0], first_ref.shape[0]
     at = pl.ds(pl.multiple_of(half * rows, rows), rows)
@@ -123,6 +160,7 @@
         ref[...] = lax.dot_general(
             block, weight_ref[...], (((1,), (1,)), ((), ())), preferred_element_type=F32
         ).astype(BF16)
+    token_ref[...] = jnp.zeros_like(token_ref)
 
 
 def atom_grads(chips, place, sums, weight):
@@ -130,9 +168,10 @@
     rows = weight.shape[0] // 2
     return pl.pallas_call(
         functools.partial(atom_grad_kernel, chips),
-        out_shape=[jax.ShapeDtypeStruct((own, rows), BF16)] * 2,
+        out_shape=[jax.ShapeDtypeStruct((own, rows), BF16)] * 2
+        + [jax.ShapeDtypeStruct((1, width), BF16)],
         in_specs=[whole_smem(), whole_vmem(), in_hbm()],
-        out_specs=[whole_vmem()] * 2,
+        out_specs=[whole_vmem()] * 3,
         scratch_shapes=[pltpu.VMEM((rows, width), BF16), pltpu.SemaphoreType.DMA],
         compiler_params=params(SMALL),
         cost_estimate=pl.CostEstimate(
@@ -195,7 +234,7 @@
     token_ref[...] = jnp.zeros_like(token_ref)
 
 
-def hot_ends(cols, rows, order, earlier, tile):
+def hot_ends(cols, rows, order, earlier, width, tile):
     edges, atoms = cols.shape[0], order.shape[0]
     fixed = lambda *shape: pl.BlockSpec(shape, lambda i: (0, 0))
     return pl.pallas_call(
@@ -204,7 +243,7 @@
         out_shape=[
             jax.ShapeDtypeStruct((edges, 2 * atoms), BF16),
             jax.ShapeDtypeStruct((2 * atoms, edges), BF16),
-            jax.ShapeDtypeStruct((8, 128), F32),
+            jax.ShapeDtypeStruct((1, width), F32),
         ],
         in_specs=[
             pl.BlockSpec((tile, 2), lambda i: (i, 0)),
@@ -216,7 +255,7 @@
         out_specs=[
             pl.BlockSpec((tile, 2 * atoms), lambda i: (i, 0)),
             pl.BlockSpec((2 * atoms, tile), lambda i: (0, i)),
-            fixed(8, 128),
+            fixed(1, width),
         ],
         compiler_params=params(),
         cost_estimate=pl.CostEstimate(
@@ -266,7 +305,7 @@
         out_shape=[
             jax.ShapeDtypeStruct((atoms, width), BF16),
             jax.ShapeDtypeStruct((edges, width), BF16),
-            jax.ShapeDtypeStruct((8, 128), F32),
+            jax.ShapeDtypeStruct((1, width), BF16),
         ],
         in_specs=[
             whole_smem(),
@@ -277,7 +316,7 @@
         out_specs=[
             in_hbm(),
             pl.BlockSpec((tile, width), lambda i: (i, 0)),
-            pl.BlockSpec((8, 128), lambda i: (0, 0)),
+            pl.BlockSpec((1, width), lambda i: (0, 0)),
         ],
         scratch_shapes=[
             pltpu.VMEM((atoms, width), BF16),
@@ -293,7 +332,7 @@
 
 
 def edge_kernel(
-    chips, place_ref, gather_ref, sum_ref, radial_ref, scaled_ref, atoms_hbm, _, *refs
+    chips, place_ref, gather_ref, sum_ref, radial_ref, scaled_ref, atoms_hbm, *refs
 ):
     blocks = 2 * chips
     block_refs = refs[:blocks]
@@ -372,7 +411,7 @@
         store.wait()
 
 
-def edge_sums(chips, place, gather, sums, radial, scaled, atoms, earlier, blocks, tile):
+def edge_sums(chips, place, gather, sums, radial, scaled, atoms, blocks, tile):
     edges, width = radial.shape
     count, width_in = atoms.shape
     flops = 2 * count * width * (2 * width_in + 5 * edges)
@@ -393,7 +432,7 @@
             pl.BlockSpec((tile, width), lambda i: (jnp.minimum(i, steps - 1), 0)),
             pl.BlockSpec((tile, width), lambda i: (jnp.minimum(i, steps - 1), 0)),
         ]
-        + [in_hbm()] * (2 + len(blocks)),
+        + [in_hbm()] * (1 + len(blocks)),
         out_specs=[fixed(*shape) for shape, _ in halves] + [in_hbm()],
         scratch_shapes=[
             pltpu.VMEM((count, width_in), BF16),
@@ -411,7 +450,7 @@
             transcendentals=edges * width,
         ),
         name="edge_sums",
-    )(place, gather, sums, radial, scaled, atoms, earlier, *blocks)
+    )(place, gather, sums, radial, scaled, atoms, *blocks)
 
 
 def shards(systems, ways, atoms, cotangent, experts, radial, coef, source, target):
@@ -438,31 +477,29 @@
         return blocks + [swap(block) for block in blocks]
 
     merged = merge_parts(place, coef, experts, parts)
-    pair = jnp.concatenate([atoms, cotangent], axis=0)
+    pair = join(atoms, cotangent, merged[-1])
     features = both_cores([pair] + [shift(pair, k) for k in range(1, chips)])
 
     at = jnp.arange(ways * own, dtype=jnp.int32)
     side, z, offset = at // (chips * own), at // own % chips, at % own
     order = (2 * z + (core ^ side)) * own + offset
     ends = jnp.concatenate([source, target])
-    hot_gather, hot_sum, hot_token = hot_ends(ends.T, ends, order, pair, tile)
+    hot_gather, hot_sum, hot_token = hot_ends(ends.T, ends, order, pair, width, tile)
     all_atoms, scaled, scaled_token = scaled_edges(place, hot_gather, radial[0], features, tile)
     own_cols = lax.dynamic_slice_in_dim(all_atoms, (me_edge % chips) * depth, depth, 1).T
 
-    total = merged[0] + hot_token[0, 0]
-    for k in range(1, systems):
-        total = total + across(merged[k], k).astype(F32)
-    held = total.astype(BF16)
+    got = [merged[0]] + [across(merged[k], k) for k in range(1, systems)]
+    held = weight_rows(got, features[1:chips] + [hot_token])
     blocks = []
     for k in range(chips):
         if k == chips - 1:
-            held = held + scaled_token[0, 0].astype(BF16)
+            held = held + scaled_token
         if k:
             held = shift(held, 1)
         blocks += [held, swap(held)]
 
     kept, sent, node_kept, node_sent, weight = edge_sums(
-        chips, place, hot_gather, hot_sum, radial[0], scaled, all_atoms, own_cols, blocks, tile
+        chips, place, hot_gather, hot_sum, radial[0], scaled, all_atoms, blocks, tile
     )
 
     def reduce(kept, other, zero):
@@ -479,18 +516,19 @@
         to = [z // shares * shares + (z + j) % shares for z in range(chips)]
         return lax.ppermute(x, "edge", [(2 * z + c, 2 * to[z] + c) for z in range(chips) for c in range(2)])
 
-    picked = both_cores([sums] + [share(sums, j) for j in range(1, shares)])
+    *terms, term_token = atom_grads(chips, place, sums, weight)
+    picked = both_cores([sums] + [share(sums, j) + term_token for j in range(1, shares)])
     grad, send, grad_token = merged_grads(place, own_cols, picked)
     grads = [grad] + [across(send, k) for k in range(1, systems)]
     expert_grad = expert_grads(place, coef, grads, experts.shape, parts)
 
     atom_grad = 0.0
-    for flip, term in enumerate(atom_grads(chips, place, sums, weight)):
+    for flip, term in enumerate(terms):
         to = [2 * (z % shares) + (z // shares ^ flip) for z in range(chips)]
         pairs = [(2 * z + c, 2 * to[z] + c) for z in range(chips) for c in range(2)]
         atom_grad = atom_grad + lax.ppermute(term, "edge", pairs).astype(F32)
 
-    node = reduce(node_kept, swap(node_sent), grad_token[0, 0])
+    node = reduce(node_kept, swap(node_sent), grad_token)
     return node[None], atom_grad[None], expert_grad
 
 

time: 177 us -> 157 us (0.89)
  waiting for transfers between devices: 86.1 us -> 56.8 us
  starting transfers between devices: 23.1 us -> 36.2 us
  local copies, waits for them, and re-layouts: 9.27 us -> 6.11 us
    ppermute x12, waiting for transfers between devices: 61.9 us -> 42.9 us  [shift(): lax.ppermute(x, 'edge', [(e, (e + 2 * k) % ways) for e in range(ways)])]
    ppermute x12, starting transfers between devices: 10.3 us -> 23.8 us  [shift(): lax.ppermute(x, 'edge', [(e, (e + 2 * k) % ways) for e in range(ways)])]
    ppermute x6, waiting for transfers between devices: 10.2 us -> 5.04 us  [across(): return lax.ppermute(x, 'sys', [(s, s ^ k) for s in range(systems)])]
    ppermute x2, waiting for transfers between devices: 3.93 us -> 0.65 us  [shards(): atom_grad = atom_grad + lax.ppermute(term, 'edge', pairs).astype(F32)]
    ppermute x1, waiting for transfers between devices: 6.45 us -> 4.03 us  [share(): lax.ppermute(x, 'edge', [(2 * z + c, 2 * to[z] + c) for z in range(chips)...]
    slice x3 -> x0, local copies, waits for them, and re-layouts: 2.22 us -> none  [the longest x1 1.19 us: shards(): total = merged[0] + hot_token[0, 0]]
    unnamed x43 -> x48, local copies, waits for them, and re-layouts: 2.48 us -> 4.2 us
  transfers between devices with their start and end apart: 33 -> 33, of which waited for: 15 -> 13; matrix products, arithmetic and copies ran while one was open for 8% -> 6% of each run, Pallas kernels for 9% -> 11%
where the time goes in v8:
time: 157 us
  waiting for transfers between devices  56.8 us (36%)
  Pallas kernels  45.9 us (29%)
  starting transfers between devices  36.2 us (23%)
  other arithmetic  10.5 us (7%)
  local copies, waits for them, and re-layouts  6.11 us (4%)
    ppermute x12, waiting for transfers between devices, shift(): lax.ppermute(x, 'edge', [(e, (e + 2 * k) % ways) for e in range(ways)])  42.9 us
    ppermute x12, starting transfers between devices, shift(): lax.ppermute(x, 'edge', [(e, (e + 2 * k) % ways) for e in range(ways)])  23.8 us
    pallas_call x1, Pallas kernels, edge_sums(): pl.pallas_call(functools.partial(edge_kernel, chips), grid=(steps + 1,),...  22.3 us
    pallas_call x1, Pallas kernels, scaled_edges(): pl.pallas_call(functools.partial(scale_kernel, slots), grid=(edges // til...  7.94 us
    ppermute x6, starting transfers between devices, across(): return lax.ppermute(x, 'sys', [(s, s ^ k) for s in range(systems)])  7.02 us
    pallas_call x1, Pallas kernels, hot_ends(): pl.pallas_call(hot_kernel, grid=(edges // tile,), out_shape=[jax.ShapeDty...  5.66 us
    ppermute x6, waiting for transfers between devices, across(): return lax.ppermute(x, 'sys', [(s, s ^ k) for s in range(systems)])  5.04 us
    ppermute x12, waiting for transfers between devices, swap(): return lax.ppermute(x, 'edge', [(e, e ^ 1) for e in range(ways)])  4.25 us
  transfers between devices with their start and end apart: 33, of which 13 were waited for; matrix products, arithmetic and copies ran while one was open for 6% of the time, Pallas kernels for 11%

profile of v8, /device:TPU:0, one launch (start us, length us, event | category | flops | bytes accessed | tf_op | source)
XLA Modules:
  0.0 156.7 jit_solution(10133748251470532982)
XLA Ops:
  0.6 0.6 pad_add_fusion.1.place_ref
  1.2 4.2 %merge_parts.1 = (f32[224,896]{1,0:T(8,128)}, bf16[224,896]{1,0:T(8,128)(2,1)}, bf16[224,896]{1,0:T(8,128)(2,1)}, bf16[224,896]{1,0:T(8,128)(2,1)}) custom-call(s32[3]{0:T(128)} %pad_add_fusion.1.place_ref, f32[4,16]{1,0:T(4,128)} %coef_ref.3, bf16[4,224,896]{2,1,0:T(8,128)(2,1)} %experts_ref.1), custom_call_target="tpu_custom_call" | custom-call | tf_op jit(solution)/shard_map/merge_parts/pallas_call | solution.py:70
  5.4 1.0 copy-done.7
  6.4 0.9 copy-done.8
  7.3 5.1 %collective-permute-start.2 = (bf16[2,64,896]{2,1,0:T(8,128)(2,1)S(1)}, bf16[2,64,896]{2,1,0:T(8,128)(2,1)S(1)}, u32[]{:S(2)}, u32[]{:S(2)}) collective-permute-start(bf16[2,64,896]{2,1,0:T(8,128)(2,1)S(1)} %join.1._.refs_0_), channel_id=1, source_target_pairs={{0,6},{1,7},{2,0},{3,1},{4,2},{5,3},{6,4},{7,5},{8,14},{9,15},{10,... | collective-permute-start | bytes 688136 | tf_op jit(solution)/shard_map/ppermute | solution.py:474
  12.4 2.4 %collective-permute-start.9 = (bf16[224,896]{1,0:T(8,128)(2,1)}, bf16[224,896]{1,0:T(8,128)(2,1)S(1)}, u32[]{:S(2)}, u32[]{:S(2)}) collective-permute-start(bf16[224,896]{1,0:T(8,128)(2,1)} %get-tuple-element.24._), channel_id=1, source_target_pairs={{0,24},{8,16},{16,8},{24,0},{1,25},{9,17},{17,9},{25,1},{2,26},{10... | collective-permute-start | bytes 1204232 | tf_op jit(solution)/shard_map/ppermute | solution.py:468
  14.8 0.5 collective-permute-start.7
  15.4 0.5 collective-permute-start.8
  15.9 1.3 pad_add_fusion
  17.2 1.3 copy.13.cols_ref
  18.6 10.1 %collective-permute-start = (bf16[2,64,896]{2,1,0:T(8,128)(2,1)S(1)}, bf16[2,64,896]{2,1,0:T(8,128)(2,1)S(1)}, u32[]{:S(2)}, u32[]{:S(2)}) collective-permute-start(bf16[2,64,896]{2,1,0:T(8,128)(2,1)S(1)} %join.1._.refs_0_), channel_id=1, source_target_pairs={{0,2},{1,3},{2,4},{3,5},{4,6},{5,7},{6,0},{7,1},{8,10},{9,11},{10,... | collective-permute-start | bytes 688136 | tf_op jit(solution)/shard_map/ppermute | solution.py:474
  28.7 0.6 fusion.29.across_ref
  29.3 0.8 fusion.13.down_ref
  30.1 5.7 %hot_ends.1 = (bf16[2048,1024]{1,0:T(8,128)(2,1)}, bf16[1024,2048]{1,0:T(8,128)(2,1)}, f32[1,896]{1,0:T(1,128)}) custom-call(s32[2048,2]{1,0:T(8,128)} %copy.13.cols_ref, s32[2,2048]{1,0:T(2,128)} %get-tuple-element.51.rows_ref, s32[1,512]{1,0:T(1,128)} %fusion.29.across_ref, s32[512,1]{1,0:T(8,128)} %fusion.13.down_ref, bf16[2,64,896]{2,1,0:T(8,128)(2,1)} %copy-done.1), custom_call_target="tpu_custom_call" | custom-call | flops 16777216 | bytes 8388608 | tf_op jit(solution)/shard_map/hot_ends/pallas_call | solution.py:240
  35.8 0.7 copy-done.11
  36.5 0.2 weight_rows.1.refs_0_
  36.7 0.1 collective-permute-start.11
  36.8 0.5 collective-permute-start.6
  37.3 0.1 collective-permute-start.5
  37.4 0.4 collective-permute-start.4
  37.9 9.0 %collective-permute-done.11.refs_2_ = bf16[224,896]{1,0:T(8,128)(2,1)S(1)} collective-permute-done((bf16[224,896]{1,0:T(8,128)(2,1)S(1)}, bf16[224,896]{1,0:T(8,128)(2,1)S(1)}, u32[]{:S(2)}, u32[]{:S(2)}) %collective-permute-start.11) | collective-permute-done | bytes 401440 | tf_op jit(solution)/shard_map/ppermute | solution.py:474
  46.9 0.6 copy-done.14
  47.6 0.1 copy-done.16
  47.7 0.1 copy-done.17
  47.8 7.9 %scaled_edges.1 = (bf16[512,896]{1,0:T(8,128)(2,1)}, bf16[2048,896]{1,0:T(8,128)(2,1)}, bf16[1,896]{1,0:T(2,128)(2,1)}) custom-call(s32[3]{0:T(128)} %pad_add_fusion.1.place_ref, bf16[2048,1024]{1,0:T(8,128)(2,1)} %get-tuple-element.25.gather_ref, bf16[2048,896]{1,0:T(8,128)(2,1)} %bitcast.50, bf16[2,64,896]{2,1,0:T(8,128)(2,1)} %copy-done.1, ...), custom_call_target="tpu_custom_call" | custom-call | flops 1879048192 | bytes 11010048 | tf_op jit(solution)/shard_map/scaled_edges/pallas_call | solution.py:302
  55.8 0.7 reduce
  56.5 1.4 collective-permute-start.15
  58.0 0.5 collective-permute-start.12
  58.5 8.8 %collective-permute-done.15.refs_6_ = bf16[224,896]{1,0:T(8,128)(2,1)S(1)} collective-permute-done((bf16[224,896]{1,0:T(8,128)(2,1)S(1)}, bf16[224,896]{1,0:T(8,128)(2,1)S(1)}, u32[]{:S(2)}, u32[]{:S(2)}) %collective-permute-start.15) | collective-permute-done | bytes 401440 | tf_op jit(solution)/shard_map/ppermute | solution.py:474
  67.3 1.7 %collective-permute-done.16.refs_7_ = bf16[224,896]{1,0:T(8,128)(2,1)S(1)} collective-permute-done((bf16[224,896]{1,0:T(8,128)(2,1)S(1)}, bf16[224,896]{1,0:T(8,128)(2,1)S(1)}, u32[]{:S(2)}, u32[]{:S(2)}) %collective-permute-start.16) | collective-permute-done | bytes 401440 | tf_op jit(solution)/shard_map/ppermute | solution.py:471
  69.0 0.7 copy-done.23
  69.7 22.3 %edge_sums.1 = (f32[4,128,896]{2,1,0:T(8,128)}, bf16[4,128,896]{2,1,0:T(8,128)(2,1)}, f32[4,64,896]{2,1,0:T(8,128)}, bf16[4,64,896]{2,1,0:T(8,128)(2,1)}, bf16[1792,896]{1,0:T(8,128)(2,1)}) custom-call(s32[3]{0:T(128)} %pad_add_fusion.1.place_ref, bf16[2048,1024]{1,0:T(8,128)(2,1)} %get-tuple-element.25.gather_ref, ...), custom_call_target="tpu_custom_call" | custom-call | flops 11039408128 | bytes 15728640 | tf_op jit(solution)/shard_map/edge_sums/pallas_call | solution.py:424
  92.0 0.2 collective-permute-start.18
  92.2 2.6 %collective-permute-done.18 = bf16[4,128,896]{2,1,0:T(8,128)(2,1)S(1)} collective-permute-done((bf16[4,128,896]{2,1,0:T(8,128)(2,1)}, bf16[4,128,896]{2,1,0:T(8,128)(2,1)S(1)}, u32[]{:S(2)}, u32[]{:S(2)}) %collective-permute-start.18) | collective-permute-done | bytes 917536 | tf_op jit(solution)/shard_map/ppermute | solution.py:471
  94.8 1.4 fusion.18
  96.2 0.7 collective-permute-start.19
  96.9 3.1 %collective-permute-start.21 = (bf16[128,896]{1,0:T(8,128)(2,1)S(1)}, bf16[128,896]{1,0:T(8,128)(2,1)S(1)}, u32[]{:S(2)}, u32[]{:S(2)}) collective-permute-start(bf16[128,896]{1,0:T(8,128)(2,1)S(1)} %get-tuple-element.46), channel_id=1, source_target_pairs={{0,6},{1,7},{2,0},{3,1},{4,2},{5,3},{6,4},{7,5},{8,14},{9,15},{10,... | collective-permute-start | bytes 688136 | tf_op jit(solution)/shard_map/ppermute | solution.py:474
  100.1 6.5 %collective-permute-done.19 = bf16[128,896]{1,0:T(8,128)(2,1)S(1)} collective-permute-done((bf16[128,896]{1,0:T(8,128)(2,1)S(1)}, bf16[128,896]{1,0:T(8,128)(2,1)S(1)}, u32[]{:S(2)}, u32[]{:S(2)}) %collective-permute-start.19) | collective-permute-done | bytes 229408 | tf_op jit(solution)/shard_map/ppermute | solution.py:474
  106.5 3.6 %collective-permute-done.21 = bf16[128,896]{1,0:T(8,128)(2,1)S(1)} collective-permute-done((bf16[128,896]{1,0:T(8,128)(2,1)S(1)}, bf16[128,896]{1,0:T(8,128)(2,1)S(1)}, u32[]{:S(2)}, u32[]{:S(2)}) %collective-permute-start.21) | collective-permute-done | bytes 229408 | tf_op jit(solution)/shard_map/ppermute | solution.py:474
  110.2 8.9 %collective-permute-done.20 = bf16[128,896]{1,0:T(8,128)(2,1)S(1)} collective-permute-done((bf16[128,896]{1,0:T(8,128)(2,1)S(1)}, bf16[128,896]{1,0:T(8,128)(2,1)S(1)}, u32[]{:S(2)}, u32[]{:S(2)}) %collective-permute-start.20) | collective-permute-done | bytes 229408 | tf_op jit(solution)/shard_map/ppermute | solution.py:474
  119.1 1.2 fusion.6.sums_ref.refs_0_
  120.3 0.1 collective-permute-start.22
  120.3 0.1 collective-permute-start.17
  120.4 0.5 collective-permute-start.23
  120.9 1.8 %atom_grads.1 = (bf16[64,896]{1,0:T(8,128)(2,1)S(1)}, bf16[64,896]{1,0:T(8,128)(2,1)S(1)}, bf16[1,896]{1,0:T(2,128)(2,1)S(1)}) custom-call(s32[3]{0:T(128)S(1)} %copy-done.9, bf16[128,896]{1,0:T(8,128)(2,1)S(1)} %fusion.6.sums_ref.refs_0_, bf16[1792,896]{1,0:T(8,128)(2,1)S(1)} %copy-done), custom_call_target="tpu_custom_call" | custom-call | flops 205520896 | bytes 1605632 | tf_op jit(solution)/shard_map/atom_grads/pallas_call | solution.py:169
  122.8 4.0 %collective-permute-done.22 = bf16[128,896]{1,0:T(8,128)(2,1)S(1)} collective-permute-done((bf16[128,896]{1,0:T(8,128)(2,1)S(1)}, bf16[128,896]{1,0:T(8,128)(2,1)S(1)}, u32[]{:S(2)}, u32[]{:S(2)}) %collective-permute-start.22) | collective-permute-done | bytes 229408 | tf_op jit(solution)/shard_map/ppermute | solution.py:517
  127.0 0.5 copy.14
  127.5 0.7 collective-permute-start.28
  128.2 2.2 %collective-permute-start.29 = (bf16[64,896]{1,0:T(8,128)(2,1)S(1)}, bf16[64,896]{1,0:T(8,128)(2,1)S(1)}, u32[]{:S(2)}, u32[]{:S(2)}) collective-permute-start(bf16[64,896]{1,0:T(8,128)(2,1)S(1)} %get-tuple-element.42), channel_id=1, source_target_pairs={{0,2},{1,3},{2,6},{3,7},{4,0},{5,1},{6,4},{7,5},{8,10},{9,11},{10,... | collective-permute-start | bytes 344072 | tf_op jit(solution)/shard_map/ppermute | solution.py:529
  130.4 1.0 merged_grads.1
  131.5 1.4 fusion.23
  132.9 0.1 collective-permute-start.25
  132.9 2.6 %collective-permute-start.32 = (bf16[224,896]{1,0:T(8,128)(2,1)S(1)}, bf16[224,896]{1,0:T(8,128)(2,1)S(1)}, u32[]{:S(2)}, u32[]{:S(2)}) collective-permute-start(bf16[224,896]{1,0:T(8,128)(2,1)S(1)} %get-tuple-element.44), channel_id=1, source_target_pairs={{0,24},{8,16},{16,8},{24,0},{1,25},{9,17},{17,9},{25,1},{2,26},{10... | collective-permute-start | bytes 1204232 | tf_op jit(solution)/shard_map/ppermute | solution.py:468
  135.6 0.4 collective-permute-start.31
  135.9 0.5 collective-permute-start.30
  136.5 0.6 collective-permute-done.29
  137.1 3.1 %collective-permute-start.27 = (bf16[64,896]{1,0:T(8,128)(2,1)S(1)}, bf16[64,896]{1,0:T(8,128)(2,1)S(1)}, u32[]{:S(2)}, u32[]{:S(2)}) collective-permute-start(bf16[64,896]{1,0:T(8,128)(2,1)S(1)} %get-tuple-element.49), channel_id=1, source_target_pairs={{0,6},{1,7},{2,0},{3,1},{4,2},{5,3},{6,4},{7,5},{8,14},{9,15},{10,... | collective-permute-start | bytes 344072 | tf_op jit(solution)/shard_map/ppermute | solution.py:474
  140.2 0.7 add_bitcast_fusion
  140.9 1.9 %collective-permute-done.27 = bf16[64,896]{1,0:T(8,128)(2,1)S(1)} collective-permute-done((bf16[64,896]{1,0:T(8,128)(2,1)S(1)}, bf16[64,896]{1,0:T(8,128)(2,1)S(1)}, u32[]{:S(2)}, u32[]{:S(2)}) %collective-permute-start.27) | collective-permute-done | bytes 114720 | tf_op jit(solution)/shard_map/ppermute | solution.py:474
  142.9 4.2 %collective-permute-done.26 = bf16[64,896]{1,0:T(8,128)(2,1)S(1)} collective-permute-done((bf16[64,896]{1,0:T(8,128)(2,1)S(1)}, bf16[64,896]{1,0:T(8,128)(2,1)S(1)}, u32[]{:S(2)}, u32[]{:S(2)}) %collective-permute-start.26) | collective-permute-done | bytes 114720 | tf_op jit(solution)/shard_map/ppermute | solution.py:474
  147.0 1.7 %fusion.28 = bf16[1,64,896]{2,1,0:T(8,128)(2,1)} fusion(bf16[64,896]{1,0:T(8,128)(2,1)S(1)} %collective-permute-done.27, bf16[64,896]{1,0:T(8,128)(2,1)S(1)} %collective-permute-done.26, bf16[64,896]{1,0:T(8,128)(2,1)S(1)} %collective-permute-done.25, f32[4,64,896]{2,1,0:T(8,128)} %get-tuple-element.34, bf16[4,64,896]{2,1,0:T(8,128)(2,1)} %collective-permute-done.17, ...), kind=kLoop, calls=%fused_computation.49 | loop fusion | flops 573440 | bytes 806400 | tf_op jit(solution)/shard_map/broadcast_in_dim | solution.py:532
  148.8 4.8 %collective-permute-done.31.refs_2_ = bf16[224,896]{1,0:T(8,128)(2,1)S(1)} collective-permute-done((bf16[224,896]{1,0:T(8,128)(2,1)S(1)}, bf16[224,896]{1,0:T(8,128)(2,1)S(1)}, u32[]{:S(2)}, u32[]{:S(2)}) %collective-permute-start.31) | collective-permute-done | bytes 401440 | tf_op jit(solution)/shard_map/ppermute | solution.py:468
  153.6 0.2 collective-permute-done.30.refs_1_
  153.8 2.8 %expert_grads.1 = f32[4,224,896]{2,1,0:T(8,128)} custom-call(s32[3]{0:T(128)S(1)} %copy-done.9, f32[4,16]{1,0:T(4,128)S(1)} %copy-done.10, f32[224,896]{1,0:T(8,128)S(1)} %get-tuple-element.43.refs_0_, bf16[224,896]{1,0:T(8,128)(2,1)S(1)} %collective-permute-done.30.refs_1_, bf16[224,896]{1,0:T(8,128)(2,1)S(1)} %collective-permute-done.31.refs_2_, ...), custom_call_target="tpu_custom_call" | custom-call | tf_op jit(solution)/shard_map/expert_grads/pallas_call | solution.py:213
  (76 shorter events, 0.5 us)
Async XLA Ops:
  5.4 30.4 %copy-start.5 = (f32[224,896]{1,0:T(8,128)S(1)}, f32[224,896]{1,0:T(8,128)}, u32[]{:S(2)}) copy-start(f32[224,896]{1,0:T(8,128)} %get-tuple-element.29.refs_0_) | copy-start | bytes 2408452
  5.4 1.0 copy-start.7
  6.4 0.9 copy-start.8
  7.3 22.8 %copy-start.1 = (bf16[2,64,896]{2,1,0:T(8,128)(2,1)}, bf16[2,64,896]{2,1,0:T(8,128)(2,1)S(1)}, u32[]{:S(2)}) copy-start(bf16[2,64,896]{2,1,0:T(8,128)(2,1)S(1)} %join.1._.refs_0_) | copy-start | bytes 688132
  7.3 11.3 %collective-permute-start.2 = (bf16[2,64,896]{2,1,0:T(8,128)(2,1)S(1)}, bf16[2,64,896]{2,1,0:T(8,128)(2,1)S(1)}, u32[]{:S(2)}, u32[]{:S(2)}) collective-permute-start(bf16[2,64,896]{2,1,0:T(8,128)(2,1)S(1)} %join.1._.refs_0_), channel_id=1, source_target_pairs={{0,6},{1,7},{2,0},{3,1},{4,2},{5,3},{6,4},{7,5},{8,14},{9,15},{10,... | collective-permute-start | bytes 688136 | tf_op jit(solution)/shard_map/ppermute | solution.py:474
  12.4 23.3 %collective-permute-start.1 = (bf16[2,64,896]{2,1,0:T(8,128)(2,1)S(1)}, bf16[2,64,896]{2,1,0:T(8,128)(2,1)S(1)}, u32[]{:S(2)}, u32[]{:S(2)}) collective-permute-start(bf16[2,64,896]{2,1,0:T(8,128)(2,1)S(1)} %join.1._.refs_0_), channel_id=1, source_target_pairs={{0,4},{1,5},{2,6},{3,7},{4,0},{5,1},{6,2},{7,3},{8,12},{9,13},{10,... | collective-permute-start | bytes 688136 | tf_op jit(solution)/shard_map/ppermute | solution.py:474
  12.4 23.4 %collective-permute-start.9 = (bf16[224,896]{1,0:T(8,128)(2,1)}, bf16[224,896]{1,0:T(8,128)(2,1)S(1)}, u32[]{:S(2)}, u32[]{:S(2)}) collective-permute-start(bf16[224,896]{1,0:T(8,128)(2,1)} %get-tuple-element.24._), channel_id=1, source_target_pairs={{0,24},{8,16},{16,8},{24,0},{1,25},{9,17},{17,9},{25,1},{2,26},{10... | collective-permute-start | bytes 1204232 | tf_op jit(solution)/shard_map/ppermute | solution.py:468
  14.8 20.9 %collective-permute-start.7 = (bf16[224,896]{1,0:T(8,128)(2,1)}, bf16[224,896]{1,0:T(8,128)(2,1)S(1)}, u32[]{:S(2)}, u32[]{:S(2)}) collective-permute-start(bf16[224,896]{1,0:T(8,128)(2,1)} %get-tuple-element.30), channel_id=1, source_target_pairs={{0,8},{8,0},{16,24},{24,16},{1,9},{9,1},{17,25},{25,17},{2,10},{10... | collective-permute-start | bytes 1204232 | tf_op jit(solution)/shard_map/ppermute | solution.py:468
  15.4 20.4 %collective-permute-start.8 = (bf16[224,896]{1,0:T(8,128)(2,1)}, bf16[224,896]{1,0:T(8,128)(2,1)S(1)}, u32[]{:S(2)}, u32[]{:S(2)}) collective-permute-start(bf16[224,896]{1,0:T(8,128)(2,1)} %get-tuple-element.31), channel_id=1, source_target_pairs={{0,16},{8,24},{16,0},{24,8},{1,17},{9,25},{17,1},{25,9},{2,18},{10... | collective-permute-start | bytes 1204232 | tf_op jit(solution)/shard_map/ppermute | solution.py:468
  18.6 28.3 %copy-start.2 = (bf16[2,64,896]{2,1,0:T(8,128)(2,1)}, bf16[2,64,896]{2,1,0:T(8,128)(2,1)S(1)}, u32[]{:S(2)}) copy-start(bf16[2,64,896]{2,1,0:T(8,128)(2,1)S(1)} %collective-permute-done.2.refs_3_.refs_6_) | copy-start | bytes 688132
  18.6 17.2 %collective-permute-start = (bf16[2,64,896]{2,1,0:T(8,128)(2,1)S(1)}, bf16[2,64,896]{2,1,0:T(8,128)(2,1)S(1)}, u32[]{:S(2)}, u32[]{:S(2)}) collective-permute-start(bf16[2,64,896]{2,1,0:T(8,128)(2,1)S(1)} %join.1._.refs_0_), channel_id=1, source_target_pairs={{0,2},{1,3},{2,4},{3,5},{4,6},{5,7},{6,0},{7,1},{8,10},{9,11},{10,... | collective-permute-start | bytes 688136 | tf_op jit(solution)/shard_map/ppermute | solution.py:474
  35.7 11.2 %copy-start.3 = (bf16[2,64,896]{2,1,0:T(8,128)(2,1)}, bf16[2,64,896]{2,1,0:T(8,128)(2,1)S(1)}, u32[]{:S(2)}) copy-start(bf16[2,64,896]{2,1,0:T(8,128)(2,1)S(1)} %collective-permute-done.1.refs_2_.refs_5_) | copy-start | bytes 688132
  35.7 11.2 %copy-start.4 = (bf16[2,64,896]{2,1,0:T(8,128)(2,1)}, bf16[2,64,896]{2,1,0:T(8,128)(2,1)S(1)}, u32[]{:S(2)}) copy-start(bf16[2,64,896]{2,1,0:T(8,128)(2,1)S(1)} %collective-permute-done.refs_1_.refs_4_) | copy-start | bytes 688132
  35.8 0.7 copy-start.11
  36.7 21.3 %copy-start.6 = (bf16[224,896]{1,0:T(8,128)(2,1)}, bf16[224,896]{1,0:T(8,128)(2,1)S(1)}, u32[]{:S(2)}) copy-start(bf16[224,896]{1,0:T(8,128)(2,1)S(1)} %weight_rows.1.refs_0_) | copy-start | bytes 1204228
  36.7 10.1 %collective-permute-start.11 = (bf16[224,896]{1,0:T(8,128)(2,1)S(1)}, bf16[224,896]{1,0:T(8,128)(2,1)S(1)}, u32[]{:S(2)}, u32[]{:S(2)}) collective-permute-start(bf16[224,896]{1,0:T(8,128)(2,1)S(1)} %weight_rows.1.refs_0_), channel_id=1, source_target_pairs={{0,2},{1,3},{2,4},{3,5},{4,6},{5,7},{6,0},{7,1},{8,10},{9,11},{10,... | collective-permute-start | bytes 1204232 | tf_op jit(solution)/shard_map/ppermute | solution.py:474
  36.8 10.0 %collective-permute-start.3 = (bf16[2,64,896]{2,1,0:T(8,128)(2,1)}, bf16[2,64,896]{2,1,0:T(8,128)(2,1)S(1)}, u32[]{:S(2)}, u32[]{:S(2)}) collective-permute-start(bf16[2,64,896]{2,1,0:T(8,128)(2,1)} %copy-done.1), channel_id=1, source_target_pairs={{0,1},{1,0},{2,3},{3,2},{4,5},{5,4},{6,7},{7,6},{8,9},{9,8},{10,11... | collective-permute-start | bytes 688136 | tf_op jit(solution)/shard_map/ppermute | solution.py:471
  36.8 10.0 %collective-permute-start.6 = (bf16[2,64,896]{2,1,0:T(8,128)(2,1)S(1)}, bf16[2,64,896]{2,1,0:T(8,128)(2,1)S(1)}, u32[]{:S(2)}, u32[]{:S(2)}) collective-permute-start(bf16[2,64,896]{2,1,0:T(8,128)(2,1)S(1)} %collective-permute-done.2.refs_3_.refs_6_), channel_id=1, source_target_pairs={{0,1},{1,0},{2,3},{3,2},{4,5},{5,4},{6,7},{7,6},{8,9},{9,8},{10,11... | collective-permute-start | bytes 688136 | tf_op jit(solution)/shard_map/ppermute | solution.py:471
  37.3 9.5 %collective-permute-start.5 = (bf16[2,64,896]{2,1,0:T(8,128)(2,1)S(1)}, bf16[2,64,896]{2,1,0:T(8,128)(2,1)S(1)}, u32[]{:S(2)}, u32[]{:S(2)}) collective-permute-start(bf16[2,64,896]{2,1,0:T(8,128)(2,1)S(1)} %collective-permute-done.1.refs_2_.refs_5_), channel_id=1, source_target_pairs={{0,1},{1,0},{2,3},{3,2},{4,5},{5,4},{6,7},{7,6},{8,9},{9,8},{10,11... | collective-permute-start | bytes 688136 | tf_op jit(solution)/shard_map/ppermute | solution.py:471
  37.4 9.5 %collective-permute-start.4 = (bf16[2,64,896]{2,1,0:T(8,128)(2,1)S(1)}, bf16[2,64,896]{2,1,0:T(8,128)(2,1)S(1)}, u32[]{:S(2)}, u32[]{:S(2)}) collective-permute-start(bf16[2,64,896]{2,1,0:T(8,128)(2,1)S(1)} %collective-permute-done.refs_1_.refs_4_), channel_id=1, source_target_pairs={{0,1},{1,0},{2,3},{3,2},{4,5},{5,4},{6,7},{7,6},{8,9},{9,8},{10,11... | collective-permute-start | bytes 688136 | tf_op jit(solution)/shard_map/ppermute | solution.py:471
  46.8 22.2 %copy-start.18 = (bf16[224,896]{1,0:T(8,128)(2,1)}, bf16[224,896]{1,0:T(8,128)(2,1)S(1)}, u32[]{:S(2)}) copy-start(bf16[224,896]{1,0:T(8,128)(2,1)S(1)} %collective-permute-done.11.refs_2_) | copy-start | bytes 1204228
  46.8 9.7 %collective-permute-start.13 = (bf16[224,896]{1,0:T(8,128)(2,1)S(1)}, bf16[224,896]{1,0:T(8,128)(2,1)S(1)}, u32[]{:S(2)}, u32[]{:S(2)}) collective-permute-start(bf16[224,896]{1,0:T(8,128)(2,1)S(1)} %collective-permute-done.11.refs_2_), channel_id=1, source_target_pairs={{0,2},{1,3},{2,4},{3,5},{4,6},{5,7},{6,0},{7,1},{8,10},{9,11},{10,... | collective-permute-start | bytes 1204232 | tf_op jit(solution)/shard_map/ppermute | solution.py:474
  46.8 0.7 copy-start.14
  46.9 0.8 copy-start.15
  46.9 0.9 copy-start.16
  46.9 0.9 copy-start.17
  56.5 12.5 %copy-start.13 = (bf16[224,896]{1,0:T(8,128)(2,1)}, bf16[224,896]{1,0:T(8,128)(2,1)S(1)}, u32[]{:S(2)}) copy-start(bf16[224,896]{1,0:T(8,128)(2,1)S(1)} %collective-permute-done.13.refs_4_) | copy-start | bytes 1204228
  56.5 10.7 %collective-permute-start.15 = (bf16[224,896]{1,0:T(8,128)(2,1)S(1)}, bf16[224,896]{1,0:T(8,128)(2,1)S(1)}, u32[]{:S(2)}, u32[]{:S(2)}) collective-permute-start(bf16[224,896]{1,0:T(8,128)(2,1)S(1)} %broadcast_add_fusion), channel_id=1, source_target_pairs={{0,2},{1,3},{2,4},{3,5},{4,6},{5,7},{6,0},{7,1},{8,10},{9,11},{10,... | collective-permute-start | bytes 1204232 | tf_op jit(solution)/shard_map/ppermute | solution.py:474
  58.0 9.3 %collective-permute-start.10 = (bf16[224,896]{1,0:T(8,128)(2,1)S(1)}, bf16[224,896]{1,0:T(8,128)(2,1)S(1)}, u32[]{:S(2)}, u32[]{:S(2)}) collective-permute-start(bf16[224,896]{1,0:T(8,128)(2,1)S(1)} %weight_rows.1.refs_0_), channel_id=1, source_target_pairs={{0,1},{1,0},{2,3},{3,2},{4,5},{5,4},{6,7},{7,6},{8,9},{9,8},{10,11... | collective-permute-start | bytes 1204232 | tf_op jit(solution)/shard_map/ppermute | solution.py:471
  58.0 9.3 %collective-permute-start.12 = (bf16[224,896]{1,0:T(8,128)(2,1)S(1)}, bf16[224,896]{1,0:T(8,128)(2,1)S(1)}, u32[]{:S(2)}, u32[]{:S(2)}) collective-permute-start(bf16[224,896]{1,0:T(8,128)(2,1)S(1)} %collective-permute-done.11.refs_2_), channel_id=1, source_target_pairs={{0,1},{1,0},{2,3},{3,2},{4,5},{5,4},{6,7},{7,6},{8,9},{9,8},{10,11... | collective-permute-start | bytes 1204232 | tf_op jit(solution)/shard_map/ppermute | solution.py:471
  58.5 8.8 %collective-permute-start.14 = (bf16[224,896]{1,0:T(8,128)(2,1)S(1)}, bf16[224,896]{1,0:T(8,128)(2,1)S(1)}, u32[]{:S(2)}, u32[]{:S(2)}) collective-permute-start(bf16[224,896]{1,0:T(8,128)(2,1)S(1)} %collective-permute-done.13.refs_4_), channel_id=1, source_target_pairs={{0,1},{1,0},{2,3},{3,2},{4,5},{5,4},{6,7},{7,6},{8,9},{9,8},{10,11... | collective-permute-start | bytes 1204232 | tf_op jit(solution)/shard_map/ppermute | solution.py:471
  67.2 1.7 %copy-start.19 = (bf16[224,896]{1,0:T(8,128)(2,1)}, bf16[224,896]{1,0:T(8,128)(2,1)S(1)}, u32[]{:S(2)}) copy-start(bf16[224,896]{1,0:T(8,128)(2,1)S(1)} %collective-permute-done.15.refs_6_) | copy-start | bytes 1204228
  67.2 1.7 %collective-permute-start.16 = (bf16[224,896]{1,0:T(8,128)(2,1)S(1)}, bf16[224,896]{1,0:T(8,128)(2,1)S(1)}, u32[]{:S(2)}, u32[]{:S(2)}) collective-permute-start(bf16[224,896]{1,0:T(8,128)(2,1)S(1)} %collective-permute-done.15.refs_6_), channel_id=1, source_target_pairs={{0,1},{1,0},{2,3},{3,2},{4,5},{5,4},{6,7},{7,6},{8,9},{9,8},{10,11... | collective-permute-start | bytes 1204232 | tf_op jit(solution)/shard_map/ppermute | solution.py:471
  67.3 1.7 %copy-start.20 = (bf16[224,896]{1,0:T(8,128)(2,1)}, bf16[224,896]{1,0:T(8,128)(2,1)S(1)}, u32[]{:S(2)}) copy-start(bf16[224,896]{1,0:T(8,128)(2,1)S(1)} %collective-permute-done.10.refs_1_) | copy-start | bytes 1204228
  67.3 1.7 %copy-start.21 = (bf16[224,896]{1,0:T(8,128)(2,1)}, bf16[224,896]{1,0:T(8,128)(2,1)S(1)}, u32[]{:S(2)}) copy-start(bf16[224,896]{1,0:T(8,128)(2,1)S(1)} %collective-permute-done.12.refs_3_) | copy-start | bytes 1204228
  67.3 1.7 %copy-start.22 = (bf16[224,896]{1,0:T(8,128)(2,1)}, bf16[224,896]{1,0:T(8,128)(2,1)S(1)}, u32[]{:S(2)}) copy-start(bf16[224,896]{1,0:T(8,128)(2,1)S(1)} %collective-permute-done.14.refs_5_) | copy-start | bytes 1204228
  69.0 0.7 copy-start.23
  92.0 28.9 %copy-start = (bf16[1792,896]{1,0:T(8,128)(2,1)S(1)}, bf16[1792,896]{1,0:T(8,128)(2,1)}, u32[]{:S(2)}) copy-start(bf16[1792,896]{1,0:T(8,128)(2,1)} %get-tuple-element.38.weight_hbm) | copy-start | bytes 9633796
  92.0 28.9 %copy-start.9 = (s32[3]{0:T(128)S(1)}, s32[3]{0:T(128)}, u32[]{:S(2)}) copy-start(s32[3]{0:T(128)} %pad_add_fusion.1.place_ref) | copy-start | bytes 40
  92.0 2.7 %collective-permute-start.18 = (bf16[4,128,896]{2,1,0:T(8,128)(2,1)}, bf16[4,128,896]{2,1,0:T(8,128)(2,1)S(1)}, u32[]{:S(2)}, u32[]{:S(2)}) collective-permute-start(bf16[4,128,896]{2,1,0:T(8,128)(2,1)} %get-tuple-element.37), channel_id=1, source_target_pairs={{0,1},{1,0},{2,3},{3,2},{4,5},{5,4},{6,7},{7,6},{8,9},{9,8},{10,11... | collective-permute-start | bytes 2752520 | tf_op jit(solution)/shard_map/ppermute | solution.py:471
  96.2 30.8 %copy-start.12 = (bf16[512,896]{1,0:T(8,128)(2,1)S(1)}, bf16[512,896]{1,0:T(8,128)(2,1)}, u32[]{:S(2)}) copy-start(bf16[512,896]{1,0:T(8,128)(2,1)} %get-tuple-element.28.atoms_hbm) | copy-start | bytes 2752516
  96.2 10.3 %collective-permute-start.19 = (bf16[128,896]{1,0:T(8,128)(2,1)S(1)}, bf16[128,896]{1,0:T(8,128)(2,1)S(1)}, u32[]{:S(2)}, u32[]{:S(2)}) collective-permute-start(bf16[128,896]{1,0:T(8,128)(2,1)S(1)} %get-tuple-element.45), channel_id=1, source_target_pairs={{0,2},{1,3},{2,4},{3,5},{4,6},{5,7},{6,0},{7,1},{8,10},{9,11},{10,... | collective-permute-start | bytes 688136 | tf_op jit(solution)/shard_map/ppermute | solution.py:474
  96.9 13.2 %collective-permute-start.21 = (bf16[128,896]{1,0:T(8,128)(2,1)S(1)}, bf16[128,896]{1,0:T(8,128)(2,1)S(1)}, u32[]{:S(2)}, u32[]{:S(2)}) collective-permute-start(bf16[128,896]{1,0:T(8,128)(2,1)S(1)} %get-tuple-element.46), channel_id=1, source_target_pairs={{0,6},{1,7},{2,0},{3,1},{4,2},{5,3},{6,4},{7,5},{8,14},{9,15},{10,... | collective-permute-start | bytes 688136 | tf_op jit(solution)/shard_map/ppermute | solution.py:474
  100.1 19.0 %collective-permute-start.20 = (bf16[128,896]{1,0:T(8,128)(2,1)S(1)}, bf16[128,896]{1,0:T(8,128)(2,1)S(1)}, u32[]{:S(2)}, u32[]{:S(2)}) collective-permute-start(bf16[128,896]{1,0:T(8,128)(2,1)S(1)} %get-tuple-element.47), channel_id=1, source_target_pairs={{0,4},{1,5},{2,6},{3,7},{4,0},{5,1},{6,2},{7,3},{8,12},{9,13},{10,... | collective-permute-start | bytes 688136 | tf_op jit(solution)/shard_map/ppermute | solution.py:474
  120.3 6.6 %collective-permute-start.22 = (bf16[128,896]{1,0:T(8,128)(2,1)S(1)}, bf16[128,896]{1,0:T(8,128)(2,1)S(1)}, u32[]{:S(2)}, u32[]{:S(2)}) collective-permute-start(bf16[128,896]{1,0:T(8,128)(2,1)S(1)} %fusion.6.sums_ref.refs_0_), channel_id=1, source_target_pairs={{0,2},{1,3},{2,0},{3,1},{4,6},{5,7},{6,4},{7,5},{8,10},{9,11},{10,... | collective-permute-start | bytes 688136 | tf_op jit(solution)/shard_map/ppermute | solution.py:517
  120.3 11.1 %collective-permute-start.17 = (bf16[4,64,896]{2,1,0:T(8,128)(2,1)}, bf16[4,64,896]{2,1,0:T(8,128)(2,1)}, u32[]{:S(2)}, u32[]{:S(2)}) collective-permute-start(bf16[4,64,896]{2,1,0:T(8,128)(2,1)} %get-tuple-element.35), channel_id=1, source_target_pairs={{0,1},{1,0},{2,3},{3,2},{4,5},{5,4},{6,7},{7,6},{8,9},{9,8},{10,11... | collective-permute-start | bytes 1376264 | tf_op jit(solution)/shard_map/ppermute | solution.py:471
  120.4 10.0 %collective-permute-start.23 = (bf16[128,896]{1,0:T(8,128)(2,1)S(1)}, bf16[128,896]{1,0:T(8,128)(2,1)S(1)}, u32[]{:S(2)}, u32[]{:S(2)}) collective-permute-start(bf16[128,896]{1,0:T(8,128)(2,1)S(1)} %fusion.6.sums_ref.refs_0_), channel_id=1, source_target_pairs={{0,1},{1,0},{2,3},{3,2},{4,5},{5,4},{6,7},{7,6},{8,9},{9,8},{10,11... | collective-permute-start | bytes 688136 | tf_op jit(solution)/shard_map/ppermute | solution.py:471
  122.8 31.0 %copy-start.10 = (f32[4,16]{1,0:T(4,128)S(1)}, f32[4,16]{1,0:T(4,128)}, u32[]{:S(2)}) copy-start(f32[4,16]{1,0:T(4,128)} %coef_ref.3) | copy-start | bytes 772
  126.9 3.5 %collective-permute-start.24 = (bf16[128,896]{1,0:T(8,128)(2,1)S(1)}, bf16[128,896]{1,0:T(8,128)(2,1)S(1)}, u32[]{:S(2)}, u32[]{:S(2)}) collective-permute-start(bf16[128,896]{1,0:T(8,128)(2,1)S(1)} %broadcast_add_fusion.1.refs_1_), channel_id=1, source_target_pairs={{0,1},{1,0},{2,3},{3,2},{4,5},{5,4},{6,7},{7,6},{8,9},{9,8},{10,11... | collective-permute-start | bytes 688136 | tf_op jit(solution)/shard_map/ppermute | solution.py:471
  127.5 8.4 %collective-permute-start.28 = (bf16[64,896]{1,0:T(8,128)(2,1)S(1)}, bf16[64,896]{1,0:T(8,128)(2,1)S(1)}, u32[]{:S(2)}, u32[]{:S(2)}) collective-permute-start(bf16[64,896]{1,0:T(8,128)(2,1)S(1)} %get-tuple-element.41), channel_id=1, source_target_pairs={{0,0},{1,1},{2,4},{3,5},{4,2},{5,3},{6,6},{7,7},{8,8},{9,9},{10,12... | collective-permute-start | bytes 344072 | tf_op jit(solution)/shard_map/ppermute | solution.py:529
  128.2 8.9 %collective-permute-start.29 = (bf16[64,896]{1,0:T(8,128)(2,1)S(1)}, bf16[64,896]{1,0:T(8,128)(2,1)S(1)}, u32[]{:S(2)}, u32[]{:S(2)}) collective-permute-start(bf16[64,896]{1,0:T(8,128)(2,1)S(1)} %get-tuple-element.42), channel_id=1, source_target_pairs={{0,2},{1,3},{2,6},{3,7},{4,0},{5,1},{6,4},{7,5},{8,10},{9,11},{10,... | collective-permute-start | bytes 344072 | tf_op jit(solution)/shard_map/ppermute | solution.py:529
  132.9 7.4 %collective-permute-start.25 = (bf16[64,896]{1,0:T(8,128)(2,1)S(1)}, bf16[64,896]{1,0:T(8,128)(2,1)S(1)}, u32[]{:S(2)}, u32[]{:S(2)}) collective-permute-start(bf16[64,896]{1,0:T(8,128)(2,1)S(1)} %get-tuple-element.48), channel_id=1, source_target_pairs={{0,2},{1,3},{2,4},{3,5},{4,6},{5,7},{6,0},{7,1},{8,10},{9,11},{10,... | collective-permute-start | bytes 344072 | tf_op jit(solution)/shard_map/ppermute | solution.py:474
  132.9 15.8 %collective-permute-start.32 = (bf16[224,896]{1,0:T(8,128)(2,1)S(1)}, bf16[224,896]{1,0:T(8,128)(2,1)S(1)}, u32[]{:S(2)}, u32[]{:S(2)}) collective-permute-start(bf16[224,896]{1,0:T(8,128)(2,1)S(1)} %get-tuple-element.44), channel_id=1, source_target_pairs={{0,24},{8,16},{16,8},{24,0},{1,25},{9,17},{17,9},{25,1},{2,26},{10... | collective-permute-start | bytes 1204232 | tf_op jit(solution)/shard_map/ppermute | solution.py:468
  135.6 18.0 %collective-permute-start.31 = (bf16[224,896]{1,0:T(8,128)(2,1)S(1)}, bf16[224,896]{1,0:T(8,128)(2,1)S(1)}, u32[]{:S(2)}, u32[]{:S(2)}) collective-permute-start(bf16[224,896]{1,0:T(8,128)(2,1)S(1)} %get-tuple-element.44), channel_id=1, source_target_pairs={{0,16},{8,24},{16,0},{24,8},{1,17},{9,25},{17,1},{25,9},{2,18},{10... | collective-permute-start | bytes 1204232 | tf_op jit(solution)/shard_map/ppermute | solution.py:468
  135.9 17.9 %collective-permute-start.30 = (bf16[224,896]{1,0:T(8,128)(2,1)S(1)}, bf16[224,896]{1,0:T(8,128)(2,1)S(1)}, u32[]{:S(2)}, u32[]{:S(2)}) collective-permute-start(bf16[224,896]{1,0:T(8,128)(2,1)S(1)} %get-tuple-element.44), channel_id=1, source_target_pairs={{0,8},{8,0},{16,24},{24,16},{1,9},{9,1},{17,25},{25,17},{2,10},{10... | collective-permute-start | bytes 1204232 | tf_op jit(solution)/shard_map/ppermute | solution.py:468
  137.1 5.7 %collective-permute-start.27 = (bf16[64,896]{1,0:T(8,128)(2,1)S(1)}, bf16[64,896]{1,0:T(8,128)(2,1)S(1)}, u32[]{:S(2)}, u32[]{:S(2)}) collective-permute-start(bf16[64,896]{1,0:T(8,128)(2,1)S(1)} %get-tuple-element.49), channel_id=1, source_target_pairs={{0,6},{1,7},{2,0},{3,1},{4,2},{5,3},{6,4},{7,5},{8,14},{9,15},{10,... | collective-permute-start | bytes 344072 | tf_op jit(solution)/shard_map/ppermute | solution.py:474
  140.2 6.8 %collective-permute-start.26 = (bf16[64,896]{1,0:T(8,128)(2,1)S(1)}, bf16[64,896]{1,0:T(8,128)(2,1)S(1)}, u32[]{:S(2)}, u32[]{:S(2)}) collective-permute-start(bf16[64,896]{1,0:T(8,128)(2,1)S(1)} %get-tuple-element.50), channel_id=1, source_target_pairs={{0,4},{1,5},{2,6},{3,7},{4,0},{5,1},{6,2},{7,3},{8,12},{9,13},{10,... | collective-permute-start | bytes 344072 | tf_op jit(solution)/shard_map/ppermute | solution.py:474

commit v9 on v8

--- a/solution.py
+++ b/solution.py
@@ -35,7 +35,7 @@
     return [(0, first), (first, depth - first)]
 
 
-def merge_kernel(parts, place_ref, coef_ref, experts_ref, *refs):
+def merge_kernel(parts, place_ref, coef_ref, experts_ref, _, *refs):
     part_refs, held_ref, sems = refs[:-2], refs[-2], refs[-1]
     systems, count = coef_ref.shape[0], experts_ref.shape[0]
     width = experts_ref.shape[2]
@@ -64,7 +64,7 @@
                     part_refs[k][at, cols] = total.astype(part_refs[k].dtype)
 
 
-def merge_parts(place, coef, experts, parts):
+def merge_parts(place, coef, experts, earlier, parts):
     _, depth, width = experts.shape
     systems = coef.shape[0]
     return pl.pallas_call(
@@ -72,7 +72,7 @@
         out_shape=[
             jax.ShapeDtypeStruct((depth, width), BF16 if k else F32) for k in range(systems)
         ],
-        in_specs=[whole_smem(), whole_smem(), in_hbm()],
+        in_specs=[whole_smem(), whole_smem(), in_hbm(), in_hbm()],
         out_specs=[whole_vmem()] * systems,
         scratch_shapes=[
             pltpu.VMEM(experts.shape, BF16),
@@ -80,23 +80,30 @@
         ],
         compiler_params=params(),
         name="merge_parts",
-    )(place, coef, experts)
-
-
-def join_kernel(atoms_ref, cot_ref, _, both_ref):
-    both_ref[0] = atoms_ref[0]
-    both_ref[1] = cot_ref[0]
-
-
-def join(atoms, cotangent, earlier):
+    )(place, coef, experts, earlier)
+
+
+def join_kernel(atoms_ref, cot_ref, both_ref, sems):
+    loads = [
+        pltpu.make_async_copy(ref.at[0], both_ref.at[i], sems.at[i])
+        for i, ref in enumerate((atoms_ref, cot_ref))
+    ]
+    for load in loads:
+        load.start()
+    for load in loads:
+        load.wait()
+
+
+def join(atoms, cotangent):
     return pl.pallas_call(
         join_kernel,
         out_shape=jax.ShapeDtypeStruct((2, *atoms.shape[1:]), BF16),
-        in_specs=[whole_vmem(), whole_vmem(), in_hbm()],
+        in_specs=[in_hbm(), in_hbm()],
         out_specs=whole_vmem(),
-        compiler_params=params(SMALL),
+        scratch_shapes=[pltpu.SemaphoreType.DMA((2,))],
+        compiler_params=params(),
         name="join",
-    )(atoms, cotangent, earlier)
+    )(atoms, cotangent)
 
 
 def rows_kernel(count, *refs):
@@ -118,8 +125,9 @@
     )(*parts, *earlier)
 
 
-def merged_grad_kernel(place_ref, cols_ref, *refs):
-    block_refs, grad_ref, sent_ref, token_ref, sums_ref = refs[:-4], *refs[-4:]
+def merged_grad_kernel(through, place_ref, cols_ref, *refs):
+    grad_ref, sent_ref, sums_ref = refs[-through - 3], refs[-through - 2], refs[-1]
+    block_refs = refs[: -2 * through - 3]
     size = block_refs[0].shape[0]
     pieces = len(block_refs) // 2
     for i, ref in enumerate(block_refs):
@@ -129,21 +137,22 @@
     grad = jnp.dot(cols_ref[...], sums_ref[...], preferred_element_type=F32)
     grad_ref[...] = grad
     sent_ref[...] = grad.astype(BF16)
-    token_ref[...] = jnp.zeros_like(token_ref)
-
-
-def merged_grads(place, cols, blocks):
+    for i in range(through):
+        refs[len(block_refs) + through + 2 + i][...] = refs[len(block_refs) + i][...]
+
+
+def merged_grads(place, cols, blocks, others):
     size, width = blocks[0].shape
     return pl.pallas_call(
-        merged_grad_kernel,
+        functools.partial(merged_grad_kernel, len(others)),
         out_shape=[jax.ShapeDtypeStruct((cols.shape[0], width), kind) for kind in (F32, BF16)]
-        + [jax.ShapeDtypeStruct((1, width), F32)],
-        in_specs=[whole_smem()] + [whole_vmem()] * (1 + len(blocks)),
-        out_specs=[whole_vmem()] * 3,
+        + [jax.ShapeDtypeStruct(other.shape, other.dtype) for other in others],
+        in_specs=[whole_smem()] + [whole_vmem()] * (1 + len(blocks) + len(others)),
+        out_specs=[whole_vmem()] * (2 + len(others)),
         scratch_shapes=[pltpu.VMEM((size * len(blocks), width), BF16)],
         compiler_params=params(SMALL),
         name="merged_grads",
-    )(place, cols, *blocks)
+    )(place, cols, *blocks, *others)
 
 
 def atom_grad_kernel(
@@ -476,8 +485,8 @@
     def both_cores(blocks):
         return blocks + [swap(block) for block in blocks]
 
-    merged = merge_parts(place, coef, experts, parts)
-    pair = join(atoms, cotangent, merged[-1])
+    pair = join(atoms, cotangent)
+    merged = merge_parts(place, coef, experts, pair, parts)
     features = both_cores([pair] + [shift(pair, k) for k in range(1, chips)])
 
     at = jnp.arange(ways * own, dtype=jnp.int32)
@@ -502,15 +511,18 @@
         chips, place, hot_gather, hot_sum, radial[0], scaled, all_atoms, blocks, tile
     )
 
-    def reduce(kept, other, zero):
-        terms = [kept[k] + other[k].astype(F32) + zero for k in range(chips)]
-        total = terms[0]
-        for k in range(1, chips):
-            total = total + shift(terms[k].astype(BF16), k).astype(F32)
+    def terms_of(kept, other):
+        terms = [kept[k] + other[k].astype(F32) for k in range(chips)]
+        return terms[0], [term.astype(BF16) for term in terms[1:]]
+
+    def reduce(total, terms):
+        for k, term in enumerate(terms, 1):
+            total = total + shift(term, k).astype(F32)
         return total.astype(BF16)
 
     shares = chips // 2
-    sums = reduce(kept, swap(sent), 0.0)
+    sums = reduce(*terms_of(kept, swap(sent)))
+    node, node_terms = terms_of(node_kept, swap(node_sent))
 
     def share(x, j):
         to = [z // shares * shares + (z + j) % shares for z in range(chips)]
@@ -518,7 +530,7 @@
 
     *terms, term_token = atom_grads(chips, place, sums, weight)
     picked = both_cores([sums] + [share(sums, j) + term_token for j in range(1, shares)])
-    grad, send, grad_token = merged_grads(place, own_cols, picked)
+    grad, send, *node_terms = merged_grads(place, own_cols, picked, node_terms)
     grads = [grad] + [across(send, k) for k in range(1, systems)]
     expert_grad = expert_grads(place, coef, grads, experts.shape, parts)
 
@@ -528,8 +540,7 @@
         pairs = [(2 * z + c, 2 * to[z] + c) for z in range(chips) for c in range(2)]
         atom_grad = atom_grad + lax.ppermute(term, "edge", pairs).astype(F32)
 
-    node = reduce(node_kept, swap(node_sent), grad_token)
-    return node[None], atom_grad[None], expert_grad
+    return reduce(node, node_terms)[None], atom_grad[None], expert_grad
 
 
 def solution(mesh):

time: 157 us -> 160 us (1.019)
  starting transfers between devices: 36.2 us -> 24.7 us
  waiting for transfers between devices: 56.8 us -> 63.9 us
  local copies, waits for them, and re-layouts: 6.11 us -> 9.75 us
  Pallas kernels: 45.9 us -> 47.9 us
    ppermute x12, starting transfers between devices: 23.8 us -> 11.3 us  [shift(): lax.ppermute(x, 'edge', [(e, (e + 2 * k) % ways) for e in range(ways)])]
    ppermute x6, waiting for transfers between devices: 5.04 us -> 10.3 us  [across(): return lax.ppermute(x, 'sys', [(s, s ^ k) for s in range(systems)])]
    ppermute x2, waiting for transfers between devices: 0.65 us -> 5.23 us  [shards(): atom_grad = atom_grad + lax.ppermute(term, 'edge', pairs).astype(F32)]
    ppermute x1, waiting for transfers between devices: 4.03 us -> 0.01 us  [share(): lax.ppermute(x, 'edge', [(2 * z + c, 2 * to[z] + c) for z in range(chips)...]
    pallas_call x1, local copies, waits for them, and re-layouts: 0.53 us -> 2.23 us  [scaled_edges(): pl.pallas_call(functools.partial(scale_kernel, slots), grid=(edges // til...]
    pallas_call x1, Pallas kernels: 0.02 us -> 1.66 us  [join(): pl.pallas_call(join_kernel, out_shape=jax.ShapeDtypeStruct((2, *atoms.sha...]
    transpose x1, local copies, waits for them, and re-layouts: 0.02 us -> 1.64 us  [shards(): lax.dynamic_slice_in_dim(all_atoms, me_edge % chips * depth, depth, 1)]
  transfers between devices with their start and end apart: 33 -> 33, of which waited for: 13 -> 14; matrix products, arithmetic and copies ran while one was open for 6% -> 9% of each run, Pallas kernels for 11% -> 13%
where the time goes in v9:
time: 160 us; the launch traced here: 159 us
  waiting for transfers between devices  63.9 us (40%)
  Pallas kernels  47.9 us (30%)
  starting transfers between devices  24.7 us (15%)
  other arithmetic  11.5 us (7%)
  local copies, waits for them, and re-layouts  9.75 us (6%)
    ppermute x12, waiting for transfers between devices, shift(): lax.ppermute(x, 'edge', [(e, (e + 2 * k) % ways) for e in range(ways)])  44.1 us
    pallas_call x1, Pallas kernels, edge_sums(): pl.pallas_call(functools.partial(edge_kernel, chips), grid=(steps + 1,),...  22.3 us
    ppermute x12, starting transfers between devices, shift(): lax.ppermute(x, 'edge', [(e, (e + 2 * k) % ways) for e in range(ways)])  11.3 us
    ppermute x6, waiting for transfers between devices, across(): return lax.ppermute(x, 'sys', [(s, s ^ k) for s in range(systems)])  10.3 us
    pallas_call x1, Pallas kernels, scaled_edges(): pl.pallas_call(functools.partial(scale_kernel, slots), grid=(edges // til...  7.95 us
    ppermute x6, starting transfers between devices, across(): return lax.ppermute(x, 'sys', [(s, s ^ k) for s in range(systems)])  7.09 us
    pallas_call x1, Pallas kernels, hot_ends(): pl.pallas_call(hot_kernel, grid=(edges // tile,), out_shape=[jax.ShapeDty...  5.65 us
    ppermute x2, waiting for transfers between devices, shards(): atom_grad = atom_grad + lax.ppermute(term, 'edge', pairs).astype(F32)  5.23 us
  transfers between devices with their start and end apart: 33, of which 14 were waited for; matrix products, arithmetic and copies ran while one was open for 9% of the time, Pallas kernels for 13%

profile of v9, /device:TPU:0, one launch (start us, length us, event | category | flops | bytes accessed | tf_op | source)
XLA Modules:
  0.0 158.9 jit_solution(15778761927300981020)
XLA Ops:
  0.6 1.7 %join.1._.refs_0_ = bf16[2,64,896]{2,1,0:T(8,128)(2,1)} custom-call(bf16[1,64,896]{2,1,0:T(8,128)(2,1)} %atoms_ref.1, bf16[1,64,896]{2,1,0:T(8,128)(2,1)} %cot_ref.1), custom_call_target="tpu_custom_call" | custom-call | tf_op jit(solution)/shard_map/join/pallas_call | solution.py:98
  2.3 5.1 %collective-permute-start.2 = (bf16[2,64,896]{2,1,0:T(8,128)(2,1)}, bf16[2,64,896]{2,1,0:T(8,128)(2,1)S(1)}, u32[]{:S(2)}, u32[]{:S(2)}) collective-permute-start(bf16[2,64,896]{2,1,0:T(8,128)(2,1)} %join.1._.refs_0_), channel_id=1, source_target_pairs={{0,6},{1,7},{2,0},{3,1},{4,2},{5,3},{6,4},{7,5},{8,14},{9,15},{10,... | collective-permute-start | bytes 688136 | tf_op jit(solution)/shard_map/ppermute | solution.py:483
  7.4 0.6 pad_add_fusion.1.place_ref
  8.0 4.1 %merge_parts.1 = (f32[224,896]{1,0:T(8,128)}, bf16[224,896]{1,0:T(8,128)(2,1)}, bf16[224,896]{1,0:T(8,128)(2,1)}, bf16[224,896]{1,0:T(8,128)(2,1)}) custom-call(s32[3]{0:T(128)} %pad_add_fusion.1.place_ref, f32[4,16]{1,0:T(4,128)} %coef_ref.3, bf16[4,224,896]{2,1,0:T(8,128)(2,1)} %experts_ref.1, bf16[2,64,896]{2,1,0:T(8,128)(2,1)} %join.1._.refs_0_), custom_call_target="tpu_custom_call" | custom-call | tf_op jit(solution)/shard_map/merge_parts/pallas_call | solution.py:70
  12.1 1.6 collective-permute-start.7
  13.7 1.5 collective-permute-start.8
  15.2 0.5 collective-permute-start.9
  15.7 1.3 pad_add_fusion
  17.0 1.3 copy.13.cols_ref
  18.4 1.0 collective-permute-start
  19.4 0.6 fusion.28.across_ref
  20.0 0.8 fusion.13.down_ref
  20.8 5.6 %hot_ends.1 = (bf16[2048,1024]{1,0:T(8,128)(2,1)}, bf16[1024,2048]{1,0:T(8,128)(2,1)}, f32[1,896]{1,0:T(1,128)}) custom-call(s32[2048,2]{1,0:T(8,128)} %copy.13.cols_ref, s32[2,2048]{1,0:T(2,128)} %get-tuple-element.55.rows_ref, s32[1,512]{1,0:T(1,128)} %fusion.28.across_ref, s32[512,1]{1,0:T(8,128)} %fusion.13.down_ref, bf16[2,64,896]{2,1,0:T(8,128)(2,1)} %join.1._.refs_0_), custom_call_target="tpu_custom_call" | custom-call | flops 16777216 | bytes 8388608 | tf_op jit(solution)/shard_map/hot_ends/pallas_call | solution.py:249
  26.4 0.7 collective-permute-done.1.refs_2_.refs_5_
  27.1 5.8 %collective-permute-done.8.refs_2_ = bf16[224,896]{1,0:T(8,128)(2,1)S(1)} collective-permute-done((bf16[224,896]{1,0:T(8,128)(2,1)}, bf16[224,896]{1,0:T(8,128)(2,1)S(1)}, u32[]{:S(2)}, u32[]{:S(2)}) %collective-permute-start.8) | collective-permute-done | bytes 401440 | tf_op jit(solution)/shard_map/ppermute | solution.py:477
  33.0 0.7 copy-done.9
  33.7 0.2 weight_rows.1.refs_0_
  33.9 0.8 collective-permute-start.11
  34.6 0.5 collective-permute-start.6
  35.2 0.5 collective-permute-start.4
  35.7 9.7 %collective-permute-done.11.refs_2_ = bf16[224,896]{1,0:T(8,128)(2,1)S(1)} collective-permute-done((bf16[224,896]{1,0:T(8,128)(2,1)S(1)}, bf16[224,896]{1,0:T(8,128)(2,1)S(1)}, u32[]{:S(2)}, u32[]{:S(2)}) %collective-permute-start.11) | collective-permute-done | bytes 401440 | tf_op jit(solution)/shard_map/ppermute | solution.py:483
  45.4 0.6 copy-done.14
  46.2 0.1 copy-done.16
  46.3 7.9 %scaled_edges.1 = (bf16[512,896]{1,0:T(8,128)(2,1)}, bf16[2048,896]{1,0:T(8,128)(2,1)}, bf16[1,896]{1,0:T(2,128)(2,1)}) custom-call(s32[3]{0:T(128)} %pad_add_fusion.1.place_ref, bf16[2048,1024]{1,0:T(8,128)(2,1)} %get-tuple-element.26.gather_ref, bf16[2048,896]{1,0:T(8,128)(2,1)} %bitcast.42, bf16[2,64,896]{2,1,0:T(8,128)(2,1)} %join.1._.refs_0_, ...), custom_call_target="tpu_custom_call" | custom-call | flops 1879048192 | bytes 11010048 | tf_op jit(solution)/shard_map/scaled_edges/pallas_call | solution.py:311
  54.3 0.7 reduce
  55.0 0.9 collective-permute-done.13.refs_4_
  55.9 0.4 collective-permute-start.15
  56.3 0.5 collective-permute-start.12
  56.8 8.8 %collective-permute-done.15.refs_6_ = bf16[224,896]{1,0:T(8,128)(2,1)S(1)} collective-permute-done((bf16[224,896]{1,0:T(8,128)(2,1)S(1)}, bf16[224,896]{1,0:T(8,128)(2,1)S(1)}, u32[]{:S(2)}, u32[]{:S(2)}) %collective-permute-start.15) | collective-permute-done | bytes 401440 | tf_op jit(solution)/shard_map/ppermute | solution.py:483
  65.7 1.7 %collective-permute-done.16.refs_7_ = bf16[224,896]{1,0:T(8,128)(2,1)S(1)} collective-permute-done((bf16[224,896]{1,0:T(8,128)(2,1)S(1)}, bf16[224,896]{1,0:T(8,128)(2,1)S(1)}, u32[]{:S(2)}, u32[]{:S(2)}) %collective-permute-start.16) | collective-permute-done | bytes 401440 | tf_op jit(solution)/shard_map/ppermute | solution.py:480
  67.4 0.7 copy-done.23
  68.1 22.3 %edge_sums.1 = (f32[4,128,896]{2,1,0:T(8,128)}, bf16[4,128,896]{2,1,0:T(8,128)(2,1)}, f32[4,64,896]{2,1,0:T(8,128)}, bf16[4,64,896]{2,1,0:T(8,128)(2,1)}, bf16[1792,896]{1,0:T(8,128)(2,1)}) custom-call(s32[3]{0:T(128)} %pad_add_fusion.1.place_ref, bf16[2048,1024]{1,0:T(8,128)(2,1)} %get-tuple-element.26.gather_ref, ...), custom_call_target="tpu_custom_call" | custom-call | flops 11039408128 | bytes 15728640 | tf_op jit(solution)/shard_map/edge_sums/pallas_call | solution.py:433
  90.4 0.2 collective-permute-start.18
  90.6 2.6 %collective-permute-done.18 = bf16[4,128,896]{2,1,0:T(8,128)(2,1)S(1)} collective-permute-done((bf16[4,128,896]{2,1,0:T(8,128)(2,1)}, bf16[4,128,896]{2,1,0:T(8,128)(2,1)S(1)}, u32[]{:S(2)}, u32[]{:S(2)}) %collective-permute-start.18) | collective-permute-done | bytes 917536 | tf_op jit(solution)/shard_map/ppermute | solution.py:480
  93.1 1.6 fusion.18
  94.8 3.8 %collective-permute-start.21 = (bf16[128,896]{1,0:T(8,128)(2,1)S(1)}, bf16[128,896]{1,0:T(8,128)(2,1)S(1)}, u32[]{:S(2)}, u32[]{:S(2)}) collective-permute-start(bf16[128,896]{1,0:T(8,128)(2,1)S(1)} %get-tuple-element.50), channel_id=1, source_target_pairs={{0,6},{1,7},{2,0},{3,1},{4,2},{5,3},{6,4},{7,5},{8,14},{9,15},{10,... | collective-permute-start | bytes 688136 | tf_op jit(solution)/shard_map/ppermute | solution.py:483
  98.6 6.5 %collective-permute-done.19 = bf16[128,896]{1,0:T(8,128)(2,1)S(1)} collective-permute-done((bf16[128,896]{1,0:T(8,128)(2,1)S(1)}, bf16[128,896]{1,0:T(8,128)(2,1)S(1)}, u32[]{:S(2)}, u32[]{:S(2)}) %collective-permute-start.19) | collective-permute-done | bytes 229408 | tf_op jit(solution)/shard_map/ppermute | solution.py:483
  105.0 3.3 %collective-permute-done.21 = bf16[128,896]{1,0:T(8,128)(2,1)S(1)} collective-permute-done((bf16[128,896]{1,0:T(8,128)(2,1)S(1)}, bf16[128,896]{1,0:T(8,128)(2,1)S(1)}, u32[]{:S(2)}, u32[]{:S(2)}) %collective-permute-start.21) | collective-permute-done | bytes 229408 | tf_op jit(solution)/shard_map/ppermute | solution.py:483
  108.4 9.0 %collective-permute-done.20 = bf16[128,896]{1,0:T(8,128)(2,1)S(1)} collective-permute-done((bf16[128,896]{1,0:T(8,128)(2,1)S(1)}, bf16[128,896]{1,0:T(8,128)(2,1)S(1)}, u32[]{:S(2)}, u32[]{:S(2)}) %collective-permute-start.20) | collective-permute-done | bytes 229408 | tf_op jit(solution)/shard_map/ppermute | solution.py:483
  117.4 1.1 fusion.6.sums_ref.refs_0_
  118.7 2.2 %copy.14 = bf16[512,896]{0,1:T(8,128)(2,1)} copy(bf16[512,896]{1,0:T(8,128)(2,1)} %get-tuple-element.29.atoms_hbm) | data formatting | bytes 1835008 | tf_op jit(solution)/shard_map/scaled_edges/pallas_call | solution.py:311
  120.9 1.6 %dynamic-slice_bitcast_fusion.cols_ref = bf16[224,512]{1,0:T(8,128)(2,1)} fusion(bf16[512,896]{0,1:T(8,128)(2,1)} %copy.14, s32[]{:T(128)S(6)} %select_n.111), kind=kLoop, calls=%fused_computation.43 | loop fusion | bytes 458756 | tf_op jit(solution)/shard_map/transpose | solution.py:498
  122.6 0.5 collective-permute-start.23
  123.1 1.8 %atom_grads.1 = (bf16[64,896]{1,0:T(8,128)(2,1)S(1)}, bf16[64,896]{1,0:T(8,128)(2,1)S(1)}, bf16[1,896]{1,0:T(2,128)(2,1)S(1)}) custom-call(s32[3]{0:T(128)S(1)} %copy-done.7, bf16[128,896]{1,0:T(8,128)(2,1)S(1)} %fusion.6.sums_ref.refs_0_, bf16[1792,896]{1,0:T(8,128)(2,1)S(1)} %copy-done), custom_call_target="tpu_custom_call" | custom-call | flops 205520896 | bytes 1605632 | tf_op jit(solution)/shard_map/atom_grads/pallas_call | solution.py:178
  124.9 0.6 copy-done.10
  125.5 0.6 copy-done.11
  126.2 1.0 broadcast_add_fusion.1.refs_1_
  127.2 0.1 collective-permute-start.24
  127.3 1.4 fusion.26
  128.6 1.6 collective-permute-start.28
  130.2 2.4 %collective-permute-start.29 = (bf16[64,896]{1,0:T(8,128)(2,1)}, bf16[64,896]{1,0:T(8,128)(2,1)S(1)}, u32[]{:S(2)}, u32[]{:S(2)}) collective-permute-start(bf16[64,896]{1,0:T(8,128)(2,1)} %copy-done.10), channel_id=1, source_target_pairs={{0,2},{1,3},{2,6},{3,7},{4,0},{5,1},{6,4},{7,5},{8,10},{9,11},{10,... | collective-permute-start | bytes 344072 | tf_op jit(solution)/shard_map/ppermute | solution.py:541
  132.6 0.9 copy-done.1
  133.5 1.4 merged_grads.1
  135.0 0.1 collective-permute-start.25
  135.0 1.4 collective-permute-start.32
  136.5 1.7 %collective-permute-start.31 = (bf16[224,896]{1,0:T(8,128)(2,1)S(1)}, bf16[224,896]{1,0:T(8,128)(2,1)S(1)}, u32[]{:S(2)}, u32[]{:S(2)}) collective-permute-start(bf16[224,896]{1,0:T(8,128)(2,1)S(1)} %get-tuple-element.48), channel_id=1, source_target_pairs={{0,16},{8,24},{16,0},{24,8},{1,17},{9,25},{17,1},{25,9},{2,18},{10... | collective-permute-start | bytes 1204232 | tf_op jit(solution)/shard_map/ppermute | solution.py:477
  138.2 0.4 collective-permute-start.30
  138.6 5.2 %collective-permute-done.29 = bf16[64,896]{1,0:T(8,128)(2,1)S(1)} collective-permute-done((bf16[64,896]{1,0:T(8,128)(2,1)}, bf16[64,896]{1,0:T(8,128)(2,1)S(1)}, u32[]{:S(2)}, u32[]{:S(2)}) %collective-permute-start.29) | collective-permute-done | bytes 114720 | tf_op jit(solution)/shard_map/ppermute | solution.py:541
  143.8 0.7 add_bitcast_fusion
  144.5 5.1 %collective-permute-done.26 = bf16[64,896]{1,0:T(8,128)(2,1)S(1)} collective-permute-done((bf16[64,896]{1,0:T(8,128)(2,1)S(1)}, bf16[64,896]{1,0:T(8,128)(2,1)S(1)}, u32[]{:S(2)}, u32[]{:S(2)}) %collective-permute-start.26) | collective-permute-done | bytes 114720 | tf_op jit(solution)/shard_map/ppermute | solution.py:483
  149.6 0.2 collective-permute-done.27
  149.8 1.7 %fusion.27 = bf16[1,64,896]{2,1,0:T(8,128)(2,1)} fusion(bf16[64,896]{1,0:T(8,128)(2,1)S(1)} %collective-permute-done.27, bf16[64,896]{1,0:T(8,128)(2,1)S(1)} %collective-permute-done.26, bf16[64,896]{1,0:T(8,128)(2,1)S(1)} %collective-permute-done.25, f32[4,64,896]{2,1,0:T(8,128)} %get-tuple-element.36, bf16[4,64,896]{2,1,0:T(8,128)(2,1)} %collective-permute-done.17), kind=kLoop, calls=%fused_computation.48 | loop fusion | flops 516096 | bytes 802816 | tf_op jit(solution)/shard_map/broadcast_in_dim | solution.py:543
  151.6 4.4 %collective-permute-done.31.refs_2_ = bf16[224,896]{1,0:T(8,128)(2,1)S(1)} collective-permute-done((bf16[224,896]{1,0:T(8,128)(2,1)S(1)}, bf16[224,896]{1,0:T(8,128)(2,1)S(1)}, u32[]{:S(2)}, u32[]{:S(2)}) %collective-permute-start.31) | collective-permute-done | bytes 401440 | tf_op jit(solution)/shard_map/ppermute | solution.py:477
  156.0 2.8 %expert_grads.1 = f32[4,224,896]{2,1,0:T(8,128)} custom-call(s32[3]{0:T(128)S(1)} %copy-done.7, f32[4,16]{1,0:T(4,128)S(1)} %copy-done.8, f32[224,896]{1,0:T(8,128)S(1)} %get-tuple-element.47.refs_0_, bf16[224,896]{1,0:T(8,128)(2,1)S(1)} %collective-permute-done.30.refs_1_, bf16[224,896]{1,0:T(8,128)(2,1)S(1)} %collective-permute-done.31.refs_2_, ...), custom_call_target="tpu_custom_call" | custom-call | tf_op jit(solution)/shard_map/expert_grads/pallas_call | solution.py:222
  (75 shorter events, 0.6 us)
Async XLA Ops:
  2.3 16.1 %collective-permute-start.2 = (bf16[2,64,896]{2,1,0:T(8,128)(2,1)}, bf16[2,64,896]{2,1,0:T(8,128)(2,1)S(1)}, u32[]{:S(2)}, u32[]{:S(2)}) collective-permute-start(bf16[2,64,896]{2,1,0:T(8,128)(2,1)} %join.1._.refs_0_), channel_id=1, source_target_pairs={{0,6},{1,7},{2,0},{3,1},{4,2},{5,3},{6,4},{7,5},{8,14},{9,15},{10,... | collective-permute-start | bytes 688136 | tf_op jit(solution)/shard_map/ppermute | solution.py:483
  7.4 19.7 %collective-permute-start.1 = (bf16[2,64,896]{2,1,0:T(8,128)(2,1)}, bf16[2,64,896]{2,1,0:T(8,128)(2,1)S(1)}, u32[]{:S(2)}, u32[]{:S(2)}) collective-permute-start(bf16[2,64,896]{2,1,0:T(8,128)(2,1)} %join.1._.refs_0_), channel_id=1, source_target_pairs={{0,4},{1,5},{2,6},{3,7},{4,0},{5,1},{6,2},{7,3},{8,12},{9,13},{10,... | collective-permute-start | bytes 688136 | tf_op jit(solution)/shard_map/ppermute | solution.py:483
  12.1 20.9 %copy-start.5 = (f32[224,896]{1,0:T(8,128)S(1)}, f32[224,896]{1,0:T(8,128)}, u32[]{:S(2)}) copy-start(f32[224,896]{1,0:T(8,128)} %get-tuple-element.30.refs_0_) | copy-start | bytes 2408452
  12.1 22.5 %copy-start.12 = (bf16[2,64,896]{2,1,0:T(8,128)(2,1)S(1)}, bf16[2,64,896]{2,1,0:T(8,128)(2,1)}, u32[]{:S(2)}) copy-start(bf16[2,64,896]{2,1,0:T(8,128)(2,1)} %join.1._.refs_0_) | copy-start | bytes 688132
  12.1 15.0 %collective-permute-start.7 = (bf16[224,896]{1,0:T(8,128)(2,1)}, bf16[224,896]{1,0:T(8,128)(2,1)S(1)}, u32[]{:S(2)}, u32[]{:S(2)}) collective-permute-start(bf16[224,896]{1,0:T(8,128)(2,1)} %get-tuple-element.31), channel_id=1, source_target_pairs={{0,8},{8,0},{16,24},{24,16},{1,9},{9,1},{17,25},{25,17},{2,10},{10... | collective-permute-start | bytes 1204232 | tf_op jit(solution)/shard_map/ppermute | solution.py:477
  13.7 19.3 %collective-permute-start.8 = (bf16[224,896]{1,0:T(8,128)(2,1)}, bf16[224,896]{1,0:T(8,128)(2,1)S(1)}, u32[]{:S(2)}, u32[]{:S(2)}) collective-permute-start(bf16[224,896]{1,0:T(8,128)(2,1)} %get-tuple-element.32), channel_id=1, source_target_pairs={{0,16},{8,24},{16,0},{24,8},{1,17},{9,25},{17,1},{25,9},{2,18},{10... | collective-permute-start | bytes 1204232 | tf_op jit(solution)/shard_map/ppermute | solution.py:477
  15.2 17.8 %collective-permute-start.9 = (bf16[224,896]{1,0:T(8,128)(2,1)}, bf16[224,896]{1,0:T(8,128)(2,1)S(1)}, u32[]{:S(2)}, u32[]{:S(2)}) collective-permute-start(bf16[224,896]{1,0:T(8,128)(2,1)} %get-tuple-element.33), channel_id=1, source_target_pairs={{0,24},{8,16},{16,8},{24,0},{1,25},{9,17},{17,9},{25,1},{2,26},{10... | collective-permute-start | bytes 1204232 | tf_op jit(solution)/shard_map/ppermute | solution.py:477
  18.4 27.1 %copy-start.2 = (bf16[2,64,896]{2,1,0:T(8,128)(2,1)}, bf16[2,64,896]{2,1,0:T(8,128)(2,1)S(1)}, u32[]{:S(2)}) copy-start(bf16[2,64,896]{2,1,0:T(8,128)(2,1)S(1)} %collective-permute-done.2.refs_3_.refs_6_) | copy-start | bytes 688132
  18.4 8.7 %collective-permute-start = (bf16[2,64,896]{2,1,0:T(8,128)(2,1)}, bf16[2,64,896]{2,1,0:T(8,128)(2,1)S(1)}, u32[]{:S(2)}, u32[]{:S(2)}) collective-permute-start(bf16[2,64,896]{2,1,0:T(8,128)(2,1)} %join.1._.refs_0_), channel_id=1, source_target_pairs={{0,2},{1,3},{2,4},{3,5},{4,6},{5,7},{6,0},{7,1},{8,10},{9,11},{10,... | collective-permute-start | bytes 688136 | tf_op jit(solution)/shard_map/ppermute | solution.py:483
  27.1 18.3 %copy-start.3 = (bf16[2,64,896]{2,1,0:T(8,128)(2,1)}, bf16[2,64,896]{2,1,0:T(8,128)(2,1)S(1)}, u32[]{:S(2)}) copy-start(bf16[2,64,896]{2,1,0:T(8,128)(2,1)S(1)} %collective-permute-done.1.refs_2_.refs_5_) | copy-start | bytes 688132
  27.1 18.3 %copy-start.4 = (bf16[2,64,896]{2,1,0:T(8,128)(2,1)}, bf16[2,64,896]{2,1,0:T(8,128)(2,1)S(1)}, u32[]{:S(2)}) copy-start(bf16[2,64,896]{2,1,0:T(8,128)(2,1)S(1)} %collective-permute-done.refs_1_.refs_4_) | copy-start | bytes 688132
  33.0 0.7 copy-start.9
  33.8 22.4 %copy-start.6 = (bf16[224,896]{1,0:T(8,128)(2,1)}, bf16[224,896]{1,0:T(8,128)(2,1)S(1)}, u32[]{:S(2)}) copy-start(bf16[224,896]{1,0:T(8,128)(2,1)S(1)} %weight_rows.1.refs_0_) | copy-start | bytes 1204228
  33.9 11.5 %collective-permute-start.11 = (bf16[224,896]{1,0:T(8,128)(2,1)S(1)}, bf16[224,896]{1,0:T(8,128)(2,1)S(1)}, u32[]{:S(2)}, u32[]{:S(2)}) collective-permute-start(bf16[224,896]{1,0:T(8,128)(2,1)S(1)} %weight_rows.1.refs_0_), channel_id=1, source_target_pairs={{0,2},{1,3},{2,4},{3,5},{4,6},{5,7},{6,0},{7,1},{8,10},{9,11},{10,... | collective-permute-start | bytes 1204232 | tf_op jit(solution)/shard_map/ppermute | solution.py:483
  34.6 10.7 %collective-permute-start.3 = (bf16[2,64,896]{2,1,0:T(8,128)(2,1)S(1)}, bf16[2,64,896]{2,1,0:T(8,128)(2,1)S(1)}, u32[]{:S(2)}, u32[]{:S(2)}) collective-permute-start(bf16[2,64,896]{2,1,0:T(8,128)(2,1)S(1)} %copy-done.12), channel_id=1, source_target_pairs={{0,1},{1,0},{2,3},{3,2},{4,5},{5,4},{6,7},{7,6},{8,9},{9,8},{10,11... | collective-permute-start | bytes 688136 | tf_op jit(solution)/shard_map/ppermute | solution.py:480
  34.6 10.7 %collective-permute-start.6 = (bf16[2,64,896]{2,1,0:T(8,128)(2,1)S(1)}, bf16[2,64,896]{2,1,0:T(8,128)(2,1)S(1)}, u32[]{:S(2)}, u32[]{:S(2)}) collective-permute-start(bf16[2,64,896]{2,1,0:T(8,128)(2,1)S(1)} %collective-permute-done.2.refs_3_.refs_6_), channel_id=1, source_target_pairs={{0,1},{1,0},{2,3},{3,2},{4,5},{5,4},{6,7},{7,6},{8,9},{9,8},{10,11... | collective-permute-start | bytes 688136 | tf_op jit(solution)/shard_map/ppermute | solution.py:480
  35.2 10.2 %collective-permute-start.5 = (bf16[2,64,896]{2,1,0:T(8,128)(2,1)S(1)}, bf16[2,64,896]{2,1,0:T(8,128)(2,1)S(1)}, u32[]{:S(2)}, u32[]{:S(2)}) collective-permute-start(bf16[2,64,896]{2,1,0:T(8,128)(2,1)S(1)} %collective-permute-done.1.refs_2_.refs_5_), channel_id=1, source_target_pairs={{0,1},{1,0},{2,3},{3,2},{4,5},{5,4},{6,7},{7,6},{8,9},{9,8},{10,11... | collective-permute-start | bytes 688136 | tf_op jit(solution)/shard_map/ppermute | solution.py:480
  35.2 10.2 %collective-permute-start.4 = (bf16[2,64,896]{2,1,0:T(8,128)(2,1)S(1)}, bf16[2,64,896]{2,1,0:T(8,128)(2,1)S(1)}, u32[]{:S(2)}, u32[]{:S(2)}) collective-permute-start(bf16[2,64,896]{2,1,0:T(8,128)(2,1)S(1)} %collective-permute-done.refs_1_.refs_4_), channel_id=1, source_target_pairs={{0,1},{1,0},{2,3},{3,2},{4,5},{5,4},{6,7},{7,6},{8,9},{9,8},{10,11... | collective-permute-start | bytes 688136 | tf_op jit(solution)/shard_map/ppermute | solution.py:480
  45.3 22.0 %copy-start.18 = (bf16[224,896]{1,0:T(8,128)(2,1)}, bf16[224,896]{1,0:T(8,128)(2,1)S(1)}, u32[]{:S(2)}) copy-start(bf16[224,896]{1,0:T(8,128)(2,1)S(1)} %collective-permute-done.11.refs_2_) | copy-start | bytes 1204228
  45.3 10.5 %collective-permute-start.13 = (bf16[224,896]{1,0:T(8,128)(2,1)S(1)}, bf16[224,896]{1,0:T(8,128)(2,1)S(1)}, u32[]{:S(2)}, u32[]{:S(2)}) collective-permute-start(bf16[224,896]{1,0:T(8,128)(2,1)S(1)} %collective-permute-done.11.refs_2_), channel_id=1, source_target_pairs={{0,2},{1,3},{2,4},{3,5},{4,6},{5,7},{6,0},{7,1},{8,10},{9,11},{10,... | collective-permute-start | bytes 1204232 | tf_op jit(solution)/shard_map/ppermute | solution.py:483
  45.3 0.7 copy-start.14
  45.4 0.8 copy-start.15
  45.4 0.8 copy-start.16
  45.4 0.9 copy-start.17
  55.8 11.5 %copy-start.13 = (bf16[224,896]{1,0:T(8,128)(2,1)}, bf16[224,896]{1,0:T(8,128)(2,1)S(1)}, u32[]{:S(2)}) copy-start(bf16[224,896]{1,0:T(8,128)(2,1)S(1)} %collective-permute-done.13.refs_4_) | copy-start | bytes 1204228
  55.9 9.7 %collective-permute-start.15 = (bf16[224,896]{1,0:T(8,128)(2,1)S(1)}, bf16[224,896]{1,0:T(8,128)(2,1)S(1)}, u32[]{:S(2)}, u32[]{:S(2)}) collective-permute-start(bf16[224,896]{1,0:T(8,128)(2,1)S(1)} %broadcast_add_fusion), channel_id=1, source_target_pairs={{0,2},{1,3},{2,4},{3,5},{4,6},{5,7},{6,0},{7,1},{8,10},{9,11},{10,... | collective-permute-start | bytes 1204232 | tf_op jit(solution)/shard_map/ppermute | solution.py:483
  56.3 9.3 %collective-permute-start.10 = (bf16[224,896]{1,0:T(8,128)(2,1)S(1)}, bf16[224,896]{1,0:T(8,128)(2,1)S(1)}, u32[]{:S(2)}, u32[]{:S(2)}) collective-permute-start(bf16[224,896]{1,0:T(8,128)(2,1)S(1)} %weight_rows.1.refs_0_), channel_id=1, source_target_pairs={{0,1},{1,0},{2,3},{3,2},{4,5},{5,4},{6,7},{7,6},{8,9},{9,8},{10,11... | collective-permute-start | bytes 1204232 | tf_op jit(solution)/shard_map/ppermute | solution.py:480
  56.3 9.3 %collective-permute-start.12 = (bf16[224,896]{1,0:T(8,128)(2,1)S(1)}, bf16[224,896]{1,0:T(8,128)(2,1)S(1)}, u32[]{:S(2)}, u32[]{:S(2)}) collective-permute-start(bf16[224,896]{1,0:T(8,128)(2,1)S(1)} %collective-permute-done.11.refs_2_), channel_id=1, source_target_pairs={{0,1},{1,0},{2,3},{3,2},{4,5},{5,4},{6,7},{7,6},{8,9},{9,8},{10,11... | collective-permute-start | bytes 1204232 | tf_op jit(solution)/shard_map/ppermute | solution.py:480
  56.8 8.8 %collective-permute-start.14 = (bf16[224,896]{1,0:T(8,128)(2,1)S(1)}, bf16[224,896]{1,0:T(8,128)(2,1)S(1)}, u32[]{:S(2)}, u32[]{:S(2)}) collective-permute-start(bf16[224,896]{1,0:T(8,128)(2,1)S(1)} %collective-permute-done.13.refs_4_), channel_id=1, source_target_pairs={{0,1},{1,0},{2,3},{3,2},{4,5},{5,4},{6,7},{7,6},{8,9},{9,8},{10,11... | collective-permute-start | bytes 1204232 | tf_op jit(solution)/shard_map/ppermute | solution.py:480
  65.6 1.7 %copy-start.19 = (bf16[224,896]{1,0:T(8,128)(2,1)}, bf16[224,896]{1,0:T(8,128)(2,1)S(1)}, u32[]{:S(2)}) copy-start(bf16[224,896]{1,0:T(8,128)(2,1)S(1)} %collective-permute-done.15.refs_6_) | copy-start | bytes 1204228
  65.6 1.7 %collective-permute-start.16 = (bf16[224,896]{1,0:T(8,128)(2,1)S(1)}, bf16[224,896]{1,0:T(8,128)(2,1)S(1)}, u32[]{:S(2)}, u32[]{:S(2)}) collective-permute-start(bf16[224,896]{1,0:T(8,128)(2,1)S(1)} %collective-permute-done.15.refs_6_), channel_id=1, source_target_pairs={{0,1},{1,0},{2,3},{3,2},{4,5},{5,4},{6,7},{7,6},{8,9},{9,8},{10,11... | collective-permute-start | bytes 1204232 | tf_op jit(solution)/shard_map/ppermute | solution.py:480
  65.6 1.7 %copy-start.20 = (bf16[224,896]{1,0:T(8,128)(2,1)}, bf16[224,896]{1,0:T(8,128)(2,1)S(1)}, u32[]{:S(2)}) copy-start(bf16[224,896]{1,0:T(8,128)(2,1)S(1)} %collective-permute-done.10.refs_1_) | copy-start | bytes 1204228
  65.6 1.7 %copy-start.21 = (bf16[224,896]{1,0:T(8,128)(2,1)}, bf16[224,896]{1,0:T(8,128)(2,1)S(1)}, u32[]{:S(2)}) copy-start(bf16[224,896]{1,0:T(8,128)(2,1)S(1)} %collective-permute-done.12.refs_3_) | copy-start | bytes 1204228
  65.7 1.7 %copy-start.22 = (bf16[224,896]{1,0:T(8,128)(2,1)}, bf16[224,896]{1,0:T(8,128)(2,1)S(1)}, u32[]{:S(2)}) copy-start(bf16[224,896]{1,0:T(8,128)(2,1)S(1)} %collective-permute-done.14.refs_5_) | copy-start | bytes 1204228
  67.3 0.8 copy-start.23
  90.4 2.7 %collective-permute-start.18 = (bf16[4,128,896]{2,1,0:T(8,128)(2,1)}, bf16[4,128,896]{2,1,0:T(8,128)(2,1)S(1)}, u32[]{:S(2)}, u32[]{:S(2)}) collective-permute-start(bf16[4,128,896]{2,1,0:T(8,128)(2,1)} %get-tuple-element.39), channel_id=1, source_target_pairs={{0,1},{1,0},{2,3},{3,2},{4,5},{5,4},{6,7},{7,6},{8,9},{9,8},{10,11... | collective-permute-start | bytes 2752520 | tf_op jit(solution)/shard_map/ppermute | solution.py:480
  93.1 29.9 %copy-start = (bf16[1792,896]{1,0:T(8,128)(2,1)S(1)}, bf16[1792,896]{1,0:T(8,128)(2,1)}, u32[]{:S(2)}) copy-start(bf16[1792,896]{1,0:T(8,128)(2,1)} %get-tuple-element.40.weight_hbm) | copy-start | bytes 9633796
  93.1 29.9 %copy-start.7 = (s32[3]{0:T(128)S(1)}, s32[3]{0:T(128)}, u32[]{:S(2)}) copy-start(s32[3]{0:T(128)} %pad_add_fusion.1.place_ref) | copy-start | bytes 40
  94.7 10.3 %collective-permute-start.19 = (bf16[128,896]{1,0:T(8,128)(2,1)S(1)}, bf16[128,896]{1,0:T(8,128)(2,1)S(1)}, u32[]{:S(2)}, u32[]{:S(2)}) collective-permute-start(bf16[128,896]{1,0:T(8,128)(2,1)S(1)} %get-tuple-element.49), channel_id=1, source_target_pairs={{0,2},{1,3},{2,4},{3,5},{4,6},{5,7},{6,0},{7,1},{8,10},{9,11},{10,... | collective-permute-start | bytes 688136 | tf_op jit(solution)/shard_map/ppermute | solution.py:483
  94.8 13.6 %collective-permute-start.21 = (bf16[128,896]{1,0:T(8,128)(2,1)S(1)}, bf16[128,896]{1,0:T(8,128)(2,1)S(1)}, u32[]{:S(2)}, u32[]{:S(2)}) collective-permute-start(bf16[128,896]{1,0:T(8,128)(2,1)S(1)} %get-tuple-element.50), channel_id=1, source_target_pairs={{0,6},{1,7},{2,0},{3,1},{4,2},{5,3},{6,4},{7,5},{8,14},{9,15},{10,... | collective-permute-start | bytes 688136 | tf_op jit(solution)/shard_map/ppermute | solution.py:483
  98.6 18.8 %collective-permute-start.20 = (bf16[128,896]{1,0:T(8,128)(2,1)S(1)}, bf16[128,896]{1,0:T(8,128)(2,1)S(1)}, u32[]{:S(2)}, u32[]{:S(2)}) collective-permute-start(bf16[128,896]{1,0:T(8,128)(2,1)S(1)} %get-tuple-element.51), channel_id=1, source_target_pairs={{0,4},{1,5},{2,6},{3,7},{4,0},{5,1},{6,2},{7,3},{8,12},{9,13},{10,... | collective-permute-start | bytes 688136 | tf_op jit(solution)/shard_map/ppermute | solution.py:483
  118.5 7.7 %collective-permute-start.22 = (bf16[128,896]{1,0:T(8,128)(2,1)S(1)}, bf16[128,896]{1,0:T(8,128)(2,1)}, u32[]{:S(2)}, u32[]{:S(2)}) collective-permute-start(bf16[128,896]{1,0:T(8,128)(2,1)S(1)} %fusion.6.sums_ref.refs_0_), channel_id=1, source_target_pairs={{0,2},{1,3},{2,0},{3,1},{4,6},{5,7},{6,4},{7,5},{8,10},{9,11},{10,... | collective-permute-start | bytes 688136 | tf_op jit(solution)/shard_map/ppermute | solution.py:529
  118.6 8.7 %collective-permute-start.17 = (bf16[4,64,896]{2,1,0:T(8,128)(2,1)}, bf16[4,64,896]{2,1,0:T(8,128)(2,1)}, u32[]{:S(2)}, u32[]{:S(2)}) collective-permute-start(bf16[4,64,896]{2,1,0:T(8,128)(2,1)} %get-tuple-element.37), channel_id=1, source_target_pairs={{0,1},{1,0},{2,3},{3,2},{4,5},{5,4},{6,7},{7,6},{8,9},{9,8},{10,11... | collective-permute-start | bytes 1376264 | tf_op jit(solution)/shard_map/ppermute | solution.py:480
  122.6 10.0 %collective-permute-start.23 = (bf16[128,896]{1,0:T(8,128)(2,1)S(1)}, bf16[128,896]{1,0:T(8,128)(2,1)}, u32[]{:S(2)}, u32[]{:S(2)}) collective-permute-start(bf16[128,896]{1,0:T(8,128)(2,1)S(1)} %fusion.6.sums_ref.refs_0_), channel_id=1, source_target_pairs={{0,1},{1,0},{2,3},{3,2},{4,5},{5,4},{6,7},{7,6},{8,9},{9,8},{10,11... | collective-permute-start | bytes 688136 | tf_op jit(solution)/shard_map/ppermute | solution.py:480
  123.1 32.9 %copy-start.8 = (f32[4,16]{1,0:T(4,128)S(1)}, f32[4,16]{1,0:T(4,128)}, u32[]{:S(2)}) copy-start(f32[4,16]{1,0:T(4,128)} %coef_ref.3) | copy-start | bytes 772
  124.9 0.6 copy-start.10
  125.5 0.6 copy-start.11
  127.2 5.4 %collective-permute-start.24 = (bf16[128,896]{1,0:T(8,128)(2,1)S(1)}, bf16[128,896]{1,0:T(8,128)(2,1)S(1)}, u32[]{:S(2)}, u32[]{:S(2)}) collective-permute-start(bf16[128,896]{1,0:T(8,128)(2,1)S(1)} %broadcast_add_fusion.1.refs_1_), channel_id=1, source_target_pairs={{0,1},{1,0},{2,3},{3,2},{4,5},{5,4},{6,7},{7,6},{8,9},{9,8},{10,11... | collective-permute-start | bytes 688136 | tf_op jit(solution)/shard_map/ppermute | solution.py:480
  128.6 9.6 %collective-permute-start.28 = (bf16[64,896]{1,0:T(8,128)(2,1)}, bf16[64,896]{1,0:T(8,128)(2,1)S(1)}, u32[]{:S(2)}, u32[]{:S(2)}) collective-permute-start(bf16[64,896]{1,0:T(8,128)(2,1)} %copy-done.11), channel_id=1, source_target_pairs={{0,0},{1,1},{2,4},{3,5},{4,2},{5,3},{6,6},{7,7},{8,8},{9,9},{10,12... | collective-permute-start | bytes 344072 | tf_op jit(solution)/shard_map/ppermute | solution.py:541
  130.2 13.6 %collective-permute-start.29 = (bf16[64,896]{1,0:T(8,128)(2,1)}, bf16[64,896]{1,0:T(8,128)(2,1)S(1)}, u32[]{:S(2)}, u32[]{:S(2)}) collective-permute-start(bf16[64,896]{1,0:T(8,128)(2,1)} %copy-done.10), channel_id=1, source_target_pairs={{0,2},{1,3},{2,6},{3,7},{4,0},{5,1},{6,4},{7,5},{8,10},{9,11},{10,... | collective-permute-start | bytes 344072 | tf_op jit(solution)/shard_map/ppermute | solution.py:541
  132.6 0.9 copy-start.1
  135.0 8.9 %collective-permute-start.25 = (bf16[64,896]{1,0:T(8,128)(2,1)S(1)}, bf16[64,896]{1,0:T(8,128)(2,1)S(1)}, u32[]{:S(2)}, u32[]{:S(2)}) collective-permute-start(bf16[64,896]{1,0:T(8,128)(2,1)S(1)} %get-tuple-element.42), channel_id=1, source_target_pairs={{0,2},{1,3},{2,4},{3,5},{4,6},{5,7},{6,0},{7,1},{8,10},{9,11},{10,... | collective-permute-start | bytes 344072 | tf_op jit(solution)/shard_map/ppermute | solution.py:483
  135.0 16.5 %collective-permute-start.32 = (bf16[224,896]{1,0:T(8,128)(2,1)S(1)}, bf16[224,896]{1,0:T(8,128)(2,1)S(1)}, u32[]{:S(2)}, u32[]{:S(2)}) collective-permute-start(bf16[224,896]{1,0:T(8,128)(2,1)S(1)} %get-tuple-element.48), channel_id=1, source_target_pairs={{0,24},{8,16},{16,8},{24,0},{1,25},{9,17},{17,9},{25,1},{2,26},{10... | collective-permute-start | bytes 1204232 | tf_op jit(solution)/shard_map/ppermute | solution.py:477
  136.5 19.5 %collective-permute-start.31 = (bf16[224,896]{1,0:T(8,128)(2,1)S(1)}, bf16[224,896]{1,0:T(8,128)(2,1)S(1)}, u32[]{:S(2)}, u32[]{:S(2)}) collective-permute-start(bf16[224,896]{1,0:T(8,128)(2,1)S(1)} %get-tuple-element.48), channel_id=1, source_target_pairs={{0,16},{8,24},{16,0},{24,8},{1,17},{9,25},{17,1},{25,9},{2,18},{10... | collective-permute-start | bytes 1204232 | tf_op jit(solution)/shard_map/ppermute | solution.py:477
  138.2 17.8 %collective-permute-start.30 = (bf16[224,896]{1,0:T(8,128)(2,1)S(1)}, bf16[224,896]{1,0:T(8,128)(2,1)S(1)}, u32[]{:S(2)}, u32[]{:S(2)}) collective-permute-start(bf16[224,896]{1,0:T(8,128)(2,1)S(1)} %get-tuple-element.48), channel_id=1, source_target_pairs={{0,8},{8,0},{16,24},{24,16},{1,9},{9,1},{17,25},{25,17},{2,10},{10... | collective-permute-start | bytes 1204232 | tf_op jit(solution)/shard_map/ppermute | solution.py:477
  143.8 5.8 %collective-permute-start.26 = (bf16[64,896]{1,0:T(8,128)(2,1)S(1)}, bf16[64,896]{1,0:T(8,128)(2,1)S(1)}, u32[]{:S(2)}, u32[]{:S(2)}) collective-permute-start(bf16[64,896]{1,0:T(8,128)(2,1)S(1)} %get-tuple-element.43), channel_id=1, source_target_pairs={{0,4},{1,5},{2,6},{3,7},{4,0},{5,1},{6,2},{7,3},{8,12},{9,13},{10,... | collective-permute-start | bytes 344072 | tf_op jit(solution)/shard_map/ppermute | solution.py:483
  143.8 6.0 %collective-permute-start.27 = (bf16[64,896]{1,0:T(8,128)(2,1)S(1)}, bf16[64,896]{1,0:T(8,128)(2,1)S(1)}, u32[]{:S(2)}, u32[]{:S(2)}) collective-permute-start(bf16[64,896]{1,0:T(8,128)(2,1)S(1)} %get-tuple-element.44), channel_id=1, source_target_pairs={{0,6},{1,7},{2,0},{3,1},{4,2},{5,3},{6,4},{7,5},{8,14},{9,15},{10,... | collective-permute-start | bytes 344072 | tf_op jit(solution)/shard_map/ppermute | solution.py:483

commit v10 on v9

--- a/solution.py
+++ b/solution.py
@@ -132,8 +132,11 @@
     pieces = len(block_refs) // 2
     for i, ref in enumerate(block_refs):
         piece = lax.rem(place_ref[1] + pieces - i % pieces, pieces)
-        at = pl.ds(pl.multiple_of((i // pieces * pieces + piece) * size, size), size)
-        sums_ref[at, :] = ref[...]
+        chips, own = 2 * pieces, size // 2
+        for b in range(2):
+            back = lax.rem(place_ref[1] - (2 * piece + b) + chips, chips)
+            at = pl.ds(pl.multiple_of((i // pieces * chips + back) * own, own), own)
+            sums_ref[at, :] = ref[b * own : (b + 1) * own, :]
     grad = jnp.dot(cols_ref[...], sums_ref[...], preferred_element_type=F32)
     grad_ref[...] = grad
     sent_ref[...] = grad.astype(BF16)
@@ -274,7 +277,7 @@
     )(cols, rows, order[None, :], order[:, None], earlier)
 
 
-def scale_kernel(slots, place_ref, gather_ref, radial_ref, *refs):
+def scale_kernel(slots, place_ref, gather_ref, radial_ref, _, *refs):
     block_refs = refs[:slots]
     atoms_out, scaled_ref, token_ref, atoms_ref, cot_ref, sems = refs[slots:]
     step = pl.program_id(0)
@@ -304,7 +307,7 @@
         store.wait()
 
 
-def scaled_edges(place, hot_gather, radial, blocks, tile):
+def scaled_edges(place, hot_gather, radial, earlier, blocks, tile):
     edges, width = radial.shape
     atoms = hot_gather.shape[1] // 2
     slots = len(blocks)
@@ -321,7 +324,7 @@
             pl.BlockSpec((tile, atoms), lambda i: (i, 1)),
             pl.BlockSpec((tile, width), lambda i: (i, 0)),
         ]
-        + [in_hbm()] * slots,
+        + [in_hbm()] * (1 + slots),
         out_specs=[
             in_hbm(),
             pl.BlockSpec((tile, width), lambda i: (i, 0)),
@@ -337,7 +340,7 @@
             flops=2 * atoms * width * edges, bytes_accessed=6 * edges * width, transcendentals=0
         ),
         name="scaled_edges",
-    )(place, hot_gather, radial, *blocks)
+    )(place, hot_gather, radial, earlier, *blocks)
 
 
 def edge_kernel(
@@ -494,8 +497,11 @@
     order = (2 * z + (core ^ side)) * own + offset
     ends = jnp.concatenate([source, target])
     hot_gather, hot_sum, hot_token = hot_ends(ends.T, ends, order, pair, width, tile)
-    all_atoms, scaled, scaled_token = scaled_edges(place, hot_gather, radial[0], features, tile)
-    own_cols = lax.dynamic_slice_in_dim(all_atoms, (me_edge % chips) * depth, depth, 1).T
+    own_cols = jnp.concatenate([block[0] for block in features], axis=0)
+    own_cols = lax.dynamic_slice_in_dim(own_cols, (me_edge % chips) * depth, depth, 1).T
+    all_atoms, scaled, scaled_token = scaled_edges(
+        place, hot_gather, radial[0], own_cols, features, tile
+    )
 
     got = [merged[0]] + [across(merged[k], k) for k in range(1, systems)]
     held = weight_rows(got, features[1:chips] + [hot_token])
@@ -530,7 +536,8 @@
 
     *terms, term_token = atom_grads(chips, place, sums, weight)
     picked = both_cores([sums] + [share(sums, j) + term_token for j in range(1, shares)])
-    grad, send, *node_terms = merged_grads(place, own_cols, picked, node_terms)
+    grad, send, *passed = merged_grads(place, own_cols, picked, terms + node_terms)
+    terms, node_terms = passed[: len(terms)], passed[len(terms) :]
     grads = [grad] + [across(send, k) for k in range(1, systems)]
     expert_grad = expert_grads(place, coef, grads, experts.shape, parts)
 

time: 160 us -> 194 us (1.21)
  local copies, waits for them, and re-layouts: 9.75 us -> 29.8 us
  waiting for transfers between devices: 63.9 us -> 82 us
  other arithmetic: 11.5 us -> 7.51 us
    ppermute x12, waiting for transfers between devices: 44.1 us -> 64.4 us  [shift(): lax.ppermute(x, 'edge', [(e, (e + 2 * k) % ways) for e in range(ways)])]
    squeeze x0 -> x8, local copies, waits for them, and re-layouts: none -> 9.79 us  [shards(): own_cols = jnp.concatenate([block[0] for block in features], axis=0)]
    ppermute x0 -> x7, local copies, waits for them, and re-layouts: none -> 9.25 us  [the longest x4 5.59 us: swap(): return lax.ppermute(x, 'edge', [(e, e ^ 1) for e in range(ways)])]
    ppermute x6, waiting for transfers between devices: 10.3 us -> 5.01 us  [across(): return lax.ppermute(x, 'sys', [(s, s ^ k) for s in range(systems)])]
    ppermute x1, waiting for transfers between devices: 0.01 us -> 4.35 us  [share(): lax.ppermute(x, 'edge', [(2 * z + c, 2 * to[z] + c) for z in range(chips)...]
    concatenate x0 -> x1, local copies, waits for them, and re-layouts: none -> 3.42 us  [shards(): own_cols = jnp.concatenate([block[0] for block in features], axis=0)]
    ppermute x2, waiting for transfers between devices: 5.23 us -> 2.66 us  [shards(): atom_grad = atom_grad + lax.ppermute(term, 'edge', pairs).astype(F32)]
    unnamed x48 -> x50, local copies, waits for them, and re-layouts: 4.53 us -> 2.36 us
  transfers between devices with their start and end apart: 33 -> 33, of which waited for: 14 -> 16; matrix products, arithmetic and copies ran while one was open for 9% -> 16% of each run, Pallas kernels for 13% -> 10%
where the time goes in v10:
time: 194 us; the launch traced here: 193 us
  waiting for transfers between devices  82 us (42%)
  Pallas kernels  47.6 us (25%)
  local copies, waits for them, and re-layouts  29.8 us (15%)
  starting transfers between devices  24.5 us (13%)
  other arithmetic  7.51 us (4%)
    ppermute x12, waiting for transfers between devices, shift(): lax.ppermute(x, 'edge', [(e, (e + 2 * k) % ways) for e in range(ways)])  64.4 us
    pallas_call x1, Pallas kernels, edge_sums(): pl.pallas_call(functools.partial(edge_kernel, chips), grid=(steps + 1,),...  22.3 us
    ppermute x12, starting transfers between devices, shift(): lax.ppermute(x, 'edge', [(e, (e + 2 * k) % ways) for e in range(ways)])  10.6 us
    squeeze x8, local copies, waits for them, and re-layouts, shards(): own_cols = jnp.concatenate([block[0] for block in features], axis=0)  9.79 us
    ppermute x6, starting transfers between devices, across(): return lax.ppermute(x, 'sys', [(s, s ^ k) for s in range(systems)])  8.06 us
    pallas_call x1, Pallas kernels, scaled_edges(): pl.pallas_call(functools.partial(scale_kernel, slots), grid=(edges // til...  7.95 us
    pallas_call x1, Pallas kernels, hot_ends(): pl.pallas_call(hot_kernel, grid=(edges // tile,), out_shape=[jax.ShapeDty...  5.72 us
    ppermute x12, waiting for transfers between devices, swap(): return lax.ppermute(x, 'edge', [(e, e ^ 1) for e in range(ways)])  5.62 us
  transfers between devices with their start and end apart: 33, of which 16 were waited for; matrix products, arithmetic and copies ran while one was open for 16% of the time, Pallas kernels for 10%

profile of v10, /device:TPU:0, one launch (start us, length us, event | category | flops | bytes accessed | tf_op | source)
XLA Modules:
  0.0 192.7 jit_solution(8548966495942801442)
XLA Ops:
  0.7 1.7 join.1._.refs_0_
  2.3 1.9 %copy.28 = bf16[2,64,896]{1,2,0:T(8,128)(2,1)} copy(bf16[2,64,896]{2,1,0:T(8,128)(2,1)} %join.1._.refs_0_) | data formatting | bytes 458752 | tf_op jit(solution)/shard_map/join/pallas_call | solution.py:98
  4.7 4.6 %collective-permute-start.2 = (bf16[2,64,896]{1,2,0:T(8,128)(2,1)}, bf16[2,64,896]{1,2,0:T(8,128)(2,1)S(1)}, u32[]{:S(2)}, u32[]{:S(2)}) collective-permute-start(bf16[2,64,896]{1,2,0:T(8,128)(2,1)} %copy.28), channel_id=1, source_target_pairs={{0,6},{1,7},{2,0},{3,1},{4,2},{5,3},{6,4},{7,5},{8,14},{9,15},{10,... | collective-permute-start | bytes 688136 | tf_op jit(solution)/shard_map/ppermute | solution.py:486
  9.3 1.0 collective-permute-start
  10.3 0.7 pad_add_fusion.1.place_ref
  11.0 4.2 %merge_parts.1 = (f32[224,896]{1,0:T(8,128)}, bf16[224,896]{1,0:T(8,128)(2,1)}, bf16[224,896]{1,0:T(8,128)(2,1)}, bf16[224,896]{1,0:T(8,128)(2,1)}) custom-call(s32[3]{0:T(128)} %pad_add_fusion.1.place_ref, f32[4,16]{1,0:T(4,128)} %coef_ref.3, bf16[4,224,896]{2,1,0:T(8,128)(2,1)} %experts_ref.1, bf16[2,64,896]{2,1,0:T(8,128)(2,1)} %join.1._.refs_0_), custom_call_target="tpu_custom_call" | custom-call | tf_op jit(solution)/shard_map/merge_parts/pallas_call | solution.py:70
  15.2 1.6 collective-permute-start.7
  16.8 0.6 fusion.28.across_ref
  17.3 0.8 fusion.13.down_ref
  18.1 0.6 pad_add_fusion
  18.7 1.3 copy.27.cols_ref
  20.1 5.7 %hot_ends.1 = (bf16[2048,1024]{1,0:T(8,128)(2,1)}, bf16[1024,2048]{1,0:T(8,128)(2,1)}, f32[1,896]{1,0:T(1,128)}) custom-call(s32[2048,2]{1,0:T(8,128)} %copy.27.cols_ref, s32[2,2048]{1,0:T(2,128)} %get-tuple-element.59.rows_ref, s32[1,512]{1,0:T(1,128)} %fusion.28.across_ref, s32[512,1]{1,0:T(8,128)} %fusion.13.down_ref, bf16[2,64,896]{2,1,0:T(8,128)(2,1)} %join.1._.refs_0_), custom_call_target="tpu_custom_call" | custom-call | flops 16777216 | bytes 8388608 | tf_op jit(solution)/shard_map/hot_ends/pallas_call | solution.py:252
  25.8 1.0 slice_bitcast_fusion.7
  26.8 1.6 collective-permute-start.8
  28.4 0.9 copy.36.refs_4_
  29.3 0.8 copy-done.10
  30.5 1.2 copy.35.refs_3_.refs_6_
  31.7 1.7 slice_bitcast_fusion.3
  33.5 16.0 %collective-permute-done.1 = bf16[2,64,896]{1,2,0:T(8,128)(2,1)} collective-permute-done((bf16[2,64,896]{1,2,0:T(8,128)(2,1)}, bf16[2,64,896]{1,2,0:T(8,128)(2,1)}, u32[]{:S(2)}, u32[]{:S(2)}) %collective-permute-start.1) | collective-permute-done | bytes 229408 | tf_op jit(solution)/shard_map/ppermute | solution.py:486
  49.5 1.2 copy.34.refs_2_.refs_5_
  50.7 1.7 slice_bitcast_fusion.4
  52.4 0.5 collective-permute-start.5
  53.0 1.2 copy.33.refs_1_.refs_4_
  54.2 1.7 slice_bitcast_fusion.5
  55.9 1.6 slice_bitcast_fusion.6
  57.9 1.0 slice_bitcast_fusion
  59.0 1.0 slice_bitcast_fusion.1
  59.9 11.5 %collective-permute-done.11.refs_2_ = bf16[224,896]{1,0:T(8,128)(2,1)S(1)} collective-permute-done((bf16[224,896]{1,0:T(8,128)(2,1)S(1)}, bf16[224,896]{1,0:T(8,128)(2,1)S(1)}, u32[]{:S(2)}, u32[]{:S(2)}) %collective-permute-start.11) | collective-permute-done | bytes 401440 | tf_op jit(solution)/shard_map/ppermute | solution.py:486
  71.4 0.8 copy-done.12
  72.2 3.4 %concatenate.7 = bf16[512,896]{0,1:T(8,128)(2,1)} concatenate(bf16[64,896]{0,1:T(8,128)(2,1)S(1)} %slice_bitcast_fusion.7, bf16[64,896]{0,1:T(8,128)(2,1)} %slice_bitcast_fusion.6, bf16[64,896]{0,1:T(8,128)(2,1)} %slice_bitcast_fusion.5, bf16[64,896]{0,1:T(8,128)(2,1)} %slice_bitcast_fusion.4, bf16[64,896]{0,1:T(8,128)(2,1)} %slice_bitcast_fusion.3, ...), dimensions={0} | concatenate | bytes 1835008 | tf_op jit(solution)/shard_map/concatenate | solution.py:500
  75.7 1.9 copy.39.refs_7_
  77.6 1.9 copy.38.refs_6_
  79.5 0.9 copy.37.refs_5_
  80.4 1.7 dynamic-slice_bitcast_fusion._.cols_ref
  82.0 7.9 %scaled_edges.1 = (bf16[512,896]{1,0:T(8,128)(2,1)}, bf16[2048,896]{1,0:T(8,128)(2,1)}, bf16[1,896]{1,0:T(2,128)(2,1)}) custom-call(s32[3]{0:T(128)} %pad_add_fusion.1.place_ref, bf16[2048,1024]{1,0:T(8,128)(2,1)} %get-tuple-element.28.gather_ref, bf16[2048,896]{1,0:T(8,128)(2,1)} %bitcast.58, bf16[224,512]{1,0:T(8,128)(2,1)} %dynamic-slice_bitcast_fusion._.cols_ref, ...), custom_call_target="tpu_custom_call" | custom-call | flops 1879048192 | bytes 11010048 | tf_op jit(solution)/shard_map/scaled_edges/pallas_call | solution.py:314
  90.0 0.7 reduce
  91.1 0.5 collective-permute-start.12
  91.7 12.0 %collective-permute-done.15.refs_6_ = bf16[224,896]{1,0:T(8,128)(2,1)S(1)} collective-permute-done((bf16[224,896]{1,0:T(8,128)(2,1)S(1)}, bf16[224,896]{1,0:T(8,128)(2,1)S(1)}, u32[]{:S(2)}, u32[]{:S(2)}) %collective-permute-start.15) | collective-permute-done | bytes 401440 | tf_op jit(solution)/shard_map/ppermute | solution.py:486
  103.8 1.7 collective-permute-done.16.refs_7_
  105.5 0.7 copy-done.24
  106.2 22.3 %edge_sums.1 = (f32[4,128,896]{2,1,0:T(8,128)}, bf16[4,128,896]{2,1,0:T(8,128)(2,1)}, f32[4,64,896]{2,1,0:T(8,128)}, bf16[4,64,896]{2,1,0:T(8,128)(2,1)}, bf16[1792,896]{1,0:T(8,128)(2,1)}) custom-call(s32[3]{0:T(128)} %pad_add_fusion.1.place_ref, bf16[2048,1024]{1,0:T(8,128)(2,1)} %get-tuple-element.28.gather_ref, ...), custom_call_target="tpu_custom_call" | custom-call | flops 11039408128 | bytes 15728640 | tf_op jit(solution)/shard_map/edge_sums/pallas_call | solution.py:436
  128.7 2.5 %collective-permute-done.18 = bf16[4,128,896]{2,1,0:T(8,128)(2,1)S(1)} collective-permute-done((bf16[4,128,896]{2,1,0:T(8,128)(2,1)}, bf16[4,128,896]{2,1,0:T(8,128)(2,1)S(1)}, u32[]{:S(2)}, u32[]{:S(2)}) %collective-permute-start.18) | collective-permute-done | bytes 917536 | tf_op jit(solution)/shard_map/ppermute | solution.py:483
  131.2 1.4 fusion.18
  132.7 3.8 %collective-permute-start.21 = (bf16[128,896]{1,0:T(8,128)(2,1)S(1)}, bf16[128,896]{1,0:T(8,128)(2,1)S(1)}, u32[]{:S(2)}, u32[]{:S(2)}) collective-permute-start(bf16[128,896]{1,0:T(8,128)(2,1)S(1)} %get-tuple-element.54), channel_id=1, source_target_pairs={{0,6},{1,7},{2,0},{3,1},{4,2},{5,3},{6,4},{7,5},{8,14},{9,15},{10,... | collective-permute-start | bytes 688136 | tf_op jit(solution)/shard_map/ppermute | solution.py:486
  136.5 6.5 %collective-permute-done.19 = bf16[128,896]{1,0:T(8,128)(2,1)S(1)} collective-permute-done((bf16[128,896]{1,0:T(8,128)(2,1)S(1)}, bf16[128,896]{1,0:T(8,128)(2,1)S(1)}, u32[]{:S(2)}, u32[]{:S(2)}) %collective-permute-start.19) | collective-permute-done | bytes 229408 | tf_op jit(solution)/shard_map/ppermute | solution.py:486
  143.0 2.9 %collective-permute-done.21 = bf16[128,896]{1,0:T(8,128)(2,1)S(1)} collective-permute-done((bf16[128,896]{1,0:T(8,128)(2,1)S(1)}, bf16[128,896]{1,0:T(8,128)(2,1)S(1)}, u32[]{:S(2)}, u32[]{:S(2)}) %collective-permute-start.21) | collective-permute-done | bytes 229408 | tf_op jit(solution)/shard_map/ppermute | solution.py:486
  146.0 9.4 %collective-permute-done.20 = bf16[128,896]{1,0:T(8,128)(2,1)S(1)} collective-permute-done((bf16[128,896]{1,0:T(8,128)(2,1)S(1)}, bf16[128,896]{1,0:T(8,128)(2,1)S(1)}, u32[]{:S(2)}, u32[]{:S(2)}) %collective-permute-start.20) | collective-permute-done | bytes 229408 | tf_op jit(solution)/shard_map/ppermute | solution.py:486
  155.4 1.2 fusion.6.sums_ref.refs_0_
  157.2 1.8 atom_grads.1
  159.1 4.3 %collective-permute-done.22 = bf16[128,896]{1,0:T(8,128)(2,1)S(1)} collective-permute-done((bf16[128,896]{1,0:T(8,128)(2,1)S(1)}, bf16[128,896]{1,0:T(8,128)(2,1)S(1)}, u32[]{:S(2)}, u32[]{:S(2)}) %collective-permute-start.22) | collective-permute-done | bytes 229408 | tf_op jit(solution)/shard_map/ppermute | solution.py:535
  163.6 1.4 collective-permute-done.24.refs_3_
  165.0 1.0 merged_grads.1
  166.4 0.7 collective-permute-start.28
  167.0 2.6 %collective-permute-start.29 = (bf16[64,896]{1,0:T(8,128)(2,1)S(1)}, bf16[64,896]{1,0:T(8,128)(2,1)S(1)}, u32[]{:S(2)}, u32[]{:S(2)}) collective-permute-start(bf16[64,896]{1,0:T(8,128)(2,1)S(1)} %get-tuple-element.50), channel_id=1, source_target_pairs={{0,2},{1,3},{2,6},{3,7},{4,0},{5,1},{6,4},{7,5},{8,10},{9,11},{10,... | collective-permute-start | bytes 344072 | tf_op jit(solution)/shard_map/ppermute | solution.py:548
  169.6 2.4 %collective-permute-start.32 = (bf16[224,896]{1,0:T(8,128)(2,1)S(1)}, bf16[224,896]{1,0:T(8,128)(2,1)S(1)}, u32[]{:S(2)}, u32[]{:S(2)}) collective-permute-start(bf16[224,896]{1,0:T(8,128)(2,1)S(1)} %get-tuple-element.52), channel_id=1, source_target_pairs={{0,24},{8,16},{16,8},{24,0},{1,25},{9,17},{17,9},{25,1},{2,26},{10... | collective-permute-start | bytes 1204232 | tf_op jit(solution)/shard_map/ppermute | solution.py:480
  172.1 0.5 collective-permute-start.31
  172.6 1.3 collective-permute-done.25
  173.9 1.5 collective-permute-start.30
  175.4 2.7 %collective-permute-done.29 = bf16[64,896]{1,0:T(8,128)(2,1)S(1)} collective-permute-done((bf16[64,896]{1,0:T(8,128)(2,1)S(1)}, bf16[64,896]{1,0:T(8,128)(2,1)S(1)}, u32[]{:S(2)}, u32[]{:S(2)}) %collective-permute-start.29) | collective-permute-done | bytes 114720 | tf_op jit(solution)/shard_map/ppermute | solution.py:548
  178.5 0.7 add_bitcast_fusion
  179.3 4.5 %collective-permute-done.26 = bf16[64,896]{1,0:T(8,128)(2,1)S(1)} collective-permute-done((bf16[64,896]{1,0:T(8,128)(2,1)S(1)}, bf16[64,896]{1,0:T(8,128)(2,1)S(1)}, u32[]{:S(2)}, u32[]{:S(2)}) %collective-permute-start.26) | collective-permute-done | bytes 114720 | tf_op jit(solution)/shard_map/ppermute | solution.py:486
  184.0 0.7 fusion.27
  184.7 4.9 %collective-permute-done.31.refs_2_ = bf16[224,896]{1,0:T(8,128)(2,1)S(1)} collective-permute-done((bf16[224,896]{1,0:T(8,128)(2,1)S(1)}, bf16[224,896]{1,0:T(8,128)(2,1)S(1)}, u32[]{:S(2)}, u32[]{:S(2)}) %collective-permute-start.31) | collective-permute-done | bytes 401440 | tf_op jit(solution)/shard_map/ppermute | solution.py:480
  189.7 2.8 %expert_grads.1 = f32[4,224,896]{2,1,0:T(8,128)} custom-call(s32[3]{0:T(128)S(1)} %copy-done.7, f32[4,16]{1,0:T(4,128)S(1)} %copy-done.8, f32[224,896]{1,0:T(8,128)S(1)} %get-tuple-element.51.refs_0_, bf16[224,896]{1,0:T(8,128)(2,1)S(1)} %collective-permute-done.30.refs_1_, bf16[224,896]{1,0:T(8,128)(2,1)S(1)} %collective-permute-done.31.refs_2_, ...), custom_call_target="tpu_custom_call" | custom-call | tf_op jit(solution)/shard_map/expert_grads/pallas_call | solution.py:225
  (93 shorter events, 4.1 us)
Async XLA Ops:
  0.6 17.5 %copy-start.16 = (s32[1,2048]{1,0:T(1,128)S(1)}, s32[1,2048]{1,0:T(1,128)}, u32[]{:S(2)}) copy-start(s32[1,2048]{1,0:T(1,128)} %param.13) | copy-start | bytes 24580
  0.6 17.5 %copy-start.17 = (s32[1,2048]{1,0:T(1,128)S(1)}, s32[1,2048]{1,0:T(1,128)}, u32[]{:S(2)}) copy-start(s32[1,2048]{1,0:T(1,128)} %param.12) | copy-start | bytes 24580
  4.3 22.5 %collective-permute-start.3 = (bf16[2,64,896]{1,2,0:T(8,128)(2,1)}, bf16[2,64,896]{1,2,0:T(8,128)(2,1)S(1)}, u32[]{:S(2)}, u32[]{:S(2)}) collective-permute-start(bf16[2,64,896]{1,2,0:T(8,128)(2,1)} %copy.28), channel_id=1, source_target_pairs={{0,1},{1,0},{2,3},{3,2},{4,5},{5,4},{6,7},{7,6},{8,9},{9,8},{10,11... | collective-permute-start | bytes 688136 | tf_op jit(solution)/shard_map/ppermute | solution.py:483
  4.7 24.5 %collective-permute-start.2 = (bf16[2,64,896]{1,2,0:T(8,128)(2,1)}, bf16[2,64,896]{1,2,0:T(8,128)(2,1)S(1)}, u32[]{:S(2)}, u32[]{:S(2)}) collective-permute-start(bf16[2,64,896]{1,2,0:T(8,128)(2,1)} %copy.28), channel_id=1, source_target_pairs={{0,6},{1,7},{2,0},{3,1},{4,2},{5,3},{6,4},{7,5},{8,14},{9,15},{10,... | collective-permute-start | bytes 688136 | tf_op jit(solution)/shard_map/ppermute | solution.py:486
  9.3 40.2 %collective-permute-start.1 = (bf16[2,64,896]{1,2,0:T(8,128)(2,1)}, bf16[2,64,896]{1,2,0:T(8,128)(2,1)}, u32[]{:S(2)}, u32[]{:S(2)}) collective-permute-start(bf16[2,64,896]{1,2,0:T(8,128)(2,1)} %copy.28), channel_id=1, source_target_pairs={{0,4},{1,5},{2,6},{3,7},{4,0},{5,1},{6,2},{7,3},{8,12},{9,13},{10,... | collective-permute-start | bytes 688136 | tf_op jit(solution)/shard_map/ppermute | solution.py:486
  9.3 43.1 %collective-permute-start = (bf16[2,64,896]{1,2,0:T(8,128)(2,1)}, bf16[2,64,896]{1,2,0:T(8,128)(2,1)}, u32[]{:S(2)}, u32[]{:S(2)}) collective-permute-start(bf16[2,64,896]{1,2,0:T(8,128)(2,1)} %copy.28), channel_id=1, source_target_pairs={{0,2},{1,3},{2,4},{3,5},{4,6},{5,7},{6,0},{7,1},{8,10},{9,11},{10,... | collective-permute-start | bytes 688136 | tf_op jit(solution)/shard_map/ppermute | solution.py:486
  15.2 42.4 %collective-permute-start.7 = (bf16[224,896]{1,0:T(8,128)(2,1)}, bf16[224,896]{1,0:T(8,128)(2,1)S(1)}, u32[]{:S(2)}, u32[]{:S(2)}) collective-permute-start(bf16[224,896]{1,0:T(8,128)(2,1)} %get-tuple-element.33), channel_id=1, source_target_pairs={{0,8},{8,0},{16,24},{24,16},{1,9},{9,1},{17,25},{25,17},{2,10},{10... | collective-permute-start | bytes 1204232 | tf_op jit(solution)/shard_map/ppermute | solution.py:480
  20.1 37.5 %copy-start.5 = (f32[224,896]{1,0:T(8,128)S(1)}, f32[224,896]{1,0:T(8,128)}, u32[]{:S(2)}) copy-start(f32[224,896]{1,0:T(8,128)} %get-tuple-element.32.refs_0_) | copy-start | bytes 2408452
  25.8 31.8 %copy-start.9 = (f32[1,896]{1,0:T(1,128)S(1)}, f32[1,896]{1,0:T(1,128)}, u32[]{:S(2)}) copy-start(f32[1,896]{1,0:T(1,128)} %get-tuple-element.36.refs_7_) | copy-start | bytes 10756
  26.8 2.5 %copy-start.11 = (bf16[2,64,896]{1,2,0:T(8,128)(2,1)}, bf16[2,64,896]{1,2,0:T(8,128)(2,1)S(1)}, u32[]{:S(2)}) copy-start(bf16[2,64,896]{1,2,0:T(8,128)(2,1)S(1)} %collective-permute-done.3) | copy-start | bytes 688132
  26.8 30.8 %collective-permute-start.8 = (bf16[224,896]{1,0:T(8,128)(2,1)}, bf16[224,896]{1,0:T(8,128)(2,1)S(1)}, u32[]{:S(2)}, u32[]{:S(2)}) collective-permute-start(bf16[224,896]{1,0:T(8,128)(2,1)} %get-tuple-element.34), channel_id=1, source_target_pairs={{0,16},{8,24},{16,0},{24,8},{1,17},{9,25},{17,1},{25,9},{2,18},{10... | collective-permute-start | bytes 1204232 | tf_op jit(solution)/shard_map/ppermute | solution.py:480
  29.3 0.8 copy-start.10
  30.0 27.6 %collective-permute-start.9 = (bf16[224,896]{1,0:T(8,128)(2,1)}, bf16[224,896]{1,0:T(8,128)(2,1)S(1)}, u32[]{:S(2)}, u32[]{:S(2)}) collective-permute-start(bf16[224,896]{1,0:T(8,128)(2,1)} %get-tuple-element.35), channel_id=1, source_target_pairs={{0,24},{8,16},{16,8},{24,0},{1,25},{9,17},{17,9},{25,1},{2,26},{10... | collective-permute-start | bytes 1204232 | tf_op jit(solution)/shard_map/ppermute | solution.py:480
  31.7 27.2 %copy-start.2 = (bf16[2,64,896]{2,1,0:T(8,128)(2,1)}, bf16[2,64,896]{2,1,0:T(8,128)(2,1)S(1)}, u32[]{:S(2)}) copy-start(bf16[2,64,896]{2,1,0:T(8,128)(2,1)S(1)} %copy.35.refs_3_.refs_6_) | copy-start | bytes 688132
  49.5 8.4 %collective-permute-start.6 = (bf16[2,64,896]{1,2,0:T(8,128)(2,1)}, bf16[2,64,896]{1,2,0:T(8,128)(2,1)}, u32[]{:S(2)}, u32[]{:S(2)}) collective-permute-start(bf16[2,64,896]{1,2,0:T(8,128)(2,1)} %copy-done.10), channel_id=1, source_target_pairs={{0,1},{1,0},{2,3},{3,2},{4,5},{5,4},{6,7},{7,6},{8,9},{9,8},{10,11... | collective-permute-start | bytes 688136 | tf_op jit(solution)/shard_map/ppermute | solution.py:483
  50.7 21.5 %copy-start.3 = (bf16[2,64,896]{2,1,0:T(8,128)(2,1)}, bf16[2,64,896]{2,1,0:T(8,128)(2,1)S(1)}, u32[]{:S(2)}) copy-start(bf16[2,64,896]{2,1,0:T(8,128)(2,1)S(1)} %copy.34.refs_2_.refs_5_) | copy-start | bytes 688132
  52.4 6.5 %collective-permute-start.5 = (bf16[2,64,896]{1,2,0:T(8,128)(2,1)}, bf16[2,64,896]{1,2,0:T(8,128)(2,1)}, u32[]{:S(2)}, u32[]{:S(2)}) collective-permute-start(bf16[2,64,896]{1,2,0:T(8,128)(2,1)} %collective-permute-done.1), channel_id=1, source_target_pairs={{0,1},{1,0},{2,3},{3,2},{4,5},{5,4},{6,7},{7,6},{8,9},{9,8},{10,11... | collective-permute-start | bytes 688136 | tf_op jit(solution)/shard_map/ppermute | solution.py:483
  54.2 21.5 %copy-start.4 = (bf16[2,64,896]{2,1,0:T(8,128)(2,1)}, bf16[2,64,896]{2,1,0:T(8,128)(2,1)S(1)}, u32[]{:S(2)}) copy-start(bf16[2,64,896]{2,1,0:T(8,128)(2,1)S(1)} %copy.33.refs_1_.refs_4_) | copy-start | bytes 688132
  57.6 13.8 %collective-permute-start.4 = (bf16[2,64,896]{1,2,0:T(8,128)(2,1)}, bf16[2,64,896]{1,2,0:T(8,128)(2,1)S(1)}, u32[]{:S(2)}, u32[]{:S(2)}) collective-permute-start(bf16[2,64,896]{1,2,0:T(8,128)(2,1)} %collective-permute-done), channel_id=1, source_target_pairs={{0,1},{1,0},{2,3},{3,2},{4,5},{5,4},{6,7},{7,6},{8,9},{9,8},{10,11... | collective-permute-start | bytes 688136 | tf_op jit(solution)/shard_map/ppermute | solution.py:483
  57.8 33.2 %copy-start.6 = (bf16[224,896]{1,0:T(8,128)(2,1)}, bf16[224,896]{1,0:T(8,128)(2,1)S(1)}, u32[]{:S(2)}) copy-start(bf16[224,896]{1,0:T(8,128)(2,1)S(1)} %weight_rows.1.refs_0_) | copy-start | bytes 1204228
  57.8 13.5 %collective-permute-start.11 = (bf16[224,896]{1,0:T(8,128)(2,1)S(1)}, bf16[224,896]{1,0:T(8,128)(2,1)S(1)}, u32[]{:S(2)}, u32[]{:S(2)}) collective-permute-start(bf16[224,896]{1,0:T(8,128)(2,1)S(1)} %weight_rows.1.refs_0_), channel_id=1, source_target_pairs={{0,2},{1,3},{2,4},{3,5},{4,6},{5,7},{6,0},{7,1},{8,10},{9,11},{10,... | collective-permute-start | bytes 1204232 | tf_op jit(solution)/shard_map/ppermute | solution.py:486
  71.4 34.1 %copy-start.19 = (bf16[224,896]{1,0:T(8,128)(2,1)}, bf16[224,896]{1,0:T(8,128)(2,1)S(1)}, u32[]{:S(2)}) copy-start(bf16[224,896]{1,0:T(8,128)(2,1)S(1)} %collective-permute-done.11.refs_2_) | copy-start | bytes 1204228
  71.4 19.3 %collective-permute-start.13 = (bf16[224,896]{1,0:T(8,128)(2,1)S(1)}, bf16[224,896]{1,0:T(8,128)(2,1)S(1)}, u32[]{:S(2)}, u32[]{:S(2)}) collective-permute-start(bf16[224,896]{1,0:T(8,128)(2,1)S(1)} %collective-permute-done.11.refs_2_), channel_id=1, source_target_pairs={{0,2},{1,3},{2,4},{3,5},{4,6},{5,7},{6,0},{7,1},{8,10},{9,11},{10,... | collective-permute-start | bytes 1204232 | tf_op jit(solution)/shard_map/ppermute | solution.py:486
  71.4 0.8 copy-start.12
  72.2 7.2 %copy-start.13 = (bf16[2,64,896]{1,2,0:T(8,128)(2,1)S(1)}, bf16[2,64,896]{1,2,0:T(8,128)(2,1)}, u32[]{:S(2)}) copy-start(bf16[2,64,896]{1,2,0:T(8,128)(2,1)} %copy-done.12) | copy-start | bytes 688132
  90.7 14.8 %copy-start.15 = (bf16[224,896]{1,0:T(8,128)(2,1)}, bf16[224,896]{1,0:T(8,128)(2,1)S(1)}, u32[]{:S(2)}) copy-start(bf16[224,896]{1,0:T(8,128)(2,1)S(1)} %collective-permute-done.13.refs_4_) | copy-start | bytes 1204228
  90.7 12.9 %collective-permute-start.15 = (bf16[224,896]{1,0:T(8,128)(2,1)S(1)}, bf16[224,896]{1,0:T(8,128)(2,1)S(1)}, u32[]{:S(2)}, u32[]{:S(2)}) collective-permute-start(bf16[224,896]{1,0:T(8,128)(2,1)S(1)} %broadcast_add_fusion), channel_id=1, source_target_pairs={{0,2},{1,3},{2,4},{3,5},{4,6},{5,7},{6,0},{7,1},{8,10},{9,11},{10,... | collective-permute-start | bytes 1204232 | tf_op jit(solution)/shard_map/ppermute | solution.py:486
  91.0 12.7 %collective-permute-start.10 = (bf16[224,896]{1,0:T(8,128)(2,1)S(1)}, bf16[224,896]{1,0:T(8,128)(2,1)S(1)}, u32[]{:S(2)}, u32[]{:S(2)}) collective-permute-start(bf16[224,896]{1,0:T(8,128)(2,1)S(1)} %weight_rows.1.refs_0_), channel_id=1, source_target_pairs={{0,1},{1,0},{2,3},{3,2},{4,5},{5,4},{6,7},{7,6},{8,9},{9,8},{10,11... | collective-permute-start | bytes 1204232 | tf_op jit(solution)/shard_map/ppermute | solution.py:483
  91.1 12.6 %collective-permute-start.12 = (bf16[224,896]{1,0:T(8,128)(2,1)S(1)}, bf16[224,896]{1,0:T(8,128)(2,1)S(1)}, u32[]{:S(2)}, u32[]{:S(2)}) collective-permute-start(bf16[224,896]{1,0:T(8,128)(2,1)S(1)} %collective-permute-done.11.refs_2_), channel_id=1, source_target_pairs={{0,1},{1,0},{2,3},{3,2},{4,5},{5,4},{6,7},{7,6},{8,9},{9,8},{10,11... | collective-permute-start | bytes 1204232 | tf_op jit(solution)/shard_map/ppermute | solution.py:483
  91.6 12.2 %collective-permute-start.14 = (bf16[224,896]{1,0:T(8,128)(2,1)S(1)}, bf16[224,896]{1,0:T(8,128)(2,1)S(1)}, u32[]{:S(2)}, u32[]{:S(2)}) collective-permute-start(bf16[224,896]{1,0:T(8,128)(2,1)S(1)} %collective-permute-done.13.refs_4_), channel_id=1, source_target_pairs={{0,1},{1,0},{2,3},{3,2},{4,5},{5,4},{6,7},{7,6},{8,9},{9,8},{10,11... | collective-permute-start | bytes 1204232 | tf_op jit(solution)/shard_map/ppermute | solution.py:483
  103.7 1.7 copy-start.20
  103.7 1.7 collective-permute-start.16
  103.7 1.7 copy-start.21
  103.7 1.7 copy-start.22
  103.7 1.7 copy-start.23
  105.4 0.7 copy-start.24
  128.4 28.2 %copy-start.18 = (bf16[4,64,896]{2,1,0:T(8,128)(2,1)S(1)}, bf16[4,64,896]{2,1,0:T(8,128)(2,1)}, u32[]{:S(2)}) copy-start(bf16[4,64,896]{2,1,0:T(8,128)(2,1)} %get-tuple-element.39) | copy-start | bytes 1376260
  128.5 28.7 %copy-start = (bf16[1792,896]{1,0:T(8,128)(2,1)S(1)}, bf16[1792,896]{1,0:T(8,128)(2,1)}, u32[]{:S(2)}) copy-start(bf16[1792,896]{1,0:T(8,128)(2,1)} %get-tuple-element.42.weight_hbm) | copy-start | bytes 9633796
  128.5 28.7 %copy-start.7 = (s32[3]{0:T(128)S(1)}, s32[3]{0:T(128)}, u32[]{:S(2)}) copy-start(s32[3]{0:T(128)} %pad_add_fusion.1.place_ref) | copy-start | bytes 40
  128.5 2.7 %collective-permute-start.18 = (bf16[4,128,896]{2,1,0:T(8,128)(2,1)}, bf16[4,128,896]{2,1,0:T(8,128)(2,1)S(1)}, u32[]{:S(2)}, u32[]{:S(2)}) collective-permute-start(bf16[4,128,896]{2,1,0:T(8,128)(2,1)} %get-tuple-element.41), channel_id=1, source_target_pairs={{0,1},{1,0},{2,3},{3,2},{4,5},{5,4},{6,7},{7,6},{8,9},{9,8},{10,11... | collective-permute-start | bytes 2752520 | tf_op jit(solution)/shard_map/ppermute | solution.py:483
  132.7 30.9 %copy-start.14 = (f32[4,64,896]{2,1,0:T(8,128)S(1)}, f32[4,64,896]{2,1,0:T(8,128)}, u32[]{:S(2)}) copy-start(f32[4,64,896]{2,1,0:T(8,128)} %get-tuple-element.38) | copy-start | bytes 2752516
  132.7 10.3 %collective-permute-start.19 = (bf16[128,896]{1,0:T(8,128)(2,1)S(1)}, bf16[128,896]{1,0:T(8,128)(2,1)S(1)}, u32[]{:S(2)}, u32[]{:S(2)}) collective-permute-start(bf16[128,896]{1,0:T(8,128)(2,1)S(1)} %get-tuple-element.53), channel_id=1, source_target_pairs={{0,2},{1,3},{2,4},{3,5},{4,6},{5,7},{6,0},{7,1},{8,10},{9,11},{10,... | collective-permute-start | bytes 688136 | tf_op jit(solution)/shard_map/ppermute | solution.py:486
  132.7 13.2 %collective-permute-start.21 = (bf16[128,896]{1,0:T(8,128)(2,1)S(1)}, bf16[128,896]{1,0:T(8,128)(2,1)S(1)}, u32[]{:S(2)}, u32[]{:S(2)}) collective-permute-start(bf16[128,896]{1,0:T(8,128)(2,1)S(1)} %get-tuple-element.54), channel_id=1, source_target_pairs={{0,6},{1,7},{2,0},{3,1},{4,2},{5,3},{6,4},{7,5},{8,14},{9,15},{10,... | collective-permute-start | bytes 688136 | tf_op jit(solution)/shard_map/ppermute | solution.py:486
  136.5 28.5 %copy-start.1 = (bf16[224,512]{1,0:T(8,128)(2,1)S(1)}, bf16[224,512]{1,0:T(8,128)(2,1)}, u32[]{:S(2)}) copy-start(bf16[224,512]{1,0:T(8,128)(2,1)} %dynamic-slice_bitcast_fusion._.cols_ref) | copy-start | bytes 688132
  136.5 18.8 %collective-permute-start.20 = (bf16[128,896]{1,0:T(8,128)(2,1)S(1)}, bf16[128,896]{1,0:T(8,128)(2,1)S(1)}, u32[]{:S(2)}, u32[]{:S(2)}) collective-permute-start(bf16[128,896]{1,0:T(8,128)(2,1)S(1)} %get-tuple-element.55), channel_id=1, source_target_pairs={{0,4},{1,5},{2,6},{3,7},{4,0},{5,1},{6,2},{7,3},{8,12},{9,13},{10,... | collective-permute-start | bytes 688136 | tf_op jit(solution)/shard_map/ppermute | solution.py:486
  156.5 6.9 %collective-permute-start.22 = (bf16[128,896]{1,0:T(8,128)(2,1)S(1)}, bf16[128,896]{1,0:T(8,128)(2,1)S(1)}, u32[]{:S(2)}, u32[]{:S(2)}) collective-permute-start(bf16[128,896]{1,0:T(8,128)(2,1)S(1)} %fusion.6.sums_ref.refs_0_), channel_id=1, source_target_pairs={{0,2},{1,3},{2,0},{3,1},{4,6},{5,7},{6,4},{7,5},{8,10},{9,11},{10,... | collective-permute-start | bytes 688136 | tf_op jit(solution)/shard_map/ppermute | solution.py:535
  156.6 6.9 %collective-permute-start.17 = (bf16[4,64,896]{2,1,0:T(8,128)(2,1)S(1)}, bf16[4,64,896]{2,1,0:T(8,128)(2,1)S(1)}, u32[]{:S(2)}, u32[]{:S(2)}) collective-permute-start(bf16[4,64,896]{2,1,0:T(8,128)(2,1)S(1)} %copy-done.18), channel_id=1, source_target_pairs={{0,1},{1,0},{2,3},{3,2},{4,5},{5,4},{6,7},{7,6},{8,9},{9,8},{10,11... | collective-permute-start | bytes 1376264 | tf_op jit(solution)/shard_map/ppermute | solution.py:483
  156.7 6.9 %collective-permute-start.23 = (bf16[128,896]{1,0:T(8,128)(2,1)S(1)}, bf16[128,896]{1,0:T(8,128)(2,1)S(1)}, u32[]{:S(2)}, u32[]{:S(2)}) collective-permute-start(bf16[128,896]{1,0:T(8,128)(2,1)S(1)} %fusion.6.sums_ref.refs_0_), channel_id=1, source_target_pairs={{0,1},{1,0},{2,3},{3,2},{4,5},{5,4},{6,7},{7,6},{8,9},{9,8},{10,11... | collective-permute-start | bytes 688136 | tf_op jit(solution)/shard_map/ppermute | solution.py:483
  159.0 30.7 %copy-start.8 = (f32[4,16]{1,0:T(4,128)S(1)}, f32[4,16]{1,0:T(4,128)}, u32[]{:S(2)}) copy-start(f32[4,16]{1,0:T(4,128)} %coef_ref.3) | copy-start | bytes 772
  163.4 1.6 collective-permute-start.24
  166.0 7.9 %collective-permute-start.25 = (bf16[64,896]{1,0:T(8,128)(2,1)S(1)}, bf16[64,896]{1,0:T(8,128)(2,1)S(1)}, u32[]{:S(2)}, u32[]{:S(2)}) collective-permute-start(bf16[64,896]{1,0:T(8,128)(2,1)S(1)} %get-tuple-element.46), channel_id=1, source_target_pairs={{0,2},{1,3},{2,4},{3,5},{4,6},{5,7},{6,0},{7,1},{8,10},{9,11},{10,... | collective-permute-start | bytes 344072 | tf_op jit(solution)/shard_map/ppermute | solution.py:486
  166.4 9.0 %collective-permute-start.28 = (bf16[64,896]{1,0:T(8,128)(2,1)S(1)}, bf16[64,896]{1,0:T(8,128)(2,1)S(1)}, u32[]{:S(2)}, u32[]{:S(2)}) collective-permute-start(bf16[64,896]{1,0:T(8,128)(2,1)S(1)} %get-tuple-element.49), channel_id=1, source_target_pairs={{0,0},{1,1},{2,4},{3,5},{4,2},{5,3},{6,6},{7,7},{8,8},{9,9},{10,12... | collective-permute-start | bytes 344072 | tf_op jit(solution)/shard_map/ppermute | solution.py:548
  167.0 11.0 %collective-permute-start.29 = (bf16[64,896]{1,0:T(8,128)(2,1)S(1)}, bf16[64,896]{1,0:T(8,128)(2,1)S(1)}, u32[]{:S(2)}, u32[]{:S(2)}) collective-permute-start(bf16[64,896]{1,0:T(8,128)(2,1)S(1)} %get-tuple-element.50), channel_id=1, source_target_pairs={{0,2},{1,3},{2,6},{3,7},{4,0},{5,1},{6,4},{7,5},{8,10},{9,11},{10,... | collective-permute-start | bytes 344072 | tf_op jit(solution)/shard_map/ppermute | solution.py:548
  169.6 15.1 %collective-permute-start.32 = (bf16[224,896]{1,0:T(8,128)(2,1)S(1)}, bf16[224,896]{1,0:T(8,128)(2,1)S(1)}, u32[]{:S(2)}, u32[]{:S(2)}) collective-permute-start(bf16[224,896]{1,0:T(8,128)(2,1)S(1)} %get-tuple-element.52), channel_id=1, source_target_pairs={{0,24},{8,16},{16,8},{24,0},{1,25},{9,17},{17,9},{25,1},{2,26},{10... | collective-permute-start | bytes 1204232 | tf_op jit(solution)/shard_map/ppermute | solution.py:480
  172.1 17.5 %collective-permute-start.31 = (bf16[224,896]{1,0:T(8,128)(2,1)S(1)}, bf16[224,896]{1,0:T(8,128)(2,1)S(1)}, u32[]{:S(2)}, u32[]{:S(2)}) collective-permute-start(bf16[224,896]{1,0:T(8,128)(2,1)S(1)} %get-tuple-element.52), channel_id=1, source_target_pairs={{0,16},{8,24},{16,0},{24,8},{1,17},{9,25},{17,1},{25,9},{2,18},{10... | collective-permute-start | bytes 1204232 | tf_op jit(solution)/shard_map/ppermute | solution.py:480
  173.9 15.8 %collective-permute-start.30 = (bf16[224,896]{1,0:T(8,128)(2,1)S(1)}, bf16[224,896]{1,0:T(8,128)(2,1)S(1)}, u32[]{:S(2)}, u32[]{:S(2)}) collective-permute-start(bf16[224,896]{1,0:T(8,128)(2,1)S(1)} %get-tuple-element.52), channel_id=1, source_target_pairs={{0,8},{8,0},{16,24},{24,16},{1,9},{9,1},{17,25},{25,17},{2,10},{10... | collective-permute-start | bytes 1204232 | tf_op jit(solution)/shard_map/ppermute | solution.py:480
  175.4 8.4 %collective-permute-start.26 = (bf16[64,896]{1,0:T(8,128)(2,1)S(1)}, bf16[64,896]{1,0:T(8,128)(2,1)S(1)}, u32[]{:S(2)}, u32[]{:S(2)}) collective-permute-start(bf16[64,896]{1,0:T(8,128)(2,1)S(1)} %get-tuple-element.47), channel_id=1, source_target_pairs={{0,4},{1,5},{2,6},{3,7},{4,0},{5,1},{6,2},{7,3},{8,12},{9,13},{10,... | collective-permute-start | bytes 344072 | tf_op jit(solution)/shard_map/ppermute | solution.py:486
  178.1 5.9 %collective-permute-start.27 = (bf16[64,896]{1,0:T(8,128)(2,1)S(1)}, bf16[64,896]{1,0:T(8,128)(2,1)S(1)}, u32[]{:S(2)}, u32[]{:S(2)}) collective-permute-start(bf16[64,896]{1,0:T(8,128)(2,1)S(1)} %get-tuple-element.48), channel_id=1, source_target_pairs={{0,6},{1,7},{2,0},{3,1},{4,2},{5,3},{6,4},{7,5},{8,14},{9,15},{10,... | collective-permute-start | bytes 344072 | tf_op jit(solution)/shard_map/ppermute | solution.py:486

commit v11 on v9

--- a/solution.py
+++ b/solution.py
@@ -276,7 +276,7 @@
 
 def scale_kernel(slots, place_ref, gather_ref, radial_ref, *refs):
     block_refs = refs[:slots]
-    atoms_out, scaled_ref, token_ref, atoms_ref, cot_ref, sems = refs[slots:]
+    atoms_out, scaled_ref, token_ref, cols_ref, atoms_ref, cot_ref, sems = refs[slots:]
     step = pl.program_id(0)
     own = block_refs[0].shape[1]
     store = pltpu.make_async_copy(atoms_ref, atoms_out, sems.at[2 * slots])
@@ -294,6 +294,14 @@
         for load in loads:
             load.wait()
         store.start()
+        depth = cols_ref.shape[0]
+        device = lax.rem(2 * place_ref[1] + place_ref[2], chips)
+        for i in range(chips):
+
+            @pl.when(device == i)
+            def _():
+                own_cols = atoms_ref[:, i * depth : (i + 1) * depth].astype(F32)
+                cols_ref[...] = own_cols.T.astype(BF16)
 
     cot = jnp.dot(gather_ref[...], cot_ref[...], preferred_element_type=F32)
     scaled_ref[...] = (cot * radial_ref[...].astype(F32)).astype(BF16)
@@ -304,7 +312,7 @@
         store.wait()
 
 
-def scaled_edges(place, hot_gather, radial, blocks, tile):
+def scaled_edges(place, hot_gather, radial, depth, blocks, tile):
     edges, width = radial.shape
     atoms = hot_gather.shape[1] // 2
     slots = len(blocks)
@@ -315,6 +323,7 @@
             jax.ShapeDtypeStruct((atoms, width), BF16),
             jax.ShapeDtypeStruct((edges, width), BF16),
             jax.ShapeDtypeStruct((1, width), BF16),
+            jax.ShapeDtypeStruct((depth, atoms), BF16),
         ],
         in_specs=[
             whole_smem(),
@@ -326,6 +335,7 @@
             in_hbm(),
             pl.BlockSpec((tile, width), lambda i: (i, 0)),
             pl.BlockSpec((1, width), lambda i: (0, 0)),
+            pl.BlockSpec((depth, atoms), lambda i: (0, 0)),
         ],
         scratch_shapes=[
             pltpu.VMEM((atoms, width), BF16),
@@ -494,8 +504,9 @@
     order = (2 * z + (core ^ side)) * own + offset
     ends = jnp.concatenate([source, target])
     hot_gather, hot_sum, hot_token = hot_ends(ends.T, ends, order, pair, width, tile)
-    all_atoms, scaled, scaled_token = scaled_edges(place, hot_gather, radial[0], features, tile)
-    own_cols = lax.dynamic_slice_in_dim(all_atoms, (me_edge % chips) * depth, depth, 1).T
+    all_atoms, scaled, scaled_token, own_cols = scaled_edges(
+        place, hot_gather, radial[0], depth, features, tile
+    )
 
     got = [merged[0]] + [across(merged[k], k) for k in range(1, systems)]
     held = weight_rows(got, features[1:chips] + [hot_token])

time: 160 us -> 154 us (0.963)
  local copies, waits for them, and re-layouts: 9.75 us -> 3.67 us
  waiting for transfers between devices: 63.9 us -> 69 us
  other arithmetic: 11.5 us -> 8.22 us
    ppermute x1, waiting for transfers between devices: 0.01 us -> 4.36 us  [share(): lax.ppermute(x, 'edge', [(2 * z + c, 2 * to[z] + c) for z in range(chips)...]
    pallas_call x1 -> x0, local copies, waits for them, and re-layouts: 2.23 us -> none  [scaled_edges(): pl.pallas_call(functools.partial(scale_kernel, slots), grid=(edges // til...]
    unnamed x48, local copies, waits for them, and re-layouts: 4.53 us -> 2.32 us
    ppermute x2, starting transfers between devices: 3.91 us -> 2.26 us  [shards(): atom_grad = atom_grad + lax.ppermute(term, 'edge', pairs).astype(F32)]
    transpose x1 -> x0, local copies, waits for them, and re-layouts: 1.64 us -> none  [shards(): lax.dynamic_slice_in_dim(all_atoms, me_edge % chips * depth, depth, 1)]
  transfers between devices with their start and end apart: 33 -> 33, of which waited for: 14 -> 15; matrix products, arithmetic and copies ran while one was open for 9% -> 5% of each run, Pallas kernels for 13% -> 14%
where the time goes in v11:
time: 154 us; the launch traced here: 153 us
  waiting for transfers between devices  69 us (45%)
  Pallas kernels  47.7 us (31%)
  starting transfers between devices  23.5 us (15%)
  other arithmetic  8.22 us (5%)
  local copies, waits for them, and re-layouts  3.67 us (2%)
    ppermute x12, waiting for transfers between devices, shift(): lax.ppermute(x, 'edge', [(e, (e + 2 * k) % ways) for e in range(ways)])  43.9 us
    pallas_call x1, Pallas kernels, edge_sums(): pl.pallas_call(functools.partial(edge_kernel, chips), grid=(steps + 1,),...  22.3 us
    ppermute x12, starting transfers between devices, shift(): lax.ppermute(x, 'edge', [(e, (e + 2 * k) % ways) for e in range(ways)])  11.7 us
    ppermute x6, waiting for transfers between devices, across(): return lax.ppermute(x, 'sys', [(s, s ^ k) for s in range(systems)])  10.2 us
    pallas_call x1, Pallas kernels, scaled_edges(): pl.pallas_call(functools.partial(scale_kernel, slots), grid=(edges // til...  8.14 us
    ppermute x6, starting transfers between devices, across(): return lax.ppermute(x, 'sys', [(s, s ^ k) for s in range(systems)])  7.09 us
    ppermute x2, waiting for transfers between devices, shards(): atom_grad = atom_grad + lax.ppermute(term, 'edge', pairs).astype(F32)  6.35 us
    pallas_call x1, Pallas kernels, hot_ends(): pl.pallas_call(hot_kernel, grid=(edges // tile,), out_shape=[jax.ShapeDty...  5.65 us
  transfers between devices with their start and end apart: 33, of which 15 were waited for; matrix products, arithmetic and copies ran while one was open for 5% of the time, Pallas kernels for 14%

profile of v11, /device:TPU:0, one launch (start us, length us, event | category | flops | bytes accessed | tf_op | source)
XLA Modules:
  0.0 153.3 jit_solution(17640897484060885972)
XLA Ops:
  0.6 1.7 %join.1._.refs_0_ = bf16[2,64,896]{2,1,0:T(8,128)(2,1)} custom-call(bf16[1,64,896]{2,1,0:T(8,128)(2,1)} %atoms_ref.1, bf16[1,64,896]{2,1,0:T(8,128)(2,1)} %cot_ref.1), custom_call_target="tpu_custom_call" | custom-call | tf_op jit(solution)/shard_map/join/pallas_call | solution.py:98
  2.3 5.1 %collective-permute-start.2 = (bf16[2,64,896]{2,1,0:T(8,128)(2,1)}, bf16[2,64,896]{2,1,0:T(8,128)(2,1)S(1)}, u32[]{:S(2)}, u32[]{:S(2)}) collective-permute-start(bf16[2,64,896]{2,1,0:T(8,128)(2,1)} %join.1._.refs_0_), channel_id=1, source_target_pairs={{0,6},{1,7},{2,0},{3,1},{4,2},{5,3},{6,4},{7,5},{8,14},{9,15},{10,... | collective-permute-start | bytes 688136 | tf_op jit(solution)/shard_map/ppermute | solution.py:493
  7.4 0.6 pad_add_fusion.1.place_ref
  8.0 4.1 %merge_parts.1 = (f32[224,896]{1,0:T(8,128)}, bf16[224,896]{1,0:T(8,128)(2,1)}, bf16[224,896]{1,0:T(8,128)(2,1)}, bf16[224,896]{1,0:T(8,128)(2,1)}) custom-call(s32[3]{0:T(128)} %pad_add_fusion.1.place_ref, f32[4,16]{1,0:T(4,128)} %coef_ref.3, bf16[4,224,896]{2,1,0:T(8,128)(2,1)} %experts_ref.1, bf16[2,64,896]{2,1,0:T(8,128)(2,1)} %join.1._.refs_0_), custom_call_target="tpu_custom_call" | custom-call | tf_op jit(solution)/shard_map/merge_parts/pallas_call | solution.py:70
  12.2 1.6 %collective-permute-start.7 = (bf16[224,896]{1,0:T(8,128)(2,1)}, bf16[224,896]{1,0:T(8,128)(2,1)S(1)}, u32[]{:S(2)}, u32[]{:S(2)}) collective-permute-start(bf16[224,896]{1,0:T(8,128)(2,1)} %get-tuple-element.32), channel_id=1, source_target_pairs={{0,8},{8,0},{16,24},{24,16},{1,9},{9,1},{17,25},{25,17},{2,10},{10... | collective-permute-start | bytes 1204232 | tf_op jit(solution)/shard_map/ppermute | solution.py:487
  13.7 1.5 collective-permute-start.8
  15.3 0.5 collective-permute-start.9
  15.7 1.3 pad_add_fusion
  17.1 1.3 copy.12.cols_ref
  18.4 1.0 collective-permute-start
  19.4 0.6 fusion.28.across_ref
  20.0 0.8 fusion.13.down_ref
  20.8 5.6 %hot_ends.1 = (bf16[2048,1024]{1,0:T(8,128)(2,1)}, bf16[1024,2048]{1,0:T(8,128)(2,1)}, f32[1,896]{1,0:T(1,128)}) custom-call(s32[2048,2]{1,0:T(8,128)} %copy.12.cols_ref, s32[2,2048]{1,0:T(2,128)} %get-tuple-element.57.rows_ref, s32[1,512]{1,0:T(1,128)} %fusion.28.across_ref, s32[512,1]{1,0:T(8,128)} %fusion.13.down_ref, bf16[2,64,896]{2,1,0:T(8,128)(2,1)} %join.1._.refs_0_), custom_call_target="tpu_custom_call" | custom-call | flops 16777216 | bytes 8388608 | tf_op jit(solution)/shard_map/hot_ends/pallas_call | solution.py:249
  26.5 0.6 collective-permute-done.1.refs_2_.refs_5_
  27.1 5.9 %collective-permute-done.8.refs_2_ = bf16[224,896]{1,0:T(8,128)(2,1)S(1)} collective-permute-done((bf16[224,896]{1,0:T(8,128)(2,1)}, bf16[224,896]{1,0:T(8,128)(2,1)S(1)}, u32[]{:S(2)}, u32[]{:S(2)}) %collective-permute-start.8) | collective-permute-done | bytes 401440 | tf_op jit(solution)/shard_map/ppermute | solution.py:487
  33.0 0.7 copy-done.9
  33.7 0.2 weight_rows.1.refs_0_
  33.9 0.8 collective-permute-start.11
  34.7 0.5 collective-permute-start.6
  35.2 0.5 collective-permute-start.4
  35.7 9.7 %collective-permute-done.11.refs_2_ = bf16[224,896]{1,0:T(8,128)(2,1)S(1)} collective-permute-done((bf16[224,896]{1,0:T(8,128)(2,1)S(1)}, bf16[224,896]{1,0:T(8,128)(2,1)S(1)}, u32[]{:S(2)}, u32[]{:S(2)}) %collective-permute-start.11) | collective-permute-done | bytes 401440 | tf_op jit(solution)/shard_map/ppermute | solution.py:493
  45.5 0.6 copy-done.13
  46.1 0.1 copy-done.14
  46.2 0.1 copy-done.15
  46.3 0.1 copy-done.16
  46.4 8.1 %scaled_edges.1 = (bf16[512,896]{1,0:T(8,128)(2,1)}, bf16[2048,896]{1,0:T(8,128)(2,1)}, bf16[1,896]{1,0:T(2,128)(2,1)}, bf16[224,512]{1,0:T(8,128)(2,1)}) custom-call(s32[3]{0:T(128)} %pad_add_fusion.1.place_ref, bf16[2048,1024]{1,0:T(8,128)(2,1)} %get-tuple-element.27.gather_ref, bf16[2048,896]{1,0:T(8,128)(2,1)} %bitcast.40, ...), custom_call_target="tpu_custom_call" | custom-call | flops 1879048192 | bytes 11010048 | tf_op jit(solution)/shard_map/scaled_edges/pallas_call | solution.py:319
  54.5 0.7 reduce
  55.2 0.7 collective-permute-done.13.refs_4_
  55.9 0.9 collective-permute-start.15
  56.8 0.5 collective-permute-start.12
  57.3 8.8 %collective-permute-done.15.refs_6_ = bf16[224,896]{1,0:T(8,128)(2,1)S(1)} collective-permute-done((bf16[224,896]{1,0:T(8,128)(2,1)S(1)}, bf16[224,896]{1,0:T(8,128)(2,1)S(1)}, u32[]{:S(2)}, u32[]{:S(2)}) %collective-permute-start.15) | collective-permute-done | bytes 401440 | tf_op jit(solution)/shard_map/ppermute | solution.py:493
  66.2 1.7 %collective-permute-done.16.refs_7_ = bf16[224,896]{1,0:T(8,128)(2,1)S(1)} collective-permute-done((bf16[224,896]{1,0:T(8,128)(2,1)S(1)}, bf16[224,896]{1,0:T(8,128)(2,1)S(1)}, u32[]{:S(2)}, u32[]{:S(2)}) %collective-permute-start.16) | collective-permute-done | bytes 401440 | tf_op jit(solution)/shard_map/ppermute | solution.py:490
  67.9 0.7 copy-done.23
  68.6 22.3 %edge_sums.1 = (f32[4,128,896]{2,1,0:T(8,128)}, bf16[4,128,896]{2,1,0:T(8,128)(2,1)}, f32[4,64,896]{2,1,0:T(8,128)}, bf16[4,64,896]{2,1,0:T(8,128)(2,1)}, bf16[1792,896]{1,0:T(8,128)(2,1)}) custom-call(s32[3]{0:T(128)} %pad_add_fusion.1.place_ref, bf16[2048,1024]{1,0:T(8,128)(2,1)} %get-tuple-element.27.gather_ref, ...), custom_call_target="tpu_custom_call" | custom-call | flops 11039408128 | bytes 15728640 | tf_op jit(solution)/shard_map/edge_sums/pallas_call | solution.py:443
  90.9 0.2 collective-permute-start.18
  91.1 2.5 %collective-permute-done.18 = bf16[4,128,896]{2,1,0:T(8,128)(2,1)S(1)} collective-permute-done((bf16[4,128,896]{2,1,0:T(8,128)(2,1)}, bf16[4,128,896]{2,1,0:T(8,128)(2,1)S(1)}, u32[]{:S(2)}, u32[]{:S(2)}) %collective-permute-start.18) | collective-permute-done | bytes 917536 | tf_op jit(solution)/shard_map/ppermute | solution.py:490
  93.7 1.4 fusion.18
  95.1 0.1 collective-permute-start.19
  95.2 3.8 %collective-permute-start.21 = (bf16[128,896]{1,0:T(8,128)(2,1)S(1)}, bf16[128,896]{1,0:T(8,128)(2,1)S(1)}, u32[]{:S(2)}, u32[]{:S(2)}) collective-permute-start(bf16[128,896]{1,0:T(8,128)(2,1)S(1)} %get-tuple-element.52), channel_id=1, source_target_pairs={{0,6},{1,7},{2,0},{3,1},{4,2},{5,3},{6,4},{7,5},{8,14},{9,15},{10,... | collective-permute-start | bytes 688136 | tf_op jit(solution)/shard_map/ppermute | solution.py:493
  99.0 6.5 %collective-permute-done.19 = bf16[128,896]{1,0:T(8,128)(2,1)S(1)} collective-permute-done((bf16[128,896]{1,0:T(8,128)(2,1)S(1)}, bf16[128,896]{1,0:T(8,128)(2,1)S(1)}, u32[]{:S(2)}, u32[]{:S(2)}) %collective-permute-start.19) | collective-permute-done | bytes 229408 | tf_op jit(solution)/shard_map/ppermute | solution.py:493
  105.5 3.0 %collective-permute-done.21 = bf16[128,896]{1,0:T(8,128)(2,1)S(1)} collective-permute-done((bf16[128,896]{1,0:T(8,128)(2,1)S(1)}, bf16[128,896]{1,0:T(8,128)(2,1)S(1)}, u32[]{:S(2)}, u32[]{:S(2)}) %collective-permute-start.21) | collective-permute-done | bytes 229408 | tf_op jit(solution)/shard_map/ppermute | solution.py:493
  108.4 9.3 %collective-permute-done.20 = bf16[128,896]{1,0:T(8,128)(2,1)S(1)} collective-permute-done((bf16[128,896]{1,0:T(8,128)(2,1)S(1)}, bf16[128,896]{1,0:T(8,128)(2,1)S(1)}, u32[]{:S(2)}, u32[]{:S(2)}) %collective-permute-start.20) | collective-permute-done | bytes 229408 | tf_op jit(solution)/shard_map/ppermute | solution.py:493
  117.8 1.2 fusion.6.sums_ref.refs_0_
  118.9 0.1 collective-permute-start.22
  119.0 0.1 collective-permute-start.17
  119.1 0.5 collective-permute-start.23
  119.6 1.8 %atom_grads.1 = (bf16[64,896]{1,0:T(8,128)(2,1)S(1)}, bf16[64,896]{1,0:T(8,128)(2,1)S(1)}, bf16[1,896]{1,0:T(2,128)(2,1)S(1)}) custom-call(s32[3]{0:T(128)S(1)} %copy-done.7, bf16[128,896]{1,0:T(8,128)(2,1)S(1)} %fusion.6.sums_ref.refs_0_, bf16[1792,896]{1,0:T(8,128)(2,1)S(1)} %copy-done), custom_call_target="tpu_custom_call" | custom-call | flops 205520896 | bytes 1605632 | tf_op jit(solution)/shard_map/atom_grads/pallas_call | solution.py:178
  121.5 4.4 %collective-permute-done.22 = bf16[128,896]{1,0:T(8,128)(2,1)S(1)} collective-permute-done((bf16[128,896]{1,0:T(8,128)(2,1)S(1)}, bf16[128,896]{1,0:T(8,128)(2,1)S(1)}, u32[]{:S(2)}, u32[]{:S(2)}) %collective-permute-start.22) | collective-permute-done | bytes 229408 | tf_op jit(solution)/shard_map/ppermute | solution.py:540
  125.9 0.1 collective-permute-start.24
  126.0 0.1 fusion.26
  126.0 0.7 collective-permute-start.28
  126.7 1.6 %collective-permute-start.29 = (bf16[64,896]{1,0:T(8,128)(2,1)S(1)}, bf16[64,896]{1,0:T(8,128)(2,1)S(1)}, u32[]{:S(2)}, u32[]{:S(2)}) collective-permute-start(bf16[64,896]{1,0:T(8,128)(2,1)S(1)} %get-tuple-element.48), channel_id=1, source_target_pairs={{0,2},{1,3},{2,6},{3,7},{4,0},{5,1},{6,4},{7,5},{8,10},{9,11},{10,... | collective-permute-start | bytes 344072 | tf_op jit(solution)/shard_map/ppermute | solution.py:552
  128.3 1.0 merged_grads.1
  129.4 0.1 collective-permute-start.25
  129.4 1.4 collective-permute-start.32
  130.9 1.7 %collective-permute-start.31 = (bf16[224,896]{1,0:T(8,128)(2,1)S(1)}, bf16[224,896]{1,0:T(8,128)(2,1)S(1)}, u32[]{:S(2)}, u32[]{:S(2)}) collective-permute-start(bf16[224,896]{1,0:T(8,128)(2,1)S(1)} %get-tuple-element.50), channel_id=1, source_target_pairs={{0,16},{8,24},{16,0},{24,8},{1,17},{9,25},{17,1},{25,9},{2,18},{10... | collective-permute-start | bytes 1204232 | tf_op jit(solution)/shard_map/ppermute | solution.py:487
  132.6 0.4 collective-permute-start.30
  133.0 6.3 %collective-permute-done.29 = bf16[64,896]{1,0:T(8,128)(2,1)S(1)} collective-permute-done((bf16[64,896]{1,0:T(8,128)(2,1)S(1)}, bf16[64,896]{1,0:T(8,128)(2,1)S(1)}, u32[]{:S(2)}, u32[]{:S(2)}) %collective-permute-start.29) | collective-permute-done | bytes 114720 | tf_op jit(solution)/shard_map/ppermute | solution.py:552
  139.3 0.7 add_bitcast_fusion
  140.1 5.1 %collective-permute-done.26 = bf16[64,896]{1,0:T(8,128)(2,1)S(1)} collective-permute-done((bf16[64,896]{1,0:T(8,128)(2,1)S(1)}, bf16[64,896]{1,0:T(8,128)(2,1)S(1)}, u32[]{:S(2)}, u32[]{:S(2)}) %collective-permute-start.26) | collective-permute-done | bytes 114720 | tf_op jit(solution)/shard_map/ppermute | solution.py:493
  145.1 0.2 collective-permute-done.27
  145.4 0.7 fusion.27
  146.1 4.3 %collective-permute-done.31.refs_2_ = bf16[224,896]{1,0:T(8,128)(2,1)S(1)} collective-permute-done((bf16[224,896]{1,0:T(8,128)(2,1)S(1)}, bf16[224,896]{1,0:T(8,128)(2,1)S(1)}, u32[]{:S(2)}, u32[]{:S(2)}) %collective-permute-start.31) | collective-permute-done | bytes 401440 | tf_op jit(solution)/shard_map/ppermute | solution.py:487
  150.4 2.8 %expert_grads.1 = f32[4,224,896]{2,1,0:T(8,128)} custom-call(s32[3]{0:T(128)S(1)} %copy-done.7, f32[4,16]{1,0:T(4,128)S(1)} %copy-done.8, f32[224,896]{1,0:T(8,128)S(1)} %get-tuple-element.49.refs_0_, bf16[224,896]{1,0:T(8,128)(2,1)S(1)} %collective-permute-done.30.refs_1_, bf16[224,896]{1,0:T(8,128)(2,1)S(1)} %collective-permute-done.31.refs_2_, ...), custom_call_target="tpu_custom_call" | custom-call | tf_op jit(solution)/shard_map/expert_grads/pallas_call | solution.py:222
  (73 shorter events, 0.3 us)
Async XLA Ops:
  2.3 16.1 %collective-permute-start.2 = (bf16[2,64,896]{2,1,0:T(8,128)(2,1)}, bf16[2,64,896]{2,1,0:T(8,128)(2,1)S(1)}, u32[]{:S(2)}, u32[]{:S(2)}) collective-permute-start(bf16[2,64,896]{2,1,0:T(8,128)(2,1)} %join.1._.refs_0_), channel_id=1, source_target_pairs={{0,6},{1,7},{2,0},{3,1},{4,2},{5,3},{6,4},{7,5},{8,14},{9,15},{10,... | collective-permute-start | bytes 688136 | tf_op jit(solution)/shard_map/ppermute | solution.py:493
  7.4 19.7 %collective-permute-start.1 = (bf16[2,64,896]{2,1,0:T(8,128)(2,1)}, bf16[2,64,896]{2,1,0:T(8,128)(2,1)S(1)}, u32[]{:S(2)}, u32[]{:S(2)}) collective-permute-start(bf16[2,64,896]{2,1,0:T(8,128)(2,1)} %join.1._.refs_0_), channel_id=1, source_target_pairs={{0,4},{1,5},{2,6},{3,7},{4,0},{5,1},{6,2},{7,3},{8,12},{9,13},{10,... | collective-permute-start | bytes 688136 | tf_op jit(solution)/shard_map/ppermute | solution.py:493
  12.2 20.9 %copy-start.4 = (f32[224,896]{1,0:T(8,128)S(1)}, f32[224,896]{1,0:T(8,128)}, u32[]{:S(2)}) copy-start(f32[224,896]{1,0:T(8,128)} %get-tuple-element.31.refs_0_) | copy-start | bytes 2408452
  12.2 22.5 %copy-start.10 = (bf16[2,64,896]{2,1,0:T(8,128)(2,1)S(1)}, bf16[2,64,896]{2,1,0:T(8,128)(2,1)}, u32[]{:S(2)}) copy-start(bf16[2,64,896]{2,1,0:T(8,128)(2,1)} %join.1._.refs_0_) | copy-start | bytes 688132
  12.2 14.9 %collective-permute-start.7 = (bf16[224,896]{1,0:T(8,128)(2,1)}, bf16[224,896]{1,0:T(8,128)(2,1)S(1)}, u32[]{:S(2)}, u32[]{:S(2)}) collective-permute-start(bf16[224,896]{1,0:T(8,128)(2,1)} %get-tuple-element.32), channel_id=1, source_target_pairs={{0,8},{8,0},{16,24},{24,16},{1,9},{9,1},{17,25},{25,17},{2,10},{10... | collective-permute-start | bytes 1204232 | tf_op jit(solution)/shard_map/ppermute | solution.py:487
  13.7 19.3 %collective-permute-start.8 = (bf16[224,896]{1,0:T(8,128)(2,1)}, bf16[224,896]{1,0:T(8,128)(2,1)S(1)}, u32[]{:S(2)}, u32[]{:S(2)}) collective-permute-start(bf16[224,896]{1,0:T(8,128)(2,1)} %get-tuple-element.33), channel_id=1, source_target_pairs={{0,16},{8,24},{16,0},{24,8},{1,17},{9,25},{17,1},{25,9},{2,18},{10... | collective-permute-start | bytes 1204232 | tf_op jit(solution)/shard_map/ppermute | solution.py:487
  15.3 17.8 %collective-permute-start.9 = (bf16[224,896]{1,0:T(8,128)(2,1)}, bf16[224,896]{1,0:T(8,128)(2,1)S(1)}, u32[]{:S(2)}, u32[]{:S(2)}) collective-permute-start(bf16[224,896]{1,0:T(8,128)(2,1)} %get-tuple-element.34), channel_id=1, source_target_pairs={{0,24},{8,16},{16,8},{24,0},{1,25},{9,17},{17,9},{25,1},{2,26},{10... | collective-permute-start | bytes 1204232 | tf_op jit(solution)/shard_map/ppermute | solution.py:487
  18.4 27.1 %copy-start.1 = (bf16[2,64,896]{2,1,0:T(8,128)(2,1)}, bf16[2,64,896]{2,1,0:T(8,128)(2,1)S(1)}, u32[]{:S(2)}) copy-start(bf16[2,64,896]{2,1,0:T(8,128)(2,1)S(1)} %collective-permute-done.2.refs_3_.refs_6_) | copy-start | bytes 688132
  18.4 8.7 %collective-permute-start = (bf16[2,64,896]{2,1,0:T(8,128)(2,1)}, bf16[2,64,896]{2,1,0:T(8,128)(2,1)S(1)}, u32[]{:S(2)}, u32[]{:S(2)}) collective-permute-start(bf16[2,64,896]{2,1,0:T(8,128)(2,1)} %join.1._.refs_0_), channel_id=1, source_target_pairs={{0,2},{1,3},{2,4},{3,5},{4,6},{5,7},{6,0},{7,1},{8,10},{9,11},{10,... | collective-permute-start | bytes 688136 | tf_op jit(solution)/shard_map/ppermute | solution.py:493
  27.1 18.4 %copy-start.2 = (bf16[2,64,896]{2,1,0:T(8,128)(2,1)}, bf16[2,64,896]{2,1,0:T(8,128)(2,1)S(1)}, u32[]{:S(2)}) copy-start(bf16[2,64,896]{2,1,0:T(8,128)(2,1)S(1)} %collective-permute-done.1.refs_2_.refs_5_) | copy-start | bytes 688132
  27.1 18.4 %copy-start.3 = (bf16[2,64,896]{2,1,0:T(8,128)(2,1)}, bf16[2,64,896]{2,1,0:T(8,128)(2,1)S(1)}, u32[]{:S(2)}) copy-start(bf16[2,64,896]{2,1,0:T(8,128)(2,1)S(1)} %collective-permute-done.refs_1_.refs_4_) | copy-start | bytes 688132
  33.0 0.7 copy-start.9
  33.9 22.9 %copy-start.5 = (bf16[224,896]{1,0:T(8,128)(2,1)}, bf16[224,896]{1,0:T(8,128)(2,1)S(1)}, u32[]{:S(2)}) copy-start(bf16[224,896]{1,0:T(8,128)(2,1)S(1)} %weight_rows.1.refs_0_) | copy-start | bytes 1204228
  33.9 11.5 %collective-permute-start.11 = (bf16[224,896]{1,0:T(8,128)(2,1)S(1)}, bf16[224,896]{1,0:T(8,128)(2,1)S(1)}, u32[]{:S(2)}, u32[]{:S(2)}) collective-permute-start(bf16[224,896]{1,0:T(8,128)(2,1)S(1)} %weight_rows.1.refs_0_), channel_id=1, source_target_pairs={{0,2},{1,3},{2,4},{3,5},{4,6},{5,7},{6,0},{7,1},{8,10},{9,11},{10,... | collective-permute-start | bytes 1204232 | tf_op jit(solution)/shard_map/ppermute | solution.py:493
  34.7 10.7 %collective-permute-start.3 = (bf16[2,64,896]{2,1,0:T(8,128)(2,1)S(1)}, bf16[2,64,896]{2,1,0:T(8,128)(2,1)S(1)}, u32[]{:S(2)}, u32[]{:S(2)}) collective-permute-start(bf16[2,64,896]{2,1,0:T(8,128)(2,1)S(1)} %copy-done.10), channel_id=1, source_target_pairs={{0,1},{1,0},{2,3},{3,2},{4,5},{5,4},{6,7},{7,6},{8,9},{9,8},{10,11... | collective-permute-start | bytes 688136 | tf_op jit(solution)/shard_map/ppermute | solution.py:490
  34.7 10.7 %collective-permute-start.6 = (bf16[2,64,896]{2,1,0:T(8,128)(2,1)S(1)}, bf16[2,64,896]{2,1,0:T(8,128)(2,1)S(1)}, u32[]{:S(2)}, u32[]{:S(2)}) collective-permute-start(bf16[2,64,896]{2,1,0:T(8,128)(2,1)S(1)} %collective-permute-done.2.refs_3_.refs_6_), channel_id=1, source_target_pairs={{0,1},{1,0},{2,3},{3,2},{4,5},{5,4},{6,7},{7,6},{8,9},{9,8},{10,11... | collective-permute-start | bytes 688136 | tf_op jit(solution)/shard_map/ppermute | solution.py:490
  35.2 10.2 %collective-permute-start.5 = (bf16[2,64,896]{2,1,0:T(8,128)(2,1)S(1)}, bf16[2,64,896]{2,1,0:T(8,128)(2,1)S(1)}, u32[]{:S(2)}, u32[]{:S(2)}) collective-permute-start(bf16[2,64,896]{2,1,0:T(8,128)(2,1)S(1)} %collective-permute-done.1.refs_2_.refs_5_), channel_id=1, source_target_pairs={{0,1},{1,0},{2,3},{3,2},{4,5},{5,4},{6,7},{7,6},{8,9},{9,8},{10,11... | collective-permute-start | bytes 688136 | tf_op jit(solution)/shard_map/ppermute | solution.py:490
  35.2 10.2 %collective-permute-start.4 = (bf16[2,64,896]{2,1,0:T(8,128)(2,1)S(1)}, bf16[2,64,896]{2,1,0:T(8,128)(2,1)S(1)}, u32[]{:S(2)}, u32[]{:S(2)}) collective-permute-start(bf16[2,64,896]{2,1,0:T(8,128)(2,1)S(1)} %collective-permute-done.refs_1_.refs_4_), channel_id=1, source_target_pairs={{0,1},{1,0},{2,3},{3,2},{4,5},{5,4},{6,7},{7,6},{8,9},{9,8},{10,11... | collective-permute-start | bytes 688136 | tf_op jit(solution)/shard_map/ppermute | solution.py:490
  45.4 22.5 %copy-start.18 = (bf16[224,896]{1,0:T(8,128)(2,1)}, bf16[224,896]{1,0:T(8,128)(2,1)S(1)}, u32[]{:S(2)}) copy-start(bf16[224,896]{1,0:T(8,128)(2,1)S(1)} %collective-permute-done.11.refs_2_) | copy-start | bytes 1204228
  45.4 10.5 %collective-permute-start.13 = (bf16[224,896]{1,0:T(8,128)(2,1)S(1)}, bf16[224,896]{1,0:T(8,128)(2,1)S(1)}, u32[]{:S(2)}, u32[]{:S(2)}) collective-permute-start(bf16[224,896]{1,0:T(8,128)(2,1)S(1)} %collective-permute-done.11.refs_2_), channel_id=1, source_target_pairs={{0,2},{1,3},{2,4},{3,5},{4,6},{5,7},{6,0},{7,1},{8,10},{9,11},{10,... | collective-permute-start | bytes 1204232 | tf_op jit(solution)/shard_map/ppermute | solution.py:493
  45.4 0.7 copy-start.13
  45.4 0.8 copy-start.14
  45.4 0.8 copy-start.15
  45.5 0.9 copy-start.16
  55.9 12.0 %copy-start.12 = (bf16[224,896]{1,0:T(8,128)(2,1)}, bf16[224,896]{1,0:T(8,128)(2,1)S(1)}, u32[]{:S(2)}) copy-start(bf16[224,896]{1,0:T(8,128)(2,1)S(1)} %collective-permute-done.13.refs_4_) | copy-start | bytes 1204228
  55.9 10.2 %collective-permute-start.15 = (bf16[224,896]{1,0:T(8,128)(2,1)S(1)}, bf16[224,896]{1,0:T(8,128)(2,1)S(1)}, u32[]{:S(2)}, u32[]{:S(2)}) collective-permute-start(bf16[224,896]{1,0:T(8,128)(2,1)S(1)} %broadcast_add_fusion), channel_id=1, source_target_pairs={{0,2},{1,3},{2,4},{3,5},{4,6},{5,7},{6,0},{7,1},{8,10},{9,11},{10,... | collective-permute-start | bytes 1204232 | tf_op jit(solution)/shard_map/ppermute | solution.py:493
  56.8 9.3 %collective-permute-start.10 = (bf16[224,896]{1,0:T(8,128)(2,1)S(1)}, bf16[224,896]{1,0:T(8,128)(2,1)S(1)}, u32[]{:S(2)}, u32[]{:S(2)}) collective-permute-start(bf16[224,896]{1,0:T(8,128)(2,1)S(1)} %weight_rows.1.refs_0_), channel_id=1, source_target_pairs={{0,1},{1,0},{2,3},{3,2},{4,5},{5,4},{6,7},{7,6},{8,9},{9,8},{10,11... | collective-permute-start | bytes 1204232 | tf_op jit(solution)/shard_map/ppermute | solution.py:490
  56.8 9.3 %collective-permute-start.12 = (bf16[224,896]{1,0:T(8,128)(2,1)S(1)}, bf16[224,896]{1,0:T(8,128)(2,1)S(1)}, u32[]{:S(2)}, u32[]{:S(2)}) collective-permute-start(bf16[224,896]{1,0:T(8,128)(2,1)S(1)} %collective-permute-done.11.refs_2_), channel_id=1, source_target_pairs={{0,1},{1,0},{2,3},{3,2},{4,5},{5,4},{6,7},{7,6},{8,9},{9,8},{10,11... | collective-permute-start | bytes 1204232 | tf_op jit(solution)/shard_map/ppermute | solution.py:490
  57.3 8.8 %collective-permute-start.14 = (bf16[224,896]{1,0:T(8,128)(2,1)S(1)}, bf16[224,896]{1,0:T(8,128)(2,1)S(1)}, u32[]{:S(2)}, u32[]{:S(2)}) collective-permute-start(bf16[224,896]{1,0:T(8,128)(2,1)S(1)} %collective-permute-done.13.refs_4_), channel_id=1, source_target_pairs={{0,1},{1,0},{2,3},{3,2},{4,5},{5,4},{6,7},{7,6},{8,9},{9,8},{10,11... | collective-permute-start | bytes 1204232 | tf_op jit(solution)/shard_map/ppermute | solution.py:490
  66.1 1.7 %copy-start.19 = (bf16[224,896]{1,0:T(8,128)(2,1)}, bf16[224,896]{1,0:T(8,128)(2,1)S(1)}, u32[]{:S(2)}) copy-start(bf16[224,896]{1,0:T(8,128)(2,1)S(1)} %collective-permute-done.15.refs_6_) | copy-start | bytes 1204228
  66.1 1.7 %collective-permute-start.16 = (bf16[224,896]{1,0:T(8,128)(2,1)S(1)}, bf16[224,896]{1,0:T(8,128)(2,1)S(1)}, u32[]{:S(2)}, u32[]{:S(2)}) collective-permute-start(bf16[224,896]{1,0:T(8,128)(2,1)S(1)} %collective-permute-done.15.refs_6_), channel_id=1, source_target_pairs={{0,1},{1,0},{2,3},{3,2},{4,5},{5,4},{6,7},{7,6},{8,9},{9,8},{10,11... | collective-permute-start | bytes 1204232 | tf_op jit(solution)/shard_map/ppermute | solution.py:490
  66.1 1.7 %copy-start.20 = (bf16[224,896]{1,0:T(8,128)(2,1)}, bf16[224,896]{1,0:T(8,128)(2,1)S(1)}, u32[]{:S(2)}) copy-start(bf16[224,896]{1,0:T(8,128)(2,1)S(1)} %collective-permute-done.10.refs_1_) | copy-start | bytes 1204228
  66.2 1.7 %copy-start.21 = (bf16[224,896]{1,0:T(8,128)(2,1)}, bf16[224,896]{1,0:T(8,128)(2,1)S(1)}, u32[]{:S(2)}) copy-start(bf16[224,896]{1,0:T(8,128)(2,1)S(1)} %collective-permute-done.12.refs_3_) | copy-start | bytes 1204228
  66.2 1.7 %copy-start.22 = (bf16[224,896]{1,0:T(8,128)(2,1)}, bf16[224,896]{1,0:T(8,128)(2,1)S(1)}, u32[]{:S(2)}) copy-start(bf16[224,896]{1,0:T(8,128)(2,1)S(1)} %collective-permute-done.14.refs_5_) | copy-start | bytes 1204228
  67.9 0.8 copy-start.23
  90.9 28.1 %copy-start.17 = (bf16[4,64,896]{2,1,0:T(8,128)(2,1)S(1)}, bf16[4,64,896]{2,1,0:T(8,128)(2,1)}, u32[]{:S(2)}) copy-start(bf16[4,64,896]{2,1,0:T(8,128)(2,1)} %get-tuple-element.38) | copy-start | bytes 1376260
  90.9 28.7 %copy-start = (bf16[1792,896]{1,0:T(8,128)(2,1)S(1)}, bf16[1792,896]{1,0:T(8,128)(2,1)}, u32[]{:S(2)}) copy-start(bf16[1792,896]{1,0:T(8,128)(2,1)} %get-tuple-element.42.weight_hbm) | copy-start | bytes 9633796
  90.9 28.7 %copy-start.7 = (s32[3]{0:T(128)S(1)}, s32[3]{0:T(128)}, u32[]{:S(2)}) copy-start(s32[3]{0:T(128)} %pad_add_fusion.1.place_ref) | copy-start | bytes 40
  90.9 2.7 %collective-permute-start.18 = (bf16[4,128,896]{2,1,0:T(8,128)(2,1)}, bf16[4,128,896]{2,1,0:T(8,128)(2,1)S(1)}, u32[]{:S(2)}, u32[]{:S(2)}) collective-permute-start(bf16[4,128,896]{2,1,0:T(8,128)(2,1)} %get-tuple-element.41), channel_id=1, source_target_pairs={{0,1},{1,0},{2,3},{3,2},{4,5},{5,4},{6,7},{7,6},{8,9},{9,8},{10,11... | collective-permute-start | bytes 2752520 | tf_op jit(solution)/shard_map/ppermute | solution.py:490
  95.1 30.8 %copy-start.11 = (f32[4,64,896]{2,1,0:T(8,128)S(1)}, f32[4,64,896]{2,1,0:T(8,128)}, u32[]{:S(2)}) copy-start(f32[4,64,896]{2,1,0:T(8,128)} %get-tuple-element.37) | copy-start | bytes 2752516
  95.1 10.3 %collective-permute-start.19 = (bf16[128,896]{1,0:T(8,128)(2,1)S(1)}, bf16[128,896]{1,0:T(8,128)(2,1)S(1)}, u32[]{:S(2)}, u32[]{:S(2)}) collective-permute-start(bf16[128,896]{1,0:T(8,128)(2,1)S(1)} %get-tuple-element.51), channel_id=1, source_target_pairs={{0,2},{1,3},{2,4},{3,5},{4,6},{5,7},{6,0},{7,1},{8,10},{9,11},{10,... | collective-permute-start | bytes 688136 | tf_op jit(solution)/shard_map/ppermute | solution.py:493
  95.2 13.3 %collective-permute-start.21 = (bf16[128,896]{1,0:T(8,128)(2,1)S(1)}, bf16[128,896]{1,0:T(8,128)(2,1)S(1)}, u32[]{:S(2)}, u32[]{:S(2)}) collective-permute-start(bf16[128,896]{1,0:T(8,128)(2,1)S(1)} %get-tuple-element.52), channel_id=1, source_target_pairs={{0,6},{1,7},{2,0},{3,1},{4,2},{5,3},{6,4},{7,5},{8,14},{9,15},{10,... | collective-permute-start | bytes 688136 | tf_op jit(solution)/shard_map/ppermute | solution.py:493
  99.0 29.3 %copy-start.6 = (bf16[224,512]{1,0:T(8,128)(2,1)S(1)}, bf16[224,512]{1,0:T(8,128)(2,1)}, u32[]{:S(2)}) copy-start(bf16[224,512]{1,0:T(8,128)(2,1)} %get-tuple-element.39.cols_ref) | copy-start | bytes 688132
  99.0 18.8 %collective-permute-start.20 = (bf16[128,896]{1,0:T(8,128)(2,1)S(1)}, bf16[128,896]{1,0:T(8,128)(2,1)S(1)}, u32[]{:S(2)}, u32[]{:S(2)}) collective-permute-start(bf16[128,896]{1,0:T(8,128)(2,1)S(1)} %get-tuple-element.53), channel_id=1, source_target_pairs={{0,4},{1,5},{2,6},{3,7},{4,0},{5,1},{6,2},{7,3},{8,12},{9,13},{10,... | collective-permute-start | bytes 688136 | tf_op jit(solution)/shard_map/ppermute | solution.py:493
  118.9 6.9 %collective-permute-start.22 = (bf16[128,896]{1,0:T(8,128)(2,1)S(1)}, bf16[128,896]{1,0:T(8,128)(2,1)S(1)}, u32[]{:S(2)}, u32[]{:S(2)}) collective-permute-start(bf16[128,896]{1,0:T(8,128)(2,1)S(1)} %fusion.6.sums_ref.refs_0_), channel_id=1, source_target_pairs={{0,2},{1,3},{2,0},{3,1},{4,6},{5,7},{6,4},{7,5},{8,10},{9,11},{10,... | collective-permute-start | bytes 688136 | tf_op jit(solution)/shard_map/ppermute | solution.py:540
  119.0 6.9 %collective-permute-start.17 = (bf16[4,64,896]{2,1,0:T(8,128)(2,1)S(1)}, bf16[4,64,896]{2,1,0:T(8,128)(2,1)S(1)}, u32[]{:S(2)}, u32[]{:S(2)}) collective-permute-start(bf16[4,64,896]{2,1,0:T(8,128)(2,1)S(1)} %copy-done.17), channel_id=1, source_target_pairs={{0,1},{1,0},{2,3},{3,2},{4,5},{5,4},{6,7},{7,6},{8,9},{9,8},{10,11... | collective-permute-start | bytes 1376264 | tf_op jit(solution)/shard_map/ppermute | solution.py:490
  119.1 9.2 %collective-permute-start.23 = (bf16[128,896]{1,0:T(8,128)(2,1)S(1)}, bf16[128,896]{1,0:T(8,128)(2,1)S(1)}, u32[]{:S(2)}, u32[]{:S(2)}) collective-permute-start(bf16[128,896]{1,0:T(8,128)(2,1)S(1)} %fusion.6.sums_ref.refs_0_), channel_id=1, source_target_pairs={{0,1},{1,0},{2,3},{3,2},{4,5},{5,4},{6,7},{7,6},{8,9},{9,8},{10,11... | collective-permute-start | bytes 688136 | tf_op jit(solution)/shard_map/ppermute | solution.py:490
  119.6 30.8 %copy-start.8 = (f32[4,16]{1,0:T(4,128)S(1)}, f32[4,16]{1,0:T(4,128)}, u32[]{:S(2)}) copy-start(f32[4,16]{1,0:T(4,128)} %coef_ref.3) | copy-start | bytes 772
  125.9 2.4 %collective-permute-start.24 = (bf16[128,896]{1,0:T(8,128)(2,1)S(1)}, bf16[128,896]{1,0:T(8,128)(2,1)S(1)}, u32[]{:S(2)}, u32[]{:S(2)}) collective-permute-start(bf16[128,896]{1,0:T(8,128)(2,1)S(1)} %broadcast_add_fusion.1.refs_1_), channel_id=1, source_target_pairs={{0,1},{1,0},{2,3},{3,2},{4,5},{5,4},{6,7},{7,6},{8,9},{9,8},{10,11... | collective-permute-start | bytes 688136 | tf_op jit(solution)/shard_map/ppermute | solution.py:490
  126.0 6.6 %collective-permute-start.28 = (bf16[64,896]{1,0:T(8,128)(2,1)S(1)}, bf16[64,896]{1,0:T(8,128)(2,1)S(1)}, u32[]{:S(2)}, u32[]{:S(2)}) collective-permute-start(bf16[64,896]{1,0:T(8,128)(2,1)S(1)} %get-tuple-element.47), channel_id=1, source_target_pairs={{0,0},{1,1},{2,4},{3,5},{4,2},{5,3},{6,6},{7,7},{8,8},{9,9},{10,12... | collective-permute-start | bytes 344072 | tf_op jit(solution)/shard_map/ppermute | solution.py:552
  126.7 12.6 %collective-permute-start.29 = (bf16[64,896]{1,0:T(8,128)(2,1)S(1)}, bf16[64,896]{1,0:T(8,128)(2,1)S(1)}, u32[]{:S(2)}, u32[]{:S(2)}) collective-permute-start(bf16[64,896]{1,0:T(8,128)(2,1)S(1)} %get-tuple-element.48), channel_id=1, source_target_pairs={{0,2},{1,3},{2,6},{3,7},{4,0},{5,1},{6,4},{7,5},{8,10},{9,11},{10,... | collective-permute-start | bytes 344072 | tf_op jit(solution)/shard_map/ppermute | solution.py:552
  129.4 10.0 %collective-permute-start.25 = (bf16[64,896]{1,0:T(8,128)(2,1)S(1)}, bf16[64,896]{1,0:T(8,128)(2,1)S(1)}, u32[]{:S(2)}, u32[]{:S(2)}) collective-permute-start(bf16[64,896]{1,0:T(8,128)(2,1)S(1)} %get-tuple-element.44), channel_id=1, source_target_pairs={{0,2},{1,3},{2,4},{3,5},{4,6},{5,7},{6,0},{7,1},{8,10},{9,11},{10,... | collective-permute-start | bytes 344072 | tf_op jit(solution)/shard_map/ppermute | solution.py:493
  129.4 16.6 %collective-permute-start.32 = (bf16[224,896]{1,0:T(8,128)(2,1)S(1)}, bf16[224,896]{1,0:T(8,128)(2,1)S(1)}, u32[]{:S(2)}, u32[]{:S(2)}) collective-permute-start(bf16[224,896]{1,0:T(8,128)(2,1)S(1)} %get-tuple-element.50), channel_id=1, source_target_pairs={{0,24},{8,16},{16,8},{24,0},{1,25},{9,17},{17,9},{25,1},{2,26},{10... | collective-permute-start | bytes 1204232 | tf_op jit(solution)/shard_map/ppermute | solution.py:487
  130.9 19.5 %collective-permute-start.31 = (bf16[224,896]{1,0:T(8,128)(2,1)S(1)}, bf16[224,896]{1,0:T(8,128)(2,1)S(1)}, u32[]{:S(2)}, u32[]{:S(2)}) collective-permute-start(bf16[224,896]{1,0:T(8,128)(2,1)S(1)} %get-tuple-element.50), channel_id=1, source_target_pairs={{0,16},{8,24},{16,0},{24,8},{1,17},{9,25},{17,1},{25,9},{2,18},{10... | collective-permute-start | bytes 1204232 | tf_op jit(solution)/shard_map/ppermute | solution.py:487
  132.6 17.8 %collective-permute-start.30 = (bf16[224,896]{1,0:T(8,128)(2,1)S(1)}, bf16[224,896]{1,0:T(8,128)(2,1)S(1)}, u32[]{:S(2)}, u32[]{:S(2)}) collective-permute-start(bf16[224,896]{1,0:T(8,128)(2,1)S(1)} %get-tuple-element.50), channel_id=1, source_target_pairs={{0,8},{8,0},{16,24},{24,16},{1,9},{9,1},{17,25},{25,17},{2,10},{10... | collective-permute-start | bytes 1204232 | tf_op jit(solution)/shard_map/ppermute | solution.py:487
  139.3 5.8 %collective-permute-start.26 = (bf16[64,896]{1,0:T(8,128)(2,1)S(1)}, bf16[64,896]{1,0:T(8,128)(2,1)S(1)}, u32[]{:S(2)}, u32[]{:S(2)}) collective-permute-start(bf16[64,896]{1,0:T(8,128)(2,1)S(1)} %get-tuple-element.45), channel_id=1, source_target_pairs={{0,4},{1,5},{2,6},{3,7},{4,0},{5,1},{6,2},{7,3},{8,12},{9,13},{10,... | collective-permute-start | bytes 344072 | tf_op jit(solution)/shard_map/ppermute | solution.py:493
  139.3 6.0 %collective-permute-start.27 = (bf16[64,896]{1,0:T(8,128)(2,1)S(1)}, bf16[64,896]{1,0:T(8,128)(2,1)S(1)}, u32[]{:S(2)}, u32[]{:S(2)}) collective-permute-start(bf16[64,896]{1,0:T(8,128)(2,1)S(1)} %get-tuple-element.46), channel_id=1, source_target_pairs={{0,6},{1,7},{2,0},{3,1},{4,2},{5,3},{6,4},{7,5},{8,14},{9,15},{10,... | collective-permute-start | bytes 344072 | tf_op jit(solution)/shard_map/ppermute | solution.py:493
